TPU v7x, 32 devices: a whole 2x2x4 slice. The times are simulated.
32 devices in a mesh: grp: 4 (over z), exp: 8 (over y, x, core).
Axes of the slice: x: 2, y: 2, z: 4, core: 2. Of those that a mesh axis runs over, the one named last changes fastest.
Arguments:
- tokens: bfloat16 [32768, 1024], P(('grp', 'exp')), may hold values from -6 to 6
- cotangent: bfloat16 [32768, 1024], P(('grp', 'exp')), may hold values from -6 to 6
- arrival: int32 [32, 1024], P(('grp', 'exp')), may hold values from 0 to 1023, each once within a row
- seq_length: int32 [32], P(('grp', 'exp')), may hold values from 256 to 1024, as said below
- w_q: bfloat16 [1024, 1024], P(('grp', 'exp')), may hold values from -0.1875 to 0.1875
- w_k: bfloat16 [1024, 1024], P(('grp', 'exp')), may hold values from -0.1875 to 0.1875
- w_v: bfloat16 [1024, 1024], P(('grp', 'exp')), may hold values from -0.1875 to 0.1875
- w_o: bfloat16 [1024, 1024], P(('grp', 'exp')), may hold values from -1.5 to 1.5
- ln1_gain: bfloat16 [1024], P(('grp', 'exp')), may hold values from 0.5 to 1.5
- ln1_bias: bfloat16 [1024], P(('grp', 'exp')), may hold values from -1 to 1
- ln2_gain: bfloat16 [1024], P(('grp', 'exp')), may hold values from 0.5 to 1.5
- ln2_bias: bfloat16 [1024], P(('grp', 'exp')), may hold values from -1 to 1
- w_in: bfloat16 [8, 1024, 4096], P('exp'), may hold values from -0.1875 to 0.1875
- w_out: bfloat16 [8, 1024, 4096], P('exp'), may hold values from -0.09375 to 0.09375
Outputs:
- output: bfloat16 [32768, 1024], P(('grp', 'exp'))
- grad_x: bfloat16 [32768, 1024], P(('grp', 'exp'))
- grad_w_q: float32 [1024, 1024], P(('grp', 'exp'))
- grad_w_k: float32 [1024, 1024], P(('grp', 'exp'))
- grad_w_v: float32 [1024, 1024], P(('grp', 'exp'))
- grad_w_o: float32 [1024, 1024], P(('grp', 'exp'))
- grad_ln1_gain: float32 [1024], P(('grp', 'exp'))
- grad_ln1_bias: float32 [1024], P(('grp', 'exp'))
- grad_ln2_gain: float32 [1024], P(('grp', 'exp'))
- grad_ln2_bias: float32 [1024], P(('grp', 'exp'))
- grad_w_in: float32 [8, 1024, 4096], P('exp', None, 'grp')
- grad_w_out: float32 [8, 1024, 4096], P('exp', None, 'grp')
Inputs may be any that keep to these rules, and one draw needn't show every extreme that they name: `seq_length`: each entry is 256 or 1024; every group has slots of both kinds.
All inputs are finite; a program needn't handle non-finite values.
Results may differ from a plain program's by a relative error of at most 0.013.
Values may be sent and summed in bfloat16 or wider, within the bound.
No kernel may reach another device: no remote copies, remote signals or barrier semaphores. Data moves between devices by JAX's collectives and lax.ppermute only.
A program may use at most 320 MiB of HBM per device.

v0:
```python
from functools import partial

import jax
import jax.numpy as jnp
from jax import lax
from jax.sharding import PartitionSpec as P

HEADS = 16
HDIM = 64


EPSILON = 1e-05
NEG_FILL = -1e30


def norm_rows(inputs):
    average = jnp.mean(inputs, -1, keepdims=True)
    centred = inputs - average
    inverse = lax.rsqrt(jnp.mean(centred * centred, -1, keepdims=True) + EPSILON)
    return (centred * inverse, inverse)


def norm_back(grad_in, normed, inverse, scaling):
    scaled = grad_in * scaling
    return inverse * (
        scaled
        - jnp.mean(scaled, -1, keepdims=True)
        - normed * jnp.mean(scaled * normed, -1, keepdims=True)
    )


def contract_rows(left_mat, right_mat):
    return lax.dot_general(
        left_mat, right_mat, (((0,), (0,)), ((), ())), preferred_element_type=jnp.float32
    )


def contract_cols(left_mat, right_mat):
    return lax.dot_general(
        left_mat, right_mat, (((1,), (1,)), ((), ())), preferred_element_type=jnp.float32
    )


def key_range(block_num, qblock, is_long):
    if is_long:
        return (0, (block_num + 1) * qblock)
    return (block_num * qblock, qblock)


def block_scores(q_block, k_part, q_start, k_start, seq_len):
    scores = jnp.einsum(
        "qhd,khd->hqk", q_block, k_part, preferred_element_type=jnp.float32
    ) * HDIM ** (-0.5)
    q_pos = q_start + jnp.arange(q_block.shape[0], dtype=jnp.int32)
    k_pos = k_start + jnp.arange(k_part.shape[0], dtype=jnp.int32)
    allowed = (k_pos[None, :] <= q_pos[:, None]) & (
        k_pos[None, :] // seq_len == q_pos[:, None] // seq_len
    )
    return jnp.where(allowed[None], scores, NEG_FILL)


def attend_block(block_num, qblock, is_long, queries, key_rows, val_rows, seq_len):
    key_start, key_count = key_range(block_num, qblock, is_long)
    q_block = queries[block_num * qblock : (block_num + 1) * qblock]
    k_part = key_rows[key_start : key_start + key_count]
    v_part = val_rows[key_start : key_start + key_count]
    scores = block_scores(q_block, k_part, block_num * qblock, key_start, seq_len)
    row_max = jnp.max(scores, -1, keepdims=True)
    exp_scores = jnp.exp(scores - row_max)
    row_sum = jnp.sum(exp_scores, -1, keepdims=True)
    soft_probs = exp_scores / row_sum
    attn_part = jnp.einsum(
        "hqk,khd->qhd", soft_probs.astype(jnp.bfloat16), v_part, preferred_element_type=jnp.float32
    )
    return (attn_part, row_max, row_sum)


def attend_back(
    block_num, qblock, is_long, queries, key_rows, val_rows, grad_attn, row_max, row_sum, seq_len
):
    key_start, key_count = key_range(block_num, qblock, is_long)
    tok_rows = key_rows.shape[0]
    q_block = queries[block_num * qblock : (block_num + 1) * qblock]
    g_block = grad_attn[block_num * qblock : (block_num + 1) * qblock]
    k_part = key_rows[key_start : key_start + key_count]
    v_part = val_rows[key_start : key_start + key_count]
    scores = block_scores(q_block, k_part, block_num * qblock, key_start, seq_len)
    soft_probs = jnp.exp(scores - row_max) / row_sum
    grad_probs = jnp.einsum("qhd,khd->hqk", g_block, v_part, preferred_element_type=jnp.float32)
    grad_v = jnp.einsum(
        "hqk,qhd->khd", soft_probs.astype(jnp.bfloat16), g_block, preferred_element_type=jnp.float32
    )
    row_delta = jnp.sum(soft_probs * grad_probs, -1, keepdims=True)
    grad_scores = (soft_probs * (grad_probs - row_delta)).astype(jnp.bfloat16)
    grad_q = jnp.einsum(
        "hqk,khd->qhd", grad_scores, k_part, preferred_element_type=jnp.float32
    ) * HDIM ** (-0.5)
    grad_k = jnp.einsum(
        "hqk,qhd->khd", grad_scores, q_block, preferred_element_type=jnp.float32
    ) * HDIM ** (-0.5)
    padding = ((key_start, tok_rows - key_start - key_count), (0, 0), (0, 0))
    return (grad_q, jnp.pad(grad_k, padding), jnp.pad(grad_v, padding))


def local(
    tokens,
    cotangent,
    arrival,
    seq_length,
    w_q,
    w_k,
    w_v,
    w_o,
    ln1_gain,
    ln1_bias,
    ln2_gain,
    ln2_bias,
    w_in,
    w_out,
):
    shared = (w_q, w_k, w_v, w_o, ln1_gain, ln1_bias, ln2_gain, ln2_bias)
    gathered = (
        lax.all_gather(shared[0], ("grp", "exp"), axis=0, tiled=True),
        lax.all_gather(shared[1], ("grp", "exp"), axis=0, tiled=True),
        lax.all_gather(shared[2], ("grp", "exp"), axis=0, tiled=True),
        lax.all_gather(shared[3], ("grp", "exp"), axis=0, tiled=True),
        lax.all_gather(shared[4], ("grp", "exp"), axis=0, tiled=True),
        lax.all_gather(shared[5], ("grp", "exp"), axis=0, tiled=True),
        lax.all_gather(shared[6], ("grp", "exp"), axis=0, tiled=True),
        lax.all_gather(shared[7], ("grp", "exp"), axis=0, tiled=True),
    )
    tok_rows = tokens.shape[0]
    width_all = tokens.shape[1]
    qblock = min(512, tok_rows)
    blocks = tok_rows // qblock
    row_order = arrival[0]
    lookup = (
        jnp.zeros((tok_rows,), jnp.int32).at[row_order].set(jnp.arange(tok_rows, dtype=jnp.int32))
    )
    seq_len = seq_length[0]
    arrived = lax.all_to_all(tokens, "exp", split_axis=0, concat_axis=0, tiled=True)
    seq_in = arrived[row_order].astype(jnp.float32)
    normed_one, inverse_one = norm_rows(seq_in)
    gain_one = gathered[4].astype(jnp.float32)
    bias_one = gathered[5].astype(jnp.float32)
    gain_two = gathered[6].astype(jnp.float32)
    bias_two = gathered[7].astype(jnp.float32)
    ln_one = (normed_one * gain_one + bias_one).astype(jnp.bfloat16)
    queries = (
        jnp.dot(ln_one, gathered[0], preferred_element_type=jnp.float32)
        .astype(jnp.bfloat16)
        .reshape(tok_rows, HEADS, HDIM)
    )
    key_rows = (
        jnp.dot(ln_one, gathered[1], preferred_element_type=jnp.float32)
        .astype(jnp.bfloat16)
        .reshape(tok_rows, HEADS, HDIM)
    )
    val_rows = (
        jnp.dot(ln_one, gathered[2], preferred_element_type=jnp.float32)
        .astype(jnp.bfloat16)
        .reshape(tok_rows, HEADS, HDIM)
    )
    pieces = []
    for block_num in range(blocks):
        pieces.append(
            lax.cond(
                seq_len > qblock,
                partial(attend_block, block_num, qblock, True),
                partial(attend_block, block_num, qblock, False),
                queries,
                key_rows,
                val_rows,
                seq_len,
            )
        )
    attn_low = (
        jnp.concatenate([part_out[0] for part_out in pieces], 0)
        .reshape(tok_rows, width_all)
        .astype(jnp.bfloat16)
    )
    mixed_rows = seq_in + jnp.dot(attn_low, gathered[3], preferred_element_type=jnp.float32)
    leaving = mixed_rows.astype(jnp.bfloat16)[lookup]
    expert_in = lax.all_to_all(leaving, "exp", split_axis=0, concat_axis=0, tiled=True)
    resid_two = expert_in.astype(jnp.float32)
    normed_two, inverse_two = norm_rows(resid_two)
    ln_two = (normed_two * gain_two + bias_two).astype(jnp.bfloat16)
    w_first = w_in[0]
    w_second = w_out[0]
    pre_act = jnp.dot(ln_two, w_first, preferred_element_type=jnp.float32)
    act_low = jax.nn.gelu(pre_act).astype(jnp.bfloat16)
    output = (resid_two + contract_cols(act_low, w_second)).astype(jnp.bfloat16)
    grad_w_out = contract_rows(cotangent, act_low)
    grad_act = jnp.dot(cotangent, w_second, preferred_element_type=jnp.float32)
    grad_pre = jax.vjp(jax.nn.gelu, pre_act)[1](grad_act)[0].astype(jnp.bfloat16)
    grad_w_in = contract_rows(ln_two, grad_pre)
    grad_ln_two = contract_cols(grad_pre, w_first)
    grad_gain_two = jnp.sum(grad_ln_two * normed_two, 0)
    grad_bias_two = jnp.sum(grad_ln_two, 0)
    grad_expert = (
        cotangent.astype(jnp.float32) + norm_back(grad_ln_two, normed_two, inverse_two, gain_two)
    ).astype(jnp.bfloat16)
    grad_arrived = lax.all_to_all(grad_expert, "exp", split_axis=0, concat_axis=0, tiled=True)
    grad_mixed = grad_arrived[row_order]
    grad_w_o = contract_rows(attn_low, grad_mixed)
    grad_attn = (
        contract_cols(grad_mixed, gathered[3]).astype(jnp.bfloat16).reshape(tok_rows, HEADS, HDIM)
    )
    grad_q_parts = []
    grad_k_sum = jnp.zeros((tok_rows, HEADS, HDIM), jnp.float32)
    grad_v_sum = jnp.zeros((tok_rows, HEADS, HDIM), jnp.float32)
    for block_num in range(blocks):
        part_out = pieces[block_num]
        result = lax.cond(
            seq_len > qblock,
            partial(attend_back, block_num, qblock, True),
            partial(attend_back, block_num, qblock, False),
            queries,
            key_rows,
            val_rows,
            grad_attn,
            part_out[1],
            part_out[2],
            seq_len,
        )
        grad_q_parts.append(result[0])
        grad_k_sum = grad_k_sum + result[1]
        grad_v_sum = grad_v_sum + result[2]
    grad_q = jnp.concatenate(grad_q_parts, 0).reshape(tok_rows, width_all).astype(jnp.bfloat16)
    grad_k = grad_k_sum.reshape(tok_rows, width_all).astype(jnp.bfloat16)
    grad_v = grad_v_sum.reshape(tok_rows, width_all).astype(jnp.bfloat16)
    grad_w_q = contract_rows(ln_one, grad_q)
    grad_w_k = contract_rows(ln_one, grad_k)
    grad_w_v = contract_rows(ln_one, grad_v)
    grad_ln_one = (
        contract_cols(grad_q, gathered[0])
        + contract_cols(grad_k, gathered[1])
        + contract_cols(grad_v, gathered[2])
    )
    grad_gain_one = jnp.sum(grad_ln_one * normed_one, 0)
    grad_bias_one = jnp.sum(grad_ln_one, 0)
    gain_back = gathered[4].astype(jnp.float32)
    grad_seq = (
        grad_mixed.astype(jnp.float32) + norm_back(grad_ln_one, normed_one, inverse_one, gain_back)
    ).astype(jnp.bfloat16)
    grad_tokens = lax.all_to_all(grad_seq[lookup], "exp", split_axis=0, concat_axis=0, tiled=True)
    grad_terms = (
        grad_w_q,
        grad_w_k,
        grad_w_v,
        grad_w_o,
        grad_gain_one,
        grad_bias_one,
        grad_gain_two,
        grad_bias_two,
    )
    summed = (
        lax.psum_scatter(grad_terms[0], ("grp", "exp"), scatter_dimension=0, tiled=True),
        lax.psum_scatter(grad_terms[1], ("grp", "exp"), scatter_dimension=0, tiled=True),
        lax.psum_scatter(grad_terms[2], ("grp", "exp"), scatter_dimension=0, tiled=True),
        lax.psum_scatter(grad_terms[3], ("grp", "exp"), scatter_dimension=0, tiled=True),
        lax.psum_scatter(grad_terms[4], ("grp", "exp"), scatter_dimension=0, tiled=True),
        lax.psum_scatter(grad_terms[5], ("grp", "exp"), scatter_dimension=0, tiled=True),
        lax.psum_scatter(grad_terms[6], ("grp", "exp"), scatter_dimension=0, tiled=True),
        lax.psum_scatter(grad_terms[7], ("grp", "exp"), scatter_dimension=0, tiled=True),
    )
    expert_sums = (
        lax.psum_scatter(
            grad_w_in[None].astype(jnp.bfloat16), "grp", scatter_dimension=2, tiled=True
        ).astype(jnp.float32),
        lax.psum_scatter(
            grad_w_out[None].astype(jnp.bfloat16), "grp", scatter_dimension=2, tiled=True
        ).astype(jnp.float32),
    )
    first_sum = expert_sums[0]
    second_sum = expert_sums[1]
    return (
        output,
        grad_tokens,
        summed[0],
        summed[1],
        summed[2],
        summed[3],
        summed[4],
        summed[5],
        summed[6],
        summed[7],
        first_sum,
        second_sum,
    )


def solution(mesh):
    in_specs = (
        P(("grp", "exp"), None),
        P(("grp", "exp"), None),
        P(("grp", "exp"), None),
        P(("grp", "exp")),
        P(("grp", "exp"), None),
        P(("grp", "exp"), None),
        P(("grp", "exp"), None),
        P(("grp", "exp"), None),
        P(("grp", "exp")),
        P(("grp", "exp")),
        P(("grp", "exp")),
        P(("grp", "exp")),
        P("exp", None, None),
        P("exp", None, None),
    )
    out_specs = (
        P(("grp", "exp"), None),
        P(("grp", "exp"), None),
        P(("grp", "exp"), None),
        P(("grp", "exp"), None),
        P(("grp", "exp"), None),
        P(("grp", "exp"), None),
        P(("grp", "exp")),
        P(("grp", "exp")),
        P(("grp", "exp")),
        P(("grp", "exp")),
        P("exp", None, "grp"),
        P("exp", None, "grp"),
    )
    return jax.shard_map(local, mesh=mesh, in_specs=in_specs, out_specs=out_specs, check_vma=False)
```

profile of v0, /device:TPU:0, one launch (start us, length us, event | category | flops | bytes accessed | tf_op | source)
XLA Modules:
  0.0 1229.9 jit_solution(4755881826180016045)
XLA Ops:
  9.4 5.2 all-to-all-start
  16.8 58.6 %all-reduce.15 = (bf16[1024]{0:T(1024)(128)(2,1)S(1)}, bf16[1024]{0:T(1024)(128)(2,1)S(1)}, bf16[1024]{0:T(1024)(128)(2,1)}, bf16[1024]{0:T(1024)(128)(2,1)}) all-reduce(bf16[1024]{0:T(1024)(128)(2,1)S(1)} %dynamic-update-slice.1, bf16[1024]{0:T(1024)(128)(2,1)S(1)} %dynamic-update-slice, ...), channel_id=1, replica_groups=mesh['grp'=4,'exp'=8] {'grp','exp'}, use_global_device_ids=true, to_apply=%add.7 | all-reduce | flops 4096 | bytes 16384
  80.9 5.3 gather_fusion
  90.7 5.7 convolution_convert_fusion.1
  96.4 36.0 %all-gather.7.cloned.1.call-done = bf16[1024,1024]{1,0:T(8,128)(2,1)} async-done(((bf16[32,1024]{1,0:T(8,128)(2,1)}), bf16[1024,1024]{1,0:T(8,128)(2,1)}) %all-gather.7.cloned.1.call-update) | async-done | bytes 2097168 | tf_op jit(solution)/shard_map/all_gather | solution.py:124
  132.4 4.9 convolution_convert_fusion.2
  137.4 53.2 %all-gather.5.cloned.1.call-done = bf16[1024,1024]{1,0:T(8,128)(2,1)} async-done(((bf16[32,1024]{1,0:T(8,128)(2,1)}), bf16[1024,1024]{1,0:T(8,128)(2,1)}) %all-gather.5.cloned.1.call-update) | async-done | bytes 2097168 | tf_op jit(solution)/shard_map/all_gather | solution.py:123
  190.6 6.3 convolution_convert_fusion.3
  196.8 54.8 %conditional.5 = (f32[16,512,1]{1,0,2:T(8,128)}, f32[16,512,1]{1,0,2:T(8,128)}, bf16[512,16,64]{0,2,1:T(8,128)(2,1)S(1)}) conditional(s32[]{:T(128)} %convert_element_type.166, (s32[]{:T(128)}, bf16[1024,16,64]{0,2,1:T(8,128)(2,1)}, bf16[1024,16,64]{0,2,1:T(8,128)(2,1)S(1)}, bf16[1024,16,64]{0,2,1:T(8,128)(2,1)}) %tuple.129, (s32[]{:T(128)}, ...), branch_computations={%region_8.11_spmd, %region_11.14_spmd} | conditional | flops 2250240512 | bytes 117620816 | solution.py:167
  205.4 16.0 %fusion.38 = (f32[16,512]{1,0:T(8,128)}, f32[16,512,1024]{2,1,0:T(8,128)}) fusion(pred[512,1024]{1,0:T(8,128)(4,1)S(1)} %fusion.41, bf16[1024,16,64]{0,2,1:T(8,128)(2,1)S(1)} %get-tuple-element.102, bf16[1024,16,64]{0,2,1:T(8,128)(2,1)} %get-tuple-element.101), kind=kOutput, calls=%fused_computation.68 | convolution fusion | flops 1098899456 | bytes 37257216 | tf_op jit(solution)/shard_map/cond/branch_1_fun/qhd,khd->hqk/dot_general | solution.py:51
  221.4 15.7 %fusion.39 = f32[16,512]{1,0:T(8,128)} fusion(f32[16,512,1024]{2,1,0:T(8,128)} %get-tuple-element.233, f32[16,512]{1,0:T(8,128)} %get-tuple-element.232, pred[512,1024]{1,0:T(8,128)(4,1)S(1)} %fusion.41), kind=kLoop, calls=%fused_computation.69 | loop fusion | flops 33546240 | bytes 34144256 | tf_op jit(solution)/shard_map/cond/branch_1_fun/reduce_sum | solution.py:70
  237.1 14.6 %fusion.43 = bf16[512,16,64]{0,2,1:T(8,128)(2,1)S(1)} fusion(bf16[1024,16,64]{0,2,1:T(8,128)(2,1)S(1)} %copy-done.20, f32[16,512,1024]{2,1,0:T(8,128)} %get-tuple-element.233, f32[16,512]{1,0:T(8,128)} %fusion.39, f32[16,512]{1,0:T(8,128)} %get-tuple-element.232, pred[512,1024]{1,0:T(8,128)(4,1)S(1)} %fusion.41), kind=kOutput, calls=%fused_computation.74 | convolution fusion | flops 1116209152 | bytes 37289984 | tf_op jit(solution)/shard_map/cond/branch_1_fun/hqk,khd->qhd/dot_general | solution.py:72
  251.6 37.1 %conditional.4 = (f32[16,512,1]{1,0,2:T(8,128)}, f32[16,512,1]{1,0,2:T(8,128)}, bf16[512,16,64]{0,2,1:T(8,128)(2,1)S(1)}) conditional(s32[]{:T(128)} %convert_element_type.166, (s32[]{:T(128)}, bf16[1024,16,64]{0,2,1:T(8,128)(2,1)}, bf16[1024,16,64]{0,2,1:T(8,128)(2,1)S(1)}, bf16[1024,16,64]{0,2,1:T(8,128)(2,1)}) %tuple.131, (s32[]{:T(128)}, ...), branch_computations={%region_2.5_spmd, %region_5.8_spmd} | conditional | flops 1125371904 | bytes 64131140 | solution.py:167
  261.5 9.0 fusion.13
  270.6 9.9 fusion.14
  280.5 8.2 fusion.17
  290.4 5.2 fusion.143
  295.6 5.3 gather_fusion.1
  305.0 26.3 %all-to-all-done.1 = bf16[8,128,1024]{2,1,0:T(8,128)(2,1)S(1)} async-done(((bf16[8,128,1024]{2,1,0:T(8,128)(2,1)}), bf16[8,128,1024]{2,1,0:T(8,128)(2,1)S(1)}, u32[]{:S(2)}, u32[]{:S(2)}) %all-to-all-start.1) | async-done | bytes 2097184 | tf_op jit(solution)/shard_map/all_to_all | solution.py:184
  333.2 14.6 %fusion.124 = f32[1024,4096]{1,0:T(8,128)} fusion(bf16[1024,1024]{1,0:T(8,128)(2,1)S(1)} %bitcast.206, bf16[1,1024,4096]{2,1,0:T(8,128)(2,1)} %param.34), kind=kOutput, calls=%fused_computation.198 | convolution fusion | flops 8589934592 | bytes 27262976 | tf_op jit(solution)/shard_map/dot_general | solution.py:190
  347.8 17.5 %convert_bitcast_fusion = bf16[1,1024,4096]{1,2,0:T(8,128)(2,1)} fusion(bf16[1024,1024]{1,0:T(8,128)(2,1)S(1)} %copy-done.30, f32[1024,4096]{1,0:T(8,128)} %fusion.124), kind=kOutput, calls=%fused_computation.200 | convolution fusion | flops 8631877632 | bytes 27262976 | tf_op jit(solution)/shard_map/dot_general | solution.py:33
  365.5 25.3 %fusion.117 = bf16[1024,4096]{1,0:T(8,128)(2,1)} fusion(f32[1024,4096]{1,0:T(8,128)} %fusion.124, bf16[1024,1024]{1,0:T(8,128)(2,1)} %param.23, bf16[1,1024,4096]{2,1,0:T(8,128)(2,1)} %param.35), kind=kOutput, calls=%fused_computation.190 | convolution fusion | flops 8673820672 | bytes 35651584 | tf_op jit(solution)/shard_map/dot_general | solution.py:194
  390.9 17.9 %fusion.161 = (f32[1024]{0:T(1024)}, f32[1024]{0:T(1024)S(1)}, f32[1024]{0:T(1024)S(1)}, f32[1024]{0:T(1024)}, bf16[1024,1024]{1,0:T(8,128)(2,1)S(1)}, /*index=5*/f32[1024,1024]{1,0:T(8,128)}) fusion(bf16[8,128,1024]{2,1,0:T(8,128)(2,1)S(1)} %all-to-all-done.1, f32[1024]{0:T(1024)S(1)} %get-tuple-element.251, f32[1024]{0:T(1024)S(1)} %get-tuple-element.249, ...), kind=kOutput, calls=%fused_computation.242 | convolution fusion | flops 8603561984 | bytes 25198592 | tf_op jit(solution)/shard_map/dot_general | solution.py:39
  408.8 11.3 convert_bitcast_fusion.1
  424.0 29.2 %all_to_all.45 = bf16[8,128,1024]{2,1,0:T(8,128)(2,1)S(1)} all-to-all(bf16[8,128,1024]{2,1,0:T(8,128)(2,1)S(1)} %bitcast.196), channel_id=1, replica_groups=mesh['grp'=4,'exp'=8] {'exp'}, dimensions={0} | all-to-all | bytes 4194304 | tf_op jit(solution)/shard_map/all_to_all | solution.py:203
  453.2 5.4 gather_fusion.2
  458.6 6.5 fusion.182
  465.2 6.2 convolution_convert_fusion
  471.4 61.6 %conditional.6 = (f32[1024,16,64]{0,2,1:T(8,128)S(1)}, f32[1024,16,64]{0,2,1:T(8,128)S(1)}, bf16[512,16,64]{0,2,1:T(8,128)(2,1)S(1)}) conditional(s32[]{:T(128)} %convert_element_type.166, (s32[]{:T(128)}, bf16[1024,16,64]{0,2,1:T(8,128)(2,1)}, bf16[1024,16,64]{0,2,1:T(8,128)(2,1)S(1)}, f32[16,512,1]{1,0,2:T(8,128)}, f32[16,512,1]{1,0,2:T(8,128)}, ...), branch_computations={%region_19.21_spmd, %region_21.23_spmd} | conditional | flops 2728652800 | bytes 210374816 | solution.py:214
  473.4 9.8 fusion.72
  483.2 12.8 %multiply_reduce_fusion.1 = (f32[16,512]{1,0:T(8,128)S(1)}, f32[16,512,512]{1,2,0:T(8,128)}) fusion(f32[16,512,512]{1,2,0:T(8,128)} %fusion.72, f32[16,512]{1,0:T(8,128)} %bitcast.18, f32[16,512]{1,0:T(8,128)} %bitcast.17, bf16[1024,16,64]{0,2,1:T(8,128)(2,1)S(1)} %get-tuple-element.113, bf16[1024,16,64]{0,2,1:T(8,128)(2,1)S(1)} %copy-done.11, ...), kind=kOutput, calls=%fused_computation.112 | convolution fusion | flops 562028544 | bytes 36012032 | tf_op jit(solution)/shard_map/cond/branch_1_fun/qhd,khd->hqk/dot_general | solution.py:51
  496.0 15.2 %multiply_convert_fusion.2 = bf16[16,512,512]{1,2,0:T(8,128)(2,1)} fusion(f32[16,512,512]{1,2,0:T(8,128)} %get-tuple-element.239, f32[16,512,512]{1,2,0:T(8,128)} %fusion.72, f32[16,512]{1,0:T(8,128)S(1)} %get-tuple-element.238), kind=kLoop, calls=%fused_computation.111 | loop fusion | flops 12582912 | bytes 41975808 | tf_op jit(solution)/shard_map/cond/branch_1_fun/convert_element_type | solution.py:94
  511.2 10.5 fusion.68
  521.7 4.9 fusion.71
  536.6 119.7 %conditional.7 = (f32[1024,16,64]{0,2,1:T(8,128)}, f32[1024,16,64]{0,2,1:T(8,128)}, bf16[512,16,64]{0,2,1:T(8,128)(2,1)S(1)}) conditional(s32[]{:T(128)} %convert_element_type.166, (s32[]{:T(128)}, bf16[1024,16,64]{0,2,1:T(8,128)(2,1)}, bf16[1024,16,64]{0,2,1:T(8,128)(2,1)S(1)}, f32[16,512,1]{1,0,2:T(8,128)}, f32[16,512,1]{1,0,2:T(8,128)}, ...), branch_computations={%region_23.25_spmd, %region_25.27_spmd} | conditional | flops 5456269824 | bytes 365052064 | solution.py:214
  549.9 17.9 %fusion.105 = f32[16,512,1024]{2,1,0:T(8,128)} fusion(bf16[1024,16,64]{0,2,1:T(8,128)(2,1)} %get-tuple-element.131, bf16[1024,16,64]{0,2,1:T(8,128)(2,1)} %get-tuple-element.130), kind=kOutput, calls=%fused_computation.169 | convolution fusion | flops 1073741824 | bytes 36700160 | tf_op jit(solution)/shard_map/cond/branch_1_fun/qhd,khd->hqk/dot_general | solution.py:89
  567.8 26.8 %multiply_reduce_fusion.3 = (f32[16,512]{1,0:T(8,128)S(1)}, f32[16,512,1024]{2,1,0:T(8,128)}) fusion(f32[16,512,1024]{2,1,0:T(8,128)} %fusion.105, f32[16,512]{1,0:T(8,128)} %bitcast.28, f32[16,512]{1,0:T(8,128)} %bitcast.27, bf16[1024,16,64]{0,2,1:T(8,128)(2,1)S(1)} %get-tuple-element.127, bf16[1024,16,64]{0,2,1:T(8,128)(2,1)S(1)} %copy-done.15, ...), kind=kOutput, calls=%fused_computation.158 | convolution fusion | flops 1124065280 | bytes 70877184 | tf_op jit(solution)/shard_map/cond/branch_1_fun/qhd,khd->hqk/dot_general | solution.py:51
  594.6 27.9 %multiply_convert_fusion.6 = bf16[16,512,1024]{2,1,0:T(8,128)(2,1)} fusion(f32[16,512,1024]{2,1,0:T(8,128)} %get-tuple-element.245, f32[16,512,1024]{2,1,0:T(8,128)} %fusion.105, f32[16,512]{1,0:T(8,128)S(1)} %get-tuple-element.244), kind=kLoop, calls=%fused_computation.157 | loop fusion | flops 25165824 | bytes 83918848 | tf_op jit(solution)/shard_map/cond/branch_1_fun/convert_element_type | solution.py:94
  622.5 15.8 %fusion.99 = f32[1024,16,64]{0,2,1:T(8,128)} fusion(f32[16,512,1024]{2,1,0:T(8,128)} %get-tuple-element.245, bf16[1024,16,64]{0,2,1:T(8,128)(2,1)S(1)} %copy-done.16), kind=kOutput, calls=%fused_computation.163 | convolution fusion | flops 1082130432 | bytes 38797312 | tf_op jit(solution)/shard_map/cond/branch_1_fun/hqk,qhd->khd/dot_general | solution.py:90
  638.3 9.5 fusion.103
  649.5 6.4 multiply_bitcast_fusion.3
  698.8 5.3 gather_fusion.3
  708.7 17.1 %fusion.150 = bf16[1024,1024]{1,0:T(8,128)(2,1)} fusion(bf16[8,128,1024]{2,1,0:T(8,128)(2,1)S(1)} %copy-done.8, bf16[1,1024,4096]{2,1,0:T(8,128)(2,1)} %param.35, f32[1024,4096]{1,0:T(8,128)} %fusion.124), kind=kOutput, calls=%fused_computation.231 | convolution fusion | flops 8630829056 | bytes 29360128 | tf_op jit(solution)/shard_map/dot_general | solution.py:39
  725.8 52.3 %all-reduce.14 = (f32[1024]{0:T(1024)S(1)}, f32[1024]{0:T(1024)S(1)}, f32[1024]{0:T(1024)S(1)}, f32[1024]{0:T(1024)S(1)}) all-reduce(f32[1024]{0:T(1024)S(1)} %get-tuple-element.210, f32[1024]{0:T(1024)S(1)} %get-tuple-element.215, f32[1024]{0:T(1024)S(1)} %copy-done.49, ...), channel_id=6, replica_groups=mesh['grp'=4,'exp'=8] {'grp','exp'}, use_global_device_ids=true, to_apply=%region_34.35.clone | all-reduce | flops 4096 | bytes 32768
  788.7 12.0 reduce-scatter.13.cloned.1.call-done
  800.6 140.0 %reduce-scatter.7.cloned.1.call-done = f32[32,1024]{1,0:T(8,128)} async-done(((f32[1024,1024]{1,0:T(8,128)}), f32[32,1024]{1,0:T(8,128)}) %reduce-scatter.7.cloned.1.call-update) | async-done | bytes 131088 | tf_op jit(solution)/shard_map/reduce_scatter | solution.py:258
  940.7 139.6 %reduce-scatter.9.cloned.1.call-done = f32[32,1024]{1,0:T(8,128)} async-done(((f32[1024,1024]{1,0:T(8,128)}), f32[32,1024]{1,0:T(8,128)}) %reduce-scatter.9.cloned.1.call-update) | async-done | bytes 131088 | tf_op jit(solution)/shard_map/reduce_scatter | solution.py:259
  1080.3 139.5 %reduce-scatter.11.cloned.1.call-done = f32[32,1024]{1,0:T(8,128)} async-done(((f32[1024,1024]{1,0:T(8,128)}), f32[32,1024]{1,0:T(8,128)}) %reduce-scatter.11.cloned.1.call-update) | async-done | bytes 131088 | tf_op jit(solution)/shard_map/reduce_scatter | solution.py:260
  (191 shorter events, 103.3 us)
Async XLA Ops:
  7.2 8.7 copy-start.55
  7.2 8.9 copy-start.56
  7.2 9.2 copy-start.57
  7.2 9.4 copy-start.58
  7.2 68.2 %copy-start.48 = (s32[1,1024]{1,0:T(1,128)S(1)}, s32[1,1024]{1,0:T(1,128)}, u32[]{:S(2)}) copy-start(s32[1,1024]{1,0:T(1,128)} %param.24) | copy-start | bytes 12292
  7.2 83.5 %all-gather.9.cloned.1.call-start = ((), (), s32[]{:S(2)}) async-start(), calls=%async_computation.12 | async-start | bytes 2162688 | tf_op jit(solution)/shard_map/all_gather | solution.py:125
  8.0 124.5 %all-gather.7.cloned.1.call-start = ((), (), s32[]{:S(2)}) async-start(), calls=%async_computation.11 | async-start | bytes 2162688 | tf_op jit(solution)/shard_map/all_gather | solution.py:124
  8.7 181.8 %all-gather.5.cloned.1.call-start = ((), (), s32[]{:S(2)}) async-start(), calls=%async_computation.10 | async-start | bytes 2162688 | tf_op jit(solution)/shard_map/all_gather | solution.py:123
  9.4 71.5 %all-to-all-start = ((bf16[8,128,1024]{2,1,0:T(8,128)(2,1)}), bf16[8,128,1024]{2,1,0:T(8,128)(2,1)S(1)}, u32[]{:S(2)}, u32[]{:S(2)}) async-start(bf16[8,128,1024]{2,1,0:T(8,128)(2,1)} %bitcast.201), calls=%async_computation | async-start | bytes 4194304 | tf_op jit(solution)/shard_map/all_to_all | solution.py:141
  14.6 275.7 %all-gather.11.cloned.1.call-start = ((), (), s32[]{:S(2)}) async-start(), calls=%async_computation.13 | async-start | bytes 2162688 | tf_op jit(solution)/shard_map/all_gather | solution.py:126
  75.4 115.1 %copy-start.46 = (f32[1024]{0:T(1024)}, f32[1024]{0:T(1024)S(1)}, u32[]{:S(2)}) copy-start(f32[1024]{0:T(1024)S(1)} %convert_element_type.168) | copy-start | bytes 12292
  75.5 115.1 %copy-start.42 = (f32[1024]{0:T(1024)}, f32[1024]{0:T(1024)S(1)}, u32[]{:S(2)}) copy-start(f32[1024]{0:T(1024)S(1)} %convert_element_type.167) | copy-start | bytes 12292
  80.3 5.9 copy-start.40
  86.3 4.4 copy-start.17
  88.4 102.2 %copy-start.38 = (f32[1024]{0:T(1024)}, f32[1024]{0:T(1024)S(1)}, u32[]{:S(2)}) copy-start(f32[1024]{0:T(1024)S(1)} %broadcast_multiply_fusion.5) | copy-start | bytes 12292
  90.7 99.9 %copy-start.44 = (f32[1024]{0:T(1024)}, f32[1024]{0:T(1024)S(1)}, u32[]{:S(2)}) copy-start(f32[1024]{0:T(1024)S(1)} %add_rsqrt_fusion.1) | copy-start | bytes 12292
  137.4 114.3 %copy-start.4 = (bf16[1024,1024]{0,1:T(8,128)(2,1)}, bf16[1024,1024]{0,1:T(8,128)(2,1)S(1)}, u32[]{:S(2)}) copy-start(bf16[1024,1024]{0,1:T(8,128)(2,1)S(1)} %convolution_convert_fusion.2) | copy-start | bytes 6291460
  221.4 15.7 %copy-start.20 = (bf16[1024,16,64]{0,2,1:T(8,128)(2,1)S(1)}, bf16[1024,16,64]{0,2,1:T(8,128)(2,1)}, u32[]{:S(2)}) copy-start(bf16[1024,16,64]{0,2,1:T(8,128)(2,1)} %get-tuple-element.103) | copy-start | bytes 6291460 | tf_op jit(solution)/shard_map/cond
  270.6 9.9 copy-start.22
  290.4 5.3 copy-start.36
  301.0 4.0 copy-start.51
  301.0 30.3 %all-to-all-start.1 = ((bf16[8,128,1024]{2,1,0:T(8,128)(2,1)}), bf16[8,128,1024]{2,1,0:T(8,128)(2,1)S(1)}, u32[]{:S(2)}, u32[]{:S(2)}) async-start(bf16[8,128,1024]{2,1,0:T(8,128)(2,1)} %bitcast.195), calls=%async_computation.1 | async-start | bytes 4194304 | tf_op jit(solution)/shard_map/all_to_all | solution.py:184
  304.7 475.8 %reduce-scatter.17.cloned.1.call-start = ((), (), s32[]{:S(2)}) async-start(), calls=%async_computation.19 | async-start | bytes 10485760 | tf_op jit(solution)/shard_map/reduce_scatter | solution.py:271
  331.3 88.9 %copy-start.7 = (bf16[8,128,1024]{2,1,0:T(8,128)(2,1)}, bf16[8,128,1024]{2,1,0:T(8,128)(2,1)S(1)}, u32[]{:S(2)}) copy-start(bf16[8,128,1024]{2,1,0:T(8,128)(2,1)S(1)} %all-to-all-done.1) | copy-start | bytes 6291460
  333.2 14.6 %copy-start.30 = (bf16[1024,1024]{1,0:T(8,128)(2,1)S(1)}, bf16[1024,1024]{1,0:T(8,128)(2,1)}, u32[]{:S(2)}) copy-start(bf16[1024,1024]{1,0:T(8,128)(2,1)} %param.23) | copy-start | bytes 6291460
  365.3 419.3 %reduce-scatter.15.cloned.1.call-start = ((), (), s32[]{:S(2)}) async-start(), calls=%async_computation.18 | async-start | bytes 10485760 | tf_op jit(solution)/shard_map/reduce_scatter | solution.py:268
  390.9 17.9 %copy-start.59 = (bf16[1024,4096]{1,0:T(8,128)(2,1)S(1)}, bf16[1024,4096]{1,0:T(8,128)(2,1)}, u32[]{:S(2)}) copy-start(bf16[1024,4096]{1,0:T(8,128)(2,1)} %fusion.117) | copy-start | bytes 25165828
  420.1 380.5 %reduce-scatter.13.cloned.1.call-start = ((), (), s32[]{:S(2)}) async-start(), calls=%async_computation.17 | async-start | bytes 4325376 | tf_op jit(solution)/shard_map/reduce_scatter | solution.py:261
  424.0 29.2 %copy-start.41 = (s32[1024]{0:T(1024)S(1)}, s32[1024]{0:T(1024)}, u32[]{:S(2)}) copy-start(s32[1024]{0:T(1024)} %copy-done.40) | copy-start | bytes 12292
  465.1 6.3 copy-start.5
  465.1 475.5 %reduce-scatter.7.cloned.1.call-start = ((), (), s32[]{:S(2)}) async-start(), calls=%async_computation.14 | async-start | bytes 4325376 | tf_op jit(solution)/shard_map/reduce_scatter | solution.py:258
  473.4 9.8 copy-start.11
  521.7 5.9 copy-start.1
  521.7 6.5 copy-start.12
  547.2 20.6 %copy-start.6 = (bf16[1024,16,64]{0,2,1:T(8,128)(2,1)}, bf16[1024,16,64]{0,2,1:T(8,128)(2,1)S(1)}, u32[]{:S(2)}) copy-start(bf16[1024,16,64]{0,2,1:T(8,128)(2,1)S(1)} %get-tuple-element.127) | copy-start | bytes 6291460 | tf_op jit(solution)/shard_map/cond
  549.9 17.9 %copy-start.15 = (bf16[1024,16,64]{0,2,1:T(8,128)(2,1)S(1)}, bf16[1024,16,64]{0,2,1:T(8,128)(2,1)}, u32[]{:S(2)}) copy-start(bf16[1024,16,64]{0,2,1:T(8,128)(2,1)} %get-tuple-element.126) | copy-start | bytes 6291460 | tf_op jit(solution)/shard_map/cond
  594.6 27.9 %copy-start.16 = (bf16[1024,16,64]{0,2,1:T(8,128)(2,1)S(1)}, bf16[1024,16,64]{0,2,1:T(8,128)(2,1)}, u32[]{:S(2)}) copy-start(bf16[1024,16,64]{0,2,1:T(8,128)(2,1)} %get-tuple-element.130) | copy-start | bytes 6291460 | tf_op jit(solution)/shard_map/cond
  638.3 11.2 copy-start.3
  664.1 416.1 %reduce-scatter.9.cloned.1.call-start = ((), (), s32[]{:S(2)}) async-start(), calls=%async_computation.15 | async-start | bytes 4325376 | tf_op jit(solution)/shard_map/reduce_scatter | solution.py:259
  674.5 545.2 %reduce-scatter.11.cloned.1.call-start = ((), (), s32[]{:S(2)}) async-start(), calls=%async_computation.16 | async-start | bytes 4325376 | tf_op jit(solution)/shard_map/reduce_scatter | solution.py:260
  685.1 4.8 copy-start.32
  685.1 4.8 copy-start.54
  692.3 4.6 copy-start.19
  692.3 4.6 copy-start.25
  704.1 4.5 copy-start.8
  704.1 76.4 %all-to-all-start.3 = ((bf16[8,128,1024]{2,1,0:T(8,128)(2,1)}), bf16[8,128,1024]{2,1,0:T(8,128)(2,1)}, u32[]{:S(2)}, u32[]{:S(2)}) async-start(bf16[8,128,1024]{2,1,0:T(8,128)(2,1)} %bitcast.194), calls=%async_computation.3 | async-start | bytes 4194304 | tf_op jit(solution)/shard_map/all_to_all | solution.py:246
  708.6 17.2 %copy-start.49 = (f32[1024]{0:T(1024)S(1)}, f32[1024]{0:T(1024)}, u32[]{:S(2)}) copy-start(f32[1024]{0:T(1024)} %get-tuple-element.208) | copy-start | bytes 12292
  708.6 17.2 %copy-start.50 = (f32[1024]{0:T(1024)S(1)}, f32[1024]{0:T(1024)}, u32[]{:S(2)}) copy-start(f32[1024]{0:T(1024)} %get-tuple-element.214) | copy-start | bytes 12292
  (16 other events, 40.5 us)
Sparse Core Ops, SparseCore 0:
  10.9 63.3 all-gather.8
  77.2 55.2 all-gather.6
  135.3 55.2 all-gather.4
  193.3 55.2 all-gather.10
  365.4 142.4 reduce-scatter.16
  510.1 145.1 reduce-scatter.14
  658.2 142.4 reduce-scatter.12
  803.5 137.1 reduce-scatter.6
  943.5 136.6 reduce-scatter.8
  1083.0 136.7 reduce-scatter.10
where the time goes:
time: 1230 us
  waiting for transfers between devices  549 us (45%)
  matrix products  329 us (27%)
  blocking collectives  140 us (11%)
  other arithmetic  103 us (8%)
  local copies, waits for them, and re-layouts  49.9 us (4%)
  loops' own time  28.2 us (2%)
  between operations  15.7 us (1%)
  starting transfers between devices  14.4 us (1%)
    reduce_scatter x1, waiting for transfers between devices, local(): lax.psum_scatter(grad_terms[0], ('grp', 'exp'), scatter_dimension=0, tile...  140 us
    reduce_scatter x1, waiting for transfers between devices, local(): lax.psum_scatter(grad_terms[1], ('grp', 'exp'), scatter_dimension=0, tile...  140 us
    reduce_scatter x1, waiting for transfers between devices, local(): lax.psum_scatter(grad_terms[2], ('grp', 'exp'), scatter_dimension=0, tile...  140 us
    unnamed x2, blocking collectives  111 us
    dot_general x4, matrix products, block_scores(): jnp.einsum('qhd,khd->hqk', q_block, k_part, preferred_element_type=jnp.fl...  64.6 us
    all_gather x1, waiting for transfers between devices, local(): lax.all_gather(shared[0], ('grp', 'exp'), axis=0, tiled=True)  53.2 us
    dot_general x6, matrix products, contract_cols(): lax.dot_general(left_mat, right_mat, (((1,), (1,)), ((), ())), preferred_...  53 us
    dot_general x6, matrix products, contract_rows(): lax.dot_general(left_mat, right_mat, (((0,), (0,)), ((), ())), preferred_...  49.6 us
  transfers between devices with their start and end apart: 13, of which 7 were waited for; matrix products, arithmetic and copies ran while one was open for 34% of the time, Pallas kernels for 0%

commit v1 on v0

v1 whole, which is shorter than its diff:
```python
from functools import partial

import jax
import jax.numpy as jnp
from jax import lax
from jax.experimental import pallas as pl
from jax.experimental.pallas import tpu as pltpu
from jax.sharding import PartitionSpec as P

HDIM = 64
QB = 256
EPSILON = 1e-05
NEG_FILL = -1e30
GELU_A = 0.7978845608028654
GELU_B = 0.044715
BF = jnp.bfloat16
F32 = jnp.float32
MIB = 1024 * 1024


def dot_nn(left, right):
    return lax.dot_general(left, right, (((1,), (0,)), ((), ())), preferred_element_type=F32)


def dot_nt(left, right):
    return lax.dot_general(left, right, (((1,), (1,)), ((), ())), preferred_element_type=F32)


def norm_rows(x):
    centred = x - jnp.mean(x, -1, keepdims=True)
    inverse = lax.rsqrt(jnp.mean(centred * centred, -1, keepdims=True) + EPSILON)
    return centred * inverse, inverse


def norm_back(grad, normed, inverse, gain):
    scaled = grad * gain
    return inverse * (
        scaled
        - jnp.mean(scaled, -1, keepdims=True)
        - normed * jnp.mean(scaled * normed, -1, keepdims=True)
    )


def gelu_both(u):
    sq = u * u
    t = jnp.tanh(GELU_A * u * (1.0 + GELU_B * sq))
    half = 0.5 * (1.0 + t)
    return u * half, half + (0.5 * u) * (1.0 - t * t) * (GELU_A + (3.0 * GELU_A * GELU_B) * sq)


def params(limit):
    return pltpu.CompilerParams(vmem_limit_bytes=limit * MIB)


def cost(gflop, mbytes):
    return pl.CostEstimate(
        flops=int(gflop * 1e9), bytes_accessed=int(mbytes * 1e6), transcendentals=0
    )


def whole(shape):
    return pl.BlockSpec(shape, lambda *_: (0,) * len(shape), pipeline_mode=pl.Buffered(1))


def one_hot(ids, other):
    return jnp.where(ids == other, 1.0, 0.0).astype(BF)


def seq_kernel(parts, rel_ref, gain_ref, bias_ref, *refs):
    chunks, (seq_ref, ln_ref, lnt_ref, rows) = refs[:parts], refs[parts:]
    size = chunks[0].shape[0]
    for k in range(parts):
        rows[k * size : (k + 1) * size] = chunks[k][...]
    total = rows.shape[0]
    for r in range(0, total, QB):
        lanes = lax.broadcasted_iota(jnp.int32, (QB, total), 1)
        x = dot_nn(one_hot(rel_ref[r : r + QB], lanes), rows[...])
        seq_ref[r : r + QB] = x.astype(BF)
        normed, _ = norm_rows(x)
        ln = (normed * gain_ref[...] + bias_ref[...]).astype(BF)
        ln_ref[r : r + QB] = ln
        lnt_ref[:, r : r + QB] = jnp.transpose(ln)


def seq_norm(rel_col, gain, bias, chunks):
    parts, (size, width) = len(chunks), chunks[0].shape
    total = parts * size
    return pl.pallas_call(
        partial(seq_kernel, parts),
        out_shape=[
            jax.ShapeDtypeStruct((total, width), BF),
            jax.ShapeDtypeStruct((total, width), BF),
            jax.ShapeDtypeStruct((width, total), BF),
        ],
        scratch_shapes=[pltpu.VMEM((total, width), BF)],
        compiler_params=params(32),
        cost_estimate=cost(3, 8),
    )(rel_col, gain, bias, *chunks)


def place(meta, refs, full, pick, step):
    groups, experts = full.shape[0], full.shape[1]
    for r in range(experts):
        for z in range(groups):
            row = lax.rem(meta[1] + (groups - z), groups)
            full[row, r ^ meta[0]] = refs[r][z, pick * step : (pick + 1) * step]


def proj_kernel(experts, pick, meta, ln_ref, *refs):
    pieces, (out_ref, full_ref) = refs[:experts], refs[experts:]
    step = full_ref.shape[2]
    place(meta, pieces, full_ref, pick, step)
    width = ln_ref.shape[1]
    out_ref[...] = dot_nn(ln_ref[...], full_ref[...].reshape(width, width)).astype(BF)


def project(meta, ln, pieces, pick):
    experts, groups = len(pieces), pieces[0].shape[0]
    total, width = ln.shape
    step = width // (experts * groups)
    full = (groups, experts, step, width)
    out, mat = pl.pallas_call(
        partial(proj_kernel, experts, pick),
        grid_spec=pltpu.PrefetchScalarGridSpec(
            num_scalar_prefetch=1,
            grid=(1,),
            in_specs=[whole((total, width))] + [whole(p.shape) for p in pieces],
            out_specs=[whole((total, width)), whole(full)],
        ),
        out_shape=[jax.ShapeDtypeStruct((total, width), BF), jax.ShapeDtypeStruct(full, BF)],
        compiler_params=params(32),
        cost_estimate=cost(2.2, 8),
    )(meta, ln, *pieces)
    return out, mat.reshape(width, width)


def attend_kernel(flag, q_ref, k_ref, v_ref, o_ref, lse_ref, lse_cols):
    total = q_ref.shape[0]
    low = lax.broadcasted_iota(jnp.int32, (1, 2 * HDIM), 1) < HDIM
    causal = lax.broadcasted_iota(jnp.int32, (QB, QB), 1) <= lax.broadcasted_iota(
        jnp.int32, (QB, QB), 0
    )

    def run(long):
        for a in range(0, total, QB):
            b = a + QB
            q = q_ref[a:b]
            outs, logs = [], []
            for keep in (low, ~low):
                qh = jnp.where(keep, q, jnp.zeros_like(q)) * BF(HDIM**-0.5)
                near = jnp.where(causal, dot_nt(qh, k_ref[a:b]), NEG_FILL)
                top = jnp.max(near, 1, keepdims=True)
                if long and a > 0:
                    far = dot_nt(qh, k_ref[0:a])
                    top = jnp.maximum(top, jnp.max(far, 1, keepdims=True))
                near = jnp.exp(near - top)
                mass = jnp.sum(near, 1, keepdims=True)
                o = dot_nn(near.astype(BF), v_ref[a:b])
                if long and a > 0:
                    far = jnp.exp(far - top)
                    mass = mass + jnp.sum(far, 1, keepdims=True)
                    o = o + dot_nn(far.astype(BF), v_ref[0:a])
                outs.append(o * (1.0 / mass))
                logs.append(top + jnp.log(mass))
            o_ref[a:b] = jnp.where(low, outs[0], outs[1]).astype(BF)
            lse_cols[a:b] = jnp.where(low, logs[0], logs[1])

    @pl.when(flag[0] > QB)
    def _():
        run(True)

    @pl.when(flag[0] <= QB)
    def _():
        run(False)

    turned = jnp.transpose(lse_cols[...])
    lse_ref[0, 0:1] = turned[0:1]
    lse_ref[0, 1:2] = turned[HDIM : HDIM + 1]


def attend(flag, q, k, v):
    total, width = q.shape
    pair = 2 * HDIM
    block = pl.BlockSpec((total, pair), lambda j, *_: (0, j))
    stat = pl.BlockSpec((1, 8, total), lambda j, *_: (j, 0, 0))
    return pl.pallas_call(
        attend_kernel,
        grid_spec=pltpu.PrefetchScalarGridSpec(
            num_scalar_prefetch=1,
            grid=(width // pair,),
            in_specs=[block] * 3,
            out_specs=[block, stat],
            scratch_shapes=[pltpu.VMEM((total, pair), F32)],
        ),
        out_shape=[
            jax.ShapeDtypeStruct((total, width), BF),
            jax.ShapeDtypeStruct((width // pair, 8, total), F32),
        ],
        compiler_params=params(32),
        cost_estimate=cost(24, 9),
    )(flag, q, k, v)


def attend_back_kernel(
    flag, q_ref, k_ref, v_ref, o_ref, g_ref, lse_ref, dq_ref, dk_ref, dv_ref, dq_turned
):
    total = q_ref.shape[0]
    low = lax.broadcasted_iota(jnp.int32, (1, 2 * HDIM), 1) < HDIM
    causal = lax.broadcasted_iota(jnp.int32, (QB, QB), 0) <= lax.broadcasted_iota(
        jnp.int32, (QB, QB), 1
    )
    prod = jnp.transpose(g_ref[...].astype(F32) * o_ref[...].astype(F32))
    delta = [jnp.sum(prod[h * HDIM : (h + 1) * HDIM], 0, keepdims=True) for h in range(2)]
    k_turned = jnp.transpose(k_ref[...])

    def run(long):
        for a in range(0, total, QB):
            b = a + QB
            ks, vs = k_ref[a:b], v_ref[a:b]
            dks, dvs = [], []
            for h, keep in enumerate((low, ~low)):
                kh = jnp.where(keep, ks, jnp.zeros_like(ks)) * BF(HDIM**-0.5)
                vh = jnp.where(keep, vs, jnp.zeros_like(vs))
                kth = k_turned[h * HDIM : (h + 1) * HDIM, a:b]
                spans = [(a, b)]
                if long and b < total:
                    spans.append((b, total))
                dk = dv = None
                for lo, hi in spans:
                    qs, gs = q_ref[lo:hi], g_ref[lo:hi]
                    probs = jnp.exp(dot_nt(kh, qs) - lse_ref[0, h : h + 1, lo:hi])
                    if lo == a:
                        probs = jnp.where(causal, probs, 0.0)
                    dp = dot_nt(vh, gs)
                    ds = (probs * (dp - delta[h][:, lo:hi])).astype(BF)
                    dv_part, dk_part = dot_nn(probs.astype(BF), gs), dot_nn(ds, qs)
                    dk = dk_part if dk is None else dk + dk_part
                    dv = dv_part if dv is None else dv + dv_part
                    rows = slice(h * HDIM, (h + 1) * HDIM)
                    if a == 0 or not long:
                        dq_turned[rows, lo:hi] = dot_nn(kth, ds)
                    else:
                        dq_turned[rows, lo:hi] += dot_nn(kth, ds)
                dks.append(dk)
                dvs.append(dv)
            dk_ref[a:b] = (jnp.where(low, dks[0], dks[1]) * HDIM**-0.5).astype(BF)
            dv_ref[a:b] = jnp.where(low, dvs[0], dvs[1]).astype(BF)

    @pl.when(flag[0] > QB)
    def _():
        run(True)

    @pl.when(flag[0] <= QB)
    def _():
        run(False)

    dq_ref[...] = (jnp.transpose(dq_turned[...]) * HDIM**-0.5).astype(BF)


def attend_back(flag, q, k, v, o, g, lse):
    total, width = q.shape
    pair = 2 * HDIM
    block = pl.BlockSpec((total, pair), lambda j, *_: (0, j))
    stat = pl.BlockSpec((1, 8, total), lambda j, *_: (j, 0, 0))
    return pl.pallas_call(
        attend_back_kernel,
        grid_spec=pltpu.PrefetchScalarGridSpec(
            num_scalar_prefetch=1,
            grid=(width // pair,),
            in_specs=[block] * 5 + [stat],
            out_specs=[block] * 3,
            scratch_shapes=[pltpu.VMEM((pair, total), F32)],
        ),
        out_shape=[jax.ShapeDtypeStruct((total, width), BF)] * 3,
        compiler_params=params(32),
        cost_estimate=cost(32, 16),
    )(flag, q, k, v, o, g, lse)


def mix_kernel(experts, meta, attn_ref, seq_ref, rel_ref, *refs):
    pieces, rest = refs[:experts], refs[experts:]
    full_ref, outs, mixed = rest[0], rest[1 : 1 + experts], rest[1 + experts]
    step = full_ref.shape[2]
    place(meta, pieces, full_ref, 1, step)
    total, width = mixed.shape
    mat = full_ref[...].reshape(width, width)
    for r in range(0, total, QB):
        x = seq_ref[r : r + QB].astype(F32) + dot_nn(attn_ref[r : r + QB], mat)
        mixed[r : r + QB] = x.astype(BF)
    to_parts(rel_ref, mixed, outs)


def to_parts(rel_ref, rows, outs):
    total, size = rows.shape[0], outs[0].shape[0]
    per = max(1, QB // size)
    for k in range(0, len(outs), per):
        ids = lax.broadcasted_iota(jnp.int32, (per * size, total), 0) + k * size
        moved = dot_nn(one_hot(ids, rel_ref[...]), rows[...]).astype(BF)
        for j in range(per):
            outs[k + j][...] = moved[j * size : (j + 1) * size]


def mix(meta, attn, seq, rel_row, pieces):
    experts, groups = len(pieces), pieces[0].shape[0]
    total, width = attn.shape
    step = width // (experts * groups)
    full = (groups, experts, step, width)
    part = (total // experts, width)
    res = pl.pallas_call(
        partial(mix_kernel, experts),
        grid_spec=pltpu.PrefetchScalarGridSpec(
            num_scalar_prefetch=1,
            grid=(1,),
            in_specs=[whole((total, width))] * 2
            + [whole((1, total))]
            + [whole(p.shape) for p in pieces],
            out_specs=[whole(full)] + [whole(part)] * experts,
            scratch_shapes=[pltpu.VMEM((total, width), BF)],
        ),
        out_shape=[jax.ShapeDtypeStruct(full, BF)] + [jax.ShapeDtypeStruct(part, BF)] * experts,
        compiler_params=params(40),
        cost_estimate=cost(5, 12),
    )(meta, attn, seq, rel_row, *pieces)
    return res[0].reshape(width, width), list(res[1:])


def expert_kernel(parts, steps, meta, *refs):
    chunks = refs[:parts]
    cot_ref, gain_ref, bias_ref, wi_ref, wo_ref = refs[parts : parts + 5]
    out_ref, x_ref = refs[parts + 5 : parts + 7]
    dx_refs = refs[parts + 7 : 2 * parts + 7]
    sums_ref, ln, out_acc, in_acc = refs[2 * parts + 7 :]
    f = pl.program_id(0)
    size = chunks[0].shape[0]
    total, width = ln.shape

    @pl.when(f == 0)
    def _():
        for k in range(parts):
            x = chunks[k][...]
            rows = slice(k * size, (k + 1) * size)
            x_ref[rows] = x
            normed, _ = norm_rows(x.astype(F32))
            ln[rows] = (normed * gain_ref[...] + bias_ref[...]).astype(BF)

    def body(first):
        for r in range(0, total, 512):
            rows = slice(r, r + 512)
            pre = dot_nn(ln[rows], wi_ref[...])
            grad = dot_nn(cot_ref[rows], wo_ref[...])
            act, slope = gelu_both(pre)
            back = (grad * slope).astype(BF)
            o, d = dot_nt(act.astype(BF), wo_ref[...]), dot_nt(back, wi_ref[...])
            if first:
                out_acc[rows], in_acc[rows] = o, d
            else:
                out_acc[rows] += o
                in_acc[rows] += d

    @pl.when(f == 0)
    def _():
        body(True)

    @pl.when(f > 0)
    def _():
        body(False)

    @pl.when(f == steps - 1)
    def _():
        gain_sum = jnp.zeros((1, width), F32)
        bias_sum = gain_sum
        for k in range(parts):
            rows = slice(k * size, (k + 1) * size)
            x = chunks[k][...].astype(F32)
            normed, inverse = norm_rows(x)
            out_ref[k ^ meta[0]] = (x + out_acc[rows]).astype(BF)
            d = in_acc[rows]
            gain_sum = gain_sum + jnp.sum(d * normed, 0, keepdims=True)
            bias_sum = bias_sum + jnp.sum(d, 0, keepdims=True)
            back = norm_back(d, normed, inverse, gain_ref[...])
            dx_refs[k][...] = (cot_ref[rows].astype(F32) + back).astype(BF)
        sums_ref[0:1] = gain_sum
        sums_ref[1:2] = bias_sum


def expert(meta, chunks, cot, gain, bias, w_in, w_out):
    parts, (size, width) = len(chunks), chunks[0].shape
    total, hidden = parts * size, w_in.shape[1]
    tile = 512
    steps = hidden // tile
    cols = pl.BlockSpec((width, tile), lambda f, *_: (0, f))
    res = pl.pallas_call(
        partial(expert_kernel, parts, steps),
        grid_spec=pltpu.PrefetchScalarGridSpec(
            num_scalar_prefetch=1,
            grid=(steps,),
            in_specs=[whole((size, width))] * parts
            + [whole((total, width)), whole((1, width)), whole((1, width)), cols, cols],
            out_specs=[whole((parts, size, width)), whole((total, width))]
            + [whole((size, width))] * parts
            + [whole((8, width))],
            scratch_shapes=[
                pltpu.VMEM((total, width), BF),
                pltpu.VMEM((total, width), F32),
                pltpu.VMEM((total, width), F32),
            ],
        ),
        out_shape=[
            jax.ShapeDtypeStruct((parts, size, width), BF),
            jax.ShapeDtypeStruct((total, width), BF),
        ]
        + [jax.ShapeDtypeStruct((size, width), BF)] * parts
        + [jax.ShapeDtypeStruct((8, width), F32)],
        compiler_params=params(52),
        cost_estimate=cost(40, 28),
    )(meta, *chunks, cot, gain, bias, w_in, w_out)
    return res[0], res[1], list(res[2 : 2 + parts]), res[-1]


def slice_kernel(count, first, last, flags, *refs):
    xs, cots = refs[:count], refs[count : 2 * count]
    gain_ref, bias_ref, wi_ref, wo_ref = refs[2 * count : 2 * count + 4]
    rest = refs[2 * count + 4 :]
    if not first:
        in_prev, out_prev = rest[:2]
        rest = rest[2:]
    in_ref, out_ref, in_acc, out_acc = rest[:4]
    lns = rest[4:]
    f = pl.program_id(0)
    total = xs[0].shape[0]
    if first:
        in_acc[...] = jnp.zeros_like(in_acc)
        out_acc[...] = jnp.zeros_like(out_acc)
    else:
        in_acc[...] = in_prev[...]
        out_acc[...] = out_prev[...]
    for n in range(count):

        @pl.when(flags[n] > 0)
        def _(n=n):
            @pl.when(f == 0)
            def _():
                for r in range(0, total, QB):
                    normed, _ = norm_rows(xs[n][r : r + QB].astype(F32))
                    lns[n][r : r + QB] = (normed * gain_ref[...] + bias_ref[...]).astype(BF)

            pre = dot_nt(wi_ref[...], lns[n][...])
            grad = dot_nt(wo_ref[...], cots[n][...])
            act, slope = gelu_both(pre)
            back = (grad * slope).astype(BF)
            in_acc[...] += dot_nn(back, lns[n][...])
            out_acc[...] += dot_nn(act.astype(BF), cots[n][...])

    if last:
        in_ref[...] = jnp.transpose(in_acc[...])
        out_ref[...] = jnp.transpose(out_acc[...])
    else:
        in_ref[...] = in_acc[...]
        out_ref[...] = out_acc[...]


def slice_grads(flags, xs, cots, gain, bias, wi_turned, wo_turned, prev, last):
    count = len(xs)
    total, width = xs[0].shape
    hidden = wi_turned.shape[0]
    tile = min(256, hidden)
    rows = pl.BlockSpec((tile, width), lambda f, *_: (f, 0))
    cols = pl.BlockSpec((width, tile), lambda f, *_: (0, f))
    first = prev is None
    shape = (width, hidden) if last else (hidden, width)
    return pl.pallas_call(
        partial(slice_kernel, count, first, last),
        grid_spec=pltpu.PrefetchScalarGridSpec(
            num_scalar_prefetch=1,
            grid=(hidden // tile,),
            in_specs=[whole((total, width))] * (2 * count)
            + [whole((1, width))] * 2
            + [rows] * (2 if first else 4),
            out_specs=[cols if last else rows] * 2,
            scratch_shapes=[pltpu.VMEM((tile, width), F32)] * 2
            + [pltpu.VMEM((total, width), BF)] * count,
        ),
        out_shape=[jax.ShapeDtypeStruct(shape, F32)] * 2,
        compiler_params=params(48),
        cost_estimate=cost(10 * count, 8 + 4 * count),
    )(flags, *xs, *cots, gain, bias, wi_turned, wo_turned, *(() if first else prev))


def back_kernel(parts, rel_ref, mat_ref, *refs):
    chunks, (dmix_ref, dattn_ref, rows) = refs[:parts], refs[parts:]
    size = chunks[0].shape[0]
    for k in range(parts):
        rows[k * size : (k + 1) * size] = chunks[k][...]
    total = rows.shape[0]
    for r in range(0, total, QB):
        lanes = lax.broadcasted_iota(jnp.int32, (QB, total), 1)
        x = dot_nn(one_hot(rel_ref[r : r + QB], lanes), rows[...]).astype(BF)
        dmix_ref[r : r + QB] = x
        dattn_ref[r : r + QB] = dot_nt(x, mat_ref[...]).astype(BF)


def back_in(rel_col, mat, chunks):
    parts, (size, width) = len(chunks), chunks[0].shape
    total = parts * size
    return pl.pallas_call(
        partial(back_kernel, parts),
        out_shape=[jax.ShapeDtypeStruct((total, width), BF)] * 2,
        scratch_shapes=[pltpu.VMEM((total, width), BF)],
        compiler_params=params(32),
        cost_estimate=cost(5, 8),
    )(rel_col, mat, *chunks)


def shared_kernel(turn, splits, meta, left_ref, *refs):
    count = len(splits)
    rights, outs, sums = refs[:count], refs[count:-1], refs[-1]
    left = jnp.transpose(left_ref[...]) if turn else left_ref[...]
    for n in range(count):
        size = rights[n].shape[1]
        sums[:, :size] = dot_nn(left, rights[n][...])
        at, cols = splits[n]
        send, keep = outs[2 * at], outs[2 * at + 1]
        half, step = send.shape[0], send.shape[2]
        for r in range(2 * half):
            start = pl.multiple_of((r ^ meta[0]) * step, step)
            ref = send if r % 2 else keep
            ref[r // 2, 0, :, cols : cols + size] = sums[pl.ds(start, step), :size].astype(BF)


def shared_grads(meta, left, rights, splits, widths, experts, groups, turn):
    total, width = rights[0].shape
    features = left.shape[1] if turn else left.shape[0]
    step = features // (experts * groups)
    block = features // groups
    if turn:
        left_spec = pl.BlockSpec((total, block), lambda g, *_: (0, g))
    else:
        left_spec = pl.BlockSpec((block, total), lambda g, *_: (g, 0))
    shapes = [(experts // 2, groups, step, w) for w in widths for _ in range(2)]
    out_specs = [pl.BlockSpec((s[0], 1, s[2], s[3]), lambda g, *_: (0, g, 0, 0)) for s in shapes]
    res = pl.pallas_call(
        partial(shared_kernel, turn, splits),
        grid_spec=pltpu.PrefetchScalarGridSpec(
            num_scalar_prefetch=1,
            grid=(groups,),
            in_specs=[left_spec] + [whole(r.shape) for r in rights],
            out_specs=out_specs,
            scratch_shapes=[pltpu.VMEM((block, width), F32)],
        ),
        out_shape=[jax.ShapeDtypeStruct(s, BF) for s in shapes],
        compiler_params=params(40),
        cost_estimate=cost(2.2 * sum(widths) / 1024, 4 + 4 * sum(widths) / 1024),
    )(meta, left, *rights)
    return [(res[2 * n], res[2 * n + 1]) for n in range(len(widths))]


def first_kernel(steps, parts, *refs):
    dq_ref, dk_ref, dv_ref, wq_ref, wk_ref, wv_ref, seq_ref, dmix_ref, gain_ref, rel_ref = refs[:10]
    outs, sums_ref, rows = refs[10 : 10 + parts], refs[10 + parts], refs[11 + parts]
    r = pl.program_id(0)
    size = dq_ref.shape[0]
    grad = dot_nt(dq_ref[...], wq_ref[...])
    grad = grad + dot_nt(dk_ref[...], wk_ref[...])
    grad = grad + dot_nt(dv_ref[...], wv_ref[...])
    normed, inverse = norm_rows(seq_ref[...].astype(F32))
    gain_sum = jnp.sum(grad * normed, 0, keepdims=True)
    bias_sum = jnp.sum(grad, 0, keepdims=True)

    @pl.when(r == 0)
    def _():
        sums_ref[0:1] = gain_sum
        sums_ref[1:2] = bias_sum

    @pl.when(r > 0)
    def _():
        sums_ref[0:1] += gain_sum
        sums_ref[1:2] += bias_sum

    back = dmix_ref[...].astype(F32) + norm_back(grad, normed, inverse, gain_ref[...])
    rows[pl.ds(pl.multiple_of(r * size, size), size)] = back.astype(BF)

    @pl.when(r == steps - 1)
    def _():
        to_parts(rel_ref, rows, outs)


def first_back(dq, dk, dv, mats, seq, dmix, gain, rel_row, parts):
    total, width = dq.shape
    steps = total // QB
    block = pl.BlockSpec((QB, width), lambda r: (r, 0))
    part = (total // parts, width)
    res = pl.pallas_call(
        partial(first_kernel, steps, parts),
        grid=(steps,),
        in_specs=[block] * 3
        + [whole((width, width))] * 3
        + [block] * 2
        + [whole((1, width)), whole((1, total))],
        out_specs=[whole(part)] * parts + [whole((8, width))],
        out_shape=[jax.ShapeDtypeStruct(part, BF)] * parts + [jax.ShapeDtypeStruct((8, width), F32)],
        scratch_shapes=[pltpu.VMEM((total, width), BF)],
        compiler_params=params(40),
        cost_estimate=cost(9, 20),
    )(dq, dk, dv, *mats, seq, dmix, gain, rel_row)
    return list(res[:parts]), res[-1]


def order_kernel(parts, meta, *refs):
    for k in range(parts):
        refs[parts][k ^ meta[0]] = refs[k][...]


def to_order(meta, chunks):
    parts, (size, width) = len(chunks), chunks[0].shape
    return pl.pallas_call(
        partial(order_kernel, parts),
        grid_spec=pltpu.PrefetchScalarGridSpec(
            num_scalar_prefetch=1,
            grid=(1,),
            in_specs=[whole((size, width))] * parts,
            out_specs=whole((parts, size, width)),
        ),
        out_shape=jax.ShapeDtypeStruct((parts, size, width), BF),
        compiler_params=params(16),
        cost_estimate=cost(0.1, 4),
    )(meta, *chunks)


def local(
    n_grp,
    n_exp,
    tokens,
    cotangent,
    arrival,
    seq_length,
    w_q,
    w_k,
    w_v,
    w_o,
    ln1_gain,
    ln1_bias,
    ln2_gain,
    ln2_bias,
    w_in,
    w_out,
):
    me, grp = lax.axis_index("exp"), lax.axis_index("grp")
    meta = jnp.stack([me, grp]).astype(jnp.int32)
    total, width = tokens.shape
    size = total // n_exp
    step = w_q.shape[0]
    hidden = w_in.shape[2] // n_grp

    def swap(a, k):
        return lax.ppermute(a, "exp", [(i, i ^ k) for i in range(n_exp)])

    def shift(a, k):
        return lax.ppermute(a, "grp", [(i, (i + k) % n_grp) for i in range(n_grp)])

    def exchange(chunks):
        return [chunks[0]] + [swap(chunks[k], k) for k in range(1, n_exp)]

    bits = []
    while 2 ** len(bits) < n_exp:
        bits.append(2 ** len(bits))

    def gather_grp(a):
        return jnp.stack([a] + [shift(a, k) for k in range(1, n_grp)])

    def gather_exp(own, order):
        have = {0: own}
        for b in order:
            have.update({r ^ b: swap(a, b) for r, a in list(have.items())})
        return [have[r] for r in range(n_exp)]

    def line(a):
        ups, downs, up, down = [], [], a, a
        for t in range(1, n_grp):
            up = lax.ppermute(up, "grp", [(i, i + 1) for i in range(t - 1, n_grp - 1)])
            down = lax.ppermute(down, "grp", [(i + 1, i) for i in range(n_grp - t)])
            ups.append(up)
            downs.append(down)
        return ups, downs

    ids = arrival[0]
    rel = ((ids // size) ^ me) * size + ids % size
    rel_row, rel_col = rel[None, :], rel[:, None]
    flag = seq_length

    tok3 = tokens.reshape(n_exp, size, width)
    tok_chunks = [lax.dynamic_index_in_dim(tok3, me ^ k, 0, False) for k in range(n_exp)]
    arrived = exchange(tok_chunks)

    gains = jnp.concatenate([ln1_gain, ln1_bias, ln2_gain, ln2_bias])[None]
    gains = gather_exp(gather_grp(gains), bits[::-1])
    gains = jnp.stack(gains)[:, :, 0]
    gains = jnp.take(gains, jnp.arange(n_exp) ^ me, axis=0)
    gains = jnp.take(gains, (grp - jnp.arange(n_grp)) % n_grp, axis=1)
    gains = gains.reshape(n_exp, n_grp, 4, step).transpose(2, 1, 0, 3).reshape(4, 1, width)
    gains = gains.astype(F32)

    pair_qk = gather_grp(jnp.concatenate([w_q, w_k]))
    pair_vo = gather_grp(jnp.concatenate([w_v, w_o]))
    cot3 = cotangent.reshape(n_exp, size, width)
    cot_chunks = [lax.dynamic_index_in_dim(cot3, me ^ k, 0, False) for k in range(n_exp)]
    cot = jnp.concatenate(cot_chunks)
    pieces_qk = gather_exp(pair_qk, bits[:0:-1] + bits[:1])
    pieces_vo = gather_exp(pair_vo, bits[1:] + bits[:1])

    halves = [cot[: total // 2], cot[total // 2 :]]
    halves, pair_vo = lax.optimization_barrier((halves, pair_vo))
    cot_lines = [line(h) for h in halves]

    w_first, w_second = w_in[0], w_out[0]
    wi_turned = lax.dynamic_slice_in_dim(w_first, grp * hidden, hidden, 1).T
    wo_turned = lax.dynamic_slice_in_dim(w_second, grp * hidden, hidden, 1).T

    seq, ln_one, ln_turned = seq_norm(rel_col, gains[0], gains[1], arrived)
    q, mat_q = project(meta, ln_one, pieces_qk, 0)
    k, mat_k = project(meta, ln_one, pieces_qk, 1)
    v, mat_v = project(meta, ln_one, pieces_vo, 0)
    attn, lse = attend(flag, q, k, v)
    mat_o, leaving = mix(meta, attn, seq, rel_row, pieces_vo)
    x_chunks = exchange(leaving)

    out, x_all, dx_chunks, sums_two = expert(
        meta, x_chunks, cot, gains[2], gains[3], w_first, w_second
    )
    output = out.reshape(total, width)
    half = n_exp // 2
    x_lines = [line(jnp.concatenate(x_chunks[:half])), line(jnp.concatenate(x_chunks[half:]))]

    back = exchange(dx_chunks)
    dmix, dattn = back_in(rel_col, mat_o, back)

    def reduce_exp(pair, order):
        send, keep = pair
        got = swap(send, 1)
        tail = send.shape[1:]
        dims = [2] * (len(bits) - 1)
        keep, got = keep.reshape(dims + list(tail)), got.reshape(dims + list(tail))
        left = list(bits[:0:-1])
        for b in order:
            axis = left.index(b)
            left.remove(b)
            pick = lambda a, n: lax.index_in_dim(a, n, axis, False)
            send = (pick(keep, 1).astype(F32) + pick(got, 1).astype(F32)).astype(BF)
            keep = (pick(keep, 0).astype(F32) + pick(got, 0).astype(F32)).astype(BF)
            got = swap(send, b)
        return keep, got

    def reduce_grp(keep, got):
        both = keep.astype(F32) + got.astype(F32)
        low = both.astype(BF)
        acc = lax.dynamic_index_in_dim(both, grp, 0, False)
        for s in range(1, n_grp):
            sent = lax.dynamic_index_in_dim(low, (grp + s) % n_grp, 0, False)
            acc = acc + shift(sent, s).astype(F32)
        return acc

    def reduce_all(pairs):
        orders = [bits[1:], bits[:0:-1]]
        return jnp.concatenate(
            [reduce_grp(*reduce_exp(pair, orders[n])) for n, pair in enumerate(pairs)], -1
        )

    mid = width // 2
    grad_o = shared_grads(
        meta,
        attn,
        [dmix[:, :mid], dmix[:, mid:]],
        ((0, 0), (1, 0)),
        (mid, mid),
        n_exp,
        n_grp,
        True,
    )
    grad_w_o = reduce_all(grad_o)

    ones = jnp.ones((), jnp.int32)
    sums = None
    for t in range(n_grp):
        if t == 0:
            xs, cots, flags = [x_all], [cot], [ones]
        else:
            xs, cots, flags = [], [], []
            for way in range(2):
                xs.append(jnp.concatenate([p[way][t - 1] for p in x_lines]))
                cots.append(jnp.concatenate([p[way][t - 1] for p in cot_lines]))
                flags.append((grp >= t if way == 0 else grp + t < n_grp).astype(jnp.int32))
        sums = slice_grads(
            jnp.stack(flags),
            xs,
            cots,
            gains[2],
            gains[3],
            wi_turned,
            wo_turned,
            sums,
            t == n_grp - 1,
        )
    grad_w_in, grad_w_out = sums

    dq, dk, dv = attend_back(flag, q, k, v, attn, dattn, lse)
    dx_first, sums_one = first_back(
        dq, dk, dv, (mat_q, mat_k, mat_v), seq, dmix, gains[0], rel_row, n_exp
    )
    grad_x = to_order(meta, exchange(dx_first)).reshape(total, width)
    grads_qkv = shared_grads(
        meta,
        ln_turned,
        [dq, dk[:, :mid], dk[:, mid:], dv],
        ((0, 0), (0, width), (1, 0), (1, mid)),
        (width + mid, width + mid),
        n_exp,
        n_grp,
        False,
    )
    grad_qkv = reduce_all(grads_qkv)

    small = jnp.concatenate([sums_one[:2], sums_two[:2]]).reshape(4, n_grp, n_exp, step)
    small = small.transpose(2, 1, 0, 3).reshape(n_exp, n_grp, 4 * step)
    small = jnp.take(small, jnp.arange(n_exp) ^ me, axis=0)
    for b in bits[::-1]:
        small = small[:b] + swap(small[b:], b)
    small = small[0]
    acc = lax.dynamic_index_in_dim(small, grp, 0, True)
    for s in range(1, n_grp):
        acc = acc + shift(lax.dynamic_index_in_dim(small, (grp + s) % n_grp, 0, True), s)
    small = acc.reshape(4, step)

    return (
        output,
        grad_x,
        grad_qkv[:, :width],
        grad_qkv[:, width : 2 * width],
        grad_qkv[:, 2 * width :],
        grad_w_o,
        small[0],
        small[1],
        small[2],
        small[3],
        grad_w_in[None],
        grad_w_out[None],
    )


def solution(mesh):
    both = ("grp", "exp")
    rows, flat, mats = P(both, None), P(both), P("exp", None, None)
    split = P("exp", None, "grp")
    return jax.shard_map(
        partial(local, mesh.shape["grp"], mesh.shape["exp"]),
        mesh=mesh,
        in_specs=(rows, rows, rows, flat) + (rows,) * 4 + (flat,) * 4 + (mats, mats),
        out_specs=(rows,) * 6 + (flat,) * 4 + (split, split),
        check_vma=False,
    )
```

time: 1230 us -> 738 us (0.60)
  matrix products: 329 us -> 0 us
  waiting for transfers between devices: 549 us -> 253 us
  Pallas kernels: 0 us -> 255 us
  blocking collectives: 140 us -> 0 us
  starting transfers between devices: 14.4 us -> 128 us
  other arithmetic: 103 us -> 29.9 us
  loops' own time: 28.2 us -> 0 us
  between operations: 15.7 us -> 3 us
    reduce_scatter x6 -> x0, waiting for transfers between devices: 431 us -> none  [the longest x1 140 us: local(): lax.psum_scatter(grad_terms[0], ('grp', 'exp'), scatter_dimension=0, tile...]
    dot_general x32 -> x0, matrix products: 329 us -> none  [the longest x4 64.6 us: block_scores(): jnp.einsum('qhd,khd->hqk', q_block, k_part, preferred_element_type=jnp.fl...]
    pallas_call x0 -> x17, Pallas kernels: none -> 255 us  [the longest x4 71.4 us: slice_grads(): pl.pallas_call(partial(slice_kernel, count, first, last), grid_spec=pltpu...]
    ppermute x0 -> x112, waiting for transfers between devices: none -> 253 us  [the longest x12 111 us: line(): down = lax.ppermute(down, 'grp', [(i + 1, i) for i in range(n_grp - t)])]
    ppermute x0 -> x112, starting transfers between devices: none -> 128 us  [the longest x64 48.2 us: swap(): return lax.ppermute(a, 'exp', [(i, i ^ k) for i in range(n_exp)])]
    unnamed x2 -> x0, blocking collectives: 111 us -> none
    all_gather x4 -> x0, waiting for transfers between devices: 89.2 us -> none  [the longest x1 53.2 us: local(): lax.all_gather(shared[0], ('grp', 'exp'), axis=0, tiled=True)]
    convert_element_type x12 -> x13, other arithmetic: 62 us -> 3.39 us  [the longest x4 2.62 us: reduce_exp(): keep = (pick(keep, 0).astype(F32) + pick(got, 0).astype(F32)).astype(BF)]
  transfers between devices with their start and end apart: 13 -> 112, of which waited for: 7 -> 37; matrix products, arithmetic and copies ran while one was open for 34% -> 9% of each run, Pallas kernels for 0% -> 25%
where the time goes in v1:
time: 738 us; the launch traced here: 728 us
  Pallas kernels  255 us (35%)
  waiting for transfers between devices  253 us (34%)
  starting transfers between devices  128 us (17%)
  local copies, waits for them, and re-layouts  59.2 us (8%)
  other arithmetic  29.9 us (4%)
    ppermute x12, waiting for transfers between devices, line(): down = lax.ppermute(down, 'grp', [(i + 1, i) for i in range(n_grp - t)])  111 us
    ppermute x64, waiting for transfers between devices, swap(): return lax.ppermute(a, 'exp', [(i, i ^ k) for i in range(n_exp)])  106 us
    pallas_call x4, Pallas kernels, slice_grads(): pl.pallas_call(partial(slice_kernel, count, first, last), grid_spec=pltpu...  71.4 us
    pallas_call x1, Pallas kernels, expert(): pl.pallas_call(partial(expert_kernel, parts, steps), grid_spec=pltpu.Pref...  50.5 us
    ppermute x64, starting transfers between devices, swap(): return lax.ppermute(a, 'exp', [(i, i ^ k) for i in range(n_exp)])  48.2 us
    pallas_call x1, Pallas kernels, attend_back(): pl.pallas_call(attend_back_kernel, grid_spec=pltpu.PrefetchScalarGridSpec...  41.9 us
    ppermute x24, starting transfers between devices, shift(): return lax.ppermute(a, 'grp', [(i, (i + k) % n_grp) for i in range(n_grp)])  41 us
    unnamed x183, local copies, waits for them, and re-layouts  37 us
  transfers between devices with their start and end apart: 112, of which 37 were waited for; matrix products, arithmetic and copies ran while one was open for 9% of the time, Pallas kernels for 25%

profile of v1, /device:TPU:0, one launch (start us, length us, event | category | flops | bytes accessed | tf_op | source)
XLA Modules:
  0.0 728.2 jit_solution(11834795598388887562)
XLA Ops:
  1.4 5.0 collective-permute-start.2
  31.5 4.7 constant_dynamic-slice_fusion
  42.0 4.0 copy.61
  46.0 4.0 copy.62
  53.9 3.8 collective-permute-start.29
  58.3 3.6 collective-permute-done.17
  63.7 8.8 %collective-permute-done.28 = bf16[64,1024]{1,0:T(8,128)(2,1)S(1)} collective-permute-done((bf16[64,1024]{1,0:T(8,128)(2,1)S(1)}, bf16[64,1024]{1,0:T(8,128)(2,1)S(1)}, u32[]{:S(2)}, u32[]{:S(2)}) %collective-permute-start.28) | collective-permute-done | bytes 131104 | tf_op jit(solution)/shard_map/ppermute | solution.py:658
  76.9 10.6 %collective-permute-done.13.refs_4_ = bf16[128,1024]{1,0:T(8,128)(2,1)S(1)} collective-permute-done((bf16[128,1024]{1,0:T(8,128)(2,1)}, bf16[128,1024]{1,0:T(8,128)(2,1)S(1)}, u32[]{:S(2)}, u32[]{:S(2)}) %collective-permute-start.13) | collective-permute-done | bytes 262176 | tf_op jit(solution)/shard_map/ppermute | solution.py:655
  96.0 7.1 collective-permute-done.23.refs_4_
  104.3 13.4 %collective-permute-done.16.refs_7_ = bf16[128,1024]{1,0:T(8,128)(2,1)} collective-permute-done((bf16[128,1024]{1,0:T(8,128)(2,1)}, bf16[128,1024]{1,0:T(8,128)(2,1)}, u32[]{:S(2)}, u32[]{:S(2)}) %collective-permute-start.16) | collective-permute-done | bytes 262176 | tf_op jit(solution)/shard_map/ppermute | solution.py:655
  121.8 6.1 collective-permute-done.25.refs_6_
  128.1 4.0 collective-permute-done.33.refs_4_
  133.7 9.7 %collective-permute-done.35.refs_6_ = bf16[4,64,1024]{2,1,0:T(8,128)(2,1)} collective-permute-done((bf16[4,64,1024]{2,1,0:T(8,128)(2,1)S(1)}, bf16[4,64,1024]{2,1,0:T(8,128)(2,1)}, u32[]{:S(2)}, u32[]{:S(2)}) %collective-permute-start.35) | collective-permute-done | bytes 524320 | tf_op jit(solution)/shard_map/ppermute | solution.py:655
  149.4 4.2 shard_map.229
  157.6 4.7 shard_map.230
  163.6 4.9 shard_map.231
  171.2 5.6 collective-permute-start.100
  178.0 4.2 shard_map.232
  183.6 29.8 %shard_map.233 = (bf16[1024,1024]{1,0:T(8,128)(2,1)S(1)}, f32[8,8,1024]{2,1,0:T(8,128)S(1)}) custom-call(s32[1]{0:T(128)S(6)} %copy.90.flag, bf16[1024,1024]{1,0:T(8,128)(2,1)S(1)} %get-tuple-element.76.q_ref, bf16[1024,1024]{1,0:T(8,128)(2,1)S(1)} %get-tuple-element.77.k_ref, bf16[1024,1024]{1,0:T(8,128)(2,1)S(1)} %get-tuple-element.78.v_ref), custom_call_target="tpu_custom_call" | custom-call | flops 24000000000 | bytes 9000000 | tf_op jit(solution)/shard_map/pallas_call | solution.py:186
  214.2 6.6 shard_map.234
  236.0 11.7 %collective-permute-done.40.refs_4_ = bf16[128,1024]{1,0:T(8,128)(2,1)S(1)} collective-permute-done((bf16[128,1024]{1,0:T(8,128)(2,1)S(1)}, bf16[128,1024]{1,0:T(8,128)(2,1)S(1)}, u32[]{:S(2)}, u32[]{:S(2)}) %collective-permute-start.40) | collective-permute-done | bytes 262176 | tf_op jit(solution)/shard_map/ppermute | solution.py:655
  247.7 4.5 collective-permute-done.41.refs_5_
  253.1 50.5 %shard_map.235 = (bf16[8,128,1024]{2,1,0:T(8,128)(2,1)}, bf16[1024,1024]{1,0:T(8,128)(2,1)}, bf16[128,1024]{1,0:T(8,128)(2,1)S(1)}, bf16[128,1024]{1,0:T(8,128)(...) custom-call(s32[2]{0:T(128)S(1)} %pad_add_fusion.meta, ...), custom_call_target="tpu_custom_call" | custom-call | flops 40000000000 | bytes 28000000 | tf_op jit(solution)/shard_map/pallas_call | solution.py:392
  309.1 15.7 %shard_map.242 = (f32[1024,1024]{1,0:T(8,128)}, f32[1024,1024]{1,0:T(8,128)}) custom-call(s32[1]{0:T(128)} %constant.237.clone.1.flags, bf16[1024,1024]{1,0:T(8,128)(2,1)S(1)} %copy-done.43, bf16[1024,1024]{1,0:T(8,128)(2,1)} %get-tuple-element.146.refs_8_.refs_1_, f32[1,1024]{1,0:T(1,128)S(1)} %squeeze.199.refs_9_.refs_2_.refs_4_, ...), custom_call_target="tpu_custom_call" | custom-call | flops 10000000000 | bytes 12000000 | tf_op jit(solution)/shard_map/pallas_call | solution.py:471
  339.1 4.6 shard_map.236
  345.1 41.9 %shard_map.237 = (bf16[1024,1024]{1,0:T(8,128)(2,1)S(1)}, bf16[1024,1024]{1,0:T(8,128)(2,1)S(1)}, bf16[1024,1024]{1,0:T(8,128)(2,1)S(1)}) custom-call(s32[1]{0:T(128)S(6)} %copy.90.flag, bf16[1024,1024]{1,0:T(8,128)(2,1)S(1)} %copy-done.29, bf16[1024,1024]{1,0:T(8,128)(2,1)S(1)} %copy-done.31, bf16[1024,1024]{1,0:T(8,128)(2,1)S(1)} %copy-done.33, ...), custom_call_target="tpu_custom_call" | custom-call | flops 32000000000 | bytes 16000000 | tf_op jit(solution)/shard_map/pallas_call | solution.py:265
  387.0 15.5 %shard_map.238 = (bf16[128,1024]{1,0:T(8,128)(2,1)S(1)}, bf16[128,1024]{1,0:T(8,128)(2,1)S(1)}, bf16[128,1024]{1,0:T(8,128)(2,1)S(1)}, bf16[128,1024]{1,0:T(8,12...) custom-call(bf16[1024,1024]{1,0:T(8,128)(2,1)S(1)} %get-tuple-elemen, ...), custom_call_target="tpu_custom_call" | custom-call | flops 8999999488 | bytes 20000000 | tf_op jit(solution)/shard_map/pallas_call | solution.py:592
  407.2 3.5 collective-permute-done.82
  412.0 10.5 %shard_map.240 = (bf16[4,4,32,1536]{3,2,1,0:T(8,128)(2,1)S(1)}, bf16[4,4,32,1536]{3,2,1,0:T(8,128)(2,1)S(1)}, bf16[4,4,32,1536]{3,2,1,0:T(8,128)(2,1)S(1)}, bf16[4,4,32,1536]{3,2,1,0:T(8,128)(2,1)S(1)}) custom-call(s32[2]{0:T(128)S(1)} %pad_add_fusion.meta, bf16[1024,1024]{1,0:T(8,128)(2,1)S(1)} %copy-done.38, bf16[1024,1024]{1,0:T(8,128)(2,1)S(1)} %copy-done.41, ...), custom_call_target="tpu_custom_call" | custom-call | flops 6600000000 | bytes 16000000 | tf_op jit(solution)/shard_map/pallas_call | solution.py:541
  424.2 4.1 shard_map.241
  429.2 3.3 collective-permute-start.86
  438.7 3.2 pad_maximum_fusion.7.refs_3_
  447.1 3.4 collective-permute-start.88
  454.3 6.5 collective-permute-done.56.refs_6_
  475.4 16.8 %collective-permute-done.88 = bf16[512,1024]{1,0:T(8,128)(2,1)S(1)} collective-permute-done((bf16[512,1024]{1,0:T(8,128)(2,1)S(1)}, bf16[512,1024]{1,0:T(8,128)(2,1)S(1)}, u32[]{:S(2)}, u32[]{:S(2)}) %collective-permute-start.88) | collective-permute-done | bytes 1048608 | tf_op jit(solution)/shard_map/ppermute | solution.py:679
  493.2 6.2 collective-permute-start.81
  503.7 11.5 %collective-permute-done.94 = bf16[512,1024]{1,0:T(8,128)(2,1)S(1)} collective-permute-done((bf16[512,1024]{1,0:T(8,128)(2,1)S(1)}, bf16[512,1024]{1,0:T(8,128)(2,1)S(1)}, u32[]{:S(2)}, u32[]{:S(2)}) %collective-permute-start.94) | collective-permute-done | bytes 1048608 | tf_op jit(solution)/shard_map/ppermute | solution.py:680
  528.0 18.0 %shard_map.243 = (f32[1024,1024]{1,0:T(8,128)}, f32[1024,1024]{1,0:T(8,128)}) custom-call(s32[2]{0:T(128)S(1)} %add_convert_fusion.14.flags, bf16[1024,1024]{1,0:T(8,128)(2,1)S(1)} %pad_maximum_fusion.8.refs_0_, bf16[1024,1024]{1,0:T(8,128)(2,1)S(1)} %pad_maximum_fusion.9.refs_1_, bf16[1024,1024]{1,0:T(8,128)(2,1)} %pad_maximum_fusion.10.refs_2_, ...), custom_call_target="tpu_custom_call" | custom-call | flops 20000000000 | bytes 16000000 | tf_op jit(solution)/shard_map/pallas_call | solution.py:471
  554.3 19.7 %collective-permute-done.108 = bf16[512,1024]{1,0:T(8,128)(2,1)} collective-permute-done((bf16[512,1024]{1,0:T(8,128)(2,1)}, bf16[512,1024]{1,0:T(8,128)(2,1)}, u32[]{:S(2)}, u32[]{:S(2)}) %collective-permute-start.108) | collective-permute-done | bytes 1048608 | tf_op jit(solution)/shard_map/ppermute | solution.py:680
  584.4 17.6 %collective-permute-done.98 = bf16[512,1024]{1,0:T(8,128)(2,1)S(1)} collective-permute-done((bf16[512,1024]{1,0:T(8,128)(2,1)S(1)}, bf16[512,1024]{1,0:T(8,128)(2,1)S(1)}, u32[]{:S(2)}, u32[]{:S(2)}) %collective-permute-start.98) | collective-permute-done | bytes 1048608 | tf_op jit(solution)/shard_map/ppermute | solution.py:680
  602.0 19.4 %collective-permute-done.95 = bf16[512,1024]{1,0:T(8,128)(2,1)S(1)} collective-permute-done((bf16[512,1024]{1,0:T(8,128)(2,1)S(1)}, bf16[512,1024]{1,0:T(8,128)(2,1)S(1)}, u32[]{:S(2)}, u32[]{:S(2)}) %collective-permute-start.95) | collective-permute-done | bytes 1048608 | tf_op jit(solution)/shard_map/ppermute | solution.py:680
  625.4 7.7 %collective-permute-done.66 = bf16[4,32,1536]{2,1,0:T(8,128)(2,1)S(1)} collective-permute-done((bf16[4,32,1536]{2,1,0:T(8,128)(2,1)S(1)}, bf16[4,32,1536]{2,1,0:T(8,128)(2,1)S(1)}, u32[]{:S(2)}, u32[]{:S(2)}) %collective-permute-start.66) | collective-permute-done | bytes 393248 | tf_op jit(solution)/shard_map/ppermute | solution.py:655
  635.5 3.4 collective-permute-start.63
  639.0 18.2 %shard_map.244 = (f32[1024,1024]{1,0:T(8,128)}, f32[1024,1024]{1,0:T(8,128)}) custom-call(s32[2]{0:T(128)S(1)} %add_convert_fusion.13.flags, bf16[1024,1024]{1,0:T(8,128)(2,1)S(1)} %pad_maximum_fusion.4.refs_0_, bf16[1024,1024]{1,0:T(8,128)(2,1)S(1)} %pad_maximum_fusion.5.refs_1_, bf16[1024,1024]{1,0:T(8,128)(2,1)} %pad_maximum_fusion.6.refs_2_, ...), custom_call_target="tpu_custom_call" | custom-call | flops 20000000000 | bytes 16000000 | tf_op jit(solution)/shard_map/pallas_call | solution.py:471
  664.2 3.7 collective-permute-done.61
  668.9 19.7 %collective-permute-done.99 = bf16[512,1024]{1,0:T(8,128)(2,1)S(1)} collective-permute-done((bf16[512,1024]{1,0:T(8,128)(2,1)S(1)}, bf16[512,1024]{1,0:T(8,128)(2,1)S(1)}, u32[]{:S(2)}, u32[]{:S(2)}) %collective-permute-start.99) | collective-permute-done | bytes 1048608 | tf_op jit(solution)/shard_map/ppermute | solution.py:680
  688.6 19.7 %collective-permute-done.96 = bf16[512,1024]{1,0:T(8,128)(2,1)S(1)} collective-permute-done((bf16[512,1024]{1,0:T(8,128)(2,1)S(1)}, bf16[512,1024]{1,0:T(8,128)(2,1)S(1)}, u32[]{:S(2)}, u32[]{:S(2)}) %collective-permute-start.96) | collective-permute-done | bytes 1048608 | tf_op jit(solution)/shard_map/ppermute | solution.py:680
  708.5 19.6 %shard_map.245 = (f32[1024,1024]{1,0:T(8,128)}, f32[1024,1024]{1,0:T(8,128)}) custom-call(s32[2]{0:T(128)S(1)} %add_convert_fusion.12.flags, bf16[1024,1024]{1,0:T(8,128)(2,1)S(1)} %pad_maximum_fusion.refs_0_, bf16[1024,1024]{1,0:T(8,128)(2,1)S(1)} %pad_maximum_fusion.1.refs_1_, bf16[1024,1024]{1,0:T(8,128)(2,1)} %pad_maximum_fusion.2.refs_2_, ...), custom_call_target="tpu_custom_call" | custom-call | flops 20000000000 | bytes 16000000 | tf_op jit(solution)/shard_map/pallas_call | solution.py:471
  (470 shorter events, 200.7 us)
Async XLA Ops:
  1.4 36.8 %collective-permute-start.2 = (bf16[1,128]{1,0:T(2,128)(2,1)S(1)}, bf16[1,128]{1,0:T(2,128)(2,1)S(1)}, u32[]{:S(2)}, u32[]{:S(2)}) collective-permute-start(bf16[1,128]{1,0:T(2,128)(2,1)S(1)} %bitcast.311), channel_id=1, source_target_pairs={{0,24},{8,0},{16,8},{24,16},{1,25},{9,1},{17,9},{25,17},{2,26},{10... | collective-permute-start | bytes 776 | tf_op jit(solution)/shard_map/ppermute | solution.py:658
  6.5 31.8 %collective-permute-start.1 = (bf16[1,128]{1,0:T(2,128)(2,1)S(1)}, bf16[1,128]{1,0:T(2,128)(2,1)S(1)}, u32[]{:S(2)}, u32[]{:S(2)}) collective-permute-start(bf16[1,128]{1,0:T(2,128)(2,1)S(1)} %bitcast.312), channel_id=1, source_target_pairs={{0,16},{8,24},{16,0},{24,8},{1,17},{9,25},{17,1},{25,9},{2,18},{10... | collective-permute-start | bytes 776 | tf_op jit(solution)/shard_map/ppermute | solution.py:658
  6.5 31.8 %collective-permute-start = (bf16[1,128]{1,0:T(2,128)(2,1)S(1)}, bf16[1,128]{1,0:T(2,128)(2,1)S(1)}, u32[]{:S(2)}, u32[]{:S(2)}) collective-permute-start(bf16[1,128]{1,0:T(2,128)(2,1)S(1)} %bitcast.313), channel_id=1, source_target_pairs={{0,8},{8,16},{16,24},{24,0},{1,9},{9,17},{17,25},{25,1},{2,10},{10... | collective-permute-start | bytes 776 | tf_op jit(solution)/shard_map/ppermute | solution.py:658
  9.2 48.5 %collective-permute-start.19 = (bf16[64,1024]{1,0:T(8,128)(2,1)S(1)}, bf16[64,1024]{1,0:T(8,128)(2,1)}, u32[]{:S(2)}, u32[]{:S(2)}) collective-permute-start(bf16[64,1024]{1,0:T(8,128)(2,1)S(1)} %constant_dynamic-update-slice_fusion.8), channel_id=1, source_target_pairs={{0,24},{8,0},{16,8},{24,16},{1,25},{9,1},{17,9},{25,17},{2,26},{10... | collective-permute-start | bytes 393224 | tf_op jit(solution)/shard_map/ppermute | solution.py:658
  12.0 46.3 %collective-permute-start.18 = (bf16[64,1024]{1,0:T(8,128)(2,1)S(1)}, bf16[64,1024]{1,0:T(8,128)(2,1)}, u32[]{:S(2)}, u32[]{:S(2)}) collective-permute-start(bf16[64,1024]{1,0:T(8,128)(2,1)S(1)} %constant_dynamic-update-slice_fusion.8), channel_id=1, source_target_pairs={{0,16},{8,24},{16,0},{24,8},{1,17},{9,25},{17,1},{25,9},{2,18},{10... | collective-permute-start | bytes 393224 | tf_op jit(solution)/shard_map/ppermute | solution.py:658
  73.6 29.5 %collective-permute-start.23 = (bf16[4,64,1024]{2,1,0:T(8,128)(2,1)S(1)}, bf16[4,64,1024]{2,1,0:T(8,128)(2,1)S(1)}, u32[]{:S(2)}, u32[]{:S(2)}) collective-permute-start(bf16[4,64,1024]{2,1,0:T(8,128)(2,1)S(1)} %pad_maximum_fusion.14.refs_0_), channel_id=1, source_target_pairs={{0,4},{1,5},{2,6},{3,7},{4,0},{5,1},{6,2},{7,3},{8,12},{9,13},{10,... | collective-permute-start | bytes 1572872 | tf_op jit(solution)/shard_map/ppermute | solution.py:655
  76.5 41.2 %collective-permute-start.20 = (bf16[4,64,1024]{2,1,0:T(8,128)(2,1)S(1)}, bf16[4,64,1024]{2,1,0:T(8,128)(2,1)S(1)}, u32[]{:S(2)}, u32[]{:S(2)}) collective-permute-start(bf16[4,64,1024]{2,1,0:T(8,128)(2,1)S(1)} %pad_maximum_fusion.14.refs_0_), channel_id=1, source_target_pairs={{0,1},{1,0},{2,3},{3,2},{4,5},{5,4},{6,7},{7,6},{8,9},{9,8},{10,11... | collective-permute-start | bytes 1572872 | tf_op jit(solution)/shard_map/ppermute | solution.py:655
  88.2 32.5 %collective-permute-start.21 = (bf16[4,64,1024]{2,1,0:T(8,128)(2,1)S(1)}, bf16[4,64,1024]{2,1,0:T(8,128)(2,1)}, u32[]{:S(2)}, u32[]{:S(2)}) collective-permute-start(bf16[4,64,1024]{2,1,0:T(8,128)(2,1)S(1)} %pad_maximum_fusion.14.refs_0_), channel_id=1, source_target_pairs={{0,2},{1,3},{2,0},{3,1},{4,6},{5,7},{6,4},{7,5},{8,10},{9,11},{10,... | collective-permute-start | bytes 1572872 | tf_op jit(solution)/shard_map/ppermute | solution.py:655
  92.0 28.8 %collective-permute-start.31 = (bf16[4,64,1024]{2,1,0:T(8,128)(2,1)S(1)}, bf16[4,64,1024]{2,1,0:T(8,128)(2,1)S(1)}, u32[]{:S(2)}, u32[]{:S(2)}) collective-permute-start(bf16[4,64,1024]{2,1,0:T(8,128)(2,1)S(1)} %pad_maximum_fusion.15.refs_0_), channel_id=1, source_target_pairs={{0,2},{1,3},{2,0},{3,1},{4,6},{5,7},{6,4},{7,5},{8,10},{9,11},{10,... | collective-permute-start | bytes 1572872 | tf_op jit(solution)/shard_map/ppermute | solution.py:655
  93.2 24.5 %collective-permute-start.16 = (bf16[128,1024]{1,0:T(8,128)(2,1)}, bf16[128,1024]{1,0:T(8,128)(2,1)}, u32[]{:S(2)}, u32[]{:S(2)}) collective-permute-start(bf16[128,1024]{1,0:T(8,128)(2,1)} %get-tuple-element.172), channel_id=1, source_target_pairs={{0,7},{1,6},{2,5},{3,4},{4,3},{5,2},{6,1},{7,0},{8,15},{9,14},{10,... | collective-permute-start | bytes 786440 | tf_op jit(solution)/shard_map/ppermute | solution.py:655
  103.1 24.7 %collective-permute-start.25 = (bf16[4,64,1024]{2,1,0:T(8,128)(2,1)S(1)}, bf16[4,64,1024]{2,1,0:T(8,128)(2,1)}, u32[]{:S(2)}, u32[]{:S(2)}) collective-permute-start(bf16[4,64,1024]{2,1,0:T(8,128)(2,1)S(1)} %collective-permute-done.23.refs_4_), channel_id=1, source_target_pairs={{0,2},{1,3},{2,0},{3,1},{4,6},{5,7},{6,4},{7,5},{8,10},{9,11},{10,... | collective-permute-start | bytes 1572872 | tf_op jit(solution)/shard_map/ppermute | solution.py:655
  127.9 27.0 %collective-permute-start.26 = (bf16[4,64,1024]{2,1,0:T(8,128)(2,1)}, bf16[4,64,1024]{2,1,0:T(8,128)(2,1)}, u32[]{:S(2)}, u32[]{:S(2)}) collective-permute-start(bf16[4,64,1024]{2,1,0:T(8,128)(2,1)} %collective-permute-done.25.refs_6_), channel_id=1, source_target_pairs={{0,1},{1,0},{2,3},{3,2},{4,5},{5,4},{6,7},{7,6},{8,9},{9,8},{10,11... | collective-permute-start | bytes 1572872 | tf_op jit(solution)/shard_map/ppermute | solution.py:655
  132.1 37.7 %collective-permute-start.30 = (bf16[4,64,1024]{2,1,0:T(8,128)(2,1)S(1)}, bf16[4,64,1024]{2,1,0:T(8,128)(2,1)S(1)}, u32[]{:S(2)}, u32[]{:S(2)}) collective-permute-start(bf16[4,64,1024]{2,1,0:T(8,128)(2,1)S(1)} %pad_maximum_fusion.15.refs_0_), channel_id=1, source_target_pairs={{0,1},{1,0},{2,3},{3,2},{4,5},{5,4},{6,7},{7,6},{8,9},{9,8},{10,11... | collective-permute-start | bytes 1572872 | tf_op jit(solution)/shard_map/ppermute | solution.py:655
  133.2 38.0 %collective-permute-start.32 = (bf16[4,64,1024]{2,1,0:T(8,128)(2,1)S(1)}, bf16[4,64,1024]{2,1,0:T(8,128)(2,1)S(1)}, u32[]{:S(2)}, u32[]{:S(2)}) collective-permute-start(bf16[4,64,1024]{2,1,0:T(8,128)(2,1)S(1)} %collective-permute-done.31.refs_2_), channel_id=1, source_target_pairs={{0,1},{1,0},{2,3},{3,2},{4,5},{5,4},{6,7},{7,6},{8,9},{9,8},{10,11... | collective-permute-start | bytes 1572872 | tf_op jit(solution)/shard_map/ppermute | solution.py:655
  133.2 43.6 %collective-permute-start.34 = (bf16[4,64,1024]{2,1,0:T(8,128)(2,1)}, bf16[4,64,1024]{2,1,0:T(8,128)(2,1)S(1)}, u32[]{:S(2)}, u32[]{:S(2)}) collective-permute-start(bf16[4,64,1024]{2,1,0:T(8,128)(2,1)} %collective-permute-done.33.refs_4_), channel_id=1, source_target_pairs={{0,1},{1,0},{2,3},{3,2},{4,5},{5,4},{6,7},{7,6},{8,9},{9,8},{10,11... | collective-permute-start | bytes 1572872 | tf_op jit(solution)/shard_map/ppermute | solution.py:655
  143.4 34.7 %collective-permute-start.36 = (bf16[4,64,1024]{2,1,0:T(8,128)(2,1)}, bf16[4,64,1024]{2,1,0:T(8,128)(2,1)S(1)}, u32[]{:S(2)}, u32[]{:S(2)}) collective-permute-start(bf16[4,64,1024]{2,1,0:T(8,128)(2,1)} %collective-permute-done.35.refs_6_), channel_id=1, source_target_pairs={{0,1},{1,0},{2,3},{3,2},{4,5},{5,4},{6,7},{7,6},{8,9},{9,8},{10,11... | collective-permute-start | bytes 1572872 | tf_op jit(solution)/shard_map/ppermute | solution.py:655
  154.9 67.3 %collective-permute-start.103 = (bf16[512,1024]{1,0:T(8,128)(2,1)}, bf16[512,1024]{1,0:T(8,128)(2,1)}, u32[]{:S(2)}, u32[]{:S(2)}) collective-permute-start(bf16[512,1024]{1,0:T(8,128)(2,1)} %pad_maximum_fusion.13), channel_id=1, source_target_pairs={{0,8},{8,16},{16,24},{1,9},{9,17},{17,25},{2,10},{10,18},{18,26},{... | collective-permute-start | bytes 3145736 | tf_op jit(solution)/shard_map/ppermute | solution.py:679
  169.9 57.4 %collective-permute-start.109 = (bf16[512,1024]{1,0:T(8,128)(2,1)}, bf16[512,1024]{1,0:T(8,128)(2,1)}, u32[]{:S(2)}, u32[]{:S(2)}) collective-permute-start(bf16[512,1024]{1,0:T(8,128)(2,1)} %pad_maximum_fusion.13), channel_id=1, source_target_pairs={{8,0},{16,8},{24,16},{9,1},{17,9},{25,17},{10,2},{18,10},{26,18},{... | collective-permute-start | bytes 3145736 | tf_op jit(solution)/shard_map/ppermute | solution.py:680
  171.2 52.5 %collective-permute-start.100 = (bf16[512,1024]{1,0:T(8,128)(2,1)}, bf16[512,1024]{1,0:T(8,128)(2,1)}, u32[]{:S(2)}, u32[]{:S(2)}) collective-permute-start(bf16[512,1024]{1,0:T(8,128)(2,1)} %pad_maximum_fusion.12), channel_id=1, source_target_pairs={{0,8},{8,16},{16,24},{1,9},{9,17},{17,25},{2,10},{10,18},{18,26},{... | collective-permute-start | bytes 3145736 | tf_op jit(solution)/shard_map/ppermute | solution.py:679
  176.7 50.6 %collective-permute-start.106 = (bf16[512,1024]{1,0:T(8,128)(2,1)}, bf16[512,1024]{1,0:T(8,128)(2,1)}, u32[]{:S(2)}, u32[]{:S(2)}) collective-permute-start(bf16[512,1024]{1,0:T(8,128)(2,1)} %pad_maximum_fusion.12), channel_id=1, source_target_pairs={{8,0},{16,8},{24,16},{9,1},{17,9},{25,17},{10,2},{18,10},{26,18},{... | collective-permute-start | bytes 3145736 | tf_op jit(solution)/shard_map/ppermute | solution.py:680
  227.3 24.8 %collective-permute-start.41 = (bf16[128,1024]{1,0:T(8,128)(2,1)S(1)}, bf16[128,1024]{1,0:T(8,128)(2,1)S(1)}, u32[]{:S(2)}, u32[]{:S(2)}) collective-permute-start(bf16[128,1024]{1,0:T(8,128)(2,1)S(1)} %get-tuple-element.86), channel_id=1, source_target_pairs={{0,5},{1,4},{2,7},{3,6},{4,1},{5,0},{6,3},{7,2},{8,13},{9,12},{10,... | collective-permute-start | bytes 786440 | tf_op jit(solution)/shard_map/ppermute | solution.py:655
  306.0 24.9 %collective-permute-start.48 = (bf16[128,1024]{1,0:T(8,128)(2,1)S(1)}, bf16[128,1024]{1,0:T(8,128)(2,1)S(1)}, u32[]{:S(2)}, u32[]{:S(2)}) collective-permute-start(bf16[128,1024]{1,0:T(8,128)(2,1)S(1)} %get-tuple-element.96), channel_id=1, source_target_pairs={{0,5},{1,4},{2,7},{3,6},{4,1},{5,0},{6,3},{7,2},{8,13},{9,12},{10,... | collective-permute-start | bytes 786440 | tf_op jit(solution)/shard_map/ppermute | solution.py:655
  327.5 96.4 %collective-permute-start.104 = (bf16[512,1024]{1,0:T(8,128)(2,1)}, bf16[512,1024]{1,0:T(8,128)(2,1)}, u32[]{:S(2)}, u32[]{:S(2)}) collective-permute-start(bf16[512,1024]{1,0:T(8,128)(2,1)} %collective-permute-done.103), channel_id=1, source_target_pairs={{8,16},{16,24},{9,17},{17,25},{10,18},{18,26},{11,19},{19,27},{12,... | collective-permute-start | bytes 3145736 | tf_op jit(solution)/shard_map/ppermute | solution.py:679
  329.2 99.2 %collective-permute-start.101 = (bf16[512,1024]{1,0:T(8,128)(2,1)}, bf16[512,1024]{1,0:T(8,128)(2,1)}, u32[]{:S(2)}, u32[]{:S(2)}) collective-permute-start(bf16[512,1024]{1,0:T(8,128)(2,1)} %collective-permute-done.100), channel_id=1, source_target_pairs={{8,16},{16,24},{9,17},{17,25},{10,18},{18,26},{11,19},{19,27},{12,... | collective-permute-start | bytes 3145736 | tf_op jit(solution)/shard_map/ppermute | solution.py:679
  330.9 98.4 %collective-permute-start.110 = (bf16[512,1024]{1,0:T(8,128)(2,1)}, bf16[512,1024]{1,0:T(8,128)(2,1)}, u32[]{:S(2)}, u32[]{:S(2)}) collective-permute-start(bf16[512,1024]{1,0:T(8,128)(2,1)} %collective-permute-done.109), channel_id=1, source_target_pairs={{8,0},{16,8},{9,1},{17,9},{10,2},{18,10},{11,3},{19,11},{12,4},{20... | collective-permute-start | bytes 3145736 | tf_op jit(solution)/shard_map/ppermute | solution.py:680
  335.0 94.2 %collective-permute-start.107 = (bf16[512,1024]{1,0:T(8,128)(2,1)}, bf16[512,1024]{1,0:T(8,128)(2,1)}, u32[]{:S(2)}, u32[]{:S(2)}) collective-permute-start(bf16[512,1024]{1,0:T(8,128)(2,1)} %collective-permute-done.106), channel_id=1, source_target_pairs={{8,0},{16,8},{9,1},{17,9},{10,2},{18,10},{11,3},{19,11},{12,4},{20... | collective-permute-start | bytes 3145736 | tf_op jit(solution)/shard_map/ppermute | solution.py:680
  444.7 29.0 %collective-permute-start.91 = (bf16[512,1024]{1,0:T(8,128)(2,1)S(1)}, bf16[512,1024]{1,0:T(8,128)(2,1)S(1)}, u32[]{:S(2)}, u32[]{:S(2)}) collective-permute-start(bf16[512,1024]{1,0:T(8,128)(2,1)S(1)} %copy-done.78), channel_id=1, source_target_pairs={{0,8},{8,16},{16,24},{1,9},{9,17},{17,25},{2,10},{10,18},{18,26},{... | collective-permute-start | bytes 3145736 | tf_op jit(solution)/shard_map/ppermute | solution.py:679
  447.1 45.1 %collective-permute-start.88 = (bf16[512,1024]{1,0:T(8,128)(2,1)S(1)}, bf16[512,1024]{1,0:T(8,128)(2,1)S(1)}, u32[]{:S(2)}, u32[]{:S(2)}) collective-permute-start(bf16[512,1024]{1,0:T(8,128)(2,1)S(1)} %copy-done.76), channel_id=1, source_target_pairs={{0,8},{8,16},{16,24},{1,9},{9,17},{17,25},{2,10},{10,18},{18,26},{... | collective-permute-start | bytes 3145736 | tf_op jit(solution)/shard_map/ppermute | solution.py:679
  464.5 36.7 %collective-permute-start.97 = (bf16[512,1024]{1,0:T(8,128)(2,1)S(1)}, bf16[512,1024]{1,0:T(8,128)(2,1)S(1)}, u32[]{:S(2)}, u32[]{:S(2)}) collective-permute-start(bf16[512,1024]{1,0:T(8,128)(2,1)S(1)} %copy-done.78), channel_id=1, source_target_pairs={{8,0},{16,8},{24,16},{9,1},{17,9},{25,17},{10,2},{18,10},{26,18},{... | collective-permute-start | bytes 3145736 | tf_op jit(solution)/shard_map/ppermute | solution.py:680
  470.7 44.4 %collective-permute-start.94 = (bf16[512,1024]{1,0:T(8,128)(2,1)S(1)}, bf16[512,1024]{1,0:T(8,128)(2,1)S(1)}, u32[]{:S(2)}, u32[]{:S(2)}) collective-permute-start(bf16[512,1024]{1,0:T(8,128)(2,1)S(1)} %copy-done.76), channel_id=1, source_target_pairs={{8,0},{16,8},{24,16},{9,1},{17,9},{25,17},{10,2},{18,10},{26,18},{... | collective-permute-start | bytes 3145736 | tf_op jit(solution)/shard_map/ppermute | solution.py:680
  472.0 54.7 %collective-permute-start.105 = (bf16[512,1024]{1,0:T(8,128)(2,1)}, bf16[512,1024]{1,0:T(8,128)(2,1)}, u32[]{:S(2)}, u32[]{:S(2)}) collective-permute-start(bf16[512,1024]{1,0:T(8,128)(2,1)} %collective-permute-done.104), channel_id=1, source_target_pairs={{16,24},{17,25},{18,26},{19,27},{20,28},{21,29},{22,30},{23,31}} | collective-permute-start | bytes 3145736 | tf_op jit(solution)/shard_map/ppermute | solution.py:679
  519.9 58.1 %collective-permute-start.64 = (bf16[4,4,32,1536]{3,2,1,0:T(8,128)(2,1)S(1)}, bf16[4,4,32,1536]{3,2,1,0:T(8,128)(2,1)}, u32[]{:S(2)}, u32[]{:S(2)}) collective-permute-start(bf16[4,4,32,1536]{3,2,1,0:T(8,128)(2,1)S(1)} %get-tuple-element.120), channel_id=1, source_target_pairs={{0,1},{1,0},{2,3},{3,2},{4,5},{5,4},{6,7},{7,6},{8,9},{9,8},{10,11... | collective-permute-start | bytes 4718600 | tf_op jit(solution)/shard_map/ppermute | solution.py:655
  520.2 60.9 %collective-permute-start.58 = (bf16[4,4,32,1536]{3,2,1,0:T(8,128)(2,1)S(1)}, bf16[4,4,32,1536]{3,2,1,0:T(8,128)(2,1)S(1)}, u32[]{:S(2)}, u32[]{:S(2)}) collective-permute-start(bf16[4,4,32,1536]{3,2,1,0:T(8,128)(2,1)S(1)} %get-tuple-element.118), channel_id=1, source_target_pairs={{0,1},{1,0},{2,3},{3,2},{4,5},{5,4},{6,7},{7,6},{8,9},{9,8},{10,11... | collective-permute-start | bytes 4718600 | tf_op jit(solution)/shard_map/ppermute | solution.py:655
  521.8 24.9 %collective-permute-start.102 = (bf16[512,1024]{1,0:T(8,128)(2,1)}, bf16[512,1024]{1,0:T(8,128)(2,1)}, u32[]{:S(2)}, u32[]{:S(2)}) collective-permute-start(bf16[512,1024]{1,0:T(8,128)(2,1)} %collective-permute-done.101), channel_id=1, source_target_pairs={{16,24},{17,25},{18,26},{19,27},{20,28},{21,29},{22,30},{23,31}} | collective-permute-start | bytes 3145736 | tf_op jit(solution)/shard_map/ppermute | solution.py:679
  525.4 28.2 %collective-permute-start.111 = (bf16[512,1024]{1,0:T(8,128)(2,1)}, bf16[512,1024]{1,0:T(8,128)(2,1)S(1)}, u32[]{:S(2)}, u32[]{:S(2)}) collective-permute-start(bf16[512,1024]{1,0:T(8,128)(2,1)} %collective-permute-done.110), channel_id=1, source_target_pairs={{8,0},{9,1},{10,2},{11,3},{12,4},{13,5},{14,6},{15,7}} | collective-permute-start | bytes 3145736 | tf_op jit(solution)/shard_map/ppermute | solution.py:680
  526.7 47.3 %collective-permute-start.108 = (bf16[512,1024]{1,0:T(8,128)(2,1)}, bf16[512,1024]{1,0:T(8,128)(2,1)}, u32[]{:S(2)}, u32[]{:S(2)}) collective-permute-start(bf16[512,1024]{1,0:T(8,128)(2,1)} %collective-permute-done.107), channel_id=1, source_target_pairs={{8,0},{9,1},{10,2},{11,3},{12,4},{13,5},{14,6},{15,7}} | collective-permute-start | bytes 3145736 | tf_op jit(solution)/shard_map/ppermute | solution.py:680
  546.7 36.4 %collective-permute-start.92 = (bf16[512,1024]{1,0:T(8,128)(2,1)S(1)}, bf16[512,1024]{1,0:T(8,128)(2,1)S(1)}, u32[]{:S(2)}, u32[]{:S(2)}) collective-permute-start(bf16[512,1024]{1,0:T(8,128)(2,1)S(1)} %collective-permute-done.91), channel_id=1, source_target_pairs={{8,16},{16,24},{9,17},{17,25},{10,18},{18,26},{11,19},{19,27},{12,... | collective-permute-start | bytes 3145736 | tf_op jit(solution)/shard_map/ppermute | solution.py:679
  553.6 29.8 %collective-permute-start.89 = (bf16[512,1024]{1,0:T(8,128)(2,1)S(1)}, bf16[512,1024]{1,0:T(8,128)(2,1)S(1)}, u32[]{:S(2)}, u32[]{:S(2)}) collective-permute-start(bf16[512,1024]{1,0:T(8,128)(2,1)S(1)} %copy-done.48), channel_id=1, source_target_pairs={{8,16},{16,24},{9,17},{17,25},{10,18},{18,26},{11,19},{19,27},{12,... | collective-permute-start | bytes 3145736 | tf_op jit(solution)/shard_map/ppermute | solution.py:679
  574.0 28.0 %collective-permute-start.98 = (bf16[512,1024]{1,0:T(8,128)(2,1)S(1)}, bf16[512,1024]{1,0:T(8,128)(2,1)S(1)}, u32[]{:S(2)}, u32[]{:S(2)}) collective-permute-start(bf16[512,1024]{1,0:T(8,128)(2,1)S(1)} %copy-done.50), channel_id=1, source_target_pairs={{8,0},{16,8},{9,1},{17,9},{10,2},{18,10},{11,3},{19,11},{12,4},{20... | collective-permute-start | bytes 3145736 | tf_op jit(solution)/shard_map/ppermute | solution.py:680
  578.0 43.3 %collective-permute-start.95 = (bf16[512,1024]{1,0:T(8,128)(2,1)S(1)}, bf16[512,1024]{1,0:T(8,128)(2,1)S(1)}, u32[]{:S(2)}, u32[]{:S(2)}) collective-permute-start(bf16[512,1024]{1,0:T(8,128)(2,1)S(1)} %copy-done.52), channel_id=1, source_target_pairs={{8,0},{16,8},{9,1},{17,9},{10,2},{18,10},{11,3},{19,11},{12,4},{20... | collective-permute-start | bytes 3145736 | tf_op jit(solution)/shard_map/ppermute | solution.py:680
  581.1 40.4 %collective-permute-start.65 = (bf16[2,4,32,1536]{3,2,1,0:T(8,128)(2,1)S(1)}, bf16[2,4,32,1536]{3,2,1,0:T(8,128)(2,1)S(1)}, u32[]{:S(2)}, u32[]{:S(2)}) collective-permute-start(bf16[2,4,32,1536]{3,2,1,0:T(8,128)(2,1)S(1)} %get-tuple-element.165), channel_id=1, source_target_pairs={{0,4},{1,5},{2,6},{3,7},{4,0},{5,1},{6,2},{7,3},{8,12},{9,13},{10,... | collective-permute-start | bytes 2359304 | tf_op jit(solution)/shard_map/ppermute | solution.py:655
  583.1 41.2 %collective-permute-start.59 = (bf16[2,4,32,1536]{3,2,1,0:T(8,128)(2,1)S(1)}, bf16[2,4,32,1536]{3,2,1,0:T(8,128)(2,1)S(1)}, u32[]{:S(2)}, u32[]{:S(2)}) collective-permute-start(bf16[2,4,32,1536]{3,2,1,0:T(8,128)(2,1)S(1)} %get-tuple-element.167), channel_id=1, source_target_pairs={{0,2},{1,3},{2,0},{3,1},{4,6},{5,7},{6,4},{7,5},{8,10},{9,11},{10,... | collective-permute-start | bytes 2359304 | tf_op jit(solution)/shard_map/ppermute | solution.py:655
  633.3 23.9 %collective-permute-start.69 = (bf16[32,1536]{1,0:T(8,128)(2,1)S(1)}, bf16[32,1536]{1,0:T(8,128)(2,1)S(1)}, u32[]{:S(2)}, u32[]{:S(2)}) collective-permute-start(bf16[32,1536]{1,0:T(8,128)(2,1)S(1)} %get-tuple-element.185), channel_id=1, source_target_pairs={{0,24},{8,0},{16,8},{24,16},{1,25},{9,1},{17,9},{25,17},{2,26},{10... | collective-permute-start | bytes 294920 | tf_op jit(solution)/shard_map/ppermute | solution.py:658
  633.3 24.6 %collective-permute-start.68 = (bf16[32,1536]{1,0:T(8,128)(2,1)S(1)}, bf16[32,1536]{1,0:T(8,128)(2,1)S(1)}, u32[]{:S(2)}, u32[]{:S(2)}) collective-permute-start(bf16[32,1536]{1,0:T(8,128)(2,1)S(1)} %get-tuple-element.186), channel_id=1, source_target_pairs={{0,16},{8,24},{16,0},{24,8},{1,17},{9,25},{17,1},{25,9},{2,18},{10... | collective-permute-start | bytes 294920 | tf_op jit(solution)/shard_map/ppermute | solution.py:658
  634.9 23.8 %collective-permute-start.67 = (bf16[32,1536]{1,0:T(8,128)(2,1)S(1)}, bf16[32,1536]{1,0:T(8,128)(2,1)S(1)}, u32[]{:S(2)}, u32[]{:S(2)}) collective-permute-start(bf16[32,1536]{1,0:T(8,128)(2,1)S(1)} %get-tuple-element.184), channel_id=1, source_target_pairs={{0,8},{8,16},{16,24},{24,0},{1,9},{9,17},{17,25},{25,1},{2,10},{10... | collective-permute-start | bytes 294920 | tf_op jit(solution)/shard_map/ppermute | solution.py:658
  635.5 24.4 %collective-permute-start.63 = (bf16[32,1536]{1,0:T(8,128)(2,1)S(1)}, bf16[32,1536]{1,0:T(8,128)(2,1)S(1)}, u32[]{:S(2)}, u32[]{:S(2)}) collective-permute-start(bf16[32,1536]{1,0:T(8,128)(2,1)S(1)} %get-tuple-element.188), channel_id=1, source_target_pairs={{0,24},{8,0},{16,8},{24,16},{1,25},{9,1},{17,9},{25,17},{2,26},{10... | collective-permute-start | bytes 294920 | tf_op jit(solution)/shard_map/ppermute | solution.py:658
  658.7 29.9 %collective-permute-start.99 = (bf16[512,1024]{1,0:T(8,128)(2,1)S(1)}, bf16[512,1024]{1,0:T(8,128)(2,1)S(1)}, u32[]{:S(2)}, u32[]{:S(2)}) collective-permute-start(bf16[512,1024]{1,0:T(8,128)(2,1)S(1)} %copy-done.58), channel_id=1, source_target_pairs={{8,0},{9,1},{10,2},{11,3},{12,4},{13,5},{14,6},{15,7}} | collective-permute-start | bytes 3145736 | tf_op jit(solution)/shard_map/ppermute | solution.py:680
  660.0 48.3 %collective-permute-start.96 = (bf16[512,1024]{1,0:T(8,128)(2,1)S(1)}, bf16[512,1024]{1,0:T(8,128)(2,1)S(1)}, u32[]{:S(2)}, u32[]{:S(2)}) collective-permute-start(bf16[512,1024]{1,0:T(8,128)(2,1)S(1)} %collective-permute-done.95), channel_id=1, source_target_pairs={{8,0},{9,1},{10,2},{11,3},{12,4},{13,5},{14,6},{15,7}} | collective-permute-start | bytes 3145736 | tf_op jit(solution)/shard_map/ppermute | solution.py:680
  (145 other events, 1577.5 us)

commit v2 on v1

v2 whole, which is shorter than its diff:
```python
from functools import partial

import jax
import jax.numpy as jnp
from jax import lax
from jax.experimental import pallas as pl
from jax.experimental.pallas import tpu as pltpu
from jax.sharding import PartitionSpec as P

HDIM = 64
QB = 256
EPSILON = 1e-05
NEG_FILL = -1e30
GELU_A = 0.7978845608028654
GELU_B = 0.044715
BF = jnp.bfloat16
F32 = jnp.float32
MIB = 1024 * 1024


def dot_nn(left, right):
    return lax.dot_general(left, right, (((1,), (0,)), ((), ())), preferred_element_type=F32)


def dot_nt(left, right):
    return lax.dot_general(left, right, (((1,), (1,)), ((), ())), preferred_element_type=F32)


def norm_rows(x):
    centred = x - jnp.mean(x, -1, keepdims=True)
    inverse = lax.rsqrt(jnp.mean(centred * centred, -1, keepdims=True) + EPSILON)
    return centred * inverse, inverse


def norm_back(grad, normed, inverse, gain):
    scaled = grad * gain
    return inverse * (
        scaled
        - jnp.mean(scaled, -1, keepdims=True)
        - normed * jnp.mean(scaled * normed, -1, keepdims=True)
    )


def gelu_both(u):
    sq = u * u
    t = jnp.tanh(GELU_A * u * (1.0 + GELU_B * sq))
    half = 0.5 * (1.0 + t)
    return u * half, half + (0.5 * u) * (1.0 - t * t) * (GELU_A + (3.0 * GELU_A * GELU_B) * sq)


def run(
    kernel,
    args,
    out_shape,
    deps=(),
    scalars=(),
    grid=(1,),
    specs=None,
    outs=None,
    scratch=(),
    micros=5,
    gates=(),
):
    specs = [whole(a.shape) for a in args] if specs is None else specs
    outs = [whole(o.shape) for o in out_shape] if outs is None else outs
    gates, deps = jax.tree.leaves(gates), jax.tree.leaves(deps)
    first, count, results = len(scalars) + len(args), len(deps) + len(gates), len(out_shape)

    def body(*refs):
        last = first + count + results
        kernel(*refs[:first], *refs[first + count : last], *refs[last + len(gates) :])

    anywhere = pl.BlockSpec(memory_space=pl.ANY)
    res = pl.pallas_call(
        body,
        grid_spec=pltpu.PrefetchScalarGridSpec(
            num_scalar_prefetch=len(scalars),
            grid=grid,
            in_specs=list(specs) + [anywhere] * count,
            out_specs=list(outs) + [anywhere] * len(gates),
            scratch_shapes=list(scratch),
        ),
        out_shape=list(out_shape) + [shaped(g.shape, g.dtype) for g in gates],
        input_output_aliases={first + len(deps) + n: results + n for n in range(len(gates))},
        compiler_params=pltpu.CompilerParams(vmem_limit_bytes=60 * MIB),
        cost_estimate=pl.CostEstimate(
            flops=int(micros * 0.517e9), bytes_accessed=10**6, transcendentals=0
        ),
    )(*scalars, *args, *deps, *gates)
    return (list(res[:results]), list(res[results:])) if gates else res


def shaped(shape, dtype=BF):
    return jax.ShapeDtypeStruct(tuple(shape), dtype)


def whole(shape):
    return pl.BlockSpec(shape, lambda *_: (0,) * len(shape), pipeline_mode=pl.Buffered(1))


def one_hot(ids, other):
    return jnp.where(ids == other, 1.0, 0.0).astype(BF)


def seq_kernel(count, ids_ref, rows_ref, *refs):
    pieces, (seq_ref, ln_ref, lnt_ref, *gain_refs) = refs[:count], refs[count:]
    gains = 0.0
    for piece in pieces:
        for z in range(piece.shape[0]):
            gains = gains + piece[z].astype(F32)
    for n, ref in enumerate(gain_refs):
        ref[...] = gains[n : n + 1]
    total = rows_ref.shape[0]
    for r in range(0, total, QB):
        lanes = lax.broadcasted_iota(jnp.int32, (QB, total), 1)
        x = dot_nn(one_hot(ids_ref[r : r + QB], lanes), rows_ref[...])
        seq_ref[r : r + QB] = x.astype(BF)
        normed, _ = norm_rows(x)
        ln = (normed * gains[0:1] + gains[1:2]).astype(BF)
        ln_ref[r : r + QB] = ln
        lnt_ref[:, r : r + QB] = jnp.transpose(ln)


def seq_norm(ids_col, rows, pieces, deps=()):
    total, width = rows.shape
    groups = pieces[0][0].shape[0]
    res = run(
        partial(seq_kernel, len(pieces)),
        (ids_col, rows, *[a for a, _ in pieces]),
        [shaped((total, width)), shaped((total, width)), shaped((width, total))]
        + [shaped((1, width), F32)] * 4,
        deps,
        specs=[whole(ids_col.shape), whole(rows.shape)]
        + [pl.BlockSpec((groups, 16, width), lambda i, n=n: (0, n, 0)) for _, n in pieces],
        micros=6,
    )
    return *res[:3], res[3:]


def place(meta, refs, full):
    groups, experts = full.shape[0], full.shape[1]
    for r in range(experts):
        for z in range(groups):
            row = lax.rem(meta[1] + (groups - z), groups)
            if len(refs) == 1:
                full[row, r] = refs[0][r, z]
            else:
                full[row, r ^ meta[0]] = refs[r][z]


def piece_specs(pieces, step):
    specs = []
    for array, n in pieces:
        shape = (*array.shape[:-2], step, array.shape[-1])
        at = (0,) * (len(shape) - 2) + (n, 0)
        specs.append(pl.BlockSpec(shape, lambda *_, at=at: at, pipeline_mode=pl.Buffered(1)))
    return specs


def stack_kernel(groups, *refs):
    ins, outs = refs[:groups], refs[groups:]
    for z in range(groups):
        row = 0
        for out in outs:
            out[z] = ins[z][row : row + out.shape[1]]
            row += out.shape[1]


def stack(blocks, rows, deps=()):
    width = blocks[0].shape[1]
    return run(
        partial(stack_kernel, len(blocks)),
        blocks,
        [shaped((len(blocks), r, width)) for r in rows],
        deps,
        micros=2,
    )


def proj_kernel(count, meta, ln_ref, *refs):
    pieces, (out_ref, full_ref) = refs[:count], refs[count:]
    place(meta, pieces, full_ref)
    width = ln_ref.shape[1]
    out_ref[...] = dot_nn(ln_ref[...], full_ref[...].reshape(width, width)).astype(BF)


def project(meta, ln, pieces, full, deps=(), gates=()):
    width = ln.shape[1]
    res = run(
        partial(proj_kernel, len(pieces)),
        (ln, *[a for a, _ in pieces]),
        [shaped(ln.shape), shaped(full)],
        deps,
        (meta,),
        specs=[whole(ln.shape)] + piece_specs(pieces, full[2]),
        gates=gates,
    )
    (out, mat), *gates = res if gates else (res,)
    return (out, mat.reshape(width, width), *gates)


def attend_kernel(flag, q_ref, k_ref, v_ref, o_ref, lse_ref, lse_cols):
    total = q_ref.shape[0]
    low = lax.broadcasted_iota(jnp.int32, (1, 2 * HDIM), 1) < HDIM
    causal = lax.broadcasted_iota(jnp.int32, (QB, QB), 1) <= lax.broadcasted_iota(
        jnp.int32, (QB, QB), 0
    )

    def run(long):
        for a in range(0, total, QB):
            b = a + QB
            q = q_ref[a:b]
            outs, logs = [], []
            for keep in (low, ~low):
                qh = jnp.where(keep, q, jnp.zeros_like(q)) * BF(HDIM**-0.5)
                near = jnp.where(causal, dot_nt(qh, k_ref[a:b]), NEG_FILL)
                top = jnp.max(near, 1, keepdims=True)
                if long and a > 0:
                    far = dot_nt(qh, k_ref[0:a])
                    top = jnp.maximum(top, jnp.max(far, 1, keepdims=True))
                near = jnp.exp(near - top)
                mass = jnp.sum(near, 1, keepdims=True)
                o = dot_nn(near.astype(BF), v_ref[a:b])
                if long and a > 0:
                    far = jnp.exp(far - top)
                    mass = mass + jnp.sum(far, 1, keepdims=True)
                    o = o + dot_nn(far.astype(BF), v_ref[0:a])
                outs.append(o * (1.0 / mass))
                logs.append(top + jnp.log(mass))
            o_ref[a:b] = jnp.where(low, outs[0], outs[1]).astype(BF)
            lse_cols[a:b] = jnp.where(low, logs[0], logs[1])

    @pl.when(flag[0] > QB)
    def _():
        run(True)

    @pl.when(flag[0] <= QB)
    def _():
        run(False)

    turned = jnp.transpose(lse_cols[...])
    lse_ref[0, 0:1] = turned[0:1]
    lse_ref[0, 1:2] = turned[HDIM : HDIM + 1]


def attend(flag, q, k, v, deps=()):
    total, width = q.shape
    pair = 2 * HDIM
    block = pl.BlockSpec((total, pair), lambda j, *_: (0, j))
    stat = pl.BlockSpec((1, 8, total), lambda j, *_: (j, 0, 0))
    return run(
        attend_kernel,
        (q, k, v),
        [shaped((total, width)), shaped((width // pair, 8, total), F32)],
        deps,
        (flag,),
        (width // pair,),
        [block] * 3,
        [block, stat],
        [pltpu.VMEM((total, pair), F32)],
        micros=30,
    )


def attend_back_kernel(
    flag, q_ref, k_ref, v_ref, o_ref, g_ref, lse_ref, dq_ref, dk_ref, dv_ref, dq_turned
):
    total = q_ref.shape[0]
    low = lax.broadcasted_iota(jnp.int32, (1, 2 * HDIM), 1) < HDIM
    causal = lax.broadcasted_iota(jnp.int32, (QB, QB), 0) <= lax.broadcasted_iota(
        jnp.int32, (QB, QB), 1
    )
    prod = jnp.transpose(g_ref[...].astype(F32) * o_ref[...].astype(F32))
    delta = [jnp.sum(prod[h * HDIM : (h + 1) * HDIM], 0, keepdims=True) for h in range(2)]
    k_turned = jnp.transpose(k_ref[...])

    def run(long):
        for a in range(0, total, QB):
            b = a + QB
            ks, vs = k_ref[a:b], v_ref[a:b]
            dks, dvs = [], []
            for h, keep in enumerate((low, ~low)):
                kh = jnp.where(keep, ks, jnp.zeros_like(ks)) * BF(HDIM**-0.5)
                vh = jnp.where(keep, vs, jnp.zeros_like(vs))
                kth = k_turned[h * HDIM : (h + 1) * HDIM, a:b]
                spans = [(a, b)]
                if long and b < total:
                    spans.append((b, total))
                dk = dv = None
                for lo, hi in spans:
                    qs, gs = q_ref[lo:hi], g_ref[lo:hi]
                    probs = jnp.exp(dot_nt(kh, qs) - lse_ref[0, h : h + 1, lo:hi])
                    if lo == a:
                        probs = jnp.where(causal, probs, 0.0)
                    dp = dot_nt(vh, gs)
                    ds = (probs * (dp - delta[h][:, lo:hi])).astype(BF)
                    dv_part, dk_part = dot_nn(probs.astype(BF), gs), dot_nn(ds, qs)
                    dk = dk_part if dk is None else dk + dk_part
                    dv = dv_part if dv is None else dv + dv_part
                    rows = slice(h * HDIM, (h + 1) * HDIM)
                    if a == 0 or not long:
                        dq_turned[rows, lo:hi] = dot_nn(kth, ds)
                    else:
                        dq_turned[rows, lo:hi] += dot_nn(kth, ds)
                dks.append(dk)
                dvs.append(dv)
            dk_ref[a:b] = (jnp.where(low, dks[0], dks[1]) * HDIM**-0.5).astype(BF)
            dv_ref[a:b] = jnp.where(low, dvs[0], dvs[1]).astype(BF)

    @pl.when(flag[0] > QB)
    def _():
        run(True)

    @pl.when(flag[0] <= QB)
    def _():
        run(False)

    dq_ref[...] = (jnp.transpose(dq_turned[...]) * HDIM**-0.5).astype(BF)


def attend_back(flag, q, k, v, o, g, lse, first, count, deps=(), gates=()):
    total = q.shape[0]
    pair = 2 * HDIM
    block = pl.BlockSpec((total, pair), lambda j, *_: (0, j + first))
    stat = pl.BlockSpec((1, 8, total), lambda j, *_: (j + first, 0, 0))
    done = pl.BlockSpec((total, pair), lambda j, *_: (0, j))
    return run(
        attend_back_kernel,
        (q, k, v, o, g, lse),
        [shaped((total, pair * count))] * 3,
        deps,
        (flag,),
        (count,),
        [block] * 5 + [stat],
        [done] * 3,
        [pltpu.VMEM((pair, total), F32)],
        micros=20,
        gates=gates,
    )


def mix_kernel(count, meta, attn_ref, seq_ref, ids_ref, *refs):
    pieces, (full_ref, out_ref, mixed) = refs[:count], refs[count:]
    place(meta, pieces, full_ref)
    total, width = mixed.shape
    mat = full_ref[...].reshape(width, width)
    for r in range(0, total, QB):
        x = seq_ref[r : r + QB].astype(F32) + dot_nn(attn_ref[r : r + QB], mat)
        mixed[r : r + QB] = x.astype(BF)
    to_experts(ids_ref, mixed, out_ref)


def to_experts(ids_ref, rows, out_ref):
    total = rows.shape[0]
    for r in range(0, total, QB):
        want = lax.broadcasted_iota(jnp.int32, (QB, total), 0) + r
        out_ref[r : r + QB] = dot_nn(one_hot(want, ids_ref[...]), rows[...]).astype(BF)


def mix(meta, attn, seq, ids_row, pieces, full, deps=()):
    width = attn.shape[1]
    mat, out = run(
        partial(mix_kernel, len(pieces)),
        (attn, seq, ids_row, *[a for a, _ in pieces]),
        [shaped(full), shaped(attn.shape)],
        deps,
        (meta,),
        specs=[whole(attn.shape)] * 2 + [whole(ids_row.shape)] + piece_specs(pieces, full[2]),
        scratch=[pltpu.VMEM(attn.shape, BF)],
        micros=9,
    )
    return mat.reshape(width, width), out


def act_grad_kernel(cot_ref, wo_ref, out_ref):
    out_ref[...] = dot_nn(cot_ref[...], wo_ref[...]).astype(BF)


def act_grad(cot, w_out, deps=()):
    total, width = cot.shape
    hidden, tile = w_out.shape[1], 512
    return run(
        act_grad_kernel,
        (cot, w_out),
        [shaped((total, hidden))],
        deps,
        (),
        (hidden // tile,),
        [whole(cot.shape), pl.BlockSpec((width, tile), lambda f: (0, f))],
        [pl.BlockSpec((total, tile), lambda f: (0, f))],
        micros=11,
    )[0]


def expert_kernel(
    steps, x_ref, cot_ref, gain_ref, bias_ref, wi_ref, dact_ref, act_ref, dx_ref, sums_ref, ln, acc
):
    f = pl.program_id(0)
    total, width = ln.shape

    @pl.when(f == 0)
    def _():
        for r in range(0, total, QB):
            normed, _ = norm_rows(x_ref[r : r + QB].astype(F32))
            ln[r : r + QB] = (normed * gain_ref[...] + bias_ref[...]).astype(BF)

    def body(first):
        for r in range(0, total, 512):
            rows = slice(r, r + 512)
            act, slope = gelu_both(dot_nn(ln[rows], wi_ref[...]))
            act_ref[rows] = act.astype(BF)
            back = (dact_ref[rows].astype(F32) * slope).astype(BF)
            if first:
                acc[rows] = dot_nt(back, wi_ref[...])
            else:
                acc[rows] += dot_nt(back, wi_ref[...])

    @pl.when(f == 0)
    def _():
        body(True)

    @pl.when(f > 0)
    def _():
        body(False)

    @pl.when(f == steps - 1)
    def _():
        gain_sum = jnp.zeros((1, width), F32)
        bias_sum = gain_sum
        for r in range(0, total, QB):
            rows = slice(r, r + QB)
            normed, inverse = norm_rows(x_ref[rows].astype(F32))
            d = acc[rows]
            gain_sum = gain_sum + jnp.sum(d * normed, 0, keepdims=True)
            bias_sum = bias_sum + jnp.sum(d, 0, keepdims=True)
            back = norm_back(d, normed, inverse, gain_ref[...])
            dx_ref[rows] = (cot_ref[rows].astype(F32) + back).astype(BF)
        sums_ref[0:1] = gain_sum
        sums_ref[1:2] = bias_sum


def expert(x, cot, gain, bias, w_in, dact, deps=()):
    total, width = x.shape
    hidden, tile = w_in.shape[1], 512
    steps = hidden // tile
    cols = pl.BlockSpec((width, tile), lambda f: (0, f))
    rows = pl.BlockSpec((total, tile), lambda f: (0, f))
    return run(
        partial(expert_kernel, steps),
        (x, cot, gain, bias, w_in, dact),
        [shaped((total, hidden)), shaped(x.shape), shaped((8, width), F32)],
        deps,
        (),
        (steps,),
        [whole(x.shape)] * 2 + [whole((1, width))] * 2 + [cols, rows],
        [rows, whole(x.shape), whole((8, width))],
        [pltpu.VMEM(x.shape, BF), pltpu.VMEM(x.shape, F32)],
        micros=34,
    )


def expert_out_kernel(x_ref, act_ref, wo_ref, out_ref):
    out = x_ref[...].astype(F32) + dot_nt(act_ref[...], wo_ref[...])
    out_ref[...] = out.astype(BF)


def expert_out(x, act, w_out, deps=()):
    total, width = x.shape
    hidden, tile = w_out.shape[1], 256
    part = pl.BlockSpec((total, tile), lambda n: (0, n))
    return run(
        expert_out_kernel,
        (x, act, w_out),
        [shaped(x.shape)],
        deps,
        (),
        (width // tile,),
        [part, whole(act.shape), pl.BlockSpec((tile, hidden), lambda n: (n, 0))],
        [part],
        micros=12,
    )[0]


def turn_kernel(meta, wi_ref, wo_ref, wit_ref, wot_ref):
    wit_ref[...] = jnp.transpose(wi_ref[...])
    wot_ref[...] = jnp.transpose(wo_ref[...])


def turn_slices(meta, w_in, w_out, hidden):
    width, tile = w_in.shape[0], min(256, hidden)
    tiles = hidden // tile
    cols = pl.BlockSpec((width, tile), lambda f, m: (0, m[1] * tiles + f))
    rows = pl.BlockSpec((tile, width), lambda f, m: (f, 0))
    return run(
        turn_kernel,
        (w_in, w_out),
        [shaped((hidden, width))] * 2,
        (),
        (meta,),
        (tiles,),
        [cols] * 2,
        [rows] * 2,
        micros=5,
    )


def slice_kernel(count, first, last, flags, *refs):
    xs, cots = refs[:count], refs[count : 2 * count]
    gain_ref, bias_ref, wi_ref, wo_ref = refs[2 * count : 2 * count + 4]
    rest = refs[2 * count + 4 :]
    if not first:
        in_prev, out_prev = rest[:2]
        rest = rest[2:]
    in_ref, out_ref, in_acc, out_acc, lns, rows, sems = rest
    f = pl.program_id(0)
    total = lns.shape[1]

    def copies(n):
        return (
            pltpu.make_async_copy(xs[n], lns.at[n], sems.at[n, 0]),
            pltpu.make_async_copy(cots[n], rows.at[n], sems.at[n, 1]),
        )

    for n in range(count):

        @pl.when((f == 0) & (flags[n] > 0))
        def _(n=n):
            for copy in copies(n):
                copy.start()

    if first:
        in_acc[...] = jnp.zeros_like(in_acc)
        out_acc[...] = jnp.zeros_like(out_acc)
    else:
        in_acc[...] = in_prev[...]
        out_acc[...] = out_prev[...]
    for n in range(count):

        @pl.when(flags[n] > 0)
        def _(n=n):
            @pl.when(f == 0)
            def _():
                for copy in copies(n):
                    copy.wait()
                for r in range(0, total, QB):
                    normed, _ = norm_rows(lns[n, r : r + QB].astype(F32))
                    lns[n, r : r + QB] = (normed * gain_ref[...] + bias_ref[...]).astype(BF)

            pre = dot_nt(wi_ref[...], lns[n])
            grad = dot_nt(wo_ref[...], rows[n])
            act, slope = gelu_both(pre)
            back = (grad * slope).astype(BF)
            in_acc[...] += dot_nn(back, lns[n])
            out_acc[...] += dot_nn(act.astype(BF), rows[n])

    if last:
        in_ref[...] = jnp.transpose(in_acc[...])
        out_ref[...] = jnp.transpose(out_acc[...])
    else:
        in_ref[...] = in_acc[...]
        out_ref[...] = out_acc[...]


def slice_grads(flags, xs, cots, gain, bias, wi_turned, wo_turned, prev, last, deps=()):
    count = len(xs)
    total, width = xs[0].shape
    hidden = wi_turned.shape[0]
    tile = min(256, hidden)
    rows = pl.BlockSpec((tile, width), lambda f, *_: (f, 0))
    cols = pl.BlockSpec((width, tile), lambda f, *_: (0, f))
    anywhere = pl.BlockSpec(memory_space=pl.ANY)
    first = prev is None
    return run(
        partial(slice_kernel, count, first, last),
        (*xs, *cots, gain, bias, wi_turned, wo_turned, *(() if first else prev)),
        [shaped((width, hidden) if last else (hidden, width), F32)] * 2,
        deps,
        (flags,),
        (hidden // tile,),
        [anywhere] * (2 * count)
        + [whole((1, width))] * 2
        + [rows] * (2 if first else 4),
        [cols if last else rows] * 2,
        [pltpu.VMEM((tile, width), F32)] * 2
        + [pltpu.VMEM((count, total, width), BF)] * 2
        + [pltpu.SemaphoreType.DMA((count, 2))],
        micros=18,
    )


def back_kernel(ids_ref, mat_ref, rows_ref, dmix_ref, dattn_ref):
    total = rows_ref.shape[0]
    for r in range(0, total, QB):
        lanes = lax.broadcasted_iota(jnp.int32, (QB, total), 1)
        x = dot_nn(one_hot(ids_ref[r : r + QB], lanes), rows_ref[...]).astype(BF)
        dmix_ref[r : r + QB] = x
        dattn_ref[r : r + QB] = dot_nt(x, mat_ref[...]).astype(BF)


def back_in(ids_col, mat, rows, deps=(), gates=()):
    return run(back_kernel, (ids_col, mat, rows), [shaped(rows.shape)] * 2, deps, gates=gates)


def shared_kernel(picks, turns, sums_in, meta, *refs):
    lefts, rights = refs[: len(turns)], refs[len(turns) : len(turns) + len(picks)]
    rest = refs[len(turns) + len(picks) :]
    small, (send, keep, sums) = rest[:sums_in], rest[sums_in:]
    half, step = send.shape[0], send.shape[2]
    turned = [jnp.transpose(l[...]) if t else l[...] for l, t in zip(lefts, turns)]

    def put(cols, size):
        for r in range(2 * half):
            row = pl.multiple_of((r ^ meta[0]) * step, step)
            ref = send if r % 2 else keep
            ref[r // 2, 0, :, cols : cols + size] = sums[pl.ds(row, step), :size].astype(BF)

    cols = 0
    for pick, right in zip(picks, rights):
        size = right.shape[1]
        sums[:, :size] = dot_nn(turned[pick], right[...])
        put(cols, size)
        cols += size
    if sums_in:
        sums[:, :128] = jnp.zeros((sums.shape[0], 128), F32)
        for n in range(sums_in):
            sums[:, 8 * n : 8 * n + 8] = jnp.transpose(small[n][...])
        put(cols, 128)


def shared_grads(meta, lefts, terms, small, experts, groups, deps=(), gates=()):
    total = terms[0][1].shape[0]
    array, is_turned = lefts[0]
    features = array.shape[0 if is_turned else 1]
    step, block = features // (experts * groups), features // groups
    width = sum(r.shape[1] for _, r in terms) + (128 if small else 0)
    as_is = pl.BlockSpec((block, total), lambda g, *_: (g, 0))
    to_turn = pl.BlockSpec((total, block), lambda g, *_: (0, g))
    sums = pl.BlockSpec((8, block), lambda g, *_: (0, g))
    shape = (experts // 2, groups, step, width)
    spec = pl.BlockSpec((shape[0], 1, step, width), lambda g, *_: (0, g, 0, 0))
    return run(
        partial(shared_kernel, [p for p, _ in terms], [not t for _, t in lefts], len(small)),
        (*[a for a, _ in lefts], *[r for _, r in terms], *small),
        [shaped(shape)] * 2,
        deps,
        (meta,),
        (groups,),
        [as_is if t else to_turn for _, t in lefts]
        + [whole(r.shape) for _, r in terms]
        + [sums] * len(small),
        [spec] * 2,
        [pltpu.VMEM((block, max(r.shape[1] for _, r in terms)), F32)],
        micros=8,
        gates=gates,
    )


def halve_kernel(keep_ref, got_ref, *outs):
    for r, out in enumerate(outs):
        both = keep_ref[r].astype(F32) + got_ref[r].astype(F32)
        out[...] = both.astype(out.dtype)


def halve(keep, got, deps=()):
    chips, tail = keep.shape[0], keep.shape[1:]
    kinds = [F32] + [BF] * (chips - 1)
    return run(halve_kernel, (keep, got), [shaped(tail, k) for k in kinds], deps, micros=2)


def total_kernel(own_ref, *refs):
    ins, (all_ref, low_ref) = refs[:-2], refs[-2:]
    total = own_ref[...]
    for ref in ins:
        total = total + ref[...].astype(F32)
    all_ref[...] = total
    low_ref[...] = total.astype(BF)


def total_of(own, others):
    return run(
        total_kernel,
        (own, *others),
        [shaped(own.shape, F32), shaped(own.shape)],
        micros=2,
    )


def final_kernel(count, heads, meta, *refs):
    owns, ins = refs[:2], refs[2 : 2 + 2 * count]
    o_ref, q_ref, k_ref, v_ref, small_ref = refs[2 + 2 * count :]
    first = owns[0][meta[1]]
    second = owns[1][meta[1]]
    for n in range(count):
        first = first + ins[2 * n][...].astype(F32)
        second = second + ins[2 * n + 1][...].astype(F32)
    width = o_ref.shape[1]
    o_ref[...] = first[:, :width]
    for n, ref in enumerate((q_ref, k_ref, v_ref)):
        ref[:, :heads] = first[:, width + n * heads : width + (n + 1) * heads]
        ref[:, heads:] = second[:, n * heads : (n + 1) * heads]
    small_ref[...] = second[:, 3 * heads :]


def final(meta, owns, pairs):
    step = owns[0].shape[1]
    heads = (owns[1].shape[2] - 128) // 3
    width = owns[0].shape[2] - 3 * heads
    return run(
        partial(final_kernel, len(pairs), heads),
        (*owns, *[a for p in pairs for a in p]),
        [shaped((step, width), F32)] * 4 + [shaped((step, 128), F32)],
        (),
        (meta,),
        micros=2,
    )


def first_kernel(steps, count, *refs):
    grads, mats = refs[: 3 * count], refs[3 * count : 3 * count + 3]
    seq_ref, dmix_ref, gain_ref, ids_ref, out_ref, sums_ref, rows = refs[3 * count + 3 :]
    r = pl.program_id(0)
    size, part = grads[0].shape
    grad = None
    for n in range(3):
        for j in range(count):
            term = dot_nt(grads[n * count + j][...], mats[n][:, j * part : (j + 1) * part])
            grad = term if grad is None else grad + term
    normed, inverse = norm_rows(seq_ref[...].astype(F32))
    gain_sum = jnp.sum(grad * normed, 0, keepdims=True)
    bias_sum = jnp.sum(grad, 0, keepdims=True)

    @pl.when(r == 0)
    def _():
        sums_ref[0:1] = gain_sum
        sums_ref[1:2] = bias_sum

    @pl.when(r > 0)
    def _():
        sums_ref[0:1] += gain_sum
        sums_ref[1:2] += bias_sum

    back = dmix_ref[...].astype(F32) + norm_back(grad, normed, inverse, gain_ref[...])
    rows[pl.ds(pl.multiple_of(r * size, size), size)] = back.astype(BF)

    @pl.when(r == steps - 1)
    def _():
        to_experts(ids_ref, rows, out_ref)


def first_back(dqs, dks, dvs, mats, seq, dmix, gain, ids_row, deps=(), gates=()):
    total, width = seq.shape
    steps, count = total // QB, len(dqs)
    block = pl.BlockSpec((QB, width), lambda r: (r, 0))
    part = pl.BlockSpec((QB, width // count), lambda r: (r, 0))
    return run(
        partial(first_kernel, steps, count),
        (*dqs, *dks, *dvs, *mats, seq, dmix, gain, ids_row),
        [shaped((total, width)), shaped((8, width), F32)],
        deps,
        (),
        (steps,),
        [part] * (3 * count)
        + [whole((width, width))] * 3
        + [block] * 2
        + [whole((1, width)), whole((1, total))],
        scratch=[pltpu.VMEM((total, width), BF)],
        micros=12,
        gates=gates,
    )


def local(
    n_grp,
    n_exp,
    tokens,
    cotangent,
    arrival,
    seq_length,
    w_q,
    w_k,
    w_v,
    w_o,
    ln1_gain,
    ln1_bias,
    ln2_gain,
    ln2_bias,
    w_in,
    w_out,
):
    me, grp = lax.axis_index("exp"), lax.axis_index("grp")
    meta = jnp.stack([me, grp]).astype(jnp.int32)
    width = tokens.shape[1]
    step = w_q.shape[0]
    hidden = w_in.shape[2] // n_grp
    both = ("grp", "exp")

    def swap(a, k):
        return lax.ppermute(a, "exp", [(i, i ^ k) for i in range(n_exp)])

    def shift(a, k):
        return lax.ppermute(a, "grp", [(i, (i + k) % n_grp) for i in range(n_grp)])

    def exchange(rows):
        return lax.all_to_all(rows, "exp", split_axis=0, concat_axis=0, tiled=True)

    bits = []
    while 2 ** len(bits) < n_exp:
        bits.append(2 ** len(bits))
    orders = [bits[:0:-1] + bits[:1], bits[1:] + bits[:1]]

    def gather_pair(own, cut):
        first = lambda a: a[0] if isinstance(a, tuple) else a[:, :cut]
        second = lambda a: a[1] if isinstance(a, tuple) else a[:, cut:]
        have = {0: own}
        for r in sorted(range(1, n_exp), key=lambda r: (bin(r).count("1"), -r)):
            b, c = (max((b for b in bits if r & b), key=order.index) for order in orders)
            if b == c and not isinstance(have[r ^ b], tuple):
                have[r] = swap(have[r ^ b], b)
            else:
                have[r] = (swap(first(have[r ^ b]), b), swap(second(have[r ^ c]), c))
        return [have[r] for r in range(n_exp)]

    def line_step(t, up, down):
        up = lax.ppermute(up, "grp", [(i, i + 1) for i in range(t - 1, n_grp - 1)])
        down = lax.ppermute(down, "grp", [(i + 1, i) for i in range(n_grp - t)])
        return up, down

    def line(a):
        steps = [(a, a)]
        for t in range(1, n_grp):
            steps.append(line_step(t, *steps[-1]))
        return steps

    ids_row = arrival
    ids_col = arrival.reshape(-1, 1)
    flag = seq_length

    gains = jnp.stack([ln1_gain, ln1_bias, ln2_gain, ln2_bias])
    mine = jnp.zeros((16, width), BF)
    mine = lax.dynamic_update_slice(mine, gains, (0, (grp * n_exp + me) * step))
    mine = jnp.concatenate([w_q, w_k, mine, w_v, w_o])
    mine = [mine] + [shift(mine, k) for k in range(1, n_grp)]
    arrived = exchange(tokens)
    w_first, w_second = w_in[0], w_out[0]
    wi_turned, wo_turned = turn_slices(meta, w_first, w_second, hidden)
    dact = act_grad(cotangent, w_second)
    pair_qk, pair_vo = stack(mine, (2 * step + 16, 2 * step), deps=(arrived, dact, wi_turned))
    pieces = gather_pair(pair_qk, step)
    all_vo = lax.all_gather(pair_vo, "exp", axis=0)

    full = (n_grp, n_exp, step, width)
    is_cut = lambda a: isinstance(a, tuple)
    pieces_q = [(a[0], 0) if is_cut(a) else (a, 0) for a in pieces]
    pieces_k = [(a[1], 0) if is_cut(a) else (a, 1) for a in pieces]
    pieces_g = [
        (a[1], step // 16) if is_cut(a) else (a, 2 * step // 16) for a in pieces
    ]
    pieces_v, pieces_o = [(all_vo, 0)], [(all_vo, 1)]

    cot_line, x_line = [(cotangent,) * 2], []

    def forward(steps, gated=None):
        if len(steps) < n_grp:
            steps.append(line_step(len(steps), *(gated or steps[-1])))
        return steps[-1]

    forward(cot_line)
    seq, ln_one, ln_turned, gains = seq_norm(ids_col, arrived, pieces_g)
    q, mat_q = project(meta, ln_one, pieces_q, full)
    k, mat_k = project(meta, ln_one, pieces_k, full)
    v, mat_v, cot_line[1] = project(meta, ln_one, pieces_v, full, deps=(q, k), gates=cot_line[1])
    forward(cot_line)
    attn, lse = attend(flag, q, k, v)
    mat_o, leaving = mix(meta, attn, seq, ids_row, pieces_o, full)
    x = exchange(leaving)

    act, dx, sums_two = expert(
        x, cotangent, gains[2], gains[3], w_first, dact, deps=cot_line[-1]
    )
    forward(cot_line)
    x_line = [(x,) * 2]
    forward(x_line)
    output = expert_out(x, act, w_second)

    def slices(t, sums, deps=()):
        flags = [(grp >= t).astype(jnp.int32), (grp + t < n_grp).astype(jnp.int32)]
        xs, cots = list(x_line[t]), list(cot_line[t])
        if t == 0:
            xs, cots, flags = xs[:1], cots[:1], flags[:1]
        return slice_grads(
            jnp.stack(flags),
            xs,
            cots,
            gains[2],
            gains[3],
            wi_turned,
            wo_turned,
            sums,
            t == n_grp - 1,
            deps,
        )

    slice_sums = slices(0, None, deps=output)
    back = exchange(dx)
    (dmix, dattn), x_line[1] = back_in(
        ids_col, mat_o, back, deps=slice_sums, gates=x_line[1]
    )
    forward(x_line)

    pairs = width // (2 * HDIM)
    early = attend_back(flag, q, k, v, attn, dattn, lse, 0, pairs // 2)
    send, keep = shared_grads(
        meta,
        [(attn, False), (ln_turned, True)],
        [(0, dmix)] + [(1, g) for g in early],
        [],
        n_exp,
        n_grp,
    )
    gates = x_line[2] if n_grp > 2 else dmix
    rest, gates = attend_back(
        flag, q, k, v, attn, dattn, lse, pairs // 2, pairs // 2, deps=send, gates=gates
    )
    if n_grp > 2:
        x_line[2] = gates
    for _ in range(3, n_grp):
        forward(cot_line)
        forward(x_line)
    first = halve(keep, swap(send, 1), deps=rest)
    dqs, dks, dvs = zip(early, rest)
    dfirst, sums_one = first_back(
        dqs, dks, dvs, (mat_q, mat_k, mat_v), seq, dmix, gains[0], ids_row, deps=first
    )
    (send, keep), dfirst = shared_grads(
        meta,
        [(ln_turned, True)],
        [(0, g) for g in rest],
        [sums_one, sums_two],
        n_exp,
        n_grp,
        gates=dfirst,
    )
    grad_x = exchange(dfirst[0])
    slice_sums = slices(1, slice_sums, send)
    second = halve(keep, swap(send, 1), deps=slice_sums)

    def over_chips(parts):
        others = [swap(parts[r], 2 * r) for r in range(1, n_exp // 2)]
        return total_of(parts[0], others)

    first = over_chips(first)
    for t in range(2, n_grp):
        deps = (first, second, x_line[-1]) if t == 2 else ()
        if t == n_grp - 1:
            second = over_chips(second)
            deps = second
        slice_sums = slices(t, slice_sums, deps)
    grad_w_in, grad_w_out = slice_sums

    parts = []
    for n in range(1, n_grp):
        at = (grp + n) % n_grp
        parts.append(
            [shift(lax.dynamic_index_in_dim(a[1], at, 0, False), n) for a in (first, second)]
        )
    *shared, small = final(meta, (first[0], second[0]), parts)
    small = [small[:, n] for n in (0, 1, 8, 9)]
    grad_w_o, *grads = shared

    return (
        output,
        grad_x,
        *grads,
        grad_w_o,
        *small,
        grad_w_in[None],
        grad_w_out[None],
    )


def solution(mesh):
    both = ("grp", "exp")
    rows, flat, mats = P(both, None), P(both), P("exp", None, None)
    split = P("exp", None, "grp")
    return jax.shard_map(
        partial(local, mesh.shape["grp"], mesh.shape["exp"]),
        mesh=mesh,
        in_specs=(rows, rows, rows, flat) + (rows,) * 4 + (flat,) * 4 + (mats, mats),
        out_specs=(rows,) * 6 + (flat,) * 4 + (split, split),
        check_vma=False,
    )
```

time: 738 us -> 521 us (0.71)
  waiting for transfers between devices: 253 us -> 49.3 us
  blocking collectives: 0 us -> 47.8 us
  local copies, waits for them, and re-layouts: 59.2 us -> 15.1 us
  Pallas kernels: 255 us -> 285 us
  other arithmetic: 29.9 us -> 2.36 us
  starting transfers between devices: 128 us -> 102 us
  between operations: 3 us -> 15.7 us
    ppermute x24 -> x12, waiting for transfers between devices: 127 us -> 28.1 us  [the longest x6 28.1 us: line_step(): down = lax.ppermute(down, 'grp', [(i + 1, i) for i in range(n_grp - t)])]
    ppermute x64 -> x17, waiting for transfers between devices: 106 us -> 21.1 us  [swap(): return lax.ppermute(a, 'exp', [(i, i ^ k) for i in range(n_exp)])]
    all_to_all x0 -> x1, blocking collectives: none -> 47.8 us  [exchange(): return lax.all_to_all(rows, 'exp', split_axis=0, concat_axis=0, tiled=True)]
    pallas_call x17 -> x26, Pallas kernels: 255 us -> 285 us  [run(): pl.pallas_call(body, grid_spec=pltpu.PrefetchScalarGridSpec(num_scalar_pr...]
    unnamed x183 -> x67, local copies, waits for them, and re-layouts: 37 us -> 9.9 us
    ppermute x64 -> x17, starting transfers between devices: 48.2 us -> 21.3 us  [swap(): return lax.ppermute(a, 'exp', [(i, i ^ k) for i in range(n_exp)])]
    concatenate x17 -> x0, other arithmetic: 22.7 us -> none  [the longest x6 18.2 us: local(): cots.append(jnp.concatenate([p[way][t - 1] for p in cot_lines]))]
    ppermute x24 -> x9, waiting for transfers between devices: 20.5 us -> 0.02 us  [shift(): return lax.ppermute(a, 'grp', [(i, (i + k) % n_grp) for i in range(n_grp)])]
  transfers between devices with their start and end apart: 112 -> 42, of which waited for: 37 -> 6; matrix products, arithmetic and copies ran while one was open for 9% -> 1% of each run, Pallas kernels for 25% -> 51%
where the time goes in v2:
time: 521 us; the launch traced here: 517 us
  Pallas kernels  285 us (55%)
  starting transfers between devices  102 us (20%)
  waiting for transfers between devices  49.3 us (9%)
  blocking collectives  47.8 us (9%)
  between operations  15.7 us (3%)
  local copies, waits for them, and re-layouts  15.1 us (3%)
    pallas_call x26, Pallas kernels, run(): pl.pallas_call(body, grid_spec=pltpu.PrefetchScalarGridSpec(num_scalar_pr...  285 us
    all_to_all x1, blocking collectives, exchange(): return lax.all_to_all(rows, 'exp', split_axis=0, concat_axis=0, tiled=True)  47.8 us
    ppermute x6, starting transfers between devices, line_step(): up = lax.ppermute(up, 'grp', [(i, i + 1) for i in range(t - 1, n_grp - 1)])  30.1 us
    ppermute x9, starting transfers between devices, shift(): return lax.ppermute(a, 'grp', [(i, (i + k) % n_grp) for i in range(n_grp)])  29 us
    ppermute x6, waiting for transfers between devices, line_step(): down = lax.ppermute(down, 'grp', [(i + 1, i) for i in range(n_grp - t)])  28.1 us
    ppermute x17, starting transfers between devices, swap(): return lax.ppermute(a, 'exp', [(i, i ^ k) for i in range(n_exp)])  21.3 us
    ppermute x17, waiting for transfers between devices, swap(): return lax.ppermute(a, 'exp', [(i, i ^ k) for i in range(n_exp)])  21.1 us
    all_to_all x3, starting transfers between devices, exchange(): return lax.all_to_all(rows, 'exp', split_axis=0, concat_axis=0, tiled=True)  12.7 us
  transfers between devices with their start and end apart: 42, of which 6 were waited for; matrix products, arithmetic and copies ran while one was open for 1% of the time, Pallas kernels for 51%

profile of v2, /device:TPU:0, one launch (start us, length us, event | category | flops | bytes accessed | tf_op | source)
XLA Modules:
  0.0 517.5 jit_solution(951007344176433364)
XLA Ops:
  7.3 5.3 %all-to-all-start = ((bf16[8,128,1024]{2,1,0:T(8,128)(2,1)}), bf16[8,128,1024]{2,1,0:T(8,128)(2,1)S(1)}, u32[]{:S(2)}, u32[]{:S(2)}) async-start(bf16[8,128,1024]{2,1,0:T(8,128)(2,1)} %bitcast.55), calls=%async_computation | async-start | bytes 4194304 | tf_op jit(solution)/shard_map/all_to_all | solution.py:804
  14.8 2.6 collective-permute-start.1
  18.7 14.3 %shard_map.229.refs_5_ = bf16[1024,4096]{1,0:T(8,128)(2,1)} custom-call(bf16[1024,1024]{1,0:T(8,128)(2,1)} %refs_2_.1, bf16[1024,4096]{1,0:T(8,128)(2,1)} %bitcast.45), custom_call_target="tpu_custom_call" | custom-call | flops 5687000064 | bytes 1000000 | tf_op jit(solution)/shard_map/pallas_call | solution.py:74
  33.6 5.6 %shard_map.230 = (bf16[1024,1024]{1,0:T(8,128)(2,1)}, bf16[1024,1024]{1,0:T(8,128)(2,1)}) custom-call(s32[2]{0:T(128)} %pad_add_fusion.refs_0_, bf16[1024,4096]{1,0:T(8,128)(2,1)} %bitcast.43, bf16[1024,4096]{1,0:T(8,128)(2,1)} %bitcast.46), custom_call_target="tpu_custom_call" | custom-call | flops 2584999936 | bytes 1000000 | tf_op jit(solution)/shard_map/pallas_call | solution.py:74
  40.9 2.3 shard_map.231
  43.2 2.0 collective-permute-start.6
  46.9 6.2 %collective-permute-start.12 = (bf16[1024,1024]{1,0:T(8,128)(2,1)}, bf16[1024,1024]{1,0:T(8,128)(2,1)S(1)}, u32[]{:S(2)}, u32[]{:S(2)}) collective-permute-start(bf16[1024,1024]{1,0:T(8,128)(2,1)} %refs_2_.1), channel_id=1, source_target_pairs={{0,8},{8,16},{16,24},{1,9},{9,17},{17,25},{2,10},{10,18},{18,26},{... | collective-permute-start | bytes 6291464 | tf_op jit(solution)/shard_map/ppermute | solution.py:824
  54.7 10.1 %collective-permute-done.6.refs_6_ = bf16[4,80,1024]{2,1,0:T(8,128)(2,1)S(1)} collective-permute-done((bf16[4,80,1024]{2,1,0:T(8,128)(2,1)}, bf16[4,80,1024]{2,1,0:T(8,128)(2,1)S(1)}, u32[]{:S(2)}, u32[]{:S(2)}) %collective-permute-start.6) | collective-permute-done | bytes 655392 | tf_op jit(solution)/shard_map/ppermute | solution.py:798
  66.2 2.2 collective-permute-done.4.refs_4_
  68.7 3.8 collective-permute-done.10.refs_8_
  72.5 5.1 collective-permute-done.8.refs_8_
  79.9 7.8 %shard_map.232 = (bf16[1024,1024]{1,0:T(8,128)(2,1)}, bf16[1024,1024]{1,0:T(8,128)(2,1)}, bf16[1024,1024]{1,0:T(8,128)(2,1)}, f32[1,1024]{1,0:T(1,128)}, f32[1,1...) custom-call(s32[1024,1]{1,0:T(8,128)} %copy.35.refs_0_, bf16[1024,1024]{1,0:T(8,128)(2,1)} %bitcast.51, ...), custom_call_target="tpu_custom_call" | custom-call | flops 3102000128 | bytes 1000000 | tf_op jit(solution)/shard_map/pallas_call | solution.py:74
  87.7 6.6 %shard_map.234 = (bf16[1024,1024]{1,0:T(8,128)(2,1)}, bf16[4,8,32,1024]{3,2,1,0:T(8,128)(2,1)}) custom-call(s32[2]{0:T(128)} %pad_add_fusion.refs_0_, bf16[1024,1024]{1,0:T(8,128)(2,1)} %get-tuple-element.83.refs_1_, bf16[4,80,1024]{2,1,0:T(8,128)(2,1)} %get-tuple-element.82.refs_2_, bf16[4,80,1024]{2,1,0:T(8,128)(2,1)} %copy-done.22, ...), custom_call_target="tpu_custom_call" | custom-call | flops 2584999936 | bytes 1000000 | tf_op jit(solution)/shard_map/pallas_call | solution.py:74
  94.9 6.6 %shard_map.233 = (bf16[1024,1024]{1,0:T(8,128)(2,1)}, bf16[4,8,32,1024]{3,2,1,0:T(8,128)(2,1)}) custom-call(s32[2]{0:T(128)} %pad_add_fusion.refs_0_, bf16[1024,1024]{1,0:T(8,128)(2,1)} %get-tuple-element.83.refs_1_, bf16[4,80,1024]{2,1,0:T(8,128)(2,1)} %get-tuple-element.82.refs_2_, bf16[4,80,1024]{2,1,0:T(8,128)(2,1)} %copy-done.22, ...), custom_call_target="tpu_custom_call" | custom-call | flops 2584999936 | bytes 1000000 | tf_op jit(solution)/shard_map/pallas_call | solution.py:74
  102.8 6.6 %shard_map.235 = (bf16[1024,1024]{1,0:T(8,128)(2,1)}, bf16[4,8,32,1024]{3,2,1,0:T(8,128)(2,1)}, bf16[1024,1024]{1,0:T(8,128)(2,1)}, bf16[1024,1024]{1,0:T(8,128)(2,1)}) custom-call(s32[2]{0:T(128)} %pad_add_fusion.refs_0_, bf16[1024,1024]{1,0:T(8,128)(2,1)} %get-tuple-element.83.refs_1_, ...), custom_call_target="tpu_custom_call", output_to_operand_aliasing={{2}: (5, {}), {3}: (6, {})} | custom-call | flops 2584999936 | bytes 1000000 | tf_op jit(solution)/shard_map/pallas_call | solution.py:74
  109.5 2.0 collective-permute-start.14
  113.0 13.1 %shard_map.236 = (bf16[1024,1024]{1,0:T(8,128)(2,1)}, f32[8,8,1024]{2,1,0:T(8,128)}) custom-call(s32[1]{0:T(128)S(6)} %copy.50.refs_0_, bf16[1024,1024]{1,0:T(8,128)(2,1)} %get-tuple-element.84.refs_3_.refs_1_, bf16[1024,1024]{1,0:T(8,128)(2,1)} %get-tuple-element.85.refs_4_.refs_2_, bf16[1024,1024]{1,0:T(8,128)(2,1)} %get-tuple-element.87.refs_3_), custom_call_target="tpu_custom_call" | custom-call | flops 15509999616 | bytes 1000000 | tf_op jit(solution)/shard_map/pallas_call | solution.py:74
  126.1 9.6 %shard_map.237 = (bf16[4,8,32,1024]{3,2,1,0:T(8,128)(2,1)}, bf16[1024,1024]{1,0:T(8,128)(2,1)}) custom-call(s32[2]{0:T(128)} %pad_add_fusion.refs_0_, bf16[1024,1024]{1,0:T(8,128)(2,1)} %get-tuple-element.88.refs_1_.refs_4_, bf16[1024,1024]{1,0:T(8,128)(2,1)} %get-tuple-element.89.refs_2_.refs_9_, s32[1,1024]{1,0:T(1,128)} %refs_12_.1, ...), custom_call_target="tpu_custom_call" | custom-call | flops 4653000192 | bytes 1000000 | tf_op jit(solution)/shard_map/pallas_call | solution.py:74
  135.7 47.8 %all_to_all.45 = bf16[8,128,1024]{2,1,0:T(8,128)(2,1)} all-to-all(bf16[8,128,1024]{2,1,0:T(8,128)(2,1)} %bitcast.58), channel_id=1, replica_groups=mesh['grp'=4,'exp'=8] {'exp'}, dimensions={0} | all-to-all | bytes 4194304 | tf_op jit(solution)/shard_map/all_to_all | solution.py:804
  183.5 15.9 %collective-permute-start.16 = (bf16[1024,1024]{1,0:T(8,128)(2,1)}, bf16[1024,1024]{1,0:T(8,128)(2,1)}, u32[]{:S(2)}, u32[]{:S(2)}) collective-permute-start(bf16[1024,1024]{1,0:T(8,128)(2,1)} %bitcast.13.refs_0_.refs_1_), channel_id=1, source_target_pairs={{0,8},{8,16},{16,24},{1,9},{9,17},{17,25},{2,10},{10,18},{18,26},{... | collective-permute-start | bytes 6291464 | tf_op jit(solution)/shard_map/ppermute | solution.py:824
  202.6 34.8 %shard_map.238 = (bf16[1024,4096]{1,0:T(8,128)(2,1)}, bf16[1024,1024]{1,0:T(8,128)(2,1)}, f32[8,1024]{1,0:T(8,128)}) custom-call(bf16[1024,1024]{1,0:T(8,128)(2,1)} %bitcast.13.refs_0_.refs_1_, bf16[1024,1024]{1,0:T(8,128)(2,1)} %refs_2_.1, f32[1,1024]{1,0:T(1,128)} %get-tuple-element.91.refs_2_.refs_3_.refs_5_, ...), custom_call_target="tpu_custom_call" | custom-call | flops 17578000384 | bytes 1000000 | tf_op jit(solution)/shard_map/pallas_call | solution.py:74
  237.4 3.8 all-to-all-start.2
  241.2 14.7 %shard_map.239.refs_7_ = bf16[1024,1024]{1,0:T(8,128)(2,1)} custom-call(bf16[1024,1024]{1,0:T(8,128)(2,1)} %bitcast.13.refs_0_.refs_1_, bf16[1024,4096]{1,0:T(8,128)(2,1)} %get-tuple-element.95.refs_1_, bf16[1024,4096]{1,0:T(8,128)(2,1)} %bitcast.47), custom_call_target="tpu_custom_call" | custom-call | flops 6204000256 | bytes 1000000 | tf_op jit(solution)/shard_map/pallas_call | solution.py:74
  255.9 16.9 %shard_map.240 = (f32[1024,1024]{1,0:T(8,128)}, f32[1024,1024]{1,0:T(8,128)}) custom-call(s32[1]{0:T(128)} %bitcast.17.refs_0_, bf16[1024,1024]{1,0:T(8,128)(2,1)} %bitcast.13.refs_0_.refs_1_, bf16[1024,1024]{1,0:T(8,128)(2,1)} %refs_2_.1, f32[1,1024]{1,0:T(1,128)} %get-tuple-element.91.refs_2_.refs_3_.refs_5_, ...), custom_call_target="tpu_custom_call" | custom-call | flops 9306000384 | bytes 1000000 | tf_op jit(solution)/shard_map/pallas_call | solution.py:74
  274.1 8.4 %shard_map.241 = (bf16[1024,1024]{1,0:T(8,128)(2,1)}, bf16[1024,1024]{1,0:T(8,128)(2,1)}, bf16[1024,1024]{1,0:T(8,128)(2,1)}, bf16[1024,1024]{1,0:T(8,128)(2,1)}) custom-call(s32[1024,1]{1,0:T(8,128)} %copy.35.refs_0_, bf16[1024,1024]{1,0:T(8,128)(2,1)} %bitcast.54, bf16[1024,1024]{1,0:T(8,128)(2,1)} %bitcast.48, ...), custom_call_target="tpu_custom_call", output_to_operand_aliasing={{2}: (5, {}), {3}: (6, {})} | custom-call | flops 2584999936 | bytes 1000000 | tf_op jit(solution)/shard_map/pallas_call | solution.py:74
  282.6 2.0 collective-permute-start.18
  286.1 12.6 %shard_map.242 = (bf16[1024,512]{1,0:T(8,128)(2,1)}, bf16[1024,512]{1,0:T(8,128)(2,1)}, bf16[1024,512]{1,0:T(8,128)(2,1)}) custom-call(s32[1]{0:T(128)S(6)} %copy.50.refs_0_, bf16[1024,1024]{1,0:T(8,128)(2,1)} %get-tuple-element.84.refs_3_.refs_1_, bf16[1024,1024]{1,0:T(8,128)(2,1)} %get-tuple-element.85.refs_4_.refs_2_, ...), custom_call_target="tpu_custom_call" | custom-call | flops 10339999744 | bytes 1000000 | tf_op jit(solution)/shard_map/pallas_call | solution.py:74
  298.7 11.2 %shard_map.243 = (bf16[4,4,32,2560]{3,2,1,0:T(8,128)(2,1)}, bf16[4,4,32,2560]{3,2,1,0:T(8,128)(2,1)}) custom-call(s32[2]{0:T(128)} %pad_add_fusion.refs_0_, bf16[1024,1024]{1,0:T(8,128)(2,1)} %get-tuple-element.88.refs_1_.refs_4_, bf16[1024,1024]{1,0:T(8,128)(2,1)} %get-tuple-element.96.refs_2_.refs_1_, ...), custom_call_target="tpu_custom_call" | custom-call | flops 4136000000 | bytes 1000000 | tf_op jit(solution)/shard_map/pallas_call | solution.py:74
  310.3 27.5 %collective-permute-done.19.refs_9_ = bf16[1024,1024]{1,0:T(8,128)(2,1)} collective-permute-done((bf16[1024,1024]{1,0:T(8,128)(2,1)}, bf16[1024,1024]{1,0:T(8,128)(2,1)}, u32[]{:S(2)}, u32[]{:S(2)}) %collective-permute-start.19) | collective-permute-done | bytes 2097184 | tf_op jit(solution)/shard_map/ppermute | solution.py:825
  337.8 12.8 %shard_map.244 = (bf16[1024,512]{1,0:T(8,128)(2,1)}, bf16[1024,512]{1,0:T(8,128)(2,1)}, bf16[1024,512]{1,0:T(8,128)(2,1)}, bf16[1024,1024]{1,0:T(8,128)(2,1)}, bf16[1024,1024]{1,0:T(8,128)(2,1)}) custom-call(s32[1]{0:T(128)S(6)} %copy.50.refs_0_, bf16[1024,1024]{1,0:T(8,128)(2,1)} %get-tuple-element.84.refs_3_.refs_1_, ...), custom_call_target="tpu_custom_call", output_to_operand_aliasing={{3}: (8, {}), {4}: (9, {})} | custom-call | flops 10339999744 | bytes 1000000 | tf_op jit(solution)/shard_map/pallas_call | solution.py:74
  350.6 2.0 collective-permute-start.34
  355.4 4.4 shard_map.245
  359.8 9.8 %collective-permute-start.21 = (bf16[4,32,2560]{2,1,0:T(8,128)(2,1)}, bf16[4,32,2560]{2,1,0:T(8,128)(2,1)S(1)}, u32[]{:S(2)}, u32[]{:S(2)}) collective-permute-start(bf16[4,32,2560]{2,1,0:T(8,128)(2,1)} %get-tuple-element.120.refs_14_), channel_id=1, source_target_pairs={{0,2},{1,3},{2,0},{3,1},{4,6},{5,7},{6,4},{7,5},{8,10},{9,11},{10,... | collective-permute-start | bytes 1966088 | tf_op jit(solution)/shard_map/ppermute | solution.py:798
  371.1 17.7 %shard_map.246 = (bf16[1024,1024]{1,0:T(8,128)(2,1)}, f32[8,1024]{1,0:T(8,128)}) custom-call(bf16[1024,512]{1,0:T(8,128)(2,1)} %get-tuple-element.105.refs_4_.refs_0_, bf16[1024,512]{1,0:T(8,128)(2,1)} %get-tuple-element.111.refs_2_.refs_1_, bf16[1024,512]{1,0:T(8,128)(2,1)} %get-tuple-element.106.refs_5_.refs_2_, ...), custom_call_target="tpu_custom_call" | custom-call | flops 6204000256 | bytes 1000000 | tf_op jit(solution)/shard_map/pallas_call | solution.py:74
  388.7 8.4 %shard_map.247 = (bf16[4,4,32,1664]{3,2,1,0:T(8,128)(2,1)}, bf16[4,4,32,1664]{3,2,1,0:T(8,128)(2,1)}, bf16[1024,1024]{1,0:T(8,128)(2,1)}) custom-call(s32[2]{0:T(128)} %pad_add_fusion.refs_0_, bf16[1024,1024]{1,0:T(8,128)(2,1)} %get-tuple-element.96.refs_2_.refs_1_, ...), custom_call_target="tpu_custom_call", output_to_operand_aliasing={{2}: (7, {})} | custom-call | flops 4136000000 | bytes 1000000 | tf_op jit(solution)/shard_map/pallas_call | solution.py:74
  399.1 3.6 all-to-all-start.3
  402.7 2.0 collective-permute-start.36
  406.0 18.8 %shard_map.249 = (f32[1024,1024]{1,0:T(8,128)}, f32[1024,1024]{1,0:T(8,128)}) custom-call(s32[2]{0:T(128)} %add_convert_fusion.refs_0_, bf16[1024,1024]{1,0:T(8,128)(2,1)} %get-tuple-element.109.refs_1_, bf16[1024,1024]{1,0:T(8,128)(2,1)} %get-tuple-element.110.refs_2_, bf16[1024,1024]{1,0:T(8,128)(2,1)} %get-tuple-element.93.refs_3_, ...), custom_call_target="tpu_custom_call" | custom-call | flops 9306000384 | bytes 1000000 | tf_op jit(solution)/shard_map/pallas_call | solution.py:74
  424.8 3.4 shard_map.248
  429.3 3.4 shard_map.250
  432.7 2.0 collective-permute-start.25
  436.2 18.9 %shard_map.253 = (f32[1024,1024]{1,0:T(8,128)}, f32[1024,1024]{1,0:T(8,128)}) custom-call(s32[2]{0:T(128)} %add_convert_fusion.2.refs_0_, bf16[1024,1024]{1,0:T(8,128)(2,1)} %get-tuple-element.144.refs_1_, bf16[1024,1024]{1,0:T(8,128)(2,1)} %get-tuple-element.145.refs_2_, bf16[1024,1024]{1,0:T(8,128)(2,1)} %collective-permute-done.14.refs_6_.refs_3_, ...), custom_call_target="tpu_custom_call" | custom-call | flops 9306000384 | bytes 1000000 | tf_op jit(solution)/shard_map/pallas_call | solution.py:74
  455.1 16.5 %collective-permute-start.28 = (bf16[32,2560]{1,0:T(8,128)(2,1)S(1)}, bf16[32,2560]{1,0:T(8,128)(2,1)S(1)}, u32[]{:S(2)}, u32[]{:S(2)}) collective-permute-start(bf16[32,2560]{1,0:T(8,128)(2,1)S(1)} %get-tuple-element.156), channel_id=1, source_target_pairs={{0,8},{8,16},{16,24},{24,0},{1,9},{9,17},{17,25},{25,1},{2,10},{10... | collective-permute-start | bytes 491528 | tf_op jit(solution)/shard_map/ppermute | solution.py:801
  471.6 3.1 collective-permute-start.32
  474.7 2.7 shard_map.251
  480.4 2.0 collective-permute-start.33
  482.4 20.4 %shard_map.254 = (f32[1024,1024]{1,0:T(8,128)}, f32[1024,1024]{1,0:T(8,128)}) custom-call(s32[2]{0:T(128)} %add_convert_fusion.1.refs_0_, bf16[1024,1024]{1,0:T(8,128)(2,1)} %collective-permute-done.34.refs_17_.refs_1_, bf16[1024,1024]{1,0:T(8,128)(2,1)} %collective-permute-done.35.refs_18_.refs_2_, bf16[1024,1024]{1,0:T(8,128)(2,1)} %collective-permute-done.36.refs_3_, ...), custom_call_target="tpu_custom_call" | custom-call | flops 9306000384 | bytes 1000000 | tf_op jit(solution)/shard_map/pallas_call | solution.py:74
  504.2 3.2 shard_map.252
  (145 shorter events, 39.2 us)
Async XLA Ops:
  7.3 32.0 %all-to-all-start = ((bf16[8,128,1024]{2,1,0:T(8,128)(2,1)}), bf16[8,128,1024]{2,1,0:T(8,128)(2,1)S(1)}, u32[]{:S(2)}, u32[]{:S(2)}) async-start(bf16[8,128,1024]{2,1,0:T(8,128)(2,1)} %bitcast.55), calls=%async_computation | async-start | bytes 4194304 | tf_op jit(solution)/shard_map/all_to_all | solution.py:804
  12.6 89.5 %all-gather.3.cloned.1.call-start = ((), (), s32[]{:S(2)}) async-start(), calls=%async_computation.4 | async-start | bytes 4718592 | tf_op jit(solution)/shard_map/all_gather | solution.py:849
  13.1 19.9 %copy-start.4 = (bf16[144,1024]{1,0:T(8,128)(2,1)}, bf16[144,1024]{1,0:T(8,128)(2,1)S(1)}, u32[]{:S(2)}) copy-start(bf16[144,1024]{1,0:T(8,128)(2,1)S(1)} %constant_dynamic-update-slice_fusion.refs_0_) | copy-start | bytes 884740
  13.2 26.1 %collective-permute-start = (bf16[144,1024]{1,0:T(8,128)(2,1)S(1)}, bf16[144,1024]{1,0:T(8,128)(2,1)S(1)}, u32[]{:S(2)}, u32[]{:S(2)}) collective-permute-start(bf16[144,1024]{1,0:T(8,128)(2,1)S(1)} %constant_dynamic-update-slice_fusion.refs_0_), channel_id=1, source_target_pairs={{0,8},{8,16},{16,24},{24,0},{1,9},{9,17},{17,25},{25,1},{2,10},{10... | collective-permute-start | bytes 884744 | tf_op jit(solution)/shard_map/ppermute | solution.py:801
  14.8 24.5 %collective-permute-start.1 = (bf16[144,1024]{1,0:T(8,128)(2,1)S(1)}, bf16[144,1024]{1,0:T(8,128)(2,1)S(1)}, u32[]{:S(2)}, u32[]{:S(2)}) collective-permute-start(bf16[144,1024]{1,0:T(8,128)(2,1)S(1)} %constant_dynamic-update-slice_fusion.refs_0_), channel_id=1, source_target_pairs={{0,16},{8,24},{16,0},{24,8},{1,17},{9,25},{17,1},{25,9},{2,18},{10... | collective-permute-start | bytes 884744 | tf_op jit(solution)/shard_map/ppermute | solution.py:801
  17.4 21.9 %collective-permute-start.2 = (bf16[144,1024]{1,0:T(8,128)(2,1)S(1)}, bf16[144,1024]{1,0:T(8,128)(2,1)S(1)}, u32[]{:S(2)}, u32[]{:S(2)}) collective-permute-start(bf16[144,1024]{1,0:T(8,128)(2,1)S(1)} %constant_dynamic-update-slice_fusion.refs_0_), channel_id=1, source_target_pairs={{0,24},{8,0},{16,8},{24,16},{1,25},{9,1},{17,9},{25,17},{2,26},{10... | collective-permute-start | bytes 884744 | tf_op jit(solution)/shard_map/ppermute | solution.py:801
  40.9 36.7 %copy-start.14 = (s32[1,1024]{1,0:T(1,128)S(1)}, s32[1,1024]{1,0:T(1,128)}, u32[]{:S(2)}) copy-start(s32[1,1024]{1,0:T(1,128)} %refs_12_.1) | copy-start | bytes 12292
  43.2 21.6 %collective-permute-start.6 = (bf16[4,80,1024]{2,1,0:T(8,128)(2,1)}, bf16[4,80,1024]{2,1,0:T(8,128)(2,1)S(1)}, u32[]{:S(2)}, u32[]{:S(2)}) collective-permute-start(bf16[4,80,1024]{2,1,0:T(8,128)(2,1)} %get-tuple-element.82.refs_2_), channel_id=1, source_target_pairs={{0,4},{1,5},{2,6},{3,7},{4,0},{5,1},{6,2},{7,3},{8,12},{9,13},{10,... | collective-permute-start | bytes 1966088 | tf_op jit(solution)/shard_map/ppermute | solution.py:798
  45.2 23.1 %collective-permute-start.4 = (bf16[4,80,1024]{2,1,0:T(8,128)(2,1)}, bf16[4,80,1024]{2,1,0:T(8,128)(2,1)S(1)}, u32[]{:S(2)}, u32[]{:S(2)}) collective-permute-start(bf16[4,80,1024]{2,1,0:T(8,128)(2,1)} %get-tuple-element.82.refs_2_), channel_id=1, source_target_pairs={{0,2},{1,3},{2,0},{3,1},{4,6},{5,7},{6,4},{7,5},{8,10},{9,11},{10,... | collective-permute-start | bytes 1966088 | tf_op jit(solution)/shard_map/ppermute | solution.py:798
  46.9 54.6 %collective-permute-start.12 = (bf16[1024,1024]{1,0:T(8,128)(2,1)}, bf16[1024,1024]{1,0:T(8,128)(2,1)S(1)}, u32[]{:S(2)}, u32[]{:S(2)}) collective-permute-start(bf16[1024,1024]{1,0:T(8,128)(2,1)} %refs_2_.1), channel_id=1, source_target_pairs={{0,8},{8,16},{16,24},{1,9},{9,17},{17,25},{2,10},{10,18},{18,26},{... | collective-permute-start | bytes 6291464 | tf_op jit(solution)/shard_map/ppermute | solution.py:824
  53.1 48.9 %collective-permute-start.13 = (bf16[1024,1024]{1,0:T(8,128)(2,1)}, bf16[1024,1024]{1,0:T(8,128)(2,1)}, u32[]{:S(2)}, u32[]{:S(2)}) collective-permute-start(bf16[1024,1024]{1,0:T(8,128)(2,1)} %refs_2_.1), channel_id=1, source_target_pairs={{8,0},{16,8},{24,16},{9,1},{17,9},{25,17},{10,2},{18,10},{26,18},{... | collective-permute-start | bytes 6291464 | tf_op jit(solution)/shard_map/ppermute | solution.py:825
  54.6 14.1 %collective-permute-start.3 = (bf16[4,80,1024]{2,1,0:T(8,128)(2,1)}, bf16[4,80,1024]{2,1,0:T(8,128)(2,1)S(1)}, u32[]{:S(2)}, u32[]{:S(2)}) collective-permute-start(bf16[4,80,1024]{2,1,0:T(8,128)(2,1)} %get-tuple-element.82.refs_2_), channel_id=1, source_target_pairs={{0,1},{1,0},{2,3},{3,2},{4,5},{5,4},{6,7},{7,6},{8,9},{9,8},{10,11... | collective-permute-start | bytes 1966088 | tf_op jit(solution)/shard_map/ppermute | solution.py:798
  64.8 15.1 %copy-start.9 = (bf16[4,80,1024]{2,1,0:T(8,128)(2,1)}, bf16[4,80,1024]{2,1,0:T(8,128)(2,1)S(1)}, u32[]{:S(2)}) copy-start(bf16[4,80,1024]{2,1,0:T(8,128)(2,1)S(1)} %collective-permute-done.6.refs_6_) | copy-start | bytes 1966084
  64.8 7.7 %collective-permute-start.10 = (bf16[4,32,1024]{2,1,0:T(8,128)(2,1)S(1)}, bf16[4,32,1024]{2,1,0:T(8,128)(2,1)S(1)}, u32[]{:S(2)}, u32[]{:S(2)}) collective-permute-start(bf16[4,32,1024]{2,1,0:T(8,128)(2,1)S(1)} %slice.25), channel_id=1, source_target_pairs={{0,2},{1,3},{2,0},{3,1},{4,6},{5,7},{6,4},{7,5},{8,10},{9,11},{10,... | collective-permute-start | bytes 786440 | tf_op jit(solution)/shard_map/ppermute | solution.py:798
  68.4 9.2 %collective-permute-start.8 = (bf16[4,48,1024]{2,1,0:T(8,128)(2,1)S(1)}, bf16[4,48,1024]{2,1,0:T(8,128)(2,1)}, u32[]{:S(2)}, u32[]{:S(2)}) collective-permute-start(bf16[4,48,1024]{2,1,0:T(8,128)(2,1)S(1)} %slice.24), channel_id=1, source_target_pairs={{0,4},{1,5},{2,6},{3,7},{4,0},{5,1},{6,2},{7,3},{8,12},{9,13},{10,... | collective-permute-start | bytes 1179656 | tf_op jit(solution)/shard_map/ppermute | solution.py:798
  68.7 10.6 %collective-permute-start.5 = (bf16[4,80,1024]{2,1,0:T(8,128)(2,1)S(1)}, bf16[4,80,1024]{2,1,0:T(8,128)(2,1)}, u32[]{:S(2)}, u32[]{:S(2)}) collective-permute-start(bf16[4,80,1024]{2,1,0:T(8,128)(2,1)S(1)} %collective-permute-done.4.refs_4_), channel_id=1, source_target_pairs={{0,1},{1,0},{2,3},{3,2},{4,5},{5,4},{6,7},{7,6},{8,9},{9,8},{10,11... | collective-permute-start | bytes 1966088 | tf_op jit(solution)/shard_map/ppermute | solution.py:798
  72.5 7.3 %collective-permute-start.7 = (bf16[4,80,1024]{2,1,0:T(8,128)(2,1)S(1)}, bf16[4,80,1024]{2,1,0:T(8,128)(2,1)}, u32[]{:S(2)}, u32[]{:S(2)}) collective-permute-start(bf16[4,80,1024]{2,1,0:T(8,128)(2,1)S(1)} %collective-permute-done.6.refs_6_), channel_id=1, source_target_pairs={{0,1},{1,0},{2,3},{3,2},{4,5},{5,4},{6,7},{7,6},{8,9},{9,8},{10,11... | collective-permute-start | bytes 1966088 | tf_op jit(solution)/shard_map/ppermute | solution.py:798
  77.6 2.3 collective-permute-start.9
  79.3 14.9 %collective-permute-start.11 = (bf16[4,32,1024]{2,1,0:T(8,128)(2,1)}, bf16[4,32,1024]{2,1,0:T(8,128)(2,1)S(1)}, u32[]{:S(2)}, u32[]{:S(2)}) collective-permute-start(bf16[4,32,1024]{2,1,0:T(8,128)(2,1)} %copy-done.25), channel_id=1, source_target_pairs={{0,1},{1,0},{2,3},{3,2},{4,5},{5,4},{6,7},{7,6},{8,9},{9,8},{10,11... | collective-permute-start | bytes 786440 | tf_op jit(solution)/shard_map/ppermute | solution.py:798
  109.5 91.7 %collective-permute-start.14 = (bf16[1024,1024]{1,0:T(8,128)(2,1)}, bf16[1024,1024]{1,0:T(8,128)(2,1)}, u32[]{:S(2)}, u32[]{:S(2)}) collective-permute-start(bf16[1024,1024]{1,0:T(8,128)(2,1)} %get-tuple-element.93.refs_3_), channel_id=1, source_target_pairs={{8,16},{16,24},{9,17},{17,25},{10,18},{18,26},{11,19},{19,27},{12,... | collective-permute-start | bytes 6291464 | tf_op jit(solution)/shard_map/ppermute | solution.py:824
  111.5 89.7 %collective-permute-start.15 = (bf16[1024,1024]{1,0:T(8,128)(2,1)}, bf16[1024,1024]{1,0:T(8,128)(2,1)S(1)}, u32[]{:S(2)}, u32[]{:S(2)}) collective-permute-start(bf16[1024,1024]{1,0:T(8,128)(2,1)} %get-tuple-element.94.refs_4_), channel_id=1, source_target_pairs={{8,0},{16,8},{9,1},{17,9},{10,2},{18,10},{11,3},{19,11},{12,4},{20... | collective-permute-start | bytes 6291464 | tf_op jit(solution)/shard_map/ppermute | solution.py:825
  183.5 89.3 %collective-permute-start.16 = (bf16[1024,1024]{1,0:T(8,128)(2,1)}, bf16[1024,1024]{1,0:T(8,128)(2,1)}, u32[]{:S(2)}, u32[]{:S(2)}) collective-permute-start(bf16[1024,1024]{1,0:T(8,128)(2,1)} %bitcast.13.refs_0_.refs_1_), channel_id=1, source_target_pairs={{0,8},{8,16},{16,24},{1,9},{9,17},{17,25},{2,10},{10,18},{18,26},{... | collective-permute-start | bytes 6291464 | tf_op jit(solution)/shard_map/ppermute | solution.py:824
  199.4 73.4 %collective-permute-start.17 = (bf16[1024,1024]{1,0:T(8,128)(2,1)}, bf16[1024,1024]{1,0:T(8,128)(2,1)}, u32[]{:S(2)}, u32[]{:S(2)}) collective-permute-start(bf16[1024,1024]{1,0:T(8,128)(2,1)} %bitcast.13.refs_0_.refs_1_), channel_id=1, source_target_pairs={{8,0},{16,8},{24,16},{9,1},{17,9},{25,17},{10,2},{18,10},{26,18},{... | collective-permute-start | bytes 6291464 | tf_op jit(solution)/shard_map/ppermute | solution.py:825
  237.4 35.4 %all-to-all-start.2 = ((bf16[8,128,1024]{2,1,0:T(8,128)(2,1)}), bf16[8,128,1024]{2,1,0:T(8,128)(2,1)S(1)}, u32[]{:S(2)}, u32[]{:S(2)}) async-start(bf16[8,128,1024]{2,1,0:T(8,128)(2,1)} %bitcast.57), calls=%async_computation.2 | async-start | bytes 4194304 | tf_op jit(solution)/shard_map/all_to_all | solution.py:804
  282.6 27.7 %collective-permute-start.18 = (bf16[1024,1024]{1,0:T(8,128)(2,1)}, bf16[1024,1024]{1,0:T(8,128)(2,1)}, u32[]{:S(2)}, u32[]{:S(2)}) collective-permute-start(bf16[1024,1024]{1,0:T(8,128)(2,1)} %get-tuple-element.109.refs_1_), channel_id=1, source_target_pairs={{8,16},{16,24},{9,17},{17,25},{10,18},{18,26},{11,19},{19,27},{12,... | collective-permute-start | bytes 6291464 | tf_op jit(solution)/shard_map/ppermute | solution.py:824
  284.6 53.2 %collective-permute-start.19 = (bf16[1024,1024]{1,0:T(8,128)(2,1)}, bf16[1024,1024]{1,0:T(8,128)(2,1)}, u32[]{:S(2)}, u32[]{:S(2)}) collective-permute-start(bf16[1024,1024]{1,0:T(8,128)(2,1)} %get-tuple-element.110.refs_2_), channel_id=1, source_target_pairs={{8,0},{16,8},{9,1},{17,9},{10,2},{18,10},{11,3},{19,11},{12,4},{20... | collective-permute-start | bytes 6291464 | tf_op jit(solution)/shard_map/ppermute | solution.py:825
  309.8 44.0 %collective-permute-start.20 = (bf16[4,4,32,2560]{3,2,1,0:T(8,128)(2,1)}, bf16[4,4,32,2560]{3,2,1,0:T(8,128)(2,1)S(1)}, u32[]{:S(2)}, u32[]{:S(2)}) collective-permute-start(bf16[4,4,32,2560]{3,2,1,0:T(8,128)(2,1)} %get-tuple-element.108.refs_7_), channel_id=1, source_target_pairs={{0,1},{1,0},{2,3},{3,2},{4,5},{5,4},{6,7},{7,6},{8,9},{9,8},{10,11... | collective-permute-start | bytes 7864328 | tf_op jit(solution)/shard_map/ppermute | solution.py:798
  350.6 84.1 %collective-permute-start.34 = (bf16[1024,1024]{1,0:T(8,128)(2,1)}, bf16[1024,1024]{1,0:T(8,128)(2,1)}, u32[]{:S(2)}, u32[]{:S(2)}) collective-permute-start(bf16[1024,1024]{1,0:T(8,128)(2,1)} %get-tuple-element.144.refs_1_), channel_id=1, source_target_pairs={{16,24},{17,25},{18,26},{19,27},{20,28},{21,29},{22,30},{23,31}} | collective-permute-start | bytes 6291464 | tf_op jit(solution)/shard_map/ppermute | solution.py:824
  352.6 83.6 %collective-permute-start.35 = (bf16[1024,1024]{1,0:T(8,128)(2,1)}, bf16[1024,1024]{1,0:T(8,128)(2,1)}, u32[]{:S(2)}, u32[]{:S(2)}) collective-permute-start(bf16[1024,1024]{1,0:T(8,128)(2,1)} %get-tuple-element.145.refs_2_), channel_id=1, source_target_pairs={{8,0},{9,1},{10,2},{11,3},{12,4},{13,5},{14,6},{15,7}} | collective-permute-start | bytes 6291464 | tf_op jit(solution)/shard_map/ppermute | solution.py:825
  359.8 37.4 %collective-permute-start.21 = (bf16[4,32,2560]{2,1,0:T(8,128)(2,1)}, bf16[4,32,2560]{2,1,0:T(8,128)(2,1)S(1)}, u32[]{:S(2)}, u32[]{:S(2)}) collective-permute-start(bf16[4,32,2560]{2,1,0:T(8,128)(2,1)} %get-tuple-element.120.refs_14_), channel_id=1, source_target_pairs={{0,2},{1,3},{2,0},{3,1},{4,6},{5,7},{6,4},{7,5},{8,10},{9,11},{10,... | collective-permute-start | bytes 1966088 | tf_op jit(solution)/shard_map/ppermute | solution.py:798
  369.6 33.1 %collective-permute-start.22 = (bf16[4,32,2560]{2,1,0:T(8,128)(2,1)}, bf16[4,32,2560]{2,1,0:T(8,128)(2,1)S(1)}, u32[]{:S(2)}, u32[]{:S(2)}) collective-permute-start(bf16[4,32,2560]{2,1,0:T(8,128)(2,1)} %get-tuple-element.121.refs_15_), channel_id=1, source_target_pairs={{0,4},{1,5},{2,6},{3,7},{4,0},{5,1},{6,2},{7,3},{8,12},{9,13},{10,... | collective-permute-start | bytes 1966088 | tf_op jit(solution)/shard_map/ppermute | solution.py:798
  369.6 35.1 %collective-permute-start.23 = (bf16[4,32,2560]{2,1,0:T(8,128)(2,1)}, bf16[4,32,2560]{2,1,0:T(8,128)(2,1)}, u32[]{:S(2)}, u32[]{:S(2)}) collective-permute-start(bf16[4,32,2560]{2,1,0:T(8,128)(2,1)} %get-tuple-element.122.refs_16_), channel_id=1, source_target_pairs={{0,6},{1,7},{2,4},{3,5},{4,2},{5,3},{6,0},{7,1},{8,14},{9,15},{10,... | collective-permute-start | bytes 1966088 | tf_op jit(solution)/shard_map/ppermute | solution.py:798
  397.2 32.1 %collective-permute-start.24 = (bf16[4,4,32,1664]{3,2,1,0:T(8,128)(2,1)}, bf16[4,4,32,1664]{3,2,1,0:T(8,128)(2,1)}, u32[]{:S(2)}, u32[]{:S(2)}) collective-permute-start(bf16[4,4,32,1664]{3,2,1,0:T(8,128)(2,1)} %get-tuple-element.129.refs_11_), channel_id=1, source_target_pairs={{0,1},{1,0},{2,3},{3,2},{4,5},{5,4},{6,7},{7,6},{8,9},{9,8},{10,11... | collective-permute-start | bytes 5111816 | tf_op jit(solution)/shard_map/ppermute | solution.py:798
  399.1 56.0 %all-to-all-start.3 = ((bf16[8,128,1024]{2,1,0:T(8,128)(2,1)}), bf16[8,128,1024]{2,1,0:T(8,128)(2,1)S(1)}, u32[]{:S(2)}, u32[]{:S(2)}) async-start(bf16[8,128,1024]{2,1,0:T(8,128)(2,1)} %bitcast.56), calls=%async_computation.3 | async-start | bytes 4194304 | tf_op jit(solution)/shard_map/all_to_all | solution.py:804
  402.7 22.1 %copy-start.21 = (bf16[4,32,2560]{2,1,0:T(8,128)(2,1)}, bf16[4,32,2560]{2,1,0:T(8,128)(2,1)S(1)}, u32[]{:S(2)}) copy-start(bf16[4,32,2560]{2,1,0:T(8,128)(2,1)S(1)} %collective-permute-done.22.refs_2_) | copy-start | bytes 1966084
  402.7 75.7 %collective-permute-start.36 = (bf16[1024,1024]{1,0:T(8,128)(2,1)}, bf16[1024,1024]{1,0:T(8,128)(2,1)}, u32[]{:S(2)}, u32[]{:S(2)}) collective-permute-start(bf16[1024,1024]{1,0:T(8,128)(2,1)} %collective-permute-done.14.refs_6_.refs_3_), channel_id=1, source_target_pairs={{16,24},{17,25},{18,26},{19,27},{20,28},{21,29},{22,30},{23,31}} | collective-permute-start | bytes 6291464 | tf_op jit(solution)/shard_map/ppermute | solution.py:824
  404.7 73.8 %collective-permute-start.37 = (bf16[1024,1024]{1,0:T(8,128)(2,1)}, bf16[1024,1024]{1,0:T(8,128)(2,1)}, u32[]{:S(2)}, u32[]{:S(2)}) collective-permute-start(bf16[1024,1024]{1,0:T(8,128)(2,1)} %copy-done.19), channel_id=1, source_target_pairs={{8,0},{9,1},{10,2},{11,3},{12,4},{13,5},{14,6},{15,7}} | collective-permute-start | bytes 6291464 | tf_op jit(solution)/shard_map/ppermute | solution.py:825
  432.7 22.4 %collective-permute-start.25 = (bf16[4,32,1664]{2,1,0:T(8,128)(2,1)}, bf16[4,32,1664]{2,1,0:T(8,128)(2,1)S(1)}, u32[]{:S(2)}, u32[]{:S(2)}) collective-permute-start(bf16[4,32,1664]{2,1,0:T(8,128)(2,1)} %get-tuple-element.133.refs_14_), channel_id=1, source_target_pairs={{0,2},{1,3},{2,0},{3,1},{4,6},{5,7},{6,4},{7,5},{8,10},{9,11},{10,... | collective-permute-start | bytes 1277960 | tf_op jit(solution)/shard_map/ppermute | solution.py:798
  434.7 36.9 %collective-permute-start.26 = (bf16[4,32,1664]{2,1,0:T(8,128)(2,1)}, bf16[4,32,1664]{2,1,0:T(8,128)(2,1)S(1)}, u32[]{:S(2)}, u32[]{:S(2)}) collective-permute-start(bf16[4,32,1664]{2,1,0:T(8,128)(2,1)} %get-tuple-element.134.refs_15_), channel_id=1, source_target_pairs={{0,4},{1,5},{2,6},{3,7},{4,0},{5,1},{6,2},{7,3},{8,12},{9,13},{10,... | collective-permute-start | bytes 1277960 | tf_op jit(solution)/shard_map/ppermute | solution.py:798
  436.1 35.5 %collective-permute-start.27 = (bf16[4,32,1664]{2,1,0:T(8,128)(2,1)}, bf16[4,32,1664]{2,1,0:T(8,128)(2,1)}, u32[]{:S(2)}, u32[]{:S(2)}) collective-permute-start(bf16[4,32,1664]{2,1,0:T(8,128)(2,1)} %get-tuple-element.135.refs_16_), channel_id=1, source_target_pairs={{0,6},{1,7},{2,4},{3,5},{4,2},{5,3},{6,0},{7,1},{8,14},{9,15},{10,... | collective-permute-start | bytes 1277960 | tf_op jit(solution)/shard_map/ppermute | solution.py:798
  455.1 19.6 %copy-start.23 = (bf16[4,32,1664]{2,1,0:T(8,128)(2,1)}, bf16[4,32,1664]{2,1,0:T(8,128)(2,1)S(1)}, u32[]{:S(2)}) copy-start(bf16[4,32,1664]{2,1,0:T(8,128)(2,1)S(1)} %collective-permute-done.25.refs_1_) | copy-start | bytes 1277956
  455.1 25.3 %collective-permute-start.28 = (bf16[32,2560]{1,0:T(8,128)(2,1)S(1)}, bf16[32,2560]{1,0:T(8,128)(2,1)S(1)}, u32[]{:S(2)}, u32[]{:S(2)}) collective-permute-start(bf16[32,2560]{1,0:T(8,128)(2,1)S(1)} %get-tuple-element.156), channel_id=1, source_target_pairs={{0,8},{8,16},{16,24},{24,0},{1,9},{9,17},{17,25},{25,1},{2,10},{10... | collective-permute-start | bytes 491528 | tf_op jit(solution)/shard_map/ppermute | solution.py:801
  471.6 31.3 %collective-permute-start.30 = (bf16[32,2560]{1,0:T(8,128)(2,1)S(1)}, bf16[32,2560]{1,0:T(8,128)(2,1)}, u32[]{:S(2)}, u32[]{:S(2)}) collective-permute-start(bf16[32,2560]{1,0:T(8,128)(2,1)S(1)} %get-tuple-element.155), channel_id=1, source_target_pairs={{0,16},{8,24},{16,0},{24,8},{1,17},{9,25},{17,1},{25,9},{2,18},{10... | collective-permute-start | bytes 491528 | tf_op jit(solution)/shard_map/ppermute | solution.py:801
  471.6 31.3 %collective-permute-start.32 = (bf16[32,2560]{1,0:T(8,128)(2,1)S(1)}, bf16[32,2560]{1,0:T(8,128)(2,1)}, u32[]{:S(2)}, u32[]{:S(2)}) collective-permute-start(bf16[32,2560]{1,0:T(8,128)(2,1)S(1)} %get-tuple-element.154), channel_id=1, source_target_pairs={{0,24},{8,0},{16,8},{24,16},{1,25},{9,1},{17,9},{25,17},{2,26},{10... | collective-permute-start | bytes 491528 | tf_op jit(solution)/shard_map/ppermute | solution.py:801
  478.5 24.4 %collective-permute-start.29 = (bf16[32,1664]{1,0:T(8,128)(2,1)S(1)}, bf16[32,1664]{1,0:T(8,128)(2,1)S(1)}, u32[]{:S(2)}, u32[]{:S(2)}) collective-permute-start(bf16[32,1664]{1,0:T(8,128)(2,1)S(1)} %get-tuple-element.159), channel_id=1, source_target_pairs={{0,8},{8,16},{16,24},{24,0},{1,9},{9,17},{17,25},{25,1},{2,10},{10... | collective-permute-start | bytes 319496 | tf_op jit(solution)/shard_map/ppermute | solution.py:801
  478.5 24.3 %collective-permute-start.31 = (bf16[32,1664]{1,0:T(8,128)(2,1)S(1)}, bf16[32,1664]{1,0:T(8,128)(2,1)S(1)}, u32[]{:S(2)}, u32[]{:S(2)}) collective-permute-start(bf16[32,1664]{1,0:T(8,128)(2,1)S(1)} %get-tuple-element.158), channel_id=1, source_target_pairs={{0,16},{8,24},{16,0},{24,8},{1,17},{9,25},{17,1},{25,9},{2,18},{10... | collective-permute-start | bytes 319496 | tf_op jit(solution)/shard_map/ppermute | solution.py:801
  480.4 22.4 %copy-start.27 = (bf16[32,2560]{1,0:T(8,128)(2,1)}, bf16[32,2560]{1,0:T(8,128)(2,1)S(1)}, u32[]{:S(2)}) copy-start(bf16[32,2560]{1,0:T(8,128)(2,1)S(1)} %collective-permute-done.28.refs_3_) | copy-start | bytes 491524
  480.4 22.5 %collective-permute-start.33 = (bf16[32,1664]{1,0:T(8,128)(2,1)S(1)}, bf16[32,1664]{1,0:T(8,128)(2,1)S(1)}, u32[]{:S(2)}, u32[]{:S(2)}) collective-permute-start(bf16[32,1664]{1,0:T(8,128)(2,1)S(1)} %get-tuple-element.157), channel_id=1, source_target_pairs={{0,24},{8,0},{16,8},{24,16},{1,25},{9,1},{17,9},{25,17},{2,26},{10... | collective-permute-start | bytes 319496 | tf_op jit(solution)/shard_map/ppermute | solution.py:801
  (25 other events, 87.8 us)
Sparse Core Ops, SparseCore 0:
  43.3 45.8 all-gather.2

commit v3 on v2

--- a/solution.py
+++ b/solution.py
@@ -43,9 +43,9 @@
 
 def gelu_both(u):
     sq = u * u
-    t = jnp.tanh(GELU_A * u * (1.0 + GELU_B * sq))
-    half = 0.5 * (1.0 + t)
-    return u * half, half + (0.5 * u) * (1.0 - t * t) * (GELU_A + (3.0 * GELU_A * GELU_B) * sq)
+    half = 0.5 + 0.5 * jnp.tanh(u * (GELU_A + (GELU_A * GELU_B) * sq))
+    act = u * half
+    return act, half + act * (1.0 - half) * (2.0 * GELU_A + (6.0 * GELU_A * GELU_B) * sq)
 
 
 def run(
@@ -102,39 +102,56 @@
     return jnp.where(ids == other, 1.0, 0.0).astype(BF)
 
 
-def seq_kernel(count, ids_ref, rows_ref, *refs):
-    pieces, (seq_ref, ln_ref, lnt_ref, *gain_refs) = refs[:count], refs[count:]
-    gains = 0.0
-    for piece in pieces:
-        for z in range(piece.shape[0]):
-            gains = gains + piece[z].astype(F32)
-    for n, ref in enumerate(gain_refs):
-        ref[...] = gains[n : n + 1]
-    total = rows_ref.shape[0]
-    for r in range(0, total, QB):
-        lanes = lax.broadcasted_iota(jnp.int32, (QB, total), 1)
-        x = dot_nn(one_hot(ids_ref[r : r + QB], lanes), rows_ref[...])
-        seq_ref[r : r + QB] = x.astype(BF)
-        normed, _ = norm_rows(x)
-        ln = (normed * gains[0:1] + gains[1:2]).astype(BF)
-        ln_ref[r : r + QB] = ln
-        lnt_ref[:, r : r + QB] = jnp.transpose(ln)
-
-
-def seq_norm(ids_col, rows, pieces, deps=()):
+def enter_kernel(count, meta, ids_ref, rows_ref, *refs):
+    pieces, refs = [refs[n * count : (n + 1) * count] for n in range(3)], refs[3 * count :]
+    seq_ref, ln_ref, lnt_ref, q_ref, k_ref, mat_q, mat_k, *gain_refs = refs
+    width = rows_ref.shape[1]
+
+    @pl.when(pl.program_id(0) == 0)
+    def _():
+        place(meta, pieces[0], mat_q)
+        place(meta, pieces[1], mat_k)
+        gains = 0.0
+        for piece in pieces[2]:
+            for z in range(piece.shape[0]):
+                gains = gains + piece[z].astype(F32)
+        for n, ref in enumerate(gain_refs):
+            ref[...] = gains[n : n + 1]
+
+    lanes = lax.broadcasted_iota(jnp.int32, (QB, rows_ref.shape[0]), 1)
+    x = dot_nn(one_hot(ids_ref[...], lanes), rows_ref[...])
+    seq_ref[...] = x.astype(BF)
+    normed, _ = norm_rows(x)
+    ln = (normed * gain_refs[0][...] + gain_refs[1][...]).astype(BF)
+    ln_ref[...] = ln
+    lnt_ref[...] = jnp.transpose(ln)
+    q_ref[...] = dot_nn(ln, mat_q[...].reshape(width, width)).astype(BF)
+    k_ref[...] = dot_nn(ln, mat_k[...].reshape(width, width)).astype(BF)
+
+
+def enter(meta, ids_col, rows, pieces_q, pieces_k, pieces_g, full, deps=()):
     total, width = rows.shape
-    groups = pieces[0][0].shape[0]
-    res = run(
-        partial(seq_kernel, len(pieces)),
-        (ids_col, rows, *[a for a, _ in pieces]),
-        [shaped((total, width)), shaped((total, width)), shaped((width, total))]
-        + [shaped((1, width), F32)] * 4,
-        deps,
-        specs=[whole(ids_col.shape), whole(rows.shape)]
-        + [pl.BlockSpec((groups, 16, width), lambda i, n=n: (0, n, 0)) for _, n in pieces],
-        micros=6,
-    )
-    return *res[:3], res[3:]
+    block = pl.BlockSpec((QB, width), lambda r, *_: (r, 0))
+    turned = pl.BlockSpec((width, QB), lambda r, *_: (0, r))
+    rows_out, gain = shaped((total, width)), shaped((1, width), F32)
+    seq, ln, lnt, q, k, mat_q, mat_k, *gains = run(
+        partial(enter_kernel, len(pieces_q)),
+        (ids_col, rows, *[a for a, _ in (*pieces_q, *pieces_k, *pieces_g)]),
+        [rows_out, rows_out, shaped((width, total)), rows_out, rows_out]
+        + [shaped(full)] * 2
+        + [gain] * 4,
+        deps,
+        (meta,),
+        (total // QB,),
+        [pl.BlockSpec((QB, 1), lambda r, *_: (r, 0)), whole(rows.shape)]
+        + piece_specs(pieces_q, full[2])
+        + piece_specs(pieces_k, full[2])
+        + piece_specs(pieces_g, 16),
+        [block, block, turned, block, block] + [whole(full)] * 2 + [whole((1, width))] * 4,
+        micros=14,
+    )
+    flat = (width, width)
+    return seq, ln, lnt, q, k, mat_q.reshape(flat), mat_k.reshape(flat), gains
 
 
 def place(meta, refs, full):
@@ -179,175 +196,206 @@
 
 def proj_kernel(count, meta, ln_ref, *refs):
     pieces, (out_ref, full_ref) = refs[:count], refs[count:]
-    place(meta, pieces, full_ref)
+
+    @pl.when(pl.program_id(0) == 0)
+    def _():
+        place(meta, pieces, full_ref)
+
     width = ln_ref.shape[1]
     out_ref[...] = dot_nn(ln_ref[...], full_ref[...].reshape(width, width)).astype(BF)
 
 
 def project(meta, ln, pieces, full, deps=(), gates=()):
-    width = ln.shape[1]
-    res = run(
+    total, width = ln.shape
+    block = pl.BlockSpec((QB, width), lambda r, *_: (r, 0))
+    (out, mat), gates = run(
         partial(proj_kernel, len(pieces)),
         (ln, *[a for a, _ in pieces]),
         [shaped(ln.shape), shaped(full)],
         deps,
         (meta,),
-        specs=[whole(ln.shape)] + piece_specs(pieces, full[2]),
+        (total // QB,),
+        [block] + piece_specs(pieces, full[2]),
+        [block, whole(full)],
         gates=gates,
     )
-    (out, mat), *gates = res if gates else (res,)
-    return (out, mat.reshape(width, width), *gates)
+    return out, mat.reshape(width, width), gates
+
+
+def head_lanes(heads):
+    pair = 2 * HDIM
+    low = lax.broadcasted_iota(jnp.int32, (1, pair), 1) < HDIM
+    cols = [slice(h // 2 * pair, (h // 2 + 1) * pair) for h in range(heads)]
+    return low, cols, [~low if h % 2 else low for h in range(heads)]
 
 
 def attend_kernel(flag, q_ref, k_ref, v_ref, o_ref, lse_ref, lse_cols):
-    total = q_ref.shape[0]
-    low = lax.broadcasted_iota(jnp.int32, (1, 2 * HDIM), 1) < HDIM
+    total, heads = q_ref.shape[0], q_ref.shape[1] // HDIM
+    low, cols, own = head_lanes(heads)
+    each = range(heads)
     causal = lax.broadcasted_iota(jnp.int32, (QB, QB), 1) <= lax.broadcasted_iota(
         jnp.int32, (QB, QB), 0
     )
 
-    def run(long):
+    def go(long):
         for a in range(0, total, QB):
             b = a + QB
-            q = q_ref[a:b]
-            outs, logs = [], []
-            for keep in (low, ~low):
-                qh = jnp.where(keep, q, jnp.zeros_like(q)) * BF(HDIM**-0.5)
-                near = jnp.where(causal, dot_nt(qh, k_ref[a:b]), NEG_FILL)
-                top = jnp.max(near, 1, keepdims=True)
-                if long and a > 0:
-                    far = dot_nt(qh, k_ref[0:a])
-                    top = jnp.maximum(top, jnp.max(far, 1, keepdims=True))
-                near = jnp.exp(near - top)
-                mass = jnp.sum(near, 1, keepdims=True)
-                o = dot_nn(near.astype(BF), v_ref[a:b])
-                if long and a > 0:
-                    far = jnp.exp(far - top)
-                    mass = mass + jnp.sum(far, 1, keepdims=True)
-                    o = o + dot_nn(far.astype(BF), v_ref[0:a])
-                outs.append(o * (1.0 / mass))
-                logs.append(top + jnp.log(mass))
-            o_ref[a:b] = jnp.where(low, outs[0], outs[1]).astype(BF)
-            lse_cols[a:b] = jnp.where(low, logs[0], logs[1])
+            further = long and a > 0
+            q = [
+                jnp.where(own[h], q_ref[a:b, cols[h]], jnp.zeros((QB, 2 * HDIM), BF))
+                * BF(HDIM**-0.5)
+                for h in each
+            ]
+            near = [jnp.where(causal, dot_nt(q[h], k_ref[a:b, cols[h]]), NEG_FILL) for h in each]
+            top = [jnp.max(near[h], 1, keepdims=True) for h in each]
+            if further:
+                far = [dot_nt(q[h], k_ref[0:a, cols[h]]) for h in each]
+                top = [jnp.maximum(top[h], jnp.max(far[h], 1, keepdims=True)) for h in each]
+            near = [jnp.exp(near[h] - top[h]) for h in each]
+            mass = [jnp.sum(near[h], 1, keepdims=True) for h in each]
+            o = [dot_nn(near[h].astype(BF), v_ref[a:b, cols[h]]) for h in each]
+            if further:
+                far = [jnp.exp(far[h] - top[h]) for h in each]
+                mass = [mass[h] + jnp.sum(far[h], 1, keepdims=True) for h in each]
+                o = [o[h] + dot_nn(far[h].astype(BF), v_ref[0:a, cols[h]]) for h in each]
+            o = [o[h] * (1.0 / mass[h]) for h in each]
+            logs = [top[h] + jnp.log(mass[h]) for h in each]
+            for h in range(0, heads, 2):
+                o_ref[a:b, cols[h]] = jnp.where(low, o[h], o[h + 1]).astype(BF)
+                lse_cols[a:b, cols[h]] = jnp.where(low, logs[h], logs[h + 1])
 
     @pl.when(flag[0] > QB)
     def _():
-        run(True)
+        go(True)
 
     @pl.when(flag[0] <= QB)
     def _():
-        run(False)
-
-    turned = jnp.transpose(lse_cols[...])
-    lse_ref[0, 0:1] = turned[0:1]
-    lse_ref[0, 1:2] = turned[HDIM : HDIM + 1]
+        go(False)
+
+    for h in range(0, heads, 2):
+        turned = jnp.transpose(lse_cols[:, cols[h]])
+        lse_ref[h // 2, 0:1] = turned[0:1]
+        lse_ref[h // 2, 1:2] = turned[HDIM : HDIM + 1]
 
 
 def attend(flag, q, k, v, deps=()):
     total, width = q.shape
-    pair = 2 * HDIM
-    block = pl.BlockSpec((total, pair), lambda j, *_: (0, j))
-    stat = pl.BlockSpec((1, 8, total), lambda j, *_: (j, 0, 0))
+    lanes = 4 * HDIM
+    block = pl.BlockSpec((total, lanes), lambda j, *_: (0, j))
+    stat = pl.BlockSpec((2, 8, total), lambda j, *_: (j, 0, 0))
     return run(
         attend_kernel,
         (q, k, v),
-        [shaped((total, width)), shaped((width // pair, 8, total), F32)],
+        [shaped((total, width)), shaped((width // (2 * HDIM), 8, total), F32)],
         deps,
         (flag,),
-        (width // pair,),
+        (width // lanes,),
         [block] * 3,
         [block, stat],
-        [pltpu.VMEM((total, pair), F32)],
-        micros=30,
+        [pltpu.VMEM((total, lanes), F32)],
+        micros=22,
     )
 
 
 def attend_back_kernel(
     flag, q_ref, k_ref, v_ref, o_ref, g_ref, lse_ref, dq_ref, dk_ref, dv_ref, dq_turned
 ):
-    total = q_ref.shape[0]
-    low = lax.broadcasted_iota(jnp.int32, (1, 2 * HDIM), 1) < HDIM
+    total, heads = q_ref.shape[0], q_ref.shape[1] // HDIM
+    low, cols, own = head_lanes(heads)
+    each = range(heads)
     causal = lax.broadcasted_iota(jnp.int32, (QB, QB), 0) <= lax.broadcasted_iota(
         jnp.int32, (QB, QB), 1
     )
-    prod = jnp.transpose(g_ref[...].astype(F32) * o_ref[...].astype(F32))
-    delta = [jnp.sum(prod[h * HDIM : (h + 1) * HDIM], 0, keepdims=True) for h in range(2)]
-    k_turned = jnp.transpose(k_ref[...])
-
-    def run(long):
+    delta, k_turned = [], []
+    for h in range(0, heads, 2):
+        prod = jnp.transpose(g_ref[:, cols[h]].astype(F32) * o_ref[:, cols[h]].astype(F32))
+        delta.append(jnp.sum(prod[:HDIM], 0, keepdims=True))
+        delta.append(jnp.sum(prod[HDIM:], 0, keepdims=True))
+        turned = jnp.transpose(k_ref[:, cols[h]])
+        k_turned += [turned[:HDIM], turned[HDIM:]]
+
+    def go(long):
         for a in range(0, total, QB):
             b = a + QB
-            ks, vs = k_ref[a:b], v_ref[a:b]
-            dks, dvs = [], []
-            for h, keep in enumerate((low, ~low)):
-                kh = jnp.where(keep, ks, jnp.zeros_like(ks)) * BF(HDIM**-0.5)
-                vh = jnp.where(keep, vs, jnp.zeros_like(vs))
-                kth = k_turned[h * HDIM : (h + 1) * HDIM, a:b]
-                spans = [(a, b)]
-                if long and b < total:
-                    spans.append((b, total))
-                dk = dv = None
-                for lo, hi in spans:
-                    qs, gs = q_ref[lo:hi], g_ref[lo:hi]
-                    probs = jnp.exp(dot_nt(kh, qs) - lse_ref[0, h : h + 1, lo:hi])
-                    if lo == a:
-                        probs = jnp.where(causal, probs, 0.0)
-                    dp = dot_nt(vh, gs)
-                    ds = (probs * (dp - delta[h][:, lo:hi])).astype(BF)
-                    dv_part, dk_part = dot_nn(probs.astype(BF), gs), dot_nn(ds, qs)
-                    dk = dk_part if dk is None else dk + dk_part
-                    dv = dv_part if dv is None else dv + dv_part
+            zero = jnp.zeros((QB, 2 * HDIM), BF)
+            k = [jnp.where(own[h], k_ref[a:b, cols[h]], zero) * BF(HDIM**-0.5) for h in each]
+            v = [jnp.where(own[h], v_ref[a:b, cols[h]], zero) for h in each]
+            dk, dv = [0.0] * heads, [0.0] * heads
+            spans = [(a, b)]
+            if long and b < total:
+                spans.append((b, total))
+            for lo, hi in spans:
+                scores = [dot_nt(k[h], q_ref[lo:hi, cols[h]]) for h in each]
+                dp = [dot_nt(v[h], g_ref[lo:hi, cols[h]]) for h in each]
+                probs = [
+                    jnp.exp(scores[h] - lse_ref[h // 2, h % 2 : h % 2 + 1, lo:hi]) for h in each
+                ]
+                if lo == a:
+                    probs = [jnp.where(causal, p, 0.0) for p in probs]
+                ds = [(probs[h] * (dp[h] - delta[h][:, lo:hi])).astype(BF) for h in each]
+                probs = [p.astype(BF) for p in probs]
+                for h in each:
+                    dv[h] = dv[h] + dot_nn(probs[h], g_ref[lo:hi, cols[h]])
+                    dk[h] = dk[h] + dot_nn(ds[h], q_ref[lo:hi, cols[h]])
                     rows = slice(h * HDIM, (h + 1) * HDIM)
                     if a == 0 or not long:
-                        dq_turned[rows, lo:hi] = dot_nn(kth, ds)
+                        dq_turned[rows, lo:hi] = dot_nn(k_turned[h][:, a:b], ds[h])
                     else:
-                        dq_turned[rows, lo:hi] += dot_nn(kth, ds)
-                dks.append(dk)
-                dvs.append(dv)
-            dk_ref[a:b] = (jnp.where(low, dks[0], dks[1]) * HDIM**-0.5).astype(BF)
-            dv_ref[a:b] = jnp.where(low, dvs[0], dvs[1]).astype(BF)
+                        dq_turned[rows, lo:hi] += dot_nn(k_turned[h][:, a:b], ds[h])
+            for h in range(0, heads, 2):
+                both = jnp.where(low, dk[h], dk[h + 1])
+                dk_ref[a:b, cols[h]] = (both * HDIM**-0.5).astype(BF)
+                dv_ref[a:b, cols[h]] = jnp.where(low, dv[h], dv[h + 1]).astype(BF)
 
     @pl.when(flag[0] > QB)
     def _():
-        run(True)
+        go(True)
 
     @pl.when(flag[0] <= QB)
     def _():
-        run(False)
+        go(False)
 
     dq_ref[...] = (jnp.transpose(dq_turned[...]) * HDIM**-0.5).astype(BF)
 
 
-def attend_back(flag, q, k, v, o, g, lse, first, count, deps=(), gates=()):
-    total = q.shape[0]
-    pair = 2 * HDIM
-    block = pl.BlockSpec((total, pair), lambda j, *_: (0, j + first))
-    stat = pl.BlockSpec((1, 8, total), lambda j, *_: (j + first, 0, 0))
-    done = pl.BlockSpec((total, pair), lambda j, *_: (0, j))
+def attend_back(flag, q, k, v, o, g, lse, part, parts, deps=(), gates=()):
+    total, width = q.shape
+    lanes = 4 * HDIM
+    count = width // lanes // parts
+    first = part * count
+    block = pl.BlockSpec((total, lanes), lambda j, *_: (0, j + first))
+    stat = pl.BlockSpec((2, 8, total), lambda j, *_: (j + first, 0, 0))
+    done = pl.BlockSpec((total, lanes), lambda j, *_: (0, j))
     return run(
         attend_back_kernel,
         (q, k, v, o, g, lse),
-        [shaped((total, pair * count))] * 3,
+        [shaped((total, width // parts))] * 3,
         deps,
         (flag,),
         (count,),
         [block] * 5 + [stat],
         [done] * 3,
-        [pltpu.VMEM((pair, total), F32)],
-        micros=20,
+        [pltpu.VMEM((lanes, total), F32)],
+        micros=18,
         gates=gates,
     )
 
 
 def mix_kernel(count, meta, attn_ref, seq_ref, ids_ref, *refs):
     pieces, (full_ref, out_ref, mixed) = refs[:count], refs[count:]
-    place(meta, pieces, full_ref)
-    total, width = mixed.shape
-    mat = full_ref[...].reshape(width, width)
-    for r in range(0, total, QB):
-        x = seq_ref[r : r + QB].astype(F32) + dot_nn(attn_ref[r : r + QB], mat)
-        mixed[r : r + QB] = x.astype(BF)
-    to_experts(ids_ref, mixed, out_ref)
+    r = pl.program_id(0)
+
+    @pl.when(r == 0)
+    def _():
+        place(meta, pieces, full_ref)
+
+    size, width = attn_ref.shape
+    x = seq_ref[...].astype(F32) + dot_nn(attn_ref[...], full_ref[...].reshape(width, width))
+    mixed[pl.ds(pl.multiple_of(r * size, size), size)] = x.astype(BF)
+
+    @pl.when(r == pl.num_programs(0) - 1)
+    def _():
+        to_experts(ids_ref, mixed, out_ref)
 
 
 def to_experts(ids_ref, rows, out_ref):
@@ -358,16 +406,19 @@
 
 
 def mix(meta, attn, seq, ids_row, pieces, full, deps=()):
-    width = attn.shape[1]
+    total, width = attn.shape
+    block = pl.BlockSpec((QB, width), lambda r, *_: (r, 0))
     mat, out = run(
         partial(mix_kernel, len(pieces)),
         (attn, seq, ids_row, *[a for a, _ in pieces]),
         [shaped(full), shaped(attn.shape)],
         deps,
         (meta,),
-        specs=[whole(attn.shape)] * 2 + [whole(ids_row.shape)] + piece_specs(pieces, full[2]),
-        scratch=[pltpu.VMEM(attn.shape, BF)],
-        micros=9,
+        (total // QB,),
+        [block, block, whole(ids_row.shape)] + piece_specs(pieces, full[2]),
+        [whole(full), whole(attn.shape)],
+        [pltpu.VMEM(attn.shape, BF)],
+        micros=8,
     )
     return mat.reshape(width, width), out
 
@@ -405,9 +456,12 @@
             ln[r : r + QB] = (normed * gain_ref[...] + bias_ref[...]).astype(BF)
 
     def body(first):
-        for r in range(0, total, 512):
-            rows = slice(r, r + 512)
-            act, slope = gelu_both(dot_nn(ln[rows], wi_ref[...]))
+        spans = [slice(r, r + QB) for r in range(0, total, QB)]
+        pre = dot_nn(ln[spans[0]], wi_ref[...])
+        for n, rows in enumerate(spans):
+            act, slope = gelu_both(pre)
+            if n + 1 < len(spans):
+                pre = dot_nn(ln[spans[n + 1]], wi_ref[...])
             act_ref[rows] = act.astype(BF)
             back = (dact_ref[rows].astype(F32) * slope).astype(BF)
             if first:
@@ -441,7 +495,7 @@
 
 def expert(x, cot, gain, bias, w_in, dact, deps=()):
     total, width = x.shape
-    hidden, tile = w_in.shape[1], 512
+    hidden, tile = w_in.shape[1], 1024
     steps = hidden // tile
     cols = pl.BlockSpec((width, tile), lambda f: (0, f))
     rows = pl.BlockSpec((total, tile), lambda f: (0, f))
@@ -504,7 +558,9 @@
     )
 
 
-def slice_kernel(count, first, last, flags, *refs):
+def slice_kernel(t, groups, first, last, meta, *refs):
+    valid = [meta[1] >= t, meta[1] + t < groups] if t else [meta[1] >= 0]
+    count = len(valid)
     xs, cots = refs[:count], refs[count : 2 * count]
     gain_ref, bias_ref, wi_ref, wo_ref = refs[2 * count : 2 * count + 4]
     rest = refs[2 * count + 4 :]
@@ -523,7 +579,7 @@
 
     for n in range(count):
 
-        @pl.when((f == 0) & (flags[n] > 0))
+        @pl.when((f == 0) & valid[n])
         def _(n=n):
             for copy in copies(n):
                 copy.start()
@@ -536,7 +592,7 @@
         out_acc[...] = out_prev[...]
     for n in range(count):
 
-        @pl.when(flags[n] > 0)
+        @pl.when(valid[n])
         def _(n=n):
             @pl.when(f == 0)
             def _():
@@ -561,7 +617,7 @@
         out_ref[...] = out_acc[...]
 
 
-def slice_grads(flags, xs, cots, gain, bias, wi_turned, wo_turned, prev, last, deps=()):
+def slice_grads(meta, t, groups, xs, cots, gain, bias, wi_turned, wo_turned, prev, deps=(), gates=()):
     count = len(xs)
     total, width = xs[0].shape
     hidden = wi_turned.shape[0]
@@ -569,13 +625,13 @@
     rows = pl.BlockSpec((tile, width), lambda f, *_: (f, 0))
     cols = pl.BlockSpec((width, tile), lambda f, *_: (0, f))
     anywhere = pl.BlockSpec(memory_space=pl.ANY)
-    first = prev is None
-    return run(
-        partial(slice_kernel, count, first, last),
+    first, last = prev is None, t == groups - 1
+    return run(
+        partial(slice_kernel, t, groups, first, last),
         (*xs, *cots, gain, bias, wi_turned, wo_turned, *(() if first else prev)),
         [shaped((width, hidden) if last else (hidden, width), F32)] * 2,
         deps,
-        (flags,),
+        (meta,),
         (hidden // tile,),
         [anywhere] * (2 * count)
         + [whole((1, width))] * 2
@@ -585,20 +641,31 @@
         + [pltpu.VMEM((count, total, width), BF)] * 2
         + [pltpu.SemaphoreType.DMA((count, 2))],
         micros=18,
+        gates=gates,
     )
 
 
 def back_kernel(ids_ref, mat_ref, rows_ref, dmix_ref, dattn_ref):
-    total = rows_ref.shape[0]
-    for r in range(0, total, QB):
-        lanes = lax.broadcasted_iota(jnp.int32, (QB, total), 1)
-        x = dot_nn(one_hot(ids_ref[r : r + QB], lanes), rows_ref[...]).astype(BF)
-        dmix_ref[r : r + QB] = x
-        dattn_ref[r : r + QB] = dot_nt(x, mat_ref[...]).astype(BF)
-
-
-def back_in(ids_col, mat, rows, deps=(), gates=()):
-    return run(back_kernel, (ids_col, mat, rows), [shaped(rows.shape)] * 2, deps, gates=gates)
+    lanes = lax.broadcasted_iota(jnp.int32, (QB, rows_ref.shape[0]), 1)
+    x = dot_nn(one_hot(ids_ref[...], lanes), rows_ref[...]).astype(BF)
+    dmix_ref[...] = x
+    dattn_ref[...] = dot_nt(x, mat_ref[...]).astype(BF)
+
+
+def back_in(ids_col, mat, rows, deps=()):
+    total, width = rows.shape
+    block = pl.BlockSpec((QB, width), lambda r: (r, 0))
+    return run(
+        back_kernel,
+        (ids_col, mat, rows),
+        [shaped(rows.shape)] * 2,
+        deps,
+        (),
+        (total // QB,),
+        [pl.BlockSpec((QB, 1), lambda r: (r, 0)), whole(mat.shape), whole(rows.shape)],
+        [block] * 2,
+        micros=7,
+    )
 
 
 def shared_kernel(picks, turns, sums_in, meta, *refs):
@@ -865,10 +932,10 @@
         return steps[-1]
 
     forward(cot_line)
-    seq, ln_one, ln_turned, gains = seq_norm(ids_col, arrived, pieces_g)
-    q, mat_q = project(meta, ln_one, pieces_q, full)
-    k, mat_k = project(meta, ln_one, pieces_k, full)
-    v, mat_v, cot_line[1] = project(meta, ln_one, pieces_v, full, deps=(q, k), gates=cot_line[1])
+    seq, ln_one, ln_turned, q, k, mat_q, mat_k, gains = enter(
+        meta, ids_col, arrived, pieces_q, pieces_k, pieces_g, full
+    )
+    v, mat_v, cot_line[1] = project(meta, ln_one, pieces_v, full, gates=cot_line[1])
     forward(cot_line)
     attn, lse = attend(flag, q, k, v)
     mat_o, leaving = mix(meta, attn, seq, ids_row, pieces_o, full)
@@ -882,33 +949,17 @@
     forward(x_line)
     output = expert_out(x, act, w_second)
 
-    def slices(t, sums, deps=()):
-        flags = [(grp >= t).astype(jnp.int32), (grp + t < n_grp).astype(jnp.int32)]
-        xs, cots = list(x_line[t]), list(cot_line[t])
-        if t == 0:
-            xs, cots, flags = xs[:1], cots[:1], flags[:1]
-        return slice_grads(
-            jnp.stack(flags),
-            xs,
-            cots,
-            gains[2],
-            gains[3],
-            wi_turned,
-            wo_turned,
-            sums,
-            t == n_grp - 1,
-            deps,
-        )
-
-    slice_sums = slices(0, None, deps=output)
+    def slices(t, sums, deps=(), gates=()):
+        xs, cots = (list(line[t])[: 2 if t else 1] for line in (x_line, cot_line))
+        last = (gains[2], gains[3], wi_turned, wo_turned, sums, deps, gates)
+        return slice_grads(meta, t, n_grp, xs, cots, *last)
+
+    slice_sums, x_line[1] = slices(0, None, deps=output, gates=x_line[1])
     back = exchange(dx)
-    (dmix, dattn), x_line[1] = back_in(
-        ids_col, mat_o, back, deps=slice_sums, gates=x_line[1]
-    )
+    dmix, dattn = back_in(ids_col, mat_o, back, deps=slice_sums)
     forward(x_line)
 
-    pairs = width // (2 * HDIM)
-    early = attend_back(flag, q, k, v, attn, dattn, lse, 0, pairs // 2)
+    early = attend_back(flag, q, k, v, attn, dattn, lse, 0, 2)
     send, keep = shared_grads(
         meta,
         [(attn, False), (ln_turned, True)],
@@ -919,7 +970,7 @@
     )
     gates = x_line[2] if n_grp > 2 else dmix
     rest, gates = attend_back(
-        flag, q, k, v, attn, dattn, lse, pairs // 2, pairs // 2, deps=send, gates=gates
+        flag, q, k, v, attn, dattn, lse, 1, 2, deps=send, gates=gates
     )
     if n_grp > 2:
         x_line[2] = gates

time: 521 us -> 490 us (0.940)
  blocking collectives: 47.8 us -> 30.9 us
  starting transfers between devices: 102 us -> 86 us
  Pallas kernels: 285 us -> 295 us
  waiting for transfers between devices: 49.3 us -> 40.3 us
    all_to_all x1, blocking collectives: 47.8 us -> 30.9 us  [exchange(): return lax.all_to_all(rows, 'exp', split_axis=0, concat_axis=0, tiled=True)]
    ppermute x6, waiting for transfers between devices: 28.1 us -> 16.6 us  [line_step(): down = lax.ppermute(down, 'grp', [(i + 1, i) for i in range(n_grp - t)])]
    pallas_call x26 -> x24, Pallas kernels: 285 us -> 295 us  [run(): pl.pallas_call(body, grid_spec=pltpu.PrefetchScalarGridSpec(num_scalar_pr...]
    ppermute x17, starting transfers between devices: 21.3 us -> 13.4 us  [swap(): return lax.ppermute(a, 'exp', [(i, i ^ k) for i in range(n_exp)])]
    ppermute x6, starting transfers between devices: 30.1 us -> 23 us  [line_step(): up = lax.ppermute(up, 'grp', [(i, i + 1) for i in range(t - 1, n_grp - 1)])]
  transfers between devices with their start and end apart: 42 -> 42, of which waited for: 6 -> 9; matrix products, arithmetic and copies ran while one was open for 1% -> 1% of each run, Pallas kernels for 51% -> 58%
where the time goes in v3:
time: 490 us; the launch traced here: 483 us
  Pallas kernels  295 us (60%)
  starting transfers between devices  86 us (18%)
  waiting for transfers between devices  40.3 us (8%)
  blocking collectives  30.9 us (6%)
  between operations  15.9 us (3%)
  local copies, waits for them, and re-layouts  15.1 us (3%)
    pallas_call x24, Pallas kernels, run(): pl.pallas_call(body, grid_spec=pltpu.PrefetchScalarGridSpec(num_scalar_pr...  295 us
    all_to_all x1, blocking collectives, exchange(): return lax.all_to_all(rows, 'exp', split_axis=0, concat_axis=0, tiled=True)  30.9 us
    ppermute x9, starting transfers between devices, shift(): return lax.ppermute(a, 'grp', [(i, (i + k) % n_grp) for i in range(n_grp)])  28.8 us
    ppermute x6, starting transfers between devices, line_step(): up = lax.ppermute(up, 'grp', [(i, i + 1) for i in range(t - 1, n_grp - 1)])  23 us
    ppermute x17, waiting for transfers between devices, swap(): return lax.ppermute(a, 'exp', [(i, i ^ k) for i in range(n_exp)])  20.6 us
    ppermute x6, waiting for transfers between devices, line_step(): down = lax.ppermute(down, 'grp', [(i + 1, i) for i in range(n_grp - t)])  16.6 us
    ppermute x17, starting transfers between devices, swap(): return lax.ppermute(a, 'exp', [(i, i ^ k) for i in range(n_exp)])  13.4 us
    all_to_all x3, starting transfers between devices, exchange(): return lax.all_to_all(rows, 'exp', split_axis=0, concat_axis=0, tiled=True)  12.8 us
  transfers between devices with their start and end apart: 42, of which 9 were waited for; matrix products, arithmetic and copies ran while one was open for 1% of the time, Pallas kernels for 58%

profile of v3, /device:TPU:0, one launch (start us, length us, event | category | flops | bytes accessed | tf_op | source)
XLA Modules:
  0.0 483.4 jit_solution(16159953048667058564)
XLA Ops:
  7.3 5.3 %all-to-all-start = ((bf16[8,128,1024]{2,1,0:T(8,128)(2,1)}), bf16[8,128,1024]{2,1,0:T(8,128)(2,1)S(1)}, u32[]{:S(2)}, u32[]{:S(2)}) async-start(bf16[8,128,1024]{2,1,0:T(8,128)(2,1)} %bitcast.46), calls=%async_computation | async-start | bytes 4194304 | tf_op jit(solution)/shard_map/all_to_all | solution.py:871
  13.2 1.6 collective-permute-start
  14.8 2.6 collective-permute-start.1
  18.7 14.3 %shard_map.229.refs_5_ = bf16[1024,4096]{1,0:T(8,128)(2,1)} custom-call(bf16[1024,1024]{1,0:T(8,128)(2,1)} %refs_2_.1, bf16[1024,4096]{1,0:T(8,128)(2,1)} %bitcast.38), custom_call_target="tpu_custom_call" | custom-call | flops 5687000064 | bytes 1000000 | tf_op jit(solution)/shard_map/pallas_call | solution.py:74
  33.6 5.6 %shard_map.230 = (bf16[1024,1024]{1,0:T(8,128)(2,1)}, bf16[1024,1024]{1,0:T(8,128)(2,1)}) custom-call(s32[2]{0:T(128)} %pad_add_fusion.refs_0_, bf16[1024,4096]{1,0:T(8,128)(2,1)} %bitcast.36, bf16[1024,4096]{1,0:T(8,128)(2,1)} %bitcast.39), custom_call_target="tpu_custom_call" | custom-call | flops 2584999936 | bytes 1000000 | tf_op jit(solution)/shard_map/pallas_call | solution.py:74
  40.9 2.3 shard_map.231
  43.2 2.2 collective-permute-start.4
  46.9 6.2 %collective-permute-start.12 = (bf16[1024,1024]{1,0:T(8,128)(2,1)}, bf16[1024,1024]{1,0:T(8,128)(2,1)S(1)}, u32[]{:S(2)}, u32[]{:S(2)}) collective-permute-start(bf16[1024,1024]{1,0:T(8,128)(2,1)} %refs_2_.1), channel_id=1, source_target_pairs={{0,8},{8,16},{16,24},{1,9},{9,17},{17,25},{2,10},{10,18},{18,26},{... | collective-permute-start | bytes 6291464 | tf_op jit(solution)/shard_map/ppermute | solution.py:891
  54.5 10.8 %collective-permute-done.4.refs_5_.refs_13_.refs_21_ = bf16[4,80,1024]{2,1,0:T(8,128)(2,1)S(1)} collective-permute-done((bf16[4,80,1024]{2,1,0:T(8,128)(2,1)}, bf16[4,80,1024]{2,1,0:T(8,128)(2,1)S(1)}, u32[]{:S(2)}, u32[]{:S(2)}) %collective-permute-start.4) | collective-permute-done | bytes 655392 | tf_op jit(solution)/shard_map/ppermute | solution.py:865
  69.3 5.6 %collective-permute-done.8.refs_9_ = bf16[4,32,1024]{2,1,0:T(8,128)(2,1)S(1)} collective-permute-done((bf16[4,32,1024]{2,1,0:T(8,128)(2,1)S(1)}, bf16[4,32,1024]{2,1,0:T(8,128)(2,1)S(1)}, u32[]{:S(2)}, u32[]{:S(2)}) %collective-permute-start.8) | collective-permute-done | bytes 262176 | tf_op jit(solution)/shard_map/ppermute | solution.py:865
  80.1 14.8 %shard_map.232 = (bf16[1024,1024]{1,0:T(8,128)(2,1)}, bf16[1024,1024]{1,0:T(8,128)(2,1)}, bf16[1024,1024]{1,0:T(8,128)(2,1)}, bf16[1024,1024]{1,0:T(8,128)(2,1)}...) custom-call(s32[2]{0:T(128)} %pad_add_fusion.refs_0_, ...), custom_call_target="tpu_custom_call" | custom-call | flops 7238000128 | bytes 1000000 | tf_op jit(solution)/shard_map/pallas_call | solution.py:74
  94.9 2.9 collective-permute-done.12.refs_3_
  97.8 4.2 collective-permute-done.13.refs_4_
  102.1 7.1 %shard_map.233 = (bf16[1024,1024]{1,0:T(8,128)(2,1)}, bf16[4,8,32,1024]{3,2,1,0:T(8,128)(2,1)}, bf16[1024,1024]{1,0:T(8,128)(2,1)}, bf16[1024,1024]{1,0:T(8,128)(2,1)}) custom-call(s32[2]{0:T(128)} %pad_add_fusion.refs_0_, bf16[1024,1024]{1,0:T(8,128)(2,1)} %get-tuple-element.85.refs_1_, ...), custom_call_target="tpu_custom_call", output_to_operand_aliasing={{2}: (3, {}), {3}: (4, {})} | custom-call | flops 2584999936 | bytes 1000000 | tf_op jit(solution)/shard_map/pallas_call | solution.py:74
  109.2 2.0 collective-permute-start.14
  112.7 21.2 %shard_map.234 = (bf16[1024,1024]{1,0:T(8,128)(2,1)}, f32[8,8,1024]{2,1,0:T(8,128)}) custom-call(s32[1]{0:T(128)S(6)} %copy.50.refs_0_, bf16[1024,1024]{1,0:T(8,128)(2,1)} %get-tuple-element.83.refs_1_, bf16[1024,1024]{1,0:T(8,128)(2,1)} %get-tuple-element.84.refs_2_, bf16[1024,1024]{1,0:T(8,128)(2,1)} %get-tuple-element.87.refs_3_), custom_call_target="tpu_custom_call" | custom-call | flops 11374000128 | bytes 1000000 | tf_op jit(solution)/shard_map/pallas_call | solution.py:74
  133.8 10.6 %shard_map.235 = (bf16[4,8,32,1024]{3,2,1,0:T(8,128)(2,1)}, bf16[1024,1024]{1,0:T(8,128)(2,1)}) custom-call(s32[2]{0:T(128)} %pad_add_fusion.refs_0_, bf16[1024,1024]{1,0:T(8,128)(2,1)} %get-tuple-element.88.refs_1_.refs_4_, bf16[1024,1024]{1,0:T(8,128)(2,1)} %get-tuple-element.89.refs_2_.refs_9_, s32[1,1024]{1,0:T(1,128)} %refs_12_.1, ...), custom_call_target="tpu_custom_call" | custom-call | flops 4136000000 | bytes 1000000 | tf_op jit(solution)/shard_map/pallas_call | solution.py:74
  144.4 30.9 %all_to_all.45 = bf16[8,128,1024]{2,1,0:T(8,128)(2,1)} all-to-all(bf16[8,128,1024]{2,1,0:T(8,128)(2,1)} %bitcast.50), channel_id=1, replica_groups=mesh['grp'=4,'exp'=8] {'exp'}, dimensions={0} | all-to-all | bytes 4194304 | tf_op jit(solution)/shard_map/all_to_all | solution.py:871
  175.4 8.9 %collective-permute-start.16 = (bf16[1024,1024]{1,0:T(8,128)(2,1)}, bf16[1024,1024]{1,0:T(8,128)(2,1)}, u32[]{:S(2)}, u32[]{:S(2)}) collective-permute-start(bf16[1024,1024]{1,0:T(8,128)(2,1)} %bitcast.13.refs_0_.refs_1_), channel_id=1, source_target_pairs={{0,8},{8,16},{16,24},{1,9},{9,17},{17,25},{2,10},{10,18},{18,26},{... | collective-permute-start | bytes 6291464 | tf_op jit(solution)/shard_map/ppermute | solution.py:891
  187.0 30.6 %shard_map.236 = (bf16[1024,4096]{1,0:T(8,128)(2,1)}, bf16[1024,1024]{1,0:T(8,128)(2,1)}, f32[8,1024]{1,0:T(8,128)}) custom-call(bf16[1024,1024]{1,0:T(8,128)(2,1)} %bitcast.13.refs_0_.refs_1_, bf16[1024,1024]{1,0:T(8,128)(2,1)} %refs_2_.1, f32[1,1024]{1,0:T(1,128)} %get-tuple-element.91.refs_2_.refs_3_.refs_5_, ...), custom_call_target="tpu_custom_call" | custom-call | flops 17578000384 | bytes 1000000 | tf_op jit(solution)/shard_map/pallas_call | solution.py:74
  217.7 3.6 all-to-all-start.2
  221.3 14.7 %shard_map.237.refs_7_ = bf16[1024,1024]{1,0:T(8,128)(2,1)} custom-call(bf16[1024,1024]{1,0:T(8,128)(2,1)} %bitcast.13.refs_0_.refs_1_, bf16[1024,4096]{1,0:T(8,128)(2,1)} %get-tuple-element.95.refs_1_, bf16[1024,4096]{1,0:T(8,128)(2,1)} %bitcast.40), custom_call_target="tpu_custom_call" | custom-call | flops 6204000256 | bytes 1000000 | tf_op jit(solution)/shard_map/pallas_call | solution.py:74
  236.0 17.4 %shard_map.238 = (f32[1024,1024]{1,0:T(8,128)}, f32[1024,1024]{1,0:T(8,128)}, bf16[1024,1024]{1,0:T(8,128)(2,1)}, bf16[1024,1024]{1,0:T(8,128)(2,1)}) custom-call(s32[2]{0:T(128)} %pad_add_fusion.refs_0_, bf16[1024,1024]{1,0:T(8,128)(2,1)} %bitcast.13.refs_0_.refs_1_, bf16[1024,1024]{1,0:T(8,128)(2,1)} %refs_2_.1, ...), custom_call_target="tpu_custom_call", output_to_operand_aliasing={{2}: (8, {}), {3}: (9, {})} | custom-call | flops 9306000384 | bytes 1000000 | tf_op jit(solution)/shard_map/pallas_call | solution.py:74
  253.5 2.0 collective-permute-start.18
  258.1 8.5 %shard_map.239 = (bf16[1024,1024]{1,0:T(8,128)(2,1)}, bf16[1024,1024]{1,0:T(8,128)(2,1)}) custom-call(s32[1024,1]{1,0:T(8,128)} %copy.35.refs_1_.refs_0_, bf16[1024,1024]{1,0:T(8,128)(2,1)} %bitcast.61, bf16[1024,1024]{1,0:T(8,128)(2,1)} %bitcast.47, f32[1024,1024]{1,0:T(8,128)} %get-tuple-element.100.refs_3_.refs_9_, ...), custom_call_target="tpu_custom_call" | custom-call | flops 3619000064 | bytes 1000000 | tf_op jit(solution)/shard_map/pallas_call | solution.py:74
  266.6 17.7 %shard_map.240 = (bf16[1024,512]{1,0:T(8,128)(2,1)}, bf16[1024,512]{1,0:T(8,128)(2,1)}, bf16[1024,512]{1,0:T(8,128)(2,1)}) custom-call(s32[1]{0:T(128)S(6)} %copy.50.refs_0_, bf16[1024,1024]{1,0:T(8,128)(2,1)} %get-tuple-element.83.refs_1_, bf16[1024,1024]{1,0:T(8,128)(2,1)} %get-tuple-element.84.refs_2_, bf16[1024,1024]{1,0:T(8,128)(2,1)} %get-tuple-element.87.refs_3_, ...), custom_call_target="tpu_custom_call" | custom-call | flops 9306000384 | bytes 1000000 | tf_op jit(solution)/shard_map/pallas_call | solution.py:74
  284.3 11.5 %shard_map.241 = (bf16[4,4,32,2560]{3,2,1,0:T(8,128)(2,1)}, bf16[4,4,32,2560]{3,2,1,0:T(8,128)(2,1)}) custom-call(s32[2]{0:T(128)} %pad_add_fusion.refs_0_, bf16[1024,1024]{1,0:T(8,128)(2,1)} %get-tuple-element.88.refs_1_.refs_4_, bf16[1024,1024]{1,0:T(8,128)(2,1)} %get-tuple-element.96.refs_2_.refs_1_, ...), custom_call_target="tpu_custom_call" | custom-call | flops 4136000000 | bytes 1000000 | tf_op jit(solution)/shard_map/pallas_call | solution.py:74
  295.9 12.4 %collective-permute-done.19.refs_9_ = bf16[1024,1024]{1,0:T(8,128)(2,1)} collective-permute-done((bf16[1024,1024]{1,0:T(8,128)(2,1)}, bf16[1024,1024]{1,0:T(8,128)(2,1)}, u32[]{:S(2)}, u32[]{:S(2)}) %collective-permute-start.19) | collective-permute-done | bytes 2097184 | tf_op jit(solution)/shard_map/ppermute | solution.py:892
  308.3 17.7 %shard_map.242 = (bf16[1024,512]{1,0:T(8,128)(2,1)}, bf16[1024,512]{1,0:T(8,128)(2,1)}, bf16[1024,512]{1,0:T(8,128)(2,1)}, bf16[1024,1024]{1,0:T(8,128)(2,1)}, bf16[1024,1024]{1,0:T(8,128)(2,1)}) custom-call(s32[1]{0:T(128)S(6)} %copy.50.refs_0_, bf16[1024,1024]{1,0:T(8,128)(2,1)} %get-tuple-element.83.refs_1_, ...), custom_call_target="tpu_custom_call", output_to_operand_aliasing={{3}: (8, {}), {4}: (9, {})} | custom-call | flops 9306000384 | bytes 1000000 | tf_op jit(solution)/shard_map/pallas_call | solution.py:74
  326.0 2.0 collective-permute-start.34
  330.7 4.5 shard_map.243
  335.2 1.7 collective-permute-start.21
  338.7 17.4 %shard_map.244 = (bf16[1024,1024]{1,0:T(8,128)(2,1)}, f32[8,1024]{1,0:T(8,128)}) custom-call(bf16[1024,512]{1,0:T(8,128)(2,1)} %get-tuple-element.105.refs_4_.refs_0_, bf16[1024,512]{1,0:T(8,128)(2,1)} %get-tuple-element.111.refs_2_.refs_1_, bf16[1024,512]{1,0:T(8,128)(2,1)} %get-tuple-element.106.refs_5_.refs_2_, ...), custom_call_target="tpu_custom_call" | custom-call | flops 6204000256 | bytes 1000000 | tf_op jit(solution)/shard_map/pallas_call | solution.py:74
  356.1 8.4 %shard_map.245 = (bf16[4,4,32,1664]{3,2,1,0:T(8,128)(2,1)}, bf16[4,4,32,1664]{3,2,1,0:T(8,128)(2,1)}, bf16[1024,1024]{1,0:T(8,128)(2,1)}) custom-call(s32[2]{0:T(128)} %pad_add_fusion.refs_0_, bf16[1024,1024]{1,0:T(8,128)(2,1)} %get-tuple-element.96.refs_2_.refs_1_, ...), custom_call_target="tpu_custom_call", output_to_operand_aliasing={{2}: (7, {})} | custom-call | flops 4136000000 | bytes 1000000 | tf_op jit(solution)/shard_map/pallas_call | solution.py:74
  365.4 3.9 all-to-all-start.3
  369.3 2.0 collective-permute-start.36
  372.6 18.5 %shard_map.247 = (f32[1024,1024]{1,0:T(8,128)}, f32[1024,1024]{1,0:T(8,128)}) custom-call(s32[2]{0:T(128)} %pad_add_fusion.refs_0_, bf16[1024,1024]{1,0:T(8,128)(2,1)} %get-tuple-element.109.refs_1_, bf16[1024,1024]{1,0:T(8,128)(2,1)} %get-tuple-element.110.refs_2_, bf16[1024,1024]{1,0:T(8,128)(2,1)} %get-tuple-element.93.refs_3_, ...), custom_call_target="tpu_custom_call" | custom-call | flops 9306000384 | bytes 1000000 | tf_op jit(solution)/shard_map/pallas_call | solution.py:74
  391.1 3.4 shard_map.246
  395.6 3.4 shard_map.248
  399.0 2.0 collective-permute-start.25
  402.5 18.7 %shard_map.251 = (f32[1024,1024]{1,0:T(8,128)}, f32[1024,1024]{1,0:T(8,128)}) custom-call(s32[2]{0:T(128)} %pad_add_fusion.refs_0_, bf16[1024,1024]{1,0:T(8,128)(2,1)} %get-tuple-element.144.refs_1_, bf16[1024,1024]{1,0:T(8,128)(2,1)} %get-tuple-element.145.refs_2_, bf16[1024,1024]{1,0:T(8,128)(2,1)} %collective-permute-done.14.refs_6_.refs_3_, ...), custom_call_target="tpu_custom_call" | custom-call | flops 9306000384 | bytes 1000000 | tf_op jit(solution)/shard_map/pallas_call | solution.py:74
  421.3 16.3 %collective-permute-start.28 = (bf16[32,2560]{1,0:T(8,128)(2,1)S(1)}, bf16[32,2560]{1,0:T(8,128)(2,1)S(1)}, u32[]{:S(2)}, u32[]{:S(2)}) collective-permute-start(bf16[32,2560]{1,0:T(8,128)(2,1)S(1)} %get-tuple-element.156), channel_id=1, source_target_pairs={{0,8},{8,16},{16,24},{24,0},{1,9},{9,17},{17,25},{25,1},{2,10},{10... | collective-permute-start | bytes 491528 | tf_op jit(solution)/shard_map/ppermute | solution.py:868
  437.7 2.9 collective-permute-start.32
  440.6 2.8 shard_map.249
  444.5 2.0 collective-permute-start.31
  446.5 1.9 collective-permute-start.33
  448.4 20.2 %shard_map.252 = (f32[1024,1024]{1,0:T(8,128)}, f32[1024,1024]{1,0:T(8,128)}) custom-call(s32[2]{0:T(128)} %pad_add_fusion.refs_0_, bf16[1024,1024]{1,0:T(8,128)(2,1)} %collective-permute-done.34.refs_17_.refs_1_, bf16[1024,1024]{1,0:T(8,128)(2,1)} %collective-permute-done.35.refs_18_.refs_2_, bf16[1024,1024]{1,0:T(8,128)(2,1)} %collective-permute-done.36.refs_3_, ...), custom_call_target="tpu_custom_call" | custom-call | flops 9306000384 | bytes 1000000 | tf_op jit(solution)/shard_map/pallas_call | solution.py:74
  470.0 3.2 shard_map.250
  (140 shorter events, 36.9 us)
Async XLA Ops:
  7.3 32.1 %all-to-all-start = ((bf16[8,128,1024]{2,1,0:T(8,128)(2,1)}), bf16[8,128,1024]{2,1,0:T(8,128)(2,1)S(1)}, u32[]{:S(2)}, u32[]{:S(2)}) async-start(bf16[8,128,1024]{2,1,0:T(8,128)(2,1)} %bitcast.46), calls=%async_computation | async-start | bytes 4194304 | tf_op jit(solution)/shard_map/all_to_all | solution.py:871
  12.6 89.5 %all-gather.3.cloned.1.call-start = ((), (), s32[]{:S(2)}) async-start(), calls=%async_computation.4 | async-start | bytes 4718592 | tf_op jit(solution)/shard_map/all_gather | solution.py:916
  13.1 19.9 %copy-start.4 = (bf16[144,1024]{1,0:T(8,128)(2,1)}, bf16[144,1024]{1,0:T(8,128)(2,1)S(1)}, u32[]{:S(2)}) copy-start(bf16[144,1024]{1,0:T(8,128)(2,1)S(1)} %constant_dynamic-update-slice_fusion.refs_0_) | copy-start | bytes 884740
  13.2 26.1 %collective-permute-start = (bf16[144,1024]{1,0:T(8,128)(2,1)S(1)}, bf16[144,1024]{1,0:T(8,128)(2,1)S(1)}, u32[]{:S(2)}, u32[]{:S(2)}) collective-permute-start(bf16[144,1024]{1,0:T(8,128)(2,1)S(1)} %constant_dynamic-update-slice_fusion.refs_0_), channel_id=1, source_target_pairs={{0,8},{8,16},{16,24},{24,0},{1,9},{9,17},{17,25},{25,1},{2,10},{10... | collective-permute-start | bytes 884744 | tf_op jit(solution)/shard_map/ppermute | solution.py:868
  14.8 24.5 %collective-permute-start.1 = (bf16[144,1024]{1,0:T(8,128)(2,1)S(1)}, bf16[144,1024]{1,0:T(8,128)(2,1)S(1)}, u32[]{:S(2)}, u32[]{:S(2)}) collective-permute-start(bf16[144,1024]{1,0:T(8,128)(2,1)S(1)} %constant_dynamic-update-slice_fusion.refs_0_), channel_id=1, source_target_pairs={{0,16},{8,24},{16,0},{24,8},{1,17},{9,25},{17,1},{25,9},{2,18},{10... | collective-permute-start | bytes 884744 | tf_op jit(solution)/shard_map/ppermute | solution.py:868
  17.4 21.9 %collective-permute-start.2 = (bf16[144,1024]{1,0:T(8,128)(2,1)S(1)}, bf16[144,1024]{1,0:T(8,128)(2,1)S(1)}, u32[]{:S(2)}, u32[]{:S(2)}) collective-permute-start(bf16[144,1024]{1,0:T(8,128)(2,1)S(1)} %constant_dynamic-update-slice_fusion.refs_0_), channel_id=1, source_target_pairs={{0,24},{8,0},{16,8},{24,16},{1,25},{9,1},{17,9},{25,17},{2,26},{10... | collective-permute-start | bytes 884744 | tf_op jit(solution)/shard_map/ppermute | solution.py:868
  40.9 37.3 %copy-start.14 = (s32[1,1024]{1,0:T(1,128)S(1)}, s32[1,1024]{1,0:T(1,128)}, u32[]{:S(2)}) copy-start(s32[1,1024]{1,0:T(1,128)} %refs_12_.1) | copy-start | bytes 12292
  43.2 22.0 %collective-permute-start.4 = (bf16[4,80,1024]{2,1,0:T(8,128)(2,1)}, bf16[4,80,1024]{2,1,0:T(8,128)(2,1)S(1)}, u32[]{:S(2)}, u32[]{:S(2)}) collective-permute-start(bf16[4,80,1024]{2,1,0:T(8,128)(2,1)} %get-tuple-element.82.refs_3_.refs_11_.refs_19_), channel_id=1, source_target_pairs={{0,2},{1,3},{2,0},{3,1},{4,6},{5,7},{6,4},{7,5},{8,10},{9,11},{10,... | collective-permute-start | bytes 1966088 | tf_op jit(solution)/shard_map/ppermute | solution.py:865
  45.4 22.9 %collective-permute-start.6 = (bf16[4,80,1024]{2,1,0:T(8,128)(2,1)}, bf16[4,80,1024]{2,1,0:T(8,128)(2,1)S(1)}, u32[]{:S(2)}, u32[]{:S(2)}) collective-permute-start(bf16[4,80,1024]{2,1,0:T(8,128)(2,1)} %get-tuple-element.82.refs_3_.refs_11_.refs_19_), channel_id=1, source_target_pairs={{0,4},{1,5},{2,6},{3,7},{4,0},{5,1},{6,2},{7,3},{8,12},{9,13},{10,... | collective-permute-start | bytes 1966088 | tf_op jit(solution)/shard_map/ppermute | solution.py:865
  46.9 50.9 %collective-permute-start.12 = (bf16[1024,1024]{1,0:T(8,128)(2,1)}, bf16[1024,1024]{1,0:T(8,128)(2,1)S(1)}, u32[]{:S(2)}, u32[]{:S(2)}) collective-permute-start(bf16[1024,1024]{1,0:T(8,128)(2,1)} %refs_2_.1), channel_id=1, source_target_pairs={{0,8},{8,16},{16,24},{1,9},{9,17},{17,25},{2,10},{10,18},{18,26},{... | collective-permute-start | bytes 6291464 | tf_op jit(solution)/shard_map/ppermute | solution.py:891
  53.1 48.9 %collective-permute-start.13 = (bf16[1024,1024]{1,0:T(8,128)(2,1)}, bf16[1024,1024]{1,0:T(8,128)(2,1)}, u32[]{:S(2)}, u32[]{:S(2)}) collective-permute-start(bf16[1024,1024]{1,0:T(8,128)(2,1)} %refs_2_.1), channel_id=1, source_target_pairs={{8,0},{16,8},{24,16},{9,1},{17,9},{25,17},{10,2},{18,10},{26,18},{... | collective-permute-start | bytes 6291464 | tf_op jit(solution)/shard_map/ppermute | solution.py:892
  54.4 14.8 %collective-permute-start.3 = (bf16[4,80,1024]{2,1,0:T(8,128)(2,1)}, bf16[4,80,1024]{2,1,0:T(8,128)(2,1)S(1)}, u32[]{:S(2)}, u32[]{:S(2)}) collective-permute-start(bf16[4,80,1024]{2,1,0:T(8,128)(2,1)} %get-tuple-element.82.refs_3_.refs_11_.refs_19_), channel_id=1, source_target_pairs={{0,1},{1,0},{2,3},{3,2},{4,5},{5,4},{6,7},{7,6},{8,9},{9,8},{10,11... | collective-permute-start | bytes 1966088 | tf_op jit(solution)/shard_map/ppermute | solution.py:865
  65.3 14.8 %copy-start.8 = (bf16[4,80,1024]{2,1,0:T(8,128)(2,1)}, bf16[4,80,1024]{2,1,0:T(8,128)(2,1)S(1)}, u32[]{:S(2)}) copy-start(bf16[4,80,1024]{2,1,0:T(8,128)(2,1)S(1)} %collective-permute-done.4.refs_5_.refs_13_.refs_21_) | copy-start | bytes 1966084
  65.3 10.4 %collective-permute-start.10 = (bf16[4,48,1024]{2,1,0:T(8,128)(2,1)S(1)}, bf16[4,48,1024]{2,1,0:T(8,128)(2,1)}, u32[]{:S(2)}, u32[]{:S(2)}) collective-permute-start(bf16[4,48,1024]{2,1,0:T(8,128)(2,1)S(1)} %slice.25), channel_id=1, source_target_pairs={{0,4},{1,5},{2,6},{3,7},{4,0},{5,1},{6,2},{7,3},{8,12},{9,13},{10,... | collective-permute-start | bytes 1179656 | tf_op jit(solution)/shard_map/ppermute | solution.py:865
  68.4 6.4 %collective-permute-start.8 = (bf16[4,32,1024]{2,1,0:T(8,128)(2,1)S(1)}, bf16[4,32,1024]{2,1,0:T(8,128)(2,1)S(1)}, u32[]{:S(2)}, u32[]{:S(2)}) collective-permute-start(bf16[4,32,1024]{2,1,0:T(8,128)(2,1)S(1)} %slice.24), channel_id=1, source_target_pairs={{0,2},{1,3},{2,0},{3,1},{4,6},{5,7},{6,4},{7,5},{8,10},{9,11},{10,... | collective-permute-start | bytes 786440 | tf_op jit(solution)/shard_map/ppermute | solution.py:865
  69.3 10.6 %collective-permute-start.5 = (bf16[4,80,1024]{2,1,0:T(8,128)(2,1)S(1)}, bf16[4,80,1024]{2,1,0:T(8,128)(2,1)}, u32[]{:S(2)}, u32[]{:S(2)}) collective-permute-start(bf16[4,80,1024]{2,1,0:T(8,128)(2,1)S(1)} %collective-permute-done.4.refs_5_.refs_13_.refs_21_), channel_id=1, source_target_pairs={{0,1},{1,0},{2,3},{3,2},{4,5},{5,4},{6,7},{7,6},{8,9},{9,8},{10,11... | collective-permute-start | bytes 1966088 | tf_op jit(solution)/shard_map/ppermute | solution.py:865
  74.8 5.0 %collective-permute-start.7 = (bf16[4,80,1024]{2,1,0:T(8,128)(2,1)S(1)}, bf16[4,80,1024]{2,1,0:T(8,128)(2,1)}, u32[]{:S(2)}, u32[]{:S(2)}) collective-permute-start(bf16[4,80,1024]{2,1,0:T(8,128)(2,1)S(1)} %collective-permute-done.6.refs_7_.refs_15_.refs_23_), channel_id=1, source_target_pairs={{0,1},{1,0},{2,3},{3,2},{4,5},{5,4},{6,7},{7,6},{8,9},{9,8},{10,11... | collective-permute-start | bytes 1966088 | tf_op jit(solution)/shard_map/ppermute | solution.py:865
  75.7 1.6 collective-permute-start.9
  78.0 2.1 collective-permute-start.11
  109.2 76.4 %collective-permute-start.14 = (bf16[1024,1024]{1,0:T(8,128)(2,1)}, bf16[1024,1024]{1,0:T(8,128)(2,1)}, u32[]{:S(2)}, u32[]{:S(2)}) collective-permute-start(bf16[1024,1024]{1,0:T(8,128)(2,1)} %get-tuple-element.93.refs_3_), channel_id=1, source_target_pairs={{8,16},{16,24},{9,17},{17,25},{10,18},{18,26},{11,19},{19,27},{12,... | collective-permute-start | bytes 6291464 | tf_op jit(solution)/shard_map/ppermute | solution.py:891
  111.2 74.4 %collective-permute-start.15 = (bf16[1024,1024]{1,0:T(8,128)(2,1)}, bf16[1024,1024]{1,0:T(8,128)(2,1)S(1)}, u32[]{:S(2)}, u32[]{:S(2)}) collective-permute-start(bf16[1024,1024]{1,0:T(8,128)(2,1)} %get-tuple-element.94.refs_4_), channel_id=1, source_target_pairs={{8,0},{16,8},{9,1},{17,9},{10,2},{18,10},{11,3},{19,11},{12,4},{20... | collective-permute-start | bytes 6291464 | tf_op jit(solution)/shard_map/ppermute | solution.py:892
  175.4 60.6 %collective-permute-start.16 = (bf16[1024,1024]{1,0:T(8,128)(2,1)}, bf16[1024,1024]{1,0:T(8,128)(2,1)}, u32[]{:S(2)}, u32[]{:S(2)}) collective-permute-start(bf16[1024,1024]{1,0:T(8,128)(2,1)} %bitcast.13.refs_0_.refs_1_), channel_id=1, source_target_pairs={{0,8},{8,16},{16,24},{1,9},{9,17},{17,25},{2,10},{10,18},{18,26},{... | collective-permute-start | bytes 6291464 | tf_op jit(solution)/shard_map/ppermute | solution.py:891
  184.3 51.7 %collective-permute-start.17 = (bf16[1024,1024]{1,0:T(8,128)(2,1)}, bf16[1024,1024]{1,0:T(8,128)(2,1)}, u32[]{:S(2)}, u32[]{:S(2)}) collective-permute-start(bf16[1024,1024]{1,0:T(8,128)(2,1)} %bitcast.13.refs_0_.refs_1_), channel_id=1, source_target_pairs={{8,0},{16,8},{24,16},{9,1},{17,9},{25,17},{10,2},{18,10},{26,18},{... | collective-permute-start | bytes 6291464 | tf_op jit(solution)/shard_map/ppermute | solution.py:892
  217.7 39.1 %all-to-all-start.2 = ((bf16[8,128,1024]{2,1,0:T(8,128)(2,1)}), bf16[8,128,1024]{2,1,0:T(8,128)(2,1)S(1)}, u32[]{:S(2)}, u32[]{:S(2)}) async-start(bf16[8,128,1024]{2,1,0:T(8,128)(2,1)} %bitcast.48), calls=%async_computation.2 | async-start | bytes 4194304 | tf_op jit(solution)/shard_map/all_to_all | solution.py:871
  253.5 42.4 %collective-permute-start.18 = (bf16[1024,1024]{1,0:T(8,128)(2,1)}, bf16[1024,1024]{1,0:T(8,128)(2,1)}, u32[]{:S(2)}, u32[]{:S(2)}) collective-permute-start(bf16[1024,1024]{1,0:T(8,128)(2,1)} %get-tuple-element.109.refs_1_), channel_id=1, source_target_pairs={{8,16},{16,24},{9,17},{17,25},{10,18},{18,26},{11,19},{19,27},{12,... | collective-permute-start | bytes 6291464 | tf_op jit(solution)/shard_map/ppermute | solution.py:891
  255.4 52.8 %collective-permute-start.19 = (bf16[1024,1024]{1,0:T(8,128)(2,1)}, bf16[1024,1024]{1,0:T(8,128)(2,1)}, u32[]{:S(2)}, u32[]{:S(2)}) collective-permute-start(bf16[1024,1024]{1,0:T(8,128)(2,1)} %get-tuple-element.110.refs_2_), channel_id=1, source_target_pairs={{8,0},{16,8},{9,1},{17,9},{10,2},{18,10},{11,3},{19,11},{12,4},{20... | collective-permute-start | bytes 6291464 | tf_op jit(solution)/shard_map/ppermute | solution.py:892
  295.8 33.4 %collective-permute-start.20 = (bf16[4,4,32,2560]{3,2,1,0:T(8,128)(2,1)}, bf16[4,4,32,2560]{3,2,1,0:T(8,128)(2,1)S(1)}, u32[]{:S(2)}, u32[]{:S(2)}) collective-permute-start(bf16[4,4,32,2560]{3,2,1,0:T(8,128)(2,1)} %get-tuple-element.108.refs_7_), channel_id=1, source_target_pairs={{0,1},{1,0},{2,3},{3,2},{4,5},{5,4},{6,7},{7,6},{8,9},{9,8},{10,11... | collective-permute-start | bytes 7864328 | tf_op jit(solution)/shard_map/ppermute | solution.py:865
  326.0 75.1 %collective-permute-start.34 = (bf16[1024,1024]{1,0:T(8,128)(2,1)}, bf16[1024,1024]{1,0:T(8,128)(2,1)}, u32[]{:S(2)}, u32[]{:S(2)}) collective-permute-start(bf16[1024,1024]{1,0:T(8,128)(2,1)} %get-tuple-element.144.refs_1_), channel_id=1, source_target_pairs={{16,24},{17,25},{18,26},{19,27},{20,28},{21,29},{22,30},{23,31}} | collective-permute-start | bytes 6291464 | tf_op jit(solution)/shard_map/ppermute | solution.py:891
  327.9 74.6 %collective-permute-start.35 = (bf16[1024,1024]{1,0:T(8,128)(2,1)}, bf16[1024,1024]{1,0:T(8,128)(2,1)}, u32[]{:S(2)}, u32[]{:S(2)}) collective-permute-start(bf16[1024,1024]{1,0:T(8,128)(2,1)} %get-tuple-element.145.refs_2_), channel_id=1, source_target_pairs={{8,0},{9,1},{10,2},{11,3},{12,4},{13,5},{14,6},{15,7}} | collective-permute-start | bytes 6291464 | tf_op jit(solution)/shard_map/ppermute | solution.py:892
  335.2 29.3 %collective-permute-start.21 = (bf16[4,32,2560]{2,1,0:T(8,128)(2,1)}, bf16[4,32,2560]{2,1,0:T(8,128)(2,1)S(1)}, u32[]{:S(2)}, u32[]{:S(2)}) collective-permute-start(bf16[4,32,2560]{2,1,0:T(8,128)(2,1)} %get-tuple-element.120.refs_14_), channel_id=1, source_target_pairs={{0,2},{1,3},{2,0},{3,1},{4,6},{5,7},{6,4},{7,5},{8,10},{9,11},{10,... | collective-permute-start | bytes 1966088 | tf_op jit(solution)/shard_map/ppermute | solution.py:865
  336.9 32.4 %collective-permute-start.22 = (bf16[4,32,2560]{2,1,0:T(8,128)(2,1)}, bf16[4,32,2560]{2,1,0:T(8,128)(2,1)S(1)}, u32[]{:S(2)}, u32[]{:S(2)}) collective-permute-start(bf16[4,32,2560]{2,1,0:T(8,128)(2,1)} %get-tuple-element.121.refs_15_), channel_id=1, source_target_pairs={{0,4},{1,5},{2,6},{3,7},{4,0},{5,1},{6,2},{7,3},{8,12},{9,13},{10,... | collective-permute-start | bytes 1966088 | tf_op jit(solution)/shard_map/ppermute | solution.py:865
  338.4 32.9 %collective-permute-start.23 = (bf16[4,32,2560]{2,1,0:T(8,128)(2,1)}, bf16[4,32,2560]{2,1,0:T(8,128)(2,1)}, u32[]{:S(2)}, u32[]{:S(2)}) collective-permute-start(bf16[4,32,2560]{2,1,0:T(8,128)(2,1)} %get-tuple-element.122.refs_16_), channel_id=1, source_target_pairs={{0,6},{1,7},{2,4},{3,5},{4,2},{5,3},{6,0},{7,1},{8,14},{9,15},{10,... | collective-permute-start | bytes 1966088 | tf_op jit(solution)/shard_map/ppermute | solution.py:865
  364.6 31.0 %collective-permute-start.24 = (bf16[4,4,32,1664]{3,2,1,0:T(8,128)(2,1)}, bf16[4,4,32,1664]{3,2,1,0:T(8,128)(2,1)}, u32[]{:S(2)}, u32[]{:S(2)}) collective-permute-start(bf16[4,4,32,1664]{3,2,1,0:T(8,128)(2,1)} %get-tuple-element.129.refs_11_), channel_id=1, source_target_pairs={{0,1},{1,0},{2,3},{3,2},{4,5},{5,4},{6,7},{7,6},{8,9},{9,8},{10,11... | collective-permute-start | bytes 5111816 | tf_op jit(solution)/shard_map/ppermute | solution.py:865
  365.4 55.9 %all-to-all-start.3 = ((bf16[8,128,1024]{2,1,0:T(8,128)(2,1)}), bf16[8,128,1024]{2,1,0:T(8,128)(2,1)S(1)}, u32[]{:S(2)}, u32[]{:S(2)}) async-start(bf16[8,128,1024]{2,1,0:T(8,128)(2,1)} %bitcast.49), calls=%async_computation.3 | async-start | bytes 4194304 | tf_op jit(solution)/shard_map/all_to_all | solution.py:871
  369.3 21.8 %copy-start.21 = (bf16[4,32,2560]{2,1,0:T(8,128)(2,1)}, bf16[4,32,2560]{2,1,0:T(8,128)(2,1)S(1)}, u32[]{:S(2)}) copy-start(bf16[4,32,2560]{2,1,0:T(8,128)(2,1)S(1)} %collective-permute-done.22.refs_2_) | copy-start | bytes 1966084
  369.3 75.1 %collective-permute-start.36 = (bf16[1024,1024]{1,0:T(8,128)(2,1)}, bf16[1024,1024]{1,0:T(8,128)(2,1)}, u32[]{:S(2)}, u32[]{:S(2)}) collective-permute-start(bf16[1024,1024]{1,0:T(8,128)(2,1)} %collective-permute-done.14.refs_6_.refs_3_), channel_id=1, source_target_pairs={{16,24},{17,25},{18,26},{19,27},{20,28},{21,29},{22,30},{23,31}} | collective-permute-start | bytes 6291464 | tf_op jit(solution)/shard_map/ppermute | solution.py:891
  371.3 73.2 %collective-permute-start.37 = (bf16[1024,1024]{1,0:T(8,128)(2,1)}, bf16[1024,1024]{1,0:T(8,128)(2,1)}, u32[]{:S(2)}, u32[]{:S(2)}) collective-permute-start(bf16[1024,1024]{1,0:T(8,128)(2,1)} %copy-done.19), channel_id=1, source_target_pairs={{8,0},{9,1},{10,2},{11,3},{12,4},{13,5},{14,6},{15,7}} | collective-permute-start | bytes 6291464 | tf_op jit(solution)/shard_map/ppermute | solution.py:892
  399.0 22.3 %collective-permute-start.25 = (bf16[4,32,1664]{2,1,0:T(8,128)(2,1)}, bf16[4,32,1664]{2,1,0:T(8,128)(2,1)S(1)}, u32[]{:S(2)}, u32[]{:S(2)}) collective-permute-start(bf16[4,32,1664]{2,1,0:T(8,128)(2,1)} %get-tuple-element.133.refs_14_), channel_id=1, source_target_pairs={{0,2},{1,3},{2,0},{3,1},{4,6},{5,7},{6,4},{7,5},{8,10},{9,11},{10,... | collective-permute-start | bytes 1277960 | tf_op jit(solution)/shard_map/ppermute | solution.py:865
  401.0 36.7 %collective-permute-start.26 = (bf16[4,32,1664]{2,1,0:T(8,128)(2,1)}, bf16[4,32,1664]{2,1,0:T(8,128)(2,1)S(1)}, u32[]{:S(2)}, u32[]{:S(2)}) collective-permute-start(bf16[4,32,1664]{2,1,0:T(8,128)(2,1)} %get-tuple-element.134.refs_15_), channel_id=1, source_target_pairs={{0,4},{1,5},{2,6},{3,7},{4,0},{5,1},{6,2},{7,3},{8,12},{9,13},{10,... | collective-permute-start | bytes 1277960 | tf_op jit(solution)/shard_map/ppermute | solution.py:865
  402.5 35.2 %collective-permute-start.27 = (bf16[4,32,1664]{2,1,0:T(8,128)(2,1)}, bf16[4,32,1664]{2,1,0:T(8,128)(2,1)}, u32[]{:S(2)}, u32[]{:S(2)}) collective-permute-start(bf16[4,32,1664]{2,1,0:T(8,128)(2,1)} %get-tuple-element.135.refs_16_), channel_id=1, source_target_pairs={{0,6},{1,7},{2,4},{3,5},{4,2},{5,3},{6,0},{7,1},{8,14},{9,15},{10,... | collective-permute-start | bytes 1277960 | tf_op jit(solution)/shard_map/ppermute | solution.py:865
  421.3 19.3 %copy-start.23 = (bf16[4,32,1664]{2,1,0:T(8,128)(2,1)}, bf16[4,32,1664]{2,1,0:T(8,128)(2,1)S(1)}, u32[]{:S(2)}) copy-start(bf16[4,32,1664]{2,1,0:T(8,128)(2,1)S(1)} %collective-permute-done.25.refs_1_) | copy-start | bytes 1277956
  421.3 25.2 %collective-permute-start.28 = (bf16[32,2560]{1,0:T(8,128)(2,1)S(1)}, bf16[32,2560]{1,0:T(8,128)(2,1)S(1)}, u32[]{:S(2)}, u32[]{:S(2)}) collective-permute-start(bf16[32,2560]{1,0:T(8,128)(2,1)S(1)} %get-tuple-element.156), channel_id=1, source_target_pairs={{0,8},{8,16},{16,24},{24,0},{1,9},{9,17},{17,25},{25,1},{2,10},{10... | collective-permute-start | bytes 491528 | tf_op jit(solution)/shard_map/ppermute | solution.py:868
  437.7 30.9 %collective-permute-start.30 = (bf16[32,2560]{1,0:T(8,128)(2,1)S(1)}, bf16[32,2560]{1,0:T(8,128)(2,1)}, u32[]{:S(2)}, u32[]{:S(2)}) collective-permute-start(bf16[32,2560]{1,0:T(8,128)(2,1)S(1)} %get-tuple-element.155), channel_id=1, source_target_pairs={{0,16},{8,24},{16,0},{24,8},{1,17},{9,25},{17,1},{25,9},{2,18},{10... | collective-permute-start | bytes 491528 | tf_op jit(solution)/shard_map/ppermute | solution.py:868
  437.7 30.9 %collective-permute-start.32 = (bf16[32,2560]{1,0:T(8,128)(2,1)S(1)}, bf16[32,2560]{1,0:T(8,128)(2,1)}, u32[]{:S(2)}, u32[]{:S(2)}) collective-permute-start(bf16[32,2560]{1,0:T(8,128)(2,1)S(1)} %get-tuple-element.154), channel_id=1, source_target_pairs={{0,24},{8,0},{16,8},{24,16},{1,25},{9,1},{17,9},{25,17},{2,26},{10... | collective-permute-start | bytes 491528 | tf_op jit(solution)/shard_map/ppermute | solution.py:868
  444.4 24.2 %collective-permute-start.29 = (bf16[32,1664]{1,0:T(8,128)(2,1)S(1)}, bf16[32,1664]{1,0:T(8,128)(2,1)S(1)}, u32[]{:S(2)}, u32[]{:S(2)}) collective-permute-start(bf16[32,1664]{1,0:T(8,128)(2,1)S(1)} %get-tuple-element.159), channel_id=1, source_target_pairs={{0,8},{8,16},{16,24},{24,0},{1,9},{9,17},{17,25},{25,1},{2,10},{10... | collective-permute-start | bytes 319496 | tf_op jit(solution)/shard_map/ppermute | solution.py:868
  444.5 24.2 %collective-permute-start.31 = (bf16[32,1664]{1,0:T(8,128)(2,1)S(1)}, bf16[32,1664]{1,0:T(8,128)(2,1)S(1)}, u32[]{:S(2)}, u32[]{:S(2)}) collective-permute-start(bf16[32,1664]{1,0:T(8,128)(2,1)S(1)} %get-tuple-element.158), channel_id=1, source_target_pairs={{0,16},{8,24},{16,0},{24,8},{1,17},{9,25},{17,1},{25,9},{2,18},{10... | collective-permute-start | bytes 319496 | tf_op jit(solution)/shard_map/ppermute | solution.py:868
  446.5 22.1 %copy-start.27 = (bf16[32,2560]{1,0:T(8,128)(2,1)}, bf16[32,2560]{1,0:T(8,128)(2,1)S(1)}, u32[]{:S(2)}) copy-start(bf16[32,2560]{1,0:T(8,128)(2,1)S(1)} %collective-permute-done.28.refs_3_) | copy-start | bytes 491524
  446.5 22.2 %collective-permute-start.33 = (bf16[32,1664]{1,0:T(8,128)(2,1)S(1)}, bf16[32,1664]{1,0:T(8,128)(2,1)S(1)}, u32[]{:S(2)}, u32[]{:S(2)}) collective-permute-start(bf16[32,1664]{1,0:T(8,128)(2,1)S(1)} %get-tuple-element.157), channel_id=1, source_target_pairs={{0,24},{8,0},{16,8},{24,16},{1,25},{9,1},{17,9},{25,17},{2,26},{10... | collective-permute-start | bytes 319496 | tf_op jit(solution)/shard_map/ppermute | solution.py:868
  (25 other events, 83.1 us)
Sparse Core Ops, SparseCore 0:
  43.4 45.3 all-gather.2

commit v4 on v3

--- a/solution.py
+++ b/solution.py
@@ -115,8 +115,9 @@
         for piece in pieces[2]:
             for z in range(piece.shape[0]):
                 gains = gains + piece[z].astype(F32)
-        for n, ref in enumerate(gain_refs):
+        for n, ref in enumerate(gain_refs[:-1]):
             ref[...] = gains[n : n + 1]
+        gain_refs[-1][...] = jnp.transpose(gains)
 
     lanes = lax.broadcasted_iota(jnp.int32, (QB, rows_ref.shape[0]), 1)
     x = dot_nn(one_hot(ids_ref[...], lanes), rows_ref[...])
@@ -139,7 +140,8 @@
         (ids_col, rows, *[a for a, _ in (*pieces_q, *pieces_k, *pieces_g)]),
         [rows_out, rows_out, shaped((width, total)), rows_out, rows_out]
         + [shaped(full)] * 2
-        + [gain] * 4,
+        + [gain] * 4
+        + [shaped((width, 16), F32)],
         deps,
         (meta,),
         (total // QB,),
@@ -147,7 +149,10 @@
         + piece_specs(pieces_q, full[2])
         + piece_specs(pieces_k, full[2])
         + piece_specs(pieces_g, 16),
-        [block, block, turned, block, block] + [whole(full)] * 2 + [whole((1, width))] * 4,
+        [block, block, turned, block, block]
+        + [whole(full)] * 2
+        + [whole((1, width))] * 4
+        + [whole((width, 16))],
         micros=14,
     )
     flat = (width, width)
@@ -668,172 +673,173 @@
     )
 
 
-def shared_kernel(picks, turns, sums_in, meta, *refs):
-    lefts, rights = refs[: len(turns)], refs[len(turns) : len(turns) + len(picks)]
-    rest = refs[len(turns) + len(picks) :]
-    small, (send, keep, sums) = rest[:sums_in], rest[sums_in:]
-    half, step = send.shape[0], send.shape[2]
-    turned = [jnp.transpose(l[...]) if t else l[...] for l, t in zip(lefts, turns)]
-
-    def put(cols, size):
-        for r in range(2 * half):
-            row = pl.multiple_of((r ^ meta[0]) * step, step)
-            ref = send if r % 2 else keep
-            ref[r // 2, 0, :, cols : cols + size] = sums[pl.ds(row, step), :size].astype(BF)
-
-    cols = 0
-    for pick, right in zip(picks, rights):
-        size = right.shape[1]
-        sums[:, :size] = dot_nn(turned[pick], right[...])
-        put(cols, size)
-        cols += size
-    if sums_in:
-        sums[:, :128] = jnp.zeros((sums.shape[0], 128), F32)
-        for n in range(sums_in):
-            sums[:, 8 * n : 8 * n + 8] = jnp.transpose(small[n][...])
-        put(cols, 128)
-
-
-def shared_grads(meta, lefts, terms, small, experts, groups, deps=(), gates=()):
-    total = terms[0][1].shape[0]
-    array, is_turned = lefts[0]
-    features = array.shape[0 if is_turned else 1]
+def shared_kernel(turn, count, norm, left_ref, *refs):
+    rights, refs = refs[:count], refs[count:]
+    if norm:
+        mats, (gains_ref, small_ref, out, tops) = refs[:count], refs[count:]
+    else:
+        (out,) = refs
+    experts, step = out.shape[0], out.shape[2]
+    left = jnp.transpose(left_ref[...]) if turn else left_ref[...]
+
+    def put(values, cols):
+        values = values.astype(BF)
+        for e in range(experts):
+            part = values[e * step : (e + 1) * step]
+            out[e, 0, :, cols : cols + values.shape[1]] = part
+
+    if norm:
+
+        @pl.when(pl.program_id(0) == 0)
+        def _():
+            for n, right in enumerate(rights):
+                tops[n : n + 1] = jnp.sum(right[...].astype(F32), 0, keepdims=True)
+
+    cols, with_gain, with_bias = 0, 0.0, 0.0
+    for n, right in enumerate(rights):
+        sums = dot_nn(left, right[...])
+        if norm:
+            mat = mats[n][...].astype(F32)
+            with_gain = with_gain + jnp.sum(mat * sums, -1, keepdims=True)
+            with_bias = with_bias + jnp.sum(mat * tops[n : n + 1], -1, keepdims=True)
+        put(sums, cols)
+        cols += right.shape[1]
+    if norm:
+        with_gain = (with_gain - gains_ref[:, 1:2] * with_bias) / gains_ref[:, 0:1]
+        rest = jnp.zeros((sums.shape[0], 120), F32)
+        extra = jnp.concatenate([jnp.transpose(small_ref[...]), rest], -1)
+        lane = lax.broadcasted_iota(jnp.int32, (1, 128), 1)
+        extra = jnp.where(lane == 8, with_gain, jnp.where(lane == 9, with_bias, extra))
+        put(extra, cols)
+
+
+def shared_grads(left, turned, rights, experts, groups, norm=(), deps=(), gates=()):
+    total = rights[0].shape[0]
+    features = left.shape[0 if turned else 1]
     step, block = features // (experts * groups), features // groups
-    width = sum(r.shape[1] for _, r in terms) + (128 if small else 0)
-    as_is = pl.BlockSpec((block, total), lambda g, *_: (g, 0))
-    to_turn = pl.BlockSpec((total, block), lambda g, *_: (0, g))
-    sums = pl.BlockSpec((8, block), lambda g, *_: (0, g))
-    shape = (experts // 2, groups, step, width)
-    spec = pl.BlockSpec((shape[0], 1, step, width), lambda g, *_: (0, g, 0, 0))
-    return run(
-        partial(shared_kernel, [p for p, _ in terms], [not t for _, t in lefts], len(small)),
-        (*[a for a, _ in lefts], *[r for _, r in terms], *small),
-        [shaped(shape)] * 2,
+    width = sum(r.shape[1] for r in rights) + (128 if norm else 0)
+    rows = pl.BlockSpec((block, total), lambda g: (g, 0))
+    specs = [rows if turned else pl.BlockSpec((total, block), lambda g: (0, g))]
+    specs += [whole(r.shape) for r in rights]
+    args, scratch = [left, *rights], []
+    if norm:
+        mats, gains, small = norm
+        args += [*mats, gains, small]
+        specs += [pl.BlockSpec((block, m.shape[1]), lambda g: (g, 0)) for m in mats]
+        specs += [pl.BlockSpec((block, 16), lambda g: (g, 0))]
+        specs += [pl.BlockSpec((8, block), lambda g: (0, g))]
+        scratch = [pltpu.VMEM((8, rights[0].shape[1]), F32)]
+    shape = (experts, groups, step, width)
+    return run(
+        partial(shared_kernel, not turned, len(rights), bool(norm)),
+        args,
+        [shaped(shape)],
+        deps,
+        (),
+        (groups,),
+        specs,
+        [pl.BlockSpec((experts, 1, step, width), lambda g: (0, g, 0, 0))],
+        scratch,
+        micros=4 * len(rights),
+        gates=gates,
+    )
+
+
+def total_kernel(meta, first_ref, second_ref, *outs):
+    groups = len(outs)
+    g = pl.program_id(0)
+    for s in range(groups):
+
+        @pl.when(g == lax.rem(meta[1] + s, groups))
+        def _(out=outs[s]):
+            col = 0
+            for ref in (first_ref, second_ref):
+                total = ref[0, 0].astype(F32)
+                for e in range(1, ref.shape[0]):
+                    total = total + ref[e, 0].astype(F32)
+                out[:, col : col + total.shape[1]] = total.astype(out.dtype)
+                col += total.shape[1]
+
+
+def total_over(meta, first, second, deps=(), gates=()):
+    groups, step = first.shape[1:3]
+    width = first.shape[3] + second.shape[3]
+    specs = []
+    for a in (first, second):
+        block = (a.shape[0], 1, *a.shape[2:])
+        specs.append(pl.BlockSpec(block, lambda g, *_: (0, g, 0, 0)))
+    return run(
+        total_kernel,
+        (first, second),
+        [shaped((step, width), F32)] + [shaped((step, width))] * (groups - 1),
         deps,
         (meta,),
         (groups,),
-        [as_is if t else to_turn for _, t in lefts]
-        + [whole(r.shape) for _, r in terms]
-        + [sums] * len(small),
-        [spec] * 2,
-        [pltpu.VMEM((block, max(r.shape[1] for _, r in terms)), F32)],
-        micros=8,
+        specs,
+        [whole((step, width))] * groups,
+        micros=5,
         gates=gates,
     )
 
 
-def halve_kernel(keep_ref, got_ref, *outs):
-    for r, out in enumerate(outs):
-        both = keep_ref[r].astype(F32) + got_ref[r].astype(F32)
-        out[...] = both.astype(out.dtype)
-
-
-def halve(keep, got, deps=()):
-    chips, tail = keep.shape[0], keep.shape[1:]
-    kinds = [F32] + [BF] * (chips - 1)
-    return run(halve_kernel, (keep, got), [shaped(tail, k) for k in kinds], deps, micros=2)
-
-
-def total_kernel(own_ref, *refs):
-    ins, (all_ref, low_ref) = refs[:-2], refs[-2:]
-    total = own_ref[...]
-    for ref in ins:
+def final_kernel(*refs):
+    ins, (o_ref, q_ref, k_ref, v_ref, *small) = refs[:-8], refs[-8:]
+    total = ins[0][...]
+    for ref in ins[1:]:
         total = total + ref[...].astype(F32)
-    all_ref[...] = total
-    low_ref[...] = total.astype(BF)
-
-
-def total_of(own, others):
-    return run(
-        total_kernel,
-        (own, *others),
-        [shaped(own.shape, F32), shaped(own.shape)],
+    width = o_ref.shape[1]
+    for n, ref in enumerate((o_ref, q_ref, k_ref, v_ref)):
+        ref[...] = total[:, n * width : (n + 1) * width]
+    turned = jnp.transpose(total[:, 4 * width :])
+    for n, ref in zip((8, 9, 0, 1), small):
+        ref[...] = turned[n : n + 1]
+
+
+def final(parts, width):
+    step = parts[0].shape[0]
+    return run(
+        final_kernel,
+        parts,
+        [shaped((step, width), F32)] * 4 + [shaped((1, step), F32)] * 4,
         micros=2,
     )
 
 
-def final_kernel(count, heads, meta, *refs):
-    owns, ins = refs[:2], refs[2 : 2 + 2 * count]
-    o_ref, q_ref, k_ref, v_ref, small_ref = refs[2 + 2 * count :]
-    first = owns[0][meta[1]]
-    second = owns[1][meta[1]]
-    for n in range(count):
-        first = first + ins[2 * n][...].astype(F32)
-        second = second + ins[2 * n + 1][...].astype(F32)
-    width = o_ref.shape[1]
-    o_ref[...] = first[:, :width]
-    for n, ref in enumerate((q_ref, k_ref, v_ref)):
-        ref[:, :heads] = first[:, width + n * heads : width + (n + 1) * heads]
-        ref[:, heads:] = second[:, n * heads : (n + 1) * heads]
-    small_ref[...] = second[:, 3 * heads :]
-
-
-def final(meta, owns, pairs):
-    step = owns[0].shape[1]
-    heads = (owns[1].shape[2] - 128) // 3
-    width = owns[0].shape[2] - 3 * heads
-    return run(
-        partial(final_kernel, len(pairs), heads),
-        (*owns, *[a for p in pairs for a in p]),
-        [shaped((step, width), F32)] * 4 + [shaped((step, 128), F32)],
-        (),
-        (meta,),
-        micros=2,
-    )
-
-
-def first_kernel(steps, count, *refs):
-    grads, mats = refs[: 3 * count], refs[3 * count : 3 * count + 3]
-    seq_ref, dmix_ref, gain_ref, ids_ref, out_ref, sums_ref, rows = refs[3 * count + 3 :]
+def first_kernel(*refs):
+    grads, mats = refs[:3], refs[3:6]
+    seq_ref, dmix_ref, gain_ref, ids_ref, out_ref, rows = refs[6:]
     r = pl.program_id(0)
-    size, part = grads[0].shape
-    grad = None
-    for n in range(3):
-        for j in range(count):
-            term = dot_nt(grads[n * count + j][...], mats[n][:, j * part : (j + 1) * part])
-            grad = term if grad is None else grad + term
+    size = seq_ref.shape[0]
+    grad = dot_nt(grads[0][...], mats[0][...])
+    for n in (1, 2):
+        grad = grad + dot_nt(grads[n][...], mats[n][...])
     normed, inverse = norm_rows(seq_ref[...].astype(F32))
-    gain_sum = jnp.sum(grad * normed, 0, keepdims=True)
-    bias_sum = jnp.sum(grad, 0, keepdims=True)
-
-    @pl.when(r == 0)
-    def _():
-        sums_ref[0:1] = gain_sum
-        sums_ref[1:2] = bias_sum
-
-    @pl.when(r > 0)
-    def _():
-        sums_ref[0:1] += gain_sum
-        sums_ref[1:2] += bias_sum
-
     back = dmix_ref[...].astype(F32) + norm_back(grad, normed, inverse, gain_ref[...])
     rows[pl.ds(pl.multiple_of(r * size, size), size)] = back.astype(BF)
 
-    @pl.when(r == steps - 1)
+    @pl.when(r == pl.num_programs(0) - 1)
     def _():
         to_experts(ids_ref, rows, out_ref)
 
 
-def first_back(dqs, dks, dvs, mats, seq, dmix, gain, ids_row, deps=(), gates=()):
+def first_back(grads, mats, seq, dmix, gain, ids_row, deps=()):
     total, width = seq.shape
-    steps, count = total // QB, len(dqs)
     block = pl.BlockSpec((QB, width), lambda r: (r, 0))
-    part = pl.BlockSpec((QB, width // count), lambda r: (r, 0))
-    return run(
-        partial(first_kernel, steps, count),
-        (*dqs, *dks, *dvs, *mats, seq, dmix, gain, ids_row),
-        [shaped((total, width)), shaped((8, width), F32)],
+    return run(
+        first_kernel,
+        (*grads, *mats, seq, dmix, gain, ids_row),
+        [shaped((total, width))],
         deps,
         (),
-        (steps,),
-        [part] * (3 * count)
+        (total // QB,),
+        [block] * 3
         + [whole((width, width))] * 3
         + [block] * 2
         + [whole((1, width)), whole((1, total))],
-        scratch=[pltpu.VMEM((total, width), BF)],
-        micros=12,
-        gates=gates,
-    )
+        [whole((total, width))],
+        [pltpu.VMEM((total, width), BF)],
+        micros=16,
+    )[0]
 
 
 def local(
@@ -944,7 +950,6 @@
     act, dx, sums_two = expert(
         x, cotangent, gains[2], gains[3], w_first, dact, deps=cot_line[-1]
     )
-    forward(cot_line)
     x_line = [(x,) * 2]
     forward(x_line)
     output = expert_out(x, act, w_second)
@@ -959,64 +964,40 @@
     dmix, dattn = back_in(ids_col, mat_o, back, deps=slice_sums)
     forward(x_line)
 
-    early = attend_back(flag, q, k, v, attn, dattn, lse, 0, 2)
-    send, keep = shared_grads(
-        meta,
-        [(attn, False), (ln_turned, True)],
-        [(0, dmix)] + [(1, g) for g in early],
-        [],
+    (first,) = shared_grads(attn, False, [dmix], n_exp, n_grp)
+    grads, cot_line[-1] = attend_back(
+        flag, q, k, v, attn, dattn, lse, 0, 1, deps=first, gates=cot_line[-1]
+    )
+    while len(cot_line) < n_grp:
+        forward(cot_line)
+    first = exchange(first)
+    (second,), x_line[-1] = shared_grads(
+        ln_turned,
+        True,
+        grads,
         n_exp,
         n_grp,
-    )
-    gates = x_line[2] if n_grp > 2 else dmix
-    rest, gates = attend_back(
-        flag, q, k, v, attn, dattn, lse, 1, 2, deps=send, gates=gates
-    )
-    if n_grp > 2:
-        x_line[2] = gates
-    for _ in range(3, n_grp):
-        forward(cot_line)
+        ((mat_q, mat_k, mat_v), gains[4], sums_two),
+        gates=x_line[-1],
+    )
+    while len(x_line) < n_grp:
         forward(x_line)
-    first = halve(keep, swap(send, 1), deps=rest)
-    dqs, dks, dvs = zip(early, rest)
-    dfirst, sums_one = first_back(
-        dqs, dks, dvs, (mat_q, mat_k, mat_v), seq, dmix, gains[0], ids_row, deps=first
-    )
-    (send, keep), dfirst = shared_grads(
-        meta,
-        [(ln_turned, True)],
-        [(0, g) for g in rest],
-        [sums_one, sums_two],
-        n_exp,
-        n_grp,
-        gates=dfirst,
-    )
-    grad_x = exchange(dfirst[0])
-    slice_sums = slices(1, slice_sums, send)
-    second = halve(keep, swap(send, 1), deps=slice_sums)
-
-    def over_chips(parts):
-        others = [swap(parts[r], 2 * r) for r in range(1, n_exp // 2)]
-        return total_of(parts[0], others)
-
-    first = over_chips(first)
-    for t in range(2, n_grp):
-        deps = (first, second, x_line[-1]) if t == 2 else ()
+    dfirst = first_back(
+        grads, (mat_q, mat_k, mat_v), seq, dmix, gains[0], ids_row, deps=(first, second)
+    )
+    second = exchange(second)
+    for t in range(1, n_grp):
+        deps = (dfirst,) if t == 1 else ()
         if t == n_grp - 1:
-            second = over_chips(second)
-            deps = second
+            deps = (deps, slice_sums, cot_line[-1])
+            parts, (dfirst,) = total_over(meta, first, second, deps, dfirst)
+            deps = parts
+            parts = [parts[0]] + [shift(a, n + 1) for n, a in enumerate(parts[1:])]
         slice_sums = slices(t, slice_sums, deps)
+    grad_x = exchange(dfirst)
     grad_w_in, grad_w_out = slice_sums
-
-    parts = []
-    for n in range(1, n_grp):
-        at = (grp + n) % n_grp
-        parts.append(
-            [shift(lax.dynamic_index_in_dim(a[1], at, 0, False), n) for a in (first, second)]
-        )
-    *shared, small = final(meta, (first[0], second[0]), parts)
-    small = [small[:, n] for n in (0, 1, 8, 9)]
-    grad_w_o, *grads = shared
+    grad_w_o, *grads = final(parts, width)
+    grads, small = grads[:3], [a[0] for a in grads[3:]]
 
     return (
         output,

time: 490 us -> 482 us (0.984)
  waiting for transfers between devices: 40.3 us -> 57.4 us
  starting transfers between devices: 86 us -> 75.6 us
  Pallas kernels: 295 us -> 285 us
    all_to_all x3 -> x5, waiting for transfers between devices: 0.01 us -> 15 us  [exchange(): return lax.all_to_all(rows, 'exp', split_axis=0, concat_axis=0, tiled=True)]
    ppermute x9 -> x6, starting transfers between devices: 28.8 us -> 17.7 us  [shift(): return lax.ppermute(a, 'grp', [(i, (i + k) % n_grp) for i in range(n_grp)])]
    pallas_call x24 -> x20, Pallas kernels: 295 us -> 285 us  [run(): pl.pallas_call(body, grid_spec=pltpu.PrefetchScalarGridSpec(num_scalar_pr...]
    all_to_all x3 -> x5, starting transfers between devices: 12.8 us -> 21.6 us  [exchange(): return lax.all_to_all(rows, 'exp', split_axis=0, concat_axis=0, tiled=True)]
    ppermute x17 -> x9, starting transfers between devices: 13.4 us -> 6.17 us  [swap(): return lax.ppermute(a, 'exp', [(i, i ^ k) for i in range(n_exp)])]
    unnamed x67 -> x65, local copies, waits for them, and re-layouts: 9.91 us -> 9.1 us
    ppermute x17 -> x9, waiting for transfers between devices: 20.6 us -> 20.6 us  [swap(): return lax.ppermute(a, 'exp', [(i, i ^ k) for i in range(n_exp)])]
  transfers between devices with their start and end apart: 42 -> 33, of which waited for: 9 -> 10; matrix products, arithmetic and copies ran while one was open for 1% -> 0% of each run, Pallas kernels for 58% -> 58%
where the time goes in v4:
time: 482 us; the launch traced here: 475 us
  Pallas kernels  285 us (59%)
  starting transfers between devices  75.6 us (16%)
  waiting for transfers between devices  57.4 us (12%)
  blocking collectives  30.9 us (6%)
  between operations  15.5 us (3%)
  local copies, waits for them, and re-layouts  10.5 us (2%)
    pallas_call x20, Pallas kernels, run(): pl.pallas_call(body, grid_spec=pltpu.PrefetchScalarGridSpec(num_scalar_pr...  285 us
    all_to_all x1, blocking collectives, exchange(): return lax.all_to_all(rows, 'exp', split_axis=0, concat_axis=0, tiled=True)  30.9 us
    ppermute x6, starting transfers between devices, line_step(): up = lax.ppermute(up, 'grp', [(i, i + 1) for i in range(t - 1, n_grp - 1)])  22.2 us
    all_to_all x5, starting transfers between devices, exchange(): return lax.all_to_all(rows, 'exp', split_axis=0, concat_axis=0, tiled=True)  21.6 us
    ppermute x9, waiting for transfers between devices, swap(): return lax.ppermute(a, 'exp', [(i, i ^ k) for i in range(n_exp)])  20.6 us
    ppermute x6, waiting for transfers between devices, line_step(): down = lax.ppermute(down, 'grp', [(i + 1, i) for i in range(n_grp - t)])  19.3 us
    ppermute x6, starting transfers between devices, shift(): return lax.ppermute(a, 'grp', [(i, (i + k) % n_grp) for i in range(n_grp)])  17.7 us
    all_to_all x5, waiting for transfers between devices, exchange(): return lax.all_to_all(rows, 'exp', split_axis=0, concat_axis=0, tiled=True)  15 us
  transfers between devices with their start and end apart: 33, of which 10 were waited for; matrix products, arithmetic and copies ran while one was open for 0% of the time, Pallas kernels for 58%

profile of v4, /device:TPU:0, one launch (start us, length us, event | category | flops | bytes accessed | tf_op | source)
XLA Modules:
  0.0 475.5 jit_solution(6070641899778526458)
XLA Ops:
  7.3 5.3 %all-to-all-start = ((bf16[8,128,1024]{2,1,0:T(8,128)(2,1)}), bf16[8,128,1024]{2,1,0:T(8,128)(2,1)S(1)}, u32[]{:S(2)}, u32[]{:S(2)}) async-start(bf16[8,128,1024]{2,1,0:T(8,128)(2,1)} %bitcast.39), calls=%async_computation | async-start | bytes 4194304 | tf_op jit(solution)/shard_map/all_to_all | solution.py:877
  13.2 1.6 collective-permute-start
  14.8 2.6 collective-permute-start.1
  18.7 14.3 %shard_map.229.refs_5_ = bf16[1024,4096]{1,0:T(8,128)(2,1)} custom-call(bf16[1024,1024]{1,0:T(8,128)(2,1)} %refs_2_.1, bf16[1024,4096]{1,0:T(8,128)(2,1)} %bitcast.30), custom_call_target="tpu_custom_call" | custom-call | flops 5687000064 | bytes 1000000 | tf_op jit(solution)/shard_map/pallas_call | solution.py:74
  33.6 5.6 %shard_map.230 = (bf16[1024,1024]{1,0:T(8,128)(2,1)}, bf16[1024,1024]{1,0:T(8,128)(2,1)}) custom-call(s32[2]{0:T(128)} %pad_add_fusion.refs_0_, bf16[1024,4096]{1,0:T(8,128)(2,1)} %bitcast.28, bf16[1024,4096]{1,0:T(8,128)(2,1)} %bitcast.31), custom_call_target="tpu_custom_call" | custom-call | flops 2584999936 | bytes 1000000 | tf_op jit(solution)/shard_map/pallas_call | solution.py:74
  40.9 2.3 shard_map.231
  43.2 2.2 collective-permute-start.4
  45.4 1.5 collective-permute-start.6
  46.9 6.3 %collective-permute-start.12 = (bf16[1024,1024]{1,0:T(8,128)(2,1)}, bf16[1024,1024]{1,0:T(8,128)(2,1)S(1)}, u32[]{:S(2)}, u32[]{:S(2)}) collective-permute-start(bf16[1024,1024]{1,0:T(8,128)(2,1)} %refs_2_.1), channel_id=1, source_target_pairs={{0,8},{8,16},{16,24},{1,9},{9,17},{17,25},{2,10},{10,18},{18,26},{... | collective-permute-start | bytes 6291464 | tf_op jit(solution)/shard_map/ppermute | solution.py:897
  54.5 10.7 %collective-permute-done.4.refs_5_.refs_13_.refs_21_ = bf16[4,80,1024]{2,1,0:T(8,128)(2,1)S(1)} collective-permute-done((bf16[4,80,1024]{2,1,0:T(8,128)(2,1)}, bf16[4,80,1024]{2,1,0:T(8,128)(2,1)S(1)}, u32[]{:S(2)}, u32[]{:S(2)}) %collective-permute-start.4) | collective-permute-done | bytes 655392 | tf_op jit(solution)/shard_map/ppermute | solution.py:871
  65.3 1.5 collective-permute-start.10
  66.7 1.6 collective-permute-done.6.refs_7_.refs_15_.refs_23_
  69.2 5.6 %collective-permute-done.8.refs_9_ = bf16[4,32,1024]{2,1,0:T(8,128)(2,1)S(1)} collective-permute-done((bf16[4,32,1024]{2,1,0:T(8,128)(2,1)S(1)}, bf16[4,32,1024]{2,1,0:T(8,128)(2,1)S(1)}, u32[]{:S(2)}, u32[]{:S(2)}) %collective-permute-start.8) | collective-permute-done | bytes 262176 | tf_op jit(solution)/shard_map/ppermute | solution.py:871
  75.6 1.7 collective-permute-done.9.refs_10_
  80.0 15.4 %shard_map.232 = (bf16[1024,1024]{1,0:T(8,128)(2,1)}, bf16[1024,1024]{1,0:T(8,128)(2,1)}, bf16[1024,1024]{1,0:T(8,128)(2,1)}, bf16[1024,1024]{1,0:T(8,128)(2,1)}...) custom-call(s32[2]{0:T(128)} %pad_add_fusion.refs_0_, ...), custom_call_target="tpu_custom_call" | custom-call | flops 7238000128 | bytes 1000000 | tf_op jit(solution)/shard_map/pallas_call | solution.py:74
  95.4 2.4 collective-permute-done.12.refs_3_
  97.8 4.2 collective-permute-done.13.refs_4_
  102.1 7.2 %shard_map.233 = (bf16[1024,1024]{1,0:T(8,128)(2,1)}, bf16[4,8,32,1024]{3,2,1,0:T(8,128)(2,1)}, bf16[1024,1024]{1,0:T(8,128)(2,1)}, bf16[1024,1024]{1,0:T(8,128)(2,1)}) custom-call(s32[2]{0:T(128)} %pad_add_fusion.refs_0_, bf16[1024,1024]{1,0:T(8,128)(2,1)} %get-tuple-element.75.refs_1_, ...), custom_call_target="tpu_custom_call", output_to_operand_aliasing={{2}: (3, {}), {3}: (4, {})} | custom-call | flops 2584999936 | bytes 1000000 | tf_op jit(solution)/shard_map/pallas_call | solution.py:74
  110.1 1.5 collective-permute-start.15
  111.6 21.2 %shard_map.234 = (bf16[1024,1024]{1,0:T(8,128)(2,1)}, f32[8,8,1024]{2,1,0:T(8,128)}) custom-call(s32[1]{0:T(128)S(6)} %copy.54.refs_0_, bf16[1024,1024]{1,0:T(8,128)(2,1)} %get-tuple-element.73.refs_1_, bf16[1024,1024]{1,0:T(8,128)(2,1)} %get-tuple-element.74.refs_2_, bf16[1024,1024]{1,0:T(8,128)(2,1)} %get-tuple-element.77.refs_3_), custom_call_target="tpu_custom_call" | custom-call | flops 11374000128 | bytes 1000000 | tf_op jit(solution)/shard_map/pallas_call | solution.py:74
  132.7 10.6 %shard_map.235 = (bf16[4,8,32,1024]{3,2,1,0:T(8,128)(2,1)}, bf16[1024,1024]{1,0:T(8,128)(2,1)}) custom-call(s32[2]{0:T(128)} %pad_add_fusion.refs_0_, bf16[1024,1024]{1,0:T(8,128)(2,1)} %get-tuple-element.78.refs_1_.refs_0_.refs_4_, bf16[1024,1024]{1,0:T(8,128)(2,1)} %get-tuple-element.79.refs_2_.refs_6_, s32[1,1024]{1,0:T(1,128)} %refs_9_.1, ...), custom_call_target="tpu_custom_call" | custom-call | flops 4136000000 | bytes 1000000 | tf_op jit(solution)/shard_map/pallas_call | solution.py:74
  143.3 30.9 %all_to_all.55 = bf16[8,128,1024]{2,1,0:T(8,128)(2,1)} all-to-all(bf16[8,128,1024]{2,1,0:T(8,128)(2,1)} %bitcast.42), channel_id=1, replica_groups=mesh['grp'=4,'exp'=8] {'exp'}, dimensions={0} | all-to-all | bytes 4194304 | tf_op jit(solution)/shard_map/all_to_all | solution.py:877
  174.2 10.4 %collective-permute-start.16 = (bf16[1024,1024]{1,0:T(8,128)(2,1)}, bf16[1024,1024]{1,0:T(8,128)(2,1)}, u32[]{:S(2)}, u32[]{:S(2)}) collective-permute-start(bf16[1024,1024]{1,0:T(8,128)(2,1)} %bitcast.13.refs_0_.refs_1_), channel_id=1, source_target_pairs={{0,8},{8,16},{16,24},{1,9},{9,17},{17,25},{2,10},{10,18},{18,26},{... | collective-permute-start | bytes 6291464 | tf_op jit(solution)/shard_map/ppermute | solution.py:897
  186.0 1.3 copy-done.20
  187.4 30.5 %shard_map.236 = (bf16[1024,4096]{1,0:T(8,128)(2,1)}, bf16[1024,1024]{1,0:T(8,128)(2,1)}, f32[8,1024]{1,0:T(8,128)}) custom-call(bf16[1024,1024]{1,0:T(8,128)(2,1)} %bitcast.13.refs_0_.refs_1_, bf16[1024,1024]{1,0:T(8,128)(2,1)} %refs_2_.1, f32[1,1024]{1,0:T(1,128)} %get-tuple-element.81.refs_2_.refs_3_.refs_5_, ...), custom_call_target="tpu_custom_call" | custom-call | flops 17578000384 | bytes 1000000 | tf_op jit(solution)/shard_map/pallas_call | solution.py:74
  217.9 3.6 all-to-all-start.2
  221.5 14.7 %shard_map.237.refs_7_ = bf16[1024,1024]{1,0:T(8,128)(2,1)} custom-call(bf16[1024,1024]{1,0:T(8,128)(2,1)} %bitcast.13.refs_0_.refs_1_, bf16[1024,4096]{1,0:T(8,128)(2,1)} %get-tuple-element.85.refs_1_, bf16[1024,4096]{1,0:T(8,128)(2,1)} %bitcast.32), custom_call_target="tpu_custom_call" | custom-call | flops 6204000256 | bytes 1000000 | tf_op jit(solution)/shard_map/pallas_call | solution.py:74
  236.2 17.4 %shard_map.238 = (f32[1024,1024]{1,0:T(8,128)}, f32[1024,1024]{1,0:T(8,128)}, bf16[1024,1024]{1,0:T(8,128)(2,1)}, bf16[1024,1024]{1,0:T(8,128)(2,1)}) custom-call(s32[2]{0:T(128)} %pad_add_fusion.refs_0_, bf16[1024,1024]{1,0:T(8,128)(2,1)} %bitcast.13.refs_0_.refs_1_, bf16[1024,1024]{1,0:T(8,128)(2,1)} %refs_2_.1, ...), custom_call_target="tpu_custom_call", output_to_operand_aliasing={{2}: (8, {}), {3}: (9, {})} | custom-call | flops 9306000384 | bytes 1000000 | tf_op jit(solution)/shard_map/pallas_call | solution.py:74
  253.7 2.0 collective-permute-start.18
  258.3 8.5 %shard_map.239 = (bf16[1024,1024]{1,0:T(8,128)(2,1)}, bf16[1024,1024]{1,0:T(8,128)(2,1)}) custom-call(s32[1024,1]{1,0:T(8,128)} %copy.37.refs_1_.refs_0_, bf16[1024,1024]{1,0:T(8,128)(2,1)} %bitcast.56, bf16[1024,1024]{1,0:T(8,128)(2,1)} %bitcast.40, f32[1024,1024]{1,0:T(8,128)} %get-tuple-element.89.refs_3_.refs_9_, ...), custom_call_target="tpu_custom_call" | custom-call | flops 3619000064 | bytes 1000000 | tf_op jit(solution)/shard_map/pallas_call | solution.py:74
  266.8 6.1 %shard_map.240.refs_7_ = bf16[8,4,32,1024]{3,2,1,0:T(8,128)(2,1)} custom-call(bf16[1024,1024]{1,0:T(8,128)(2,1)} %get-tuple-element.78.refs_1_.refs_0_.refs_4_, bf16[1024,1024]{1,0:T(8,128)(2,1)} %get-tuple-element.91.refs_1_.refs_7_), custom_call_target="tpu_custom_call" | custom-call | flops 2068000000 | bytes 1000000 | tf_op jit(solution)/shard_map/pallas_call | solution.py:74
  272.9 4.1 all-to-all-start.3
  277.0 32.8 %shard_map.241 = (bf16[1024,1024]{1,0:T(8,128)(2,1)}, bf16[1024,1024]{1,0:T(8,128)(2,1)}, bf16[1024,1024]{1,0:T(8,128)(2,1)}, bf16[1024,1024]{1,0:T(8,128)(2,1)}, bf16[1024,1024]{1,0:T(8,128)(2,1)}) custom-call(s32[1]{0:T(128)S(6)} %copy.54.refs_0_, bf16[1024,1024]{1,0:T(8,128)(2,1)} %get-tuple-element.73.refs_1_, ...), custom_call_target="tpu_custom_call", output_to_operand_aliasing={{3}: (8, {}), {4}: (9, {})} | custom-call | flops 9306000384 | bytes 1000000 | tf_op jit(solution)/shard_map/pallas_call | solution.py:74
  309.8 15.5 %shard_map.242 = (bf16[8,4,32,3200]{3,2,1,0:T(8,128)(2,1)}, bf16[1024,1024]{1,0:T(8,128)(2,1)}, bf16[1024,1024]{1,0:T(8,128)(2,1)}) custom-call(bf16[1024,1024]{1,0:T(8,128)(2,1)} %get-tuple-element.92.refs_0_, bf16[1024,1024]{1,0:T(8,128)(2,1)} %get-tuple-element.95.refs_1_.refs_0_, ...), custom_call_target="tpu_custom_call", output_to_operand_aliasing={{1}: (9, {}), {2}: (10, {})} | custom-call | flops 6204000256 | bytes 1000000 | tf_op jit(solution)/shard_map/pallas_call | solution.py:74
  326.7 4.8 %all-to-all-start.4 = ((bf16[8,4,32,3200]{3,2,1,0:T(8,128)(2,1)}), bf16[8,4,32,3200]{3,2,1,0:T(8,128)(2,1)}, u32[]{:S(2)}, u32[]{:S(2)}) async-start(bf16[8,4,32,3200]{3,2,1,0:T(8,128)(2,1)} %get-tuple-element.105.refs_11_), calls=%async_computation.4 | async-start | bytes 13107200 | tf_op jit(solution)/shard_map/all_to_all | solution.py:877
  333.6 2.0 collective-permute-start.25
  336.9 17.0 %shard_map.243.refs_11_.refs_7_ = bf16[1024,1024]{1,0:T(8,128)(2,1)} custom-call(bf16[1024,1024]{1,0:T(8,128)(2,1)} %get-tuple-element.95.refs_1_.refs_0_, bf16[1024,1024]{1,0:T(8,128)(2,1)} %get-tuple-element.96.refs_2_.refs_1_, bf16[1024,1024]{1,0:T(8,128)(2,1)} %get-tuple-element.97.refs_3_.refs_2_, bf16[1024,1024]{1,0:T(8,128)(2,1)} %bitcast.53, ...), custom_call_target="tpu_custom_call" | custom-call | flops 8272000000 | bytes 1000000 | tf_op jit(solution)/shard_map/pallas_call | solution.py:74
  353.9 18.4 %shard_map.244 = (f32[1024,1024]{1,0:T(8,128)}, f32[1024,1024]{1,0:T(8,128)}) custom-call(s32[2]{0:T(128)} %pad_add_fusion.refs_0_, bf16[1024,1024]{1,0:T(8,128)(2,1)} %get-tuple-element.103.refs_1_, bf16[1024,1024]{1,0:T(8,128)(2,1)} %get-tuple-element.104.refs_2_, bf16[1024,1024]{1,0:T(8,128)(2,1)} %get-tuple-element.83.refs_3_, ...), custom_call_target="tpu_custom_call" | custom-call | flops 9306000384 | bytes 1000000 | tf_op jit(solution)/shard_map/pallas_call | solution.py:74
  372.2 18.6 %shard_map.245 = (f32[1024,1024]{1,0:T(8,128)}, f32[1024,1024]{1,0:T(8,128)}) custom-call(s32[2]{0:T(128)} %pad_add_fusion.refs_0_, bf16[1024,1024]{1,0:T(8,128)(2,1)} %get-tuple-element.106.refs_1_, bf16[1024,1024]{1,0:T(8,128)(2,1)} %get-tuple-element.107.refs_2_, bf16[1024,1024]{1,0:T(8,128)(2,1)} %get-tuple-element.108.refs_3_, ...), custom_call_target="tpu_custom_call" | custom-call | flops 9306000384 | bytes 1000000 | tf_op jit(solution)/shard_map/pallas_call | solution.py:74
  390.9 15.0 %all-to-all-done.4.refs_2_ = bf16[8,4,32,3200]{3,2,1,0:T(8,128)(2,1)} async-done(((bf16[8,4,32,3200]{3,2,1,0:T(8,128)(2,1)}), bf16[8,4,32,3200]{3,2,1,0:T(8,128)(2,1)}, u32[]{:S(2)}, u32[]{:S(2)}) %all-to-all-start.4) | async-done | bytes 6553632 | tf_op jit(solution)/shard_map/all_to_all | solution.py:877
  405.9 6.4 %shard_map.246 = (f32[32,4224]{1,0:T(8,128)}, bf16[32,4224]{1,0:T(8,128)(2,1)}, bf16[32,4224]{1,0:T(8,128)(2,1)}, bf16[32,4224]{1,0:T(8,128)(2,1)}, bf16[1024,1024]{1,0:T(8,128)(2,1)}) custom-call(s32[2]{0:T(128)} %pad_add_fusion.refs_0_, bf16[8,4,32,1024]{3,2,1,0:T(8,128)(2,1)} %copy-done, ...), custom_call_target="tpu_custom_call", output_to_operand_aliasing={{4}: (7, {})} | custom-call | flops 2584999936 | bytes 1000000 | tf_op jit(solution)/shard_map/pallas_call | solution.py:74
  412.3 3.7 all-to-all-start.5
  416.1 6.7 %collective-permute-start.22 = (bf16[32,4224]{1,0:T(8,128)(2,1)S(1)}, bf16[32,4224]{1,0:T(8,128)(2,1)S(1)}, u32[]{:S(2)}, u32[]{:S(2)}) collective-permute-start(bf16[32,4224]{1,0:T(8,128)(2,1)S(1)} %copy-done.26), channel_id=1, source_target_pairs={{0,8},{8,16},{16,24},{24,0},{1,9},{9,17},{17,25},{25,1},{2,10},{10... | collective-permute-start | bytes 811016 | tf_op jit(solution)/shard_map/ppermute | solution.py:874
  422.7 2.6 collective-permute-start.23
  425.3 2.8 collective-permute-start.24
  428.2 15.1 %collective-permute-done.26.refs_2_ = bf16[1024,1024]{1,0:T(8,128)(2,1)} collective-permute-done((bf16[1024,1024]{1,0:T(8,128)(2,1)}, bf16[1024,1024]{1,0:T(8,128)(2,1)}, u32[]{:S(2)}, u32[]{:S(2)}) %collective-permute-start.26) | collective-permute-done | bytes 2097184 | tf_op jit(solution)/shard_map/ppermute | solution.py:898
  443.3 20.2 %shard_map.248 = (f32[1024,1024]{1,0:T(8,128)}, f32[1024,1024]{1,0:T(8,128)}) custom-call(s32[2]{0:T(128)} %pad_add_fusion.refs_0_, bf16[1024,1024]{1,0:T(8,128)(2,1)} %collective-permute-done.25.refs_1_, bf16[1024,1024]{1,0:T(8,128)(2,1)} %collective-permute-done.26.refs_2_, bf16[1024,1024]{1,0:T(8,128)(2,1)} %copy-done.2, ...), custom_call_target="tpu_custom_call" | custom-call | flops 9306000384 | bytes 1000000 | tf_op jit(solution)/shard_map/pallas_call | solution.py:74
  465.0 2.1 shard_map.247
  (113 shorter events, 21.3 us)
Async XLA Ops:
  7.2 5.4 %copy-start.16 = (bf16[32]{0:T(256)(128)(2,1)S(1)}, bf16[32]{0:T(256)(128)(2,1)}, u32[]{:S(2)}) copy-start(bf16[32]{0:T(256)(128)(2,1)} %param.25) | copy-start | bytes 196
  7.2 5.4 %copy-start.17 = (bf16[32]{0:T(256)(128)(2,1)S(1)}, bf16[32]{0:T(256)(128)(2,1)}, u32[]{:S(2)}) copy-start(bf16[32]{0:T(256)(128)(2,1)} %param.24) | copy-start | bytes 196
  7.2 5.4 %copy-start.18 = (bf16[32]{0:T(256)(128)(2,1)S(1)}, bf16[32]{0:T(256)(128)(2,1)}, u32[]{:S(2)}) copy-start(bf16[32]{0:T(256)(128)(2,1)} %param.23) | copy-start | bytes 196
  7.2 5.8 %copy-start.11 = (bf16[32,1024]{1,0:T(8,128)(2,1)S(1)}, bf16[32,1024]{1,0:T(8,128)(2,1)}, u32[]{:S(2)}) copy-start(bf16[32,1024]{1,0:T(8,128)(2,1)} %param.18) | copy-start | bytes 196612
  7.2 5.8 %copy-start.12 = (bf16[32,1024]{1,0:T(8,128)(2,1)S(1)}, bf16[32,1024]{1,0:T(8,128)(2,1)}, u32[]{:S(2)}) copy-start(bf16[32,1024]{1,0:T(8,128)(2,1)} %param.19) | copy-start | bytes 196612
  7.2 5.9 %copy-start.13 = (bf16[32,1024]{1,0:T(8,128)(2,1)S(1)}, bf16[32,1024]{1,0:T(8,128)(2,1)}, u32[]{:S(2)}) copy-start(bf16[32,1024]{1,0:T(8,128)(2,1)} %param.20) | copy-start | bytes 196612
  7.3 5.9 %copy-start.14 = (bf16[32,1024]{1,0:T(8,128)(2,1)S(1)}, bf16[32,1024]{1,0:T(8,128)(2,1)}, u32[]{:S(2)}) copy-start(bf16[32,1024]{1,0:T(8,128)(2,1)} %param.21) | copy-start | bytes 196612
  7.3 32.0 %all-to-all-start = ((bf16[8,128,1024]{2,1,0:T(8,128)(2,1)}), bf16[8,128,1024]{2,1,0:T(8,128)(2,1)S(1)}, u32[]{:S(2)}, u32[]{:S(2)}) async-start(bf16[8,128,1024]{2,1,0:T(8,128)(2,1)} %bitcast.39), calls=%async_computation | async-start | bytes 4194304 | tf_op jit(solution)/shard_map/all_to_all | solution.py:877
  12.6 89.5 %all-gather.3.cloned.1.call-start = ((), (), s32[]{:S(2)}) async-start(), calls=%async_computation.6 | async-start | bytes 4718592 | tf_op jit(solution)/shard_map/all_gather | solution.py:922
  13.1 19.9 %copy-start.5 = (bf16[144,1024]{1,0:T(8,128)(2,1)}, bf16[144,1024]{1,0:T(8,128)(2,1)S(1)}, u32[]{:S(2)}) copy-start(bf16[144,1024]{1,0:T(8,128)(2,1)S(1)} %constant_dynamic-update-slice_fusion.refs_0_) | copy-start | bytes 884740
  13.2 26.1 %collective-permute-start = (bf16[144,1024]{1,0:T(8,128)(2,1)S(1)}, bf16[144,1024]{1,0:T(8,128)(2,1)S(1)}, u32[]{:S(2)}, u32[]{:S(2)}) collective-permute-start(bf16[144,1024]{1,0:T(8,128)(2,1)S(1)} %constant_dynamic-update-slice_fusion.refs_0_), channel_id=1, source_target_pairs={{0,8},{8,16},{16,24},{24,0},{1,9},{9,17},{17,25},{25,1},{2,10},{10... | collective-permute-start | bytes 884744 | tf_op jit(solution)/shard_map/ppermute | solution.py:874
  14.8 24.5 %collective-permute-start.1 = (bf16[144,1024]{1,0:T(8,128)(2,1)S(1)}, bf16[144,1024]{1,0:T(8,128)(2,1)S(1)}, u32[]{:S(2)}, u32[]{:S(2)}) collective-permute-start(bf16[144,1024]{1,0:T(8,128)(2,1)S(1)} %constant_dynamic-update-slice_fusion.refs_0_), channel_id=1, source_target_pairs={{0,16},{8,24},{16,0},{24,8},{1,17},{9,25},{17,1},{25,9},{2,18},{10... | collective-permute-start | bytes 884744 | tf_op jit(solution)/shard_map/ppermute | solution.py:874
  17.4 21.9 %collective-permute-start.2 = (bf16[144,1024]{1,0:T(8,128)(2,1)S(1)}, bf16[144,1024]{1,0:T(8,128)(2,1)S(1)}, u32[]{:S(2)}, u32[]{:S(2)}) collective-permute-start(bf16[144,1024]{1,0:T(8,128)(2,1)S(1)} %constant_dynamic-update-slice_fusion.refs_0_), channel_id=1, source_target_pairs={{0,24},{8,0},{16,8},{24,16},{1,25},{9,1},{17,9},{25,17},{2,26},{10... | collective-permute-start | bytes 884744 | tf_op jit(solution)/shard_map/ppermute | solution.py:874
  40.9 37.3 %copy-start.15 = (s32[1,1024]{1,0:T(1,128)S(1)}, s32[1,1024]{1,0:T(1,128)}, u32[]{:S(2)}) copy-start(s32[1,1024]{1,0:T(1,128)} %refs_9_.1) | copy-start | bytes 12292
  43.2 22.0 %collective-permute-start.4 = (bf16[4,80,1024]{2,1,0:T(8,128)(2,1)}, bf16[4,80,1024]{2,1,0:T(8,128)(2,1)S(1)}, u32[]{:S(2)}, u32[]{:S(2)}) collective-permute-start(bf16[4,80,1024]{2,1,0:T(8,128)(2,1)} %get-tuple-element.72.refs_3_.refs_11_.refs_19_), channel_id=1, source_target_pairs={{0,2},{1,3},{2,0},{3,1},{4,6},{5,7},{6,4},{7,5},{8,10},{9,11},{10,... | collective-permute-start | bytes 1966088 | tf_op jit(solution)/shard_map/ppermute | solution.py:871
  45.4 22.9 %collective-permute-start.6 = (bf16[4,80,1024]{2,1,0:T(8,128)(2,1)}, bf16[4,80,1024]{2,1,0:T(8,128)(2,1)S(1)}, u32[]{:S(2)}, u32[]{:S(2)}) collective-permute-start(bf16[4,80,1024]{2,1,0:T(8,128)(2,1)} %get-tuple-element.72.refs_3_.refs_11_.refs_19_), channel_id=1, source_target_pairs={{0,4},{1,5},{2,6},{3,7},{4,0},{5,1},{6,2},{7,3},{8,12},{9,13},{10,... | collective-permute-start | bytes 1966088 | tf_op jit(solution)/shard_map/ppermute | solution.py:871
  46.9 50.9 %collective-permute-start.12 = (bf16[1024,1024]{1,0:T(8,128)(2,1)}, bf16[1024,1024]{1,0:T(8,128)(2,1)S(1)}, u32[]{:S(2)}, u32[]{:S(2)}) collective-permute-start(bf16[1024,1024]{1,0:T(8,128)(2,1)} %refs_2_.1), channel_id=1, source_target_pairs={{0,8},{8,16},{16,24},{1,9},{9,17},{17,25},{2,10},{10,18},{18,26},{... | collective-permute-start | bytes 6291464 | tf_op jit(solution)/shard_map/ppermute | solution.py:897
  53.2 48.9 %collective-permute-start.13 = (bf16[1024,1024]{1,0:T(8,128)(2,1)}, bf16[1024,1024]{1,0:T(8,128)(2,1)}, u32[]{:S(2)}, u32[]{:S(2)}) collective-permute-start(bf16[1024,1024]{1,0:T(8,128)(2,1)} %refs_2_.1), channel_id=1, source_target_pairs={{8,0},{16,8},{24,16},{9,1},{17,9},{25,17},{10,2},{18,10},{26,18},{... | collective-permute-start | bytes 6291464 | tf_op jit(solution)/shard_map/ppermute | solution.py:898
  54.5 14.8 %collective-permute-start.3 = (bf16[4,80,1024]{2,1,0:T(8,128)(2,1)}, bf16[4,80,1024]{2,1,0:T(8,128)(2,1)S(1)}, u32[]{:S(2)}, u32[]{:S(2)}) collective-permute-start(bf16[4,80,1024]{2,1,0:T(8,128)(2,1)} %get-tuple-element.72.refs_3_.refs_11_.refs_19_), channel_id=1, source_target_pairs={{0,1},{1,0},{2,3},{3,2},{4,5},{5,4},{6,7},{7,6},{8,9},{9,8},{10,11... | collective-permute-start | bytes 1966088 | tf_op jit(solution)/shard_map/ppermute | solution.py:871
  65.2 14.8 %copy-start.9 = (bf16[4,80,1024]{2,1,0:T(8,128)(2,1)}, bf16[4,80,1024]{2,1,0:T(8,128)(2,1)S(1)}, u32[]{:S(2)}) copy-start(bf16[4,80,1024]{2,1,0:T(8,128)(2,1)S(1)} %collective-permute-done.4.refs_5_.refs_13_.refs_21_) | copy-start | bytes 1966084
  65.3 10.3 %collective-permute-start.10 = (bf16[4,48,1024]{2,1,0:T(8,128)(2,1)S(1)}, bf16[4,48,1024]{2,1,0:T(8,128)(2,1)}, u32[]{:S(2)}, u32[]{:S(2)}) collective-permute-start(bf16[4,48,1024]{2,1,0:T(8,128)(2,1)S(1)} %slice.9), channel_id=1, source_target_pairs={{0,4},{1,5},{2,6},{3,7},{4,0},{5,1},{6,2},{7,3},{8,12},{9,13},{10,... | collective-permute-start | bytes 1179656 | tf_op jit(solution)/shard_map/ppermute | solution.py:871
  68.4 11.7 %copy-start.10 = (bf16[4,80,1024]{2,1,0:T(8,128)(2,1)}, bf16[4,80,1024]{2,1,0:T(8,128)(2,1)S(1)}, u32[]{:S(2)}) copy-start(bf16[4,80,1024]{2,1,0:T(8,128)(2,1)S(1)} %collective-permute-done.6.refs_7_.refs_15_.refs_23_) | copy-start | bytes 1966084
  68.4 6.4 %collective-permute-start.8 = (bf16[4,32,1024]{2,1,0:T(8,128)(2,1)S(1)}, bf16[4,32,1024]{2,1,0:T(8,128)(2,1)S(1)}, u32[]{:S(2)}, u32[]{:S(2)}) collective-permute-start(bf16[4,32,1024]{2,1,0:T(8,128)(2,1)S(1)} %slice.8), channel_id=1, source_target_pairs={{0,2},{1,3},{2,0},{3,1},{4,6},{5,7},{6,4},{7,5},{8,10},{9,11},{10,... | collective-permute-start | bytes 786440 | tf_op jit(solution)/shard_map/ppermute | solution.py:871
  69.2 6.4 %copy-start.21 = (bf16[4,80,1024]{2,1,0:T(8,128)(2,1)}, bf16[4,80,1024]{2,1,0:T(8,128)(2,1)S(1)}, u32[]{:S(2)}) copy-start(bf16[4,80,1024]{2,1,0:T(8,128)(2,1)S(1)} %collective-permute-done.3.refs_4_.refs_12_.refs_20_) | copy-start | bytes 1966084
  69.2 10.6 %collective-permute-start.5 = (bf16[4,80,1024]{2,1,0:T(8,128)(2,1)S(1)}, bf16[4,80,1024]{2,1,0:T(8,128)(2,1)}, u32[]{:S(2)}, u32[]{:S(2)}) collective-permute-start(bf16[4,80,1024]{2,1,0:T(8,128)(2,1)S(1)} %collective-permute-done.4.refs_5_.refs_13_.refs_21_), channel_id=1, source_target_pairs={{0,1},{1,0},{2,3},{3,2},{4,5},{5,4},{6,7},{7,6},{8,9},{9,8},{10,11... | collective-permute-start | bytes 1966088 | tf_op jit(solution)/shard_map/ppermute | solution.py:871
  74.8 5.0 %collective-permute-start.7 = (bf16[4,80,1024]{2,1,0:T(8,128)(2,1)S(1)}, bf16[4,80,1024]{2,1,0:T(8,128)(2,1)}, u32[]{:S(2)}, u32[]{:S(2)}) collective-permute-start(bf16[4,80,1024]{2,1,0:T(8,128)(2,1)S(1)} %collective-permute-done.6.refs_7_.refs_15_.refs_23_), channel_id=1, source_target_pairs={{0,1},{1,0},{2,3},{3,2},{4,5},{5,4},{6,7},{7,6},{8,9},{9,8},{10,11... | collective-permute-start | bytes 1966088 | tf_op jit(solution)/shard_map/ppermute | solution.py:871
  75.6 1.7 collective-permute-start.9
  78.0 2.1 collective-permute-start.11
  109.3 76.7 %collective-permute-start.14 = (bf16[1024,1024]{1,0:T(8,128)(2,1)}, bf16[1024,1024]{1,0:T(8,128)(2,1)S(1)}, u32[]{:S(2)}, u32[]{:S(2)}) collective-permute-start(bf16[1024,1024]{1,0:T(8,128)(2,1)} %get-tuple-element.83.refs_3_), channel_id=1, source_target_pairs={{8,16},{16,24},{9,17},{17,25},{10,18},{18,26},{11,19},{19,27},{12,... | collective-permute-start | bytes 6291464 | tf_op jit(solution)/shard_map/ppermute | solution.py:897
  110.1 75.9 %collective-permute-start.15 = (bf16[1024,1024]{1,0:T(8,128)(2,1)}, bf16[1024,1024]{1,0:T(8,128)(2,1)}, u32[]{:S(2)}, u32[]{:S(2)}) collective-permute-start(bf16[1024,1024]{1,0:T(8,128)(2,1)} %get-tuple-element.84.refs_4_), channel_id=1, source_target_pairs={{8,0},{16,8},{9,1},{17,9},{10,2},{18,10},{11,3},{19,11},{12,4},{20... | collective-permute-start | bytes 6291464 | tf_op jit(solution)/shard_map/ppermute | solution.py:898
  174.2 62.0 %collective-permute-start.16 = (bf16[1024,1024]{1,0:T(8,128)(2,1)}, bf16[1024,1024]{1,0:T(8,128)(2,1)}, u32[]{:S(2)}, u32[]{:S(2)}) collective-permute-start(bf16[1024,1024]{1,0:T(8,128)(2,1)} %bitcast.13.refs_0_.refs_1_), channel_id=1, source_target_pairs={{0,8},{8,16},{16,24},{1,9},{9,17},{17,25},{2,10},{10,18},{18,26},{... | collective-permute-start | bytes 6291464 | tf_op jit(solution)/shard_map/ppermute | solution.py:897
  184.7 51.6 %collective-permute-start.17 = (bf16[1024,1024]{1,0:T(8,128)(2,1)}, bf16[1024,1024]{1,0:T(8,128)(2,1)}, u32[]{:S(2)}, u32[]{:S(2)}) collective-permute-start(bf16[1024,1024]{1,0:T(8,128)(2,1)} %bitcast.13.refs_0_.refs_1_), channel_id=1, source_target_pairs={{8,0},{16,8},{24,16},{9,1},{17,9},{25,17},{10,2},{18,10},{26,18},{... | collective-permute-start | bytes 6291464 | tf_op jit(solution)/shard_map/ppermute | solution.py:898
  217.9 39.1 %all-to-all-start.2 = ((bf16[8,128,1024]{2,1,0:T(8,128)(2,1)}), bf16[8,128,1024]{2,1,0:T(8,128)(2,1)S(1)}, u32[]{:S(2)}, u32[]{:S(2)}) async-start(bf16[8,128,1024]{2,1,0:T(8,128)(2,1)} %bitcast.41), calls=%async_computation.2 | async-start | bytes 4194304 | tf_op jit(solution)/shard_map/all_to_all | solution.py:877
  253.7 56.1 %collective-permute-start.18 = (bf16[1024,1024]{1,0:T(8,128)(2,1)}, bf16[1024,1024]{1,0:T(8,128)(2,1)}, u32[]{:S(2)}, u32[]{:S(2)}) collective-permute-start(bf16[1024,1024]{1,0:T(8,128)(2,1)} %get-tuple-element.103.refs_1_), channel_id=1, source_target_pairs={{8,16},{16,24},{9,17},{17,25},{10,18},{18,26},{11,19},{19,27},{12,... | collective-permute-start | bytes 6291464 | tf_op jit(solution)/shard_map/ppermute | solution.py:897
  255.7 54.1 %collective-permute-start.19 = (bf16[1024,1024]{1,0:T(8,128)(2,1)}, bf16[1024,1024]{1,0:T(8,128)(2,1)}, u32[]{:S(2)}, u32[]{:S(2)}) collective-permute-start(bf16[1024,1024]{1,0:T(8,128)(2,1)} %get-tuple-element.104.refs_2_), channel_id=1, source_target_pairs={{8,0},{16,8},{9,1},{17,9},{10,2},{18,10},{11,3},{19,11},{12,4},{20... | collective-permute-start | bytes 6291464 | tf_op jit(solution)/shard_map/ppermute | solution.py:898
  272.9 52.5 %all-to-all-start.3 = ((bf16[8,4,32,1024]{3,2,1,0:T(8,128)(2,1)}), bf16[8,4,32,1024]{3,2,1,0:T(8,128)(2,1)S(1)}, u32[]{:S(2)}, u32[]{:S(2)}) async-start(bf16[8,4,32,1024]{3,2,1,0:T(8,128)(2,1)} %shard_map.240.refs_7_), calls=%async_computation.3 | async-start | bytes 4194304 | tf_op jit(solution)/shard_map/all_to_all | solution.py:877
  326.7 79.2 %all-to-all-start.4 = ((bf16[8,4,32,3200]{3,2,1,0:T(8,128)(2,1)}), bf16[8,4,32,3200]{3,2,1,0:T(8,128)(2,1)}, u32[]{:S(2)}, u32[]{:S(2)}) async-start(bf16[8,4,32,3200]{3,2,1,0:T(8,128)(2,1)} %get-tuple-element.105.refs_11_), calls=%async_computation.4 | async-start | bytes 13107200 | tf_op jit(solution)/shard_map/all_to_all | solution.py:877
  331.5 59.4 %collective-permute-start.20 = (bf16[1024,1024]{1,0:T(8,128)(2,1)}, bf16[1024,1024]{1,0:T(8,128)(2,1)S(1)}, u32[]{:S(2)}, u32[]{:S(2)}) collective-permute-start(bf16[1024,1024]{1,0:T(8,128)(2,1)} %get-tuple-element.108.refs_3_), channel_id=1, source_target_pairs={{16,24},{17,25},{18,26},{19,27},{20,28},{21,29},{22,30},{23,31}} | collective-permute-start | bytes 6291464 | tf_op jit(solution)/shard_map/ppermute | solution.py:897
  332.3 58.6 %collective-permute-start.21 = (bf16[1024,1024]{1,0:T(8,128)(2,1)}, bf16[1024,1024]{1,0:T(8,128)(2,1)}, u32[]{:S(2)}, u32[]{:S(2)}) collective-permute-start(bf16[1024,1024]{1,0:T(8,128)(2,1)} %get-tuple-element.109.refs_4_), channel_id=1, source_target_pairs={{8,0},{9,1},{10,2},{11,3},{12,4},{13,5},{14,6},{15,7}} | collective-permute-start | bytes 6291464 | tf_op jit(solution)/shard_map/ppermute | solution.py:898
  333.6 94.6 %collective-permute-start.25 = (bf16[1024,1024]{1,0:T(8,128)(2,1)}, bf16[1024,1024]{1,0:T(8,128)(2,1)}, u32[]{:S(2)}, u32[]{:S(2)}) collective-permute-start(bf16[1024,1024]{1,0:T(8,128)(2,1)} %get-tuple-element.106.refs_1_), channel_id=1, source_target_pairs={{16,24},{17,25},{18,26},{19,27},{20,28},{21,29},{22,30},{23,31}} | collective-permute-start | bytes 6291464 | tf_op jit(solution)/shard_map/ppermute | solution.py:897
  335.6 107.7 %collective-permute-start.26 = (bf16[1024,1024]{1,0:T(8,128)(2,1)}, bf16[1024,1024]{1,0:T(8,128)(2,1)}, u32[]{:S(2)}, u32[]{:S(2)}) collective-permute-start(bf16[1024,1024]{1,0:T(8,128)(2,1)} %get-tuple-element.107.refs_2_), channel_id=1, source_target_pairs={{8,0},{9,1},{10,2},{11,3},{12,4},{13,5},{14,6},{15,7}} | collective-permute-start | bytes 6291464 | tf_op jit(solution)/shard_map/ppermute | solution.py:898
  390.9 15.0 %copy-start.2 = (bf16[1024,1024]{1,0:T(8,128)(2,1)}, bf16[1024,1024]{1,0:T(8,128)(2,1)S(1)}, u32[]{:S(2)}) copy-start(bf16[1024,1024]{1,0:T(8,128)(2,1)S(1)} %collective-permute-done.20.refs_5_.refs_3_) | copy-start | bytes 6291460
  412.3 10.4 %copy-start.24 = (bf16[32,4224]{1,0:T(8,128)(2,1)S(1)}, bf16[32,4224]{1,0:T(8,128)(2,1)}, u32[]{:S(2)}) copy-start(bf16[32,4224]{1,0:T(8,128)(2,1)} %get-tuple-element.118.refs_13_) | copy-start | bytes 811012
  412.3 13.0 %copy-start.22 = (bf16[32,4224]{1,0:T(8,128)(2,1)S(1)}, bf16[32,4224]{1,0:T(8,128)(2,1)}, u32[]{:S(2)}) copy-start(bf16[32,4224]{1,0:T(8,128)(2,1)} %get-tuple-element.119.refs_14_) | copy-start | bytes 811012
  412.3 54.8 %all-to-all-start.5 = ((bf16[8,128,1024]{2,1,0:T(8,128)(2,1)}), bf16[8,128,1024]{2,1,0:T(8,128)(2,1)S(1)}, u32[]{:S(2)}, u32[]{:S(2)}) async-start(bf16[8,128,1024]{2,1,0:T(8,128)(2,1)} %bitcast.33), calls=%async_computation.5 | async-start | bytes 4194304 | tf_op jit(solution)/shard_map/all_to_all | solution.py:877
  416.1 47.4 %collective-permute-start.22 = (bf16[32,4224]{1,0:T(8,128)(2,1)S(1)}, bf16[32,4224]{1,0:T(8,128)(2,1)S(1)}, u32[]{:S(2)}, u32[]{:S(2)}) collective-permute-start(bf16[32,4224]{1,0:T(8,128)(2,1)S(1)} %copy-done.26), channel_id=1, source_target_pairs={{0,8},{8,16},{16,24},{24,0},{1,9},{9,17},{17,25},{25,1},{2,10},{10... | collective-permute-start | bytes 811016 | tf_op jit(solution)/shard_map/ppermute | solution.py:874
  422.7 40.8 %collective-permute-start.23 = (bf16[32,4224]{1,0:T(8,128)(2,1)S(1)}, bf16[32,4224]{1,0:T(8,128)(2,1)S(1)}, u32[]{:S(2)}, u32[]{:S(2)}) collective-permute-start(bf16[32,4224]{1,0:T(8,128)(2,1)S(1)} %copy-done.24), channel_id=1, source_target_pairs={{0,16},{8,24},{16,0},{24,8},{1,17},{9,25},{17,1},{25,9},{2,18},{10... | collective-permute-start | bytes 811016 | tf_op jit(solution)/shard_map/ppermute | solution.py:874
  425.3 38.2 %collective-permute-start.24 = (bf16[32,4224]{1,0:T(8,128)(2,1)S(1)}, bf16[32,4224]{1,0:T(8,128)(2,1)S(1)}, u32[]{:S(2)}, u32[]{:S(2)}) collective-permute-start(bf16[32,4224]{1,0:T(8,128)(2,1)S(1)} %copy-done.22), channel_id=1, source_target_pairs={{0,24},{8,0},{16,8},{24,16},{1,25},{9,1},{17,9},{25,17},{2,26},{10... | collective-permute-start | bytes 811016 | tf_op jit(solution)/shard_map/ppermute | solution.py:874
  (15 other events, 25.1 us)
Sparse Core Ops, SparseCore 0:
  43.3 45.3 all-gather.2

commit v5 on v4

--- a/solution.py
+++ b/solution.py
@@ -838,7 +838,7 @@
         + [whole((1, width)), whole((1, total))],
         [whole((total, width))],
         [pltpu.VMEM((total, width), BF)],
-        micros=16,
+        micros=1,
     )[0]
 
 
@@ -964,12 +964,12 @@
     dmix, dattn = back_in(ids_col, mat_o, back, deps=slice_sums)
     forward(x_line)
 
-    (first,) = shared_grads(attn, False, [dmix], n_exp, n_grp)
-    grads, cot_line[-1] = attend_back(
-        flag, q, k, v, attn, dattn, lse, 0, 1, deps=first, gates=cot_line[-1]
+    (first,), cot_line[-1] = shared_grads(
+        attn, False, [dmix], n_exp, n_grp, gates=cot_line[-1]
     )
     while len(cot_line) < n_grp:
         forward(cot_line)
+    grads = attend_back(flag, q, k, v, attn, dattn, lse, 0, 1, deps=first)
     first = exchange(first)
     (second,), x_line[-1] = shared_grads(
         ln_turned,
@@ -987,9 +987,9 @@
     )
     second = exchange(second)
     for t in range(1, n_grp):
-        deps = (dfirst,) if t == 1 else ()
+        deps = (dfirst, cot_line[-1]) if t == 1 else ()
         if t == n_grp - 1:
-            deps = (deps, slice_sums, cot_line[-1])
+            deps = (deps, slice_sums)
             parts, (dfirst,) = total_over(meta, first, second, deps, dfirst)
             deps = parts
             parts = [parts[0]] + [shift(a, n + 1) for n, a in enumerate(parts[1:])]

time: 482 us -> 490 us (1.017)
  Pallas kernels: 285 us -> 258 us
  waiting for transfers between devices: 57.4 us -> 76.5 us
  blocking collectives: 30.9 us -> 38.9 us
  starting transfers between devices: 75.6 us -> 83.5 us
    ppermute x6, waiting for transfers between devices: 19.3 us -> 53.4 us  [line_step(): down = lax.ppermute(down, 'grp', [(i + 1, i) for i in range(n_grp - t)])]
    pallas_call x20, Pallas kernels: 285 us -> 258 us  [run(): pl.pallas_call(body, grid_spec=pltpu.PrefetchScalarGridSpec(num_scalar_pr...]
    all_to_all x5, waiting for transfers between devices: 15 us -> 0.01 us  [exchange(): return lax.all_to_all(rows, 'exp', split_axis=0, concat_axis=0, tiled=True)]
    all_to_all x1, blocking collectives: 30.9 us -> 38.9 us  [exchange(): return lax.all_to_all(rows, 'exp', split_axis=0, concat_axis=0, tiled=True)]
  transfers between devices with their start and end apart: 33 -> 33, of which waited for: 10 -> 10; matrix products, arithmetic and copies ran while one was open for 0% -> 0% of each run, Pallas kernels for 58% -> 51%
where the time goes in v5:
time: 490 us; the launch traced here: 484 us
  Pallas kernels  258 us (53%)
  starting transfers between devices  83.5 us (17%)
  waiting for transfers between devices  76.5 us (16%)
  blocking collectives  38.9 us (8%)
  between operations  15.5 us (3%)
  local copies, waits for them, and re-layouts  10.6 us (2%)
    pallas_call x20, Pallas kernels, run(): pl.pallas_call(body, grid_spec=pltpu.PrefetchScalarGridSpec(num_scalar_pr...  258 us
    ppermute x6, waiting for transfers between devices, line_step(): down = lax.ppermute(down, 'grp', [(i + 1, i) for i in range(n_grp - t)])  53.4 us
    all_to_all x1, blocking collectives, exchange(): return lax.all_to_all(rows, 'exp', split_axis=0, concat_axis=0, tiled=True)  38.9 us
    ppermute x6, starting transfers between devices, line_step(): up = lax.ppermute(up, 'grp', [(i, i + 1) for i in range(t - 1, n_grp - 1)])  24.6 us
    all_to_all x5, starting transfers between devices, exchange(): return lax.all_to_all(rows, 'exp', split_axis=0, concat_axis=0, tiled=True)  22.7 us
    ppermute x6, starting transfers between devices, shift(): return lax.ppermute(a, 'grp', [(i, (i + k) % n_grp) for i in range(n_grp)])  22.2 us
    ppermute x9, waiting for transfers between devices, swap(): return lax.ppermute(a, 'exp', [(i, i ^ k) for i in range(n_exp)])  20.6 us
  transfers between devices with their start and end apart: 33, of which 10 were waited for; matrix products, arithmetic and copies ran while one was open for 0% of the time, Pallas kernels for 51%

profile of v5, /device:TPU:0, one launch (start us, length us, event | category | flops | bytes accessed | tf_op | source)
XLA Modules:
  0.0 483.7 jit_solution(12599027609245105918)
XLA Ops:
  7.3 5.3 %all-to-all-start = ((bf16[8,128,1024]{2,1,0:T(8,128)(2,1)}), bf16[8,128,1024]{2,1,0:T(8,128)(2,1)S(1)}, u32[]{:S(2)}, u32[]{:S(2)}) async-start(bf16[8,128,1024]{2,1,0:T(8,128)(2,1)} %bitcast.45), calls=%async_computation | async-start | bytes 4194304 | tf_op jit(solution)/shard_map/all_to_all | solution.py:877
  13.2 1.6 collective-permute-start
  14.8 2.6 collective-permute-start.1
  18.7 14.2 %shard_map.229.refs_5_ = bf16[1024,4096]{1,0:T(8,128)(2,1)} custom-call(bf16[1024,1024]{1,0:T(8,128)(2,1)} %refs_2_.1, bf16[1024,4096]{1,0:T(8,128)(2,1)} %bitcast.31), custom_call_target="tpu_custom_call" | custom-call | flops 5687000064 | bytes 1000000 | tf_op jit(solution)/shard_map/pallas_call | solution.py:74
  33.6 5.6 %shard_map.230 = (bf16[1024,1024]{1,0:T(8,128)(2,1)}, bf16[1024,1024]{1,0:T(8,128)(2,1)}) custom-call(s32[2]{0:T(128)} %pad_add_fusion.refs_0_, bf16[1024,4096]{1,0:T(8,128)(2,1)} %bitcast.29, bf16[1024,4096]{1,0:T(8,128)(2,1)} %bitcast.32), custom_call_target="tpu_custom_call" | custom-call | flops 2584999936 | bytes 1000000 | tf_op jit(solution)/shard_map/pallas_call | solution.py:74
  40.8 2.3 shard_map.231
  43.2 2.2 collective-permute-start.4
  45.4 1.5 collective-permute-start.6
  46.8 6.3 %collective-permute-start.12 = (bf16[1024,1024]{1,0:T(8,128)(2,1)}, bf16[1024,1024]{1,0:T(8,128)(2,1)S(1)}, u32[]{:S(2)}, u32[]{:S(2)}) collective-permute-start(bf16[1024,1024]{1,0:T(8,128)(2,1)} %refs_2_.1), channel_id=1, source_target_pairs={{0,8},{8,16},{16,24},{1,9},{9,17},{17,25},{2,10},{10,18},{18,26},{... | collective-permute-start | bytes 6291464 | tf_op jit(solution)/shard_map/ppermute | solution.py:897
  54.5 10.7 %collective-permute-done.4.refs_5_.refs_13_.refs_21_ = bf16[4,80,1024]{2,1,0:T(8,128)(2,1)S(1)} collective-permute-done((bf16[4,80,1024]{2,1,0:T(8,128)(2,1)}, bf16[4,80,1024]{2,1,0:T(8,128)(2,1)S(1)}, u32[]{:S(2)}, u32[]{:S(2)}) %collective-permute-start.4) | collective-permute-done | bytes 655392 | tf_op jit(solution)/shard_map/ppermute | solution.py:871
  65.2 1.4 collective-permute-start.10
  66.6 1.7 collective-permute-done.6.refs_7_.refs_15_.refs_23_
  69.1 5.6 %collective-permute-done.8.refs_9_ = bf16[4,32,1024]{2,1,0:T(8,128)(2,1)S(1)} collective-permute-done((bf16[4,32,1024]{2,1,0:T(8,128)(2,1)S(1)}, bf16[4,32,1024]{2,1,0:T(8,128)(2,1)S(1)}, u32[]{:S(2)}, u32[]{:S(2)}) %collective-permute-start.8) | collective-permute-done | bytes 262176 | tf_op jit(solution)/shard_map/ppermute | solution.py:871
  75.5 1.7 collective-permute-done.9.refs_10_
  80.0 15.4 %shard_map.232 = (bf16[1024,1024]{1,0:T(8,128)(2,1)}, bf16[1024,1024]{1,0:T(8,128)(2,1)}, bf16[1024,1024]{1,0:T(8,128)(2,1)}, bf16[1024,1024]{1,0:T(8,128)(2,1)}...) custom-call(s32[2]{0:T(128)} %pad_add_fusion.refs_0_, ...), custom_call_target="tpu_custom_call" | custom-call | flops 7238000128 | bytes 1000000 | tf_op jit(solution)/shard_map/pallas_call | solution.py:74
  95.4 2.4 collective-permute-done.12.refs_3_
  97.8 4.2 collective-permute-done.13.refs_4_
  102.1 7.2 %shard_map.233 = (bf16[1024,1024]{1,0:T(8,128)(2,1)}, bf16[4,8,32,1024]{3,2,1,0:T(8,128)(2,1)}, bf16[1024,1024]{1,0:T(8,128)(2,1)}, bf16[1024,1024]{1,0:T(8,128)(2,1)}) custom-call(s32[2]{0:T(128)} %pad_add_fusion.refs_0_, bf16[1024,1024]{1,0:T(8,128)(2,1)} %get-tuple-element.76.refs_1_, ...), custom_call_target="tpu_custom_call", output_to_operand_aliasing={{2}: (3, {}), {3}: (4, {})} | custom-call | flops 2584999936 | bytes 1000000 | tf_op jit(solution)/shard_map/pallas_call | solution.py:74
  110.1 1.5 collective-permute-start.15
  111.5 10.9 %shard_map.234 = (bf16[1024,1024]{1,0:T(8,128)(2,1)}, f32[8,8,1024]{2,1,0:T(8,128)}) custom-call(s32[1]{0:T(128)S(6)} %copy.54.refs_0_, bf16[1024,1024]{1,0:T(8,128)(2,1)} %get-tuple-element.74.refs_1_, bf16[1024,1024]{1,0:T(8,128)(2,1)} %get-tuple-element.75.refs_2_, bf16[1024,1024]{1,0:T(8,128)(2,1)} %get-tuple-element.78.refs_3_), custom_call_target="tpu_custom_call" | custom-call | flops 11374000128 | bytes 1000000 | tf_op jit(solution)/shard_map/pallas_call | solution.py:74
  122.4 10.6 %shard_map.235 = (bf16[4,8,32,1024]{3,2,1,0:T(8,128)(2,1)}, bf16[1024,1024]{1,0:T(8,128)(2,1)}) custom-call(s32[2]{0:T(128)} %pad_add_fusion.refs_0_, bf16[1024,1024]{1,0:T(8,128)(2,1)} %get-tuple-element.79.refs_1_.refs_0_.refs_4_, bf16[1024,1024]{1,0:T(8,128)(2,1)} %get-tuple-element.80.refs_2_.refs_6_, s32[1,1024]{1,0:T(1,128)} %refs_9_.1, ...), custom_call_target="tpu_custom_call" | custom-call | flops 4136000000 | bytes 1000000 | tf_op jit(solution)/shard_map/pallas_call | solution.py:74
  133.0 38.9 %all_to_all.55 = bf16[8,128,1024]{2,1,0:T(8,128)(2,1)} all-to-all(bf16[8,128,1024]{2,1,0:T(8,128)(2,1)} %bitcast.48), channel_id=1, replica_groups=mesh['grp'=4,'exp'=8] {'exp'}, dimensions={0} | all-to-all | bytes 4194304 | tf_op jit(solution)/shard_map/all_to_all | solution.py:877
  171.9 12.7 %collective-permute-start.16 = (bf16[1024,1024]{1,0:T(8,128)(2,1)}, bf16[1024,1024]{1,0:T(8,128)(2,1)}, u32[]{:S(2)}, u32[]{:S(2)}) collective-permute-start(bf16[1024,1024]{1,0:T(8,128)(2,1)} %bitcast.13.refs_0_.refs_1_), channel_id=1, source_target_pairs={{0,8},{8,16},{16,24},{1,9},{9,17},{17,25},{2,10},{10,18},{18,26},{... | collective-permute-start | bytes 6291464 | tf_op jit(solution)/shard_map/ppermute | solution.py:897
  187.3 30.5 %shard_map.236 = (bf16[1024,4096]{1,0:T(8,128)(2,1)}, bf16[1024,1024]{1,0:T(8,128)(2,1)}, f32[8,1024]{1,0:T(8,128)}) custom-call(bf16[1024,1024]{1,0:T(8,128)(2,1)} %bitcast.13.refs_0_.refs_1_, bf16[1024,1024]{1,0:T(8,128)(2,1)} %refs_2_.1, f32[1,1024]{1,0:T(1,128)} %get-tuple-element.82.refs_2_.refs_3_.refs_5_, ...), custom_call_target="tpu_custom_call" | custom-call | flops 17578000384 | bytes 1000000 | tf_op jit(solution)/shard_map/pallas_call | solution.py:74
  217.8 3.6 all-to-all-start.2
  221.4 14.7 %shard_map.237.refs_7_ = bf16[1024,1024]{1,0:T(8,128)(2,1)} custom-call(bf16[1024,1024]{1,0:T(8,128)(2,1)} %bitcast.13.refs_0_.refs_1_, bf16[1024,4096]{1,0:T(8,128)(2,1)} %get-tuple-element.86.refs_1_, bf16[1024,4096]{1,0:T(8,128)(2,1)} %bitcast.33), custom_call_target="tpu_custom_call" | custom-call | flops 6204000256 | bytes 1000000 | tf_op jit(solution)/shard_map/pallas_call | solution.py:74
  236.2 17.4 %shard_map.238 = (f32[1024,1024]{1,0:T(8,128)}, f32[1024,1024]{1,0:T(8,128)}, bf16[1024,1024]{1,0:T(8,128)(2,1)}, bf16[1024,1024]{1,0:T(8,128)(2,1)}) custom-call(s32[2]{0:T(128)} %pad_add_fusion.refs_0_, bf16[1024,1024]{1,0:T(8,128)(2,1)} %bitcast.13.refs_0_.refs_1_, bf16[1024,1024]{1,0:T(8,128)(2,1)} %refs_2_.1, ...), custom_call_target="tpu_custom_call", output_to_operand_aliasing={{2}: (8, {}), {3}: (9, {})} | custom-call | flops 9306000384 | bytes 1000000 | tf_op jit(solution)/shard_map/pallas_call | solution.py:74
  253.6 2.0 collective-permute-start.18
  258.2 8.5 %shard_map.239 = (bf16[1024,1024]{1,0:T(8,128)(2,1)}, bf16[1024,1024]{1,0:T(8,128)(2,1)}) custom-call(s32[1024,1]{1,0:T(8,128)} %copy.37.refs_1_.refs_0_, bf16[1024,1024]{1,0:T(8,128)(2,1)} %bitcast.56, bf16[1024,1024]{1,0:T(8,128)(2,1)} %bitcast.46, f32[1024,1024]{1,0:T(8,128)} %get-tuple-element.90.refs_3_.refs_9_, ...), custom_call_target="tpu_custom_call" | custom-call | flops 3619000064 | bytes 1000000 | tf_op jit(solution)/shard_map/pallas_call | solution.py:74
  266.7 6.2 %shard_map.240 = (bf16[8,4,32,1024]{3,2,1,0:T(8,128)(2,1)}, bf16[1024,1024]{1,0:T(8,128)(2,1)}, bf16[1024,1024]{1,0:T(8,128)(2,1)}) custom-call(bf16[1024,1024]{1,0:T(8,128)(2,1)} %get-tuple-element.79.refs_1_.refs_0_.refs_4_, bf16[1024,1024]{1,0:T(8,128)(2,1)} %get-tuple-element.92.refs_1_.refs_7_, ...), custom_call_target="tpu_custom_call", output_to_operand_aliasing={{1}: (2, {}), {2}: (3, {})} | custom-call | flops 2068000000 | bytes 1000000 | tf_op jit(solution)/shard_map/pallas_call | solution.py:74
  272.9 4.1 all-to-all-start.3
  277.0 16.2 %shard_map.241 = (bf16[1024,1024]{1,0:T(8,128)(2,1)}, bf16[1024,1024]{1,0:T(8,128)(2,1)}, bf16[1024,1024]{1,0:T(8,128)(2,1)}) custom-call(s32[1]{0:T(128)S(6)} %copy.54.refs_0_, bf16[1024,1024]{1,0:T(8,128)(2,1)} %get-tuple-element.74.refs_1_, bf16[1024,1024]{1,0:T(8,128)(2,1)} %get-tuple-element.75.refs_2_, bf16[1024,1024]{1,0:T(8,128)(2,1)} %get-tuple-element.78.refs_3_, ...), custom_call_target="tpu_custom_call" | custom-call | flops 9306000384 | bytes 1000000 | tf_op jit(solution)/shard_map/pallas_call | solution.py:74
  293.2 16.4 %collective-permute-done.19.refs_10_ = bf16[1024,1024]{1,0:T(8,128)(2,1)} collective-permute-done((bf16[1024,1024]{1,0:T(8,128)(2,1)}, bf16[1024,1024]{1,0:T(8,128)(2,1)}, u32[]{:S(2)}, u32[]{:S(2)}) %collective-permute-start.19) | collective-permute-done | bytes 2097184 | tf_op jit(solution)/shard_map/ppermute | solution.py:898
  309.7 15.5 %shard_map.242 = (bf16[8,4,32,3200]{3,2,1,0:T(8,128)(2,1)}, bf16[1024,1024]{1,0:T(8,128)(2,1)}, bf16[1024,1024]{1,0:T(8,128)(2,1)}) custom-call(bf16[1024,1024]{1,0:T(8,128)(2,1)} %get-tuple-element.94.refs_0_, bf16[1024,1024]{1,0:T(8,128)(2,1)} %get-tuple-element.97.refs_1_.refs_0_, ...), custom_call_target="tpu_custom_call", output_to_operand_aliasing={{1}: (9, {}), {2}: (10, {})} | custom-call | flops 6204000256 | bytes 1000000 | tf_op jit(solution)/shard_map/pallas_call | solution.py:74
  325.2 1.4 copy-done
  326.6 4.8 all-to-all-start.4
  333.5 2.0 collective-permute-start.25
  336.7 17.0 %shard_map.243.refs_11_.refs_5_ = bf16[1024,1024]{1,0:T(8,128)(2,1)} custom-call(bf16[1024,1024]{1,0:T(8,128)(2,1)} %get-tuple-element.97.refs_1_.refs_0_, bf16[1024,1024]{1,0:T(8,128)(2,1)} %get-tuple-element.98.refs_2_.refs_1_, bf16[1024,1024]{1,0:T(8,128)(2,1)} %get-tuple-element.99.refs_3_.refs_2_, bf16[1024,1024]{1,0:T(8,128)(2,1)} %bitcast.40, ...), custom_call_target="tpu_custom_call" | custom-call | flops 517000000 | bytes 1000000 | tf_op jit(solution)/shard_map/pallas_call | solution.py:74
  353.7 32.7 %collective-permute-done.21.refs_13_.refs_4_ = bf16[1024,1024]{1,0:T(8,128)(2,1)} collective-permute-done((bf16[1024,1024]{1,0:T(8,128)(2,1)}, bf16[1024,1024]{1,0:T(8,128)(2,1)}, u32[]{:S(2)}, u32[]{:S(2)}) %collective-permute-start.21) | collective-permute-done | bytes 2097184 | tf_op jit(solution)/shard_map/ppermute | solution.py:898
  386.5 18.3 %shard_map.244 = (f32[1024,1024]{1,0:T(8,128)}, f32[1024,1024]{1,0:T(8,128)}) custom-call(s32[2]{0:T(128)} %pad_add_fusion.refs_0_, bf16[1024,1024]{1,0:T(8,128)(2,1)} %get-tuple-element.105.refs_1_, bf16[1024,1024]{1,0:T(8,128)(2,1)} %get-tuple-element.106.refs_2_, bf16[1024,1024]{1,0:T(8,128)(2,1)} %get-tuple-element.84.refs_3_, ...), custom_call_target="tpu_custom_call" | custom-call | flops 9306000384 | bytes 1000000 | tf_op jit(solution)/shard_map/pallas_call | solution.py:74
  404.8 18.6 %shard_map.245 = (f32[1024,1024]{1,0:T(8,128)}, f32[1024,1024]{1,0:T(8,128)}) custom-call(s32[2]{0:T(128)} %pad_add_fusion.refs_0_, bf16[1024,1024]{1,0:T(8,128)(2,1)} %get-tuple-element.108.refs_1_, bf16[1024,1024]{1,0:T(8,128)(2,1)} %get-tuple-element.109.refs_2_, bf16[1024,1024]{1,0:T(8,128)(2,1)} %get-tuple-element.110.refs_3_, ...), custom_call_target="tpu_custom_call" | custom-call | flops 9306000384 | bytes 1000000 | tf_op jit(solution)/shard_map/pallas_call | solution.py:74
  423.5 6.3 %shard_map.246 = (f32[32,4224]{1,0:T(8,128)}, bf16[32,4224]{1,0:T(8,128)(2,1)}, bf16[32,4224]{1,0:T(8,128)(2,1)}, bf16[32,4224]{1,0:T(8,128)(2,1)}, bf16[1024,1024]{1,0:T(8,128)(2,1)}) custom-call(s32[2]{0:T(128)} %pad_add_fusion.refs_0_, bf16[8,4,32,1024]{3,2,1,0:T(8,128)(2,1)} %copy-done, ...), custom_call_target="tpu_custom_call", output_to_operand_aliasing={{4}: (5, {})} | custom-call | flops 2584999936 | bytes 1000000 | tf_op jit(solution)/shard_map/pallas_call | solution.py:74
  429.8 4.9 %all-to-all-start.5 = ((bf16[8,128,1024]{2,1,0:T(8,128)(2,1)}), bf16[8,128,1024]{2,1,0:T(8,128)(2,1)S(1)}, u32[]{:S(2)}, u32[]{:S(2)}) async-start(bf16[8,128,1024]{2,1,0:T(8,128)(2,1)} %bitcast.28), calls=%async_computation.5 | async-start | bytes 4194304 | tf_op jit(solution)/shard_map/all_to_all | solution.py:877
  434.7 10.5 %collective-permute-start.22 = (bf16[32,4224]{1,0:T(8,128)(2,1)S(1)}, bf16[32,4224]{1,0:T(8,128)(2,1)S(1)}, u32[]{:S(2)}, u32[]{:S(2)}) collective-permute-start(bf16[32,4224]{1,0:T(8,128)(2,1)S(1)} %copy-done.26), channel_id=1, source_target_pairs={{0,8},{8,16},{16,24},{24,0},{1,9},{9,17},{17,25},{25,1},{2,10},{10... | collective-permute-start | bytes 811016 | tf_op jit(solution)/shard_map/ppermute | solution.py:874
  445.2 3.3 collective-permute-start.23
  448.5 2.8 collective-permute-start.24
  451.3 20.3 %shard_map.248 = (f32[1024,1024]{1,0:T(8,128)}, f32[1024,1024]{1,0:T(8,128)}) custom-call(s32[2]{0:T(128)} %pad_add_fusion.refs_0_, bf16[1024,1024]{1,0:T(8,128)(2,1)} %collective-permute-done.25.refs_1_, bf16[1024,1024]{1,0:T(8,128)(2,1)} %collective-permute-done.26.refs_2_, bf16[1024,1024]{1,0:T(8,128)(2,1)} %copy-done.20, ...), custom_call_target="tpu_custom_call" | custom-call | flops 9306000384 | bytes 1000000 | tf_op jit(solution)/shard_map/pallas_call | solution.py:74
  473.1 2.1 shard_map.247
  (113 shorter events, 21.2 us)
Async XLA Ops:
  7.2 5.4 %copy-start.16 = (bf16[32]{0:T(256)(128)(2,1)S(1)}, bf16[32]{0:T(256)(128)(2,1)}, u32[]{:S(2)}) copy-start(bf16[32]{0:T(256)(128)(2,1)} %param.25) | copy-start | bytes 196
  7.2 5.4 %copy-start.17 = (bf16[32]{0:T(256)(128)(2,1)S(1)}, bf16[32]{0:T(256)(128)(2,1)}, u32[]{:S(2)}) copy-start(bf16[32]{0:T(256)(128)(2,1)} %param.24) | copy-start | bytes 196
  7.2 5.4 %copy-start.18 = (bf16[32]{0:T(256)(128)(2,1)S(1)}, bf16[32]{0:T(256)(128)(2,1)}, u32[]{:S(2)}) copy-start(bf16[32]{0:T(256)(128)(2,1)} %param.23) | copy-start | bytes 196
  7.2 5.8 %copy-start.11 = (bf16[32,1024]{1,0:T(8,128)(2,1)S(1)}, bf16[32,1024]{1,0:T(8,128)(2,1)}, u32[]{:S(2)}) copy-start(bf16[32,1024]{1,0:T(8,128)(2,1)} %param.18) | copy-start | bytes 196612
  7.2 5.8 %copy-start.12 = (bf16[32,1024]{1,0:T(8,128)(2,1)S(1)}, bf16[32,1024]{1,0:T(8,128)(2,1)}, u32[]{:S(2)}) copy-start(bf16[32,1024]{1,0:T(8,128)(2,1)} %param.19) | copy-start | bytes 196612
  7.2 5.9 %copy-start.13 = (bf16[32,1024]{1,0:T(8,128)(2,1)S(1)}, bf16[32,1024]{1,0:T(8,128)(2,1)}, u32[]{:S(2)}) copy-start(bf16[32,1024]{1,0:T(8,128)(2,1)} %param.20) | copy-start | bytes 196612
  7.3 5.9 %copy-start.14 = (bf16[32,1024]{1,0:T(8,128)(2,1)S(1)}, bf16[32,1024]{1,0:T(8,128)(2,1)}, u32[]{:S(2)}) copy-start(bf16[32,1024]{1,0:T(8,128)(2,1)} %param.21) | copy-start | bytes 196612
  7.3 32.0 %all-to-all-start = ((bf16[8,128,1024]{2,1,0:T(8,128)(2,1)}), bf16[8,128,1024]{2,1,0:T(8,128)(2,1)S(1)}, u32[]{:S(2)}, u32[]{:S(2)}) async-start(bf16[8,128,1024]{2,1,0:T(8,128)(2,1)} %bitcast.45), calls=%async_computation | async-start | bytes 4194304 | tf_op jit(solution)/shard_map/all_to_all | solution.py:877
  12.6 89.5 %all-gather.3.cloned.1.call-start = ((), (), s32[]{:S(2)}) async-start(), calls=%async_computation.6 | async-start | bytes 4718592 | tf_op jit(solution)/shard_map/all_gather | solution.py:922
  13.1 19.8 %copy-start.5 = (bf16[144,1024]{1,0:T(8,128)(2,1)}, bf16[144,1024]{1,0:T(8,128)(2,1)S(1)}, u32[]{:S(2)}) copy-start(bf16[144,1024]{1,0:T(8,128)(2,1)S(1)} %constant_dynamic-update-slice_fusion.refs_0_) | copy-start | bytes 884740
  13.2 26.0 %collective-permute-start = (bf16[144,1024]{1,0:T(8,128)(2,1)S(1)}, bf16[144,1024]{1,0:T(8,128)(2,1)S(1)}, u32[]{:S(2)}, u32[]{:S(2)}) collective-permute-start(bf16[144,1024]{1,0:T(8,128)(2,1)S(1)} %constant_dynamic-update-slice_fusion.refs_0_), channel_id=1, source_target_pairs={{0,8},{8,16},{16,24},{24,0},{1,9},{9,17},{17,25},{25,1},{2,10},{10... | collective-permute-start | bytes 884744 | tf_op jit(solution)/shard_map/ppermute | solution.py:874
  14.8 24.4 %collective-permute-start.1 = (bf16[144,1024]{1,0:T(8,128)(2,1)S(1)}, bf16[144,1024]{1,0:T(8,128)(2,1)S(1)}, u32[]{:S(2)}, u32[]{:S(2)}) collective-permute-start(bf16[144,1024]{1,0:T(8,128)(2,1)S(1)} %constant_dynamic-update-slice_fusion.refs_0_), channel_id=1, source_target_pairs={{0,16},{8,24},{16,0},{24,8},{1,17},{9,25},{17,1},{25,9},{2,18},{10... | collective-permute-start | bytes 884744 | tf_op jit(solution)/shard_map/ppermute | solution.py:874
  17.4 21.8 %collective-permute-start.2 = (bf16[144,1024]{1,0:T(8,128)(2,1)S(1)}, bf16[144,1024]{1,0:T(8,128)(2,1)S(1)}, u32[]{:S(2)}, u32[]{:S(2)}) collective-permute-start(bf16[144,1024]{1,0:T(8,128)(2,1)S(1)} %constant_dynamic-update-slice_fusion.refs_0_), channel_id=1, source_target_pairs={{0,24},{8,0},{16,8},{24,16},{1,25},{9,1},{17,9},{25,17},{2,26},{10... | collective-permute-start | bytes 884744 | tf_op jit(solution)/shard_map/ppermute | solution.py:874
  40.8 37.3 %copy-start.15 = (s32[1,1024]{1,0:T(1,128)S(1)}, s32[1,1024]{1,0:T(1,128)}, u32[]{:S(2)}) copy-start(s32[1,1024]{1,0:T(1,128)} %refs_9_.1) | copy-start | bytes 12292
  43.2 22.0 %collective-permute-start.4 = (bf16[4,80,1024]{2,1,0:T(8,128)(2,1)}, bf16[4,80,1024]{2,1,0:T(8,128)(2,1)S(1)}, u32[]{:S(2)}, u32[]{:S(2)}) collective-permute-start(bf16[4,80,1024]{2,1,0:T(8,128)(2,1)} %get-tuple-element.73.refs_3_.refs_11_.refs_19_), channel_id=1, source_target_pairs={{0,2},{1,3},{2,0},{3,1},{4,6},{5,7},{6,4},{7,5},{8,10},{9,11},{10,... | collective-permute-start | bytes 1966088 | tf_op jit(solution)/shard_map/ppermute | solution.py:871
  45.4 22.9 %collective-permute-start.6 = (bf16[4,80,1024]{2,1,0:T(8,128)(2,1)}, bf16[4,80,1024]{2,1,0:T(8,128)(2,1)S(1)}, u32[]{:S(2)}, u32[]{:S(2)}) collective-permute-start(bf16[4,80,1024]{2,1,0:T(8,128)(2,1)} %get-tuple-element.73.refs_3_.refs_11_.refs_19_), channel_id=1, source_target_pairs={{0,4},{1,5},{2,6},{3,7},{4,0},{5,1},{6,2},{7,3},{8,12},{9,13},{10,... | collective-permute-start | bytes 1966088 | tf_op jit(solution)/shard_map/ppermute | solution.py:871
  46.8 51.0 %collective-permute-start.12 = (bf16[1024,1024]{1,0:T(8,128)(2,1)}, bf16[1024,1024]{1,0:T(8,128)(2,1)S(1)}, u32[]{:S(2)}, u32[]{:S(2)}) collective-permute-start(bf16[1024,1024]{1,0:T(8,128)(2,1)} %refs_2_.1), channel_id=1, source_target_pairs={{0,8},{8,16},{16,24},{1,9},{9,17},{17,25},{2,10},{10,18},{18,26},{... | collective-permute-start | bytes 6291464 | tf_op jit(solution)/shard_map/ppermute | solution.py:897
  53.1 48.9 %collective-permute-start.13 = (bf16[1024,1024]{1,0:T(8,128)(2,1)}, bf16[1024,1024]{1,0:T(8,128)(2,1)}, u32[]{:S(2)}, u32[]{:S(2)}) collective-permute-start(bf16[1024,1024]{1,0:T(8,128)(2,1)} %refs_2_.1), channel_id=1, source_target_pairs={{8,0},{16,8},{24,16},{9,1},{17,9},{25,17},{10,2},{18,10},{26,18},{... | collective-permute-start | bytes 6291464 | tf_op jit(solution)/shard_map/ppermute | solution.py:898
  54.4 14.7 %collective-permute-start.3 = (bf16[4,80,1024]{2,1,0:T(8,128)(2,1)}, bf16[4,80,1024]{2,1,0:T(8,128)(2,1)S(1)}, u32[]{:S(2)}, u32[]{:S(2)}) collective-permute-start(bf16[4,80,1024]{2,1,0:T(8,128)(2,1)} %get-tuple-element.73.refs_3_.refs_11_.refs_19_), channel_id=1, source_target_pairs={{0,1},{1,0},{2,3},{3,2},{4,5},{5,4},{6,7},{7,6},{8,9},{9,8},{10,11... | collective-permute-start | bytes 1966088 | tf_op jit(solution)/shard_map/ppermute | solution.py:871
  65.2 14.8 %copy-start.9 = (bf16[4,80,1024]{2,1,0:T(8,128)(2,1)}, bf16[4,80,1024]{2,1,0:T(8,128)(2,1)S(1)}, u32[]{:S(2)}) copy-start(bf16[4,80,1024]{2,1,0:T(8,128)(2,1)S(1)} %collective-permute-done.4.refs_5_.refs_13_.refs_21_) | copy-start | bytes 1966084
  65.2 10.3 %collective-permute-start.10 = (bf16[4,48,1024]{2,1,0:T(8,128)(2,1)S(1)}, bf16[4,48,1024]{2,1,0:T(8,128)(2,1)}, u32[]{:S(2)}, u32[]{:S(2)}) collective-permute-start(bf16[4,48,1024]{2,1,0:T(8,128)(2,1)S(1)} %slice.9), channel_id=1, source_target_pairs={{0,4},{1,5},{2,6},{3,7},{4,0},{5,1},{6,2},{7,3},{8,12},{9,13},{10,... | collective-permute-start | bytes 1179656 | tf_op jit(solution)/shard_map/ppermute | solution.py:871
  68.3 11.7 %copy-start.10 = (bf16[4,80,1024]{2,1,0:T(8,128)(2,1)}, bf16[4,80,1024]{2,1,0:T(8,128)(2,1)S(1)}, u32[]{:S(2)}) copy-start(bf16[4,80,1024]{2,1,0:T(8,128)(2,1)S(1)} %collective-permute-done.6.refs_7_.refs_15_.refs_23_) | copy-start | bytes 1966084
  68.3 6.4 %collective-permute-start.8 = (bf16[4,32,1024]{2,1,0:T(8,128)(2,1)S(1)}, bf16[4,32,1024]{2,1,0:T(8,128)(2,1)S(1)}, u32[]{:S(2)}, u32[]{:S(2)}) collective-permute-start(bf16[4,32,1024]{2,1,0:T(8,128)(2,1)S(1)} %slice.8), channel_id=1, source_target_pairs={{0,2},{1,3},{2,0},{3,1},{4,6},{5,7},{6,4},{7,5},{8,10},{9,11},{10,... | collective-permute-start | bytes 786440 | tf_op jit(solution)/shard_map/ppermute | solution.py:871
  69.1 6.4 %copy-start.21 = (bf16[4,80,1024]{2,1,0:T(8,128)(2,1)}, bf16[4,80,1024]{2,1,0:T(8,128)(2,1)S(1)}, u32[]{:S(2)}) copy-start(bf16[4,80,1024]{2,1,0:T(8,128)(2,1)S(1)} %collective-permute-done.3.refs_4_.refs_12_.refs_20_) | copy-start | bytes 1966084
  69.1 10.6 %collective-permute-start.5 = (bf16[4,80,1024]{2,1,0:T(8,128)(2,1)S(1)}, bf16[4,80,1024]{2,1,0:T(8,128)(2,1)}, u32[]{:S(2)}, u32[]{:S(2)}) collective-permute-start(bf16[4,80,1024]{2,1,0:T(8,128)(2,1)S(1)} %collective-permute-done.4.refs_5_.refs_13_.refs_21_), channel_id=1, source_target_pairs={{0,1},{1,0},{2,3},{3,2},{4,5},{5,4},{6,7},{7,6},{8,9},{9,8},{10,11... | collective-permute-start | bytes 1966088 | tf_op jit(solution)/shard_map/ppermute | solution.py:871
  74.8 5.0 %collective-permute-start.7 = (bf16[4,80,1024]{2,1,0:T(8,128)(2,1)S(1)}, bf16[4,80,1024]{2,1,0:T(8,128)(2,1)}, u32[]{:S(2)}, u32[]{:S(2)}) collective-permute-start(bf16[4,80,1024]{2,1,0:T(8,128)(2,1)S(1)} %collective-permute-done.6.refs_7_.refs_15_.refs_23_), channel_id=1, source_target_pairs={{0,1},{1,0},{2,3},{3,2},{4,5},{5,4},{6,7},{7,6},{8,9},{9,8},{10,11... | collective-permute-start | bytes 1966088 | tf_op jit(solution)/shard_map/ppermute | solution.py:871
  75.5 1.8 collective-permute-start.9
  77.9 2.1 collective-permute-start.11
  109.3 76.6 %collective-permute-start.14 = (bf16[1024,1024]{1,0:T(8,128)(2,1)}, bf16[1024,1024]{1,0:T(8,128)(2,1)S(1)}, u32[]{:S(2)}, u32[]{:S(2)}) collective-permute-start(bf16[1024,1024]{1,0:T(8,128)(2,1)} %get-tuple-element.84.refs_3_), channel_id=1, source_target_pairs={{8,16},{16,24},{9,17},{17,25},{10,18},{18,26},{11,19},{19,27},{12,... | collective-permute-start | bytes 6291464 | tf_op jit(solution)/shard_map/ppermute | solution.py:897
  110.1 75.9 %collective-permute-start.15 = (bf16[1024,1024]{1,0:T(8,128)(2,1)}, bf16[1024,1024]{1,0:T(8,128)(2,1)}, u32[]{:S(2)}, u32[]{:S(2)}) collective-permute-start(bf16[1024,1024]{1,0:T(8,128)(2,1)} %get-tuple-element.85.refs_4_), channel_id=1, source_target_pairs={{8,0},{16,8},{9,1},{17,9},{10,2},{18,10},{11,3},{19,11},{12,4},{20... | collective-permute-start | bytes 6291464 | tf_op jit(solution)/shard_map/ppermute | solution.py:898
  171.9 64.3 %collective-permute-start.16 = (bf16[1024,1024]{1,0:T(8,128)(2,1)}, bf16[1024,1024]{1,0:T(8,128)(2,1)}, u32[]{:S(2)}, u32[]{:S(2)}) collective-permute-start(bf16[1024,1024]{1,0:T(8,128)(2,1)} %bitcast.13.refs_0_.refs_1_), channel_id=1, source_target_pairs={{0,8},{8,16},{16,24},{1,9},{9,17},{17,25},{2,10},{10,18},{18,26},{... | collective-permute-start | bytes 6291464 | tf_op jit(solution)/shard_map/ppermute | solution.py:897
  184.6 51.6 %collective-permute-start.17 = (bf16[1024,1024]{1,0:T(8,128)(2,1)}, bf16[1024,1024]{1,0:T(8,128)(2,1)}, u32[]{:S(2)}, u32[]{:S(2)}) collective-permute-start(bf16[1024,1024]{1,0:T(8,128)(2,1)} %bitcast.13.refs_0_.refs_1_), channel_id=1, source_target_pairs={{8,0},{16,8},{24,16},{9,1},{17,9},{25,17},{10,2},{18,10},{26,18},{... | collective-permute-start | bytes 6291464 | tf_op jit(solution)/shard_map/ppermute | solution.py:898
  217.8 39.1 %all-to-all-start.2 = ((bf16[8,128,1024]{2,1,0:T(8,128)(2,1)}), bf16[8,128,1024]{2,1,0:T(8,128)(2,1)S(1)}, u32[]{:S(2)}, u32[]{:S(2)}) async-start(bf16[8,128,1024]{2,1,0:T(8,128)(2,1)} %bitcast.47), calls=%async_computation.2 | async-start | bytes 4194304 | tf_op jit(solution)/shard_map/all_to_all | solution.py:877
  253.6 39.6 %collective-permute-start.18 = (bf16[1024,1024]{1,0:T(8,128)(2,1)}, bf16[1024,1024]{1,0:T(8,128)(2,1)}, u32[]{:S(2)}, u32[]{:S(2)}) collective-permute-start(bf16[1024,1024]{1,0:T(8,128)(2,1)} %get-tuple-element.105.refs_1_), channel_id=1, source_target_pairs={{8,16},{16,24},{9,17},{17,25},{10,18},{18,26},{11,19},{19,27},{12,... | collective-permute-start | bytes 6291464 | tf_op jit(solution)/shard_map/ppermute | solution.py:897
  255.6 54.0 %collective-permute-start.19 = (bf16[1024,1024]{1,0:T(8,128)(2,1)}, bf16[1024,1024]{1,0:T(8,128)(2,1)}, u32[]{:S(2)}, u32[]{:S(2)}) collective-permute-start(bf16[1024,1024]{1,0:T(8,128)(2,1)} %get-tuple-element.106.refs_2_), channel_id=1, source_target_pairs={{8,0},{16,8},{9,1},{17,9},{10,2},{18,10},{11,3},{19,11},{12,4},{20... | collective-permute-start | bytes 6291464 | tf_op jit(solution)/shard_map/ppermute | solution.py:898
  272.9 52.3 %all-to-all-start.3 = ((bf16[8,4,32,1024]{3,2,1,0:T(8,128)(2,1)}), bf16[8,4,32,1024]{3,2,1,0:T(8,128)(2,1)S(1)}, u32[]{:S(2)}, u32[]{:S(2)}) async-start(bf16[8,4,32,1024]{3,2,1,0:T(8,128)(2,1)} %get-tuple-element.93.refs_7_), calls=%async_computation.3 | async-start | bytes 4194304 | tf_op jit(solution)/shard_map/all_to_all | solution.py:877
  326.6 96.9 %all-to-all-start.4 = ((bf16[8,4,32,3200]{3,2,1,0:T(8,128)(2,1)}), bf16[8,4,32,3200]{3,2,1,0:T(8,128)(2,1)}, u32[]{:S(2)}, u32[]{:S(2)}) async-start(bf16[8,4,32,3200]{3,2,1,0:T(8,128)(2,1)} %get-tuple-element.107.refs_11_), calls=%async_computation.4 | async-start | bytes 13107200 | tf_op jit(solution)/shard_map/all_to_all | solution.py:877
  331.4 22.4 %collective-permute-start.20 = (bf16[1024,1024]{1,0:T(8,128)(2,1)}, bf16[1024,1024]{1,0:T(8,128)(2,1)S(1)}, u32[]{:S(2)}, u32[]{:S(2)}) collective-permute-start(bf16[1024,1024]{1,0:T(8,128)(2,1)} %get-tuple-element.110.refs_3_), channel_id=1, source_target_pairs={{16,24},{17,25},{18,26},{19,27},{20,28},{21,29},{22,30},{23,31}} | collective-permute-start | bytes 6291464 | tf_op jit(solution)/shard_map/ppermute | solution.py:897
  332.2 54.3 %collective-permute-start.21 = (bf16[1024,1024]{1,0:T(8,128)(2,1)}, bf16[1024,1024]{1,0:T(8,128)(2,1)}, u32[]{:S(2)}, u32[]{:S(2)}) collective-permute-start(bf16[1024,1024]{1,0:T(8,128)(2,1)} %get-tuple-element.111.refs_4_), channel_id=1, source_target_pairs={{8,0},{9,1},{10,2},{11,3},{12,4},{13,5},{14,6},{15,7}} | collective-permute-start | bytes 6291464 | tf_op jit(solution)/shard_map/ppermute | solution.py:898
  333.5 117.8 %collective-permute-start.25 = (bf16[1024,1024]{1,0:T(8,128)(2,1)}, bf16[1024,1024]{1,0:T(8,128)(2,1)}, u32[]{:S(2)}, u32[]{:S(2)}) collective-permute-start(bf16[1024,1024]{1,0:T(8,128)(2,1)} %get-tuple-element.108.refs_1_), channel_id=1, source_target_pairs={{16,24},{17,25},{18,26},{19,27},{20,28},{21,29},{22,30},{23,31}} | collective-permute-start | bytes 6291464 | tf_op jit(solution)/shard_map/ppermute | solution.py:897
  335.4 115.9 %collective-permute-start.26 = (bf16[1024,1024]{1,0:T(8,128)(2,1)}, bf16[1024,1024]{1,0:T(8,128)(2,1)}, u32[]{:S(2)}, u32[]{:S(2)}) collective-permute-start(bf16[1024,1024]{1,0:T(8,128)(2,1)} %get-tuple-element.109.refs_2_), channel_id=1, source_target_pairs={{8,0},{9,1},{10,2},{11,3},{12,4},{13,5},{14,6},{15,7}} | collective-permute-start | bytes 6291464 | tf_op jit(solution)/shard_map/ppermute | solution.py:898
  353.7 32.7 %copy-start.20 = (bf16[1024,1024]{1,0:T(8,128)(2,1)}, bf16[1024,1024]{1,0:T(8,128)(2,1)S(1)}, u32[]{:S(2)}) copy-start(bf16[1024,1024]{1,0:T(8,128)(2,1)S(1)} %collective-permute-done.20.refs_12_.refs_3_) | copy-start | bytes 6291460
  429.8 15.4 %copy-start.24 = (bf16[32,4224]{1,0:T(8,128)(2,1)S(1)}, bf16[32,4224]{1,0:T(8,128)(2,1)}, u32[]{:S(2)}) copy-start(bf16[32,4224]{1,0:T(8,128)(2,1)} %get-tuple-element.120.refs_13_) | copy-start | bytes 811012
  429.8 18.7 %copy-start.22 = (bf16[32,4224]{1,0:T(8,128)(2,1)S(1)}, bf16[32,4224]{1,0:T(8,128)(2,1)}, u32[]{:S(2)}) copy-start(bf16[32,4224]{1,0:T(8,128)(2,1)} %get-tuple-element.121.refs_14_) | copy-start | bytes 811012
  429.8 45.5 %all-to-all-start.5 = ((bf16[8,128,1024]{2,1,0:T(8,128)(2,1)}), bf16[8,128,1024]{2,1,0:T(8,128)(2,1)S(1)}, u32[]{:S(2)}, u32[]{:S(2)}) async-start(bf16[8,128,1024]{2,1,0:T(8,128)(2,1)} %bitcast.28), calls=%async_computation.5 | async-start | bytes 4194304 | tf_op jit(solution)/shard_map/all_to_all | solution.py:877
  434.7 36.9 %collective-permute-start.22 = (bf16[32,4224]{1,0:T(8,128)(2,1)S(1)}, bf16[32,4224]{1,0:T(8,128)(2,1)S(1)}, u32[]{:S(2)}, u32[]{:S(2)}) collective-permute-start(bf16[32,4224]{1,0:T(8,128)(2,1)S(1)} %copy-done.26), channel_id=1, source_target_pairs={{0,8},{8,16},{16,24},{24,0},{1,9},{9,17},{17,25},{25,1},{2,10},{10... | collective-permute-start | bytes 811016 | tf_op jit(solution)/shard_map/ppermute | solution.py:874
  445.2 26.4 %collective-permute-start.23 = (bf16[32,4224]{1,0:T(8,128)(2,1)S(1)}, bf16[32,4224]{1,0:T(8,128)(2,1)S(1)}, u32[]{:S(2)}, u32[]{:S(2)}) collective-permute-start(bf16[32,4224]{1,0:T(8,128)(2,1)S(1)} %copy-done.24), channel_id=1, source_target_pairs={{0,16},{8,24},{16,0},{24,8},{1,17},{9,25},{17,1},{25,9},{2,18},{10... | collective-permute-start | bytes 811016 | tf_op jit(solution)/shard_map/ppermute | solution.py:874
  448.5 23.2 %collective-permute-start.24 = (bf16[32,4224]{1,0:T(8,128)(2,1)S(1)}, bf16[32,4224]{1,0:T(8,128)(2,1)S(1)}, u32[]{:S(2)}, u32[]{:S(2)}) collective-permute-start(bf16[32,4224]{1,0:T(8,128)(2,1)S(1)} %copy-done.22), channel_id=1, source_target_pairs={{0,24},{8,0},{16,8},{24,16},{1,25},{9,1},{17,9},{25,17},{2,26},{10... | collective-permute-start | bytes 811016 | tf_op jit(solution)/shard_map/ppermute | solution.py:874
  (15 other events, 26.3 us)
Sparse Core Ops, SparseCore 0:
  43.3 45.4 all-gather.2

commit v6 on v4

--- a/solution.py
+++ b/solution.py
@@ -567,6 +567,8 @@
     valid = [meta[1] >= t, meta[1] + t < groups] if t else [meta[1] >= 0]
     count = len(valid)
     xs, cots = refs[:count], refs[count : 2 * count]
+    froms = [lax.max(meta[1] - t, 0), lax.min(meta[1] + t, groups - 1)]
+    cots = [c.at[f] if t > 1 else c for c, f in zip(cots, froms)]
     gain_ref, bias_ref, wi_ref, wo_ref = refs[2 * count : 2 * count + 4]
     rest = refs[2 * count + 4 :]
     if not first:
@@ -941,21 +943,22 @@
     seq, ln_one, ln_turned, q, k, mat_q, mat_k, gains = enter(
         meta, ids_col, arrived, pieces_q, pieces_k, pieces_g, full
     )
-    v, mat_v, cot_line[1] = project(meta, ln_one, pieces_v, full, gates=cot_line[1])
-    forward(cot_line)
+    v, mat_v, (cot_gated,) = project(meta, ln_one, pieces_v, full, gates=cotangent)
+    cot_all = lax.all_gather(cot_gated, "grp", axis=0)
     attn, lse = attend(flag, q, k, v)
     mat_o, leaving = mix(meta, attn, seq, ids_row, pieces_o, full)
     x = exchange(leaving)
 
     act, dx, sums_two = expert(
-        x, cotangent, gains[2], gains[3], w_first, dact, deps=cot_line[-1]
+        x, cotangent, gains[2], gains[3], w_first, dact
     )
     x_line = [(x,) * 2]
     forward(x_line)
     output = expert_out(x, act, w_second)
 
     def slices(t, sums, deps=(), gates=()):
-        xs, cots = (list(line[t])[: 2 if t else 1] for line in (x_line, cot_line))
+        xs = list(x_line[t])[: 2 if t else 1]
+        cots = [cot_all] * 2 if t > 1 else list(cot_line[t])[: len(xs)]
         last = (gains[2], gains[3], wi_turned, wo_turned, sums, deps, gates)
         return slice_grads(meta, t, n_grp, xs, cots, *last)
 
@@ -965,11 +968,7 @@
     forward(x_line)
 
     (first,) = shared_grads(attn, False, [dmix], n_exp, n_grp)
-    grads, cot_line[-1] = attend_back(
-        flag, q, k, v, attn, dattn, lse, 0, 1, deps=first, gates=cot_line[-1]
-    )
-    while len(cot_line) < n_grp:
-        forward(cot_line)
+    grads = attend_back(flag, q, k, v, attn, dattn, lse, 0, 1, deps=first)
     first = exchange(first)
     (second,), x_line[-1] = shared_grads(
         ln_turned,
@@ -989,7 +988,7 @@
     for t in range(1, n_grp):
         deps = (dfirst,) if t == 1 else ()
         if t == n_grp - 1:
-            deps = (deps, slice_sums, cot_line[-1])
+            deps = (deps, slice_sums)
             parts, (dfirst,) = total_over(meta, first, second, deps, dfirst)
             deps = parts
             parts = [parts[0]] + [shift(a, n + 1) for n, a in enumerate(parts[1:])]

time: 482 us -> 565 us (1.17)
  waiting for transfers between devices: 57.4 us -> 136 us
  Pallas kernels: 285 us -> 270 us
  blocking collectives: 30.9 us -> 40.8 us
    ppermute x6 -> x4, waiting for transfers between devices: 2.41 us -> 63.6 us  [line_step(): up = lax.ppermute(up, 'grp', [(i, i + 1) for i in range(t - 1, n_grp - 1)])]
    ppermute x6 -> x4, waiting for transfers between devices: 19.3 us -> 43.1 us  [line_step(): down = lax.ppermute(down, 'grp', [(i + 1, i) for i in range(n_grp - t)])]
    pallas_call x20, Pallas kernels: 285 us -> 270 us  [run(): pl.pallas_call(body, grid_spec=pltpu.PrefetchScalarGridSpec(num_scalar_pr...]
    all_to_all x5, waiting for transfers between devices: 15 us -> 0.01 us  [exchange(): return lax.all_to_all(rows, 'exp', split_axis=0, concat_axis=0, tiled=True)]
    all_to_all x1, blocking collectives: 30.9 us -> 40.8 us  [exchange(): return lax.all_to_all(rows, 'exp', split_axis=0, concat_axis=0, tiled=True)]
    ppermute x9, waiting for transfers between devices: 20.6 us -> 29.3 us  [swap(): return lax.ppermute(a, 'exp', [(i, i ^ k) for i in range(n_exp)])]
    unnamed x65 -> x62, local copies, waits for them, and re-layouts: 9.1 us -> 11.5 us
    ppermute x6 -> x4, starting transfers between devices: 22.2 us -> 23 us  [line_step(): up = lax.ppermute(up, 'grp', [(i, i + 1) for i in range(t - 1, n_grp - 1)])]
  transfers between devices with their start and end apart: 33 -> 30, of which waited for: 10 -> 9; matrix products, arithmetic and copies ran while one was open for 0% -> 1% of each run, Pallas kernels for 58% -> 47%
where the time goes in v6:
time: 565 us; the launch traced here: 554 us
  Pallas kernels  270 us (48%)
  waiting for transfers between devices  136 us (24%)
  starting transfers between devices  78.9 us (14%)
  blocking collectives  40.8 us (7%)
  between operations  15.5 us (3%)
  local copies, waits for them, and re-layouts  12.9 us (2%)
    pallas_call x20, Pallas kernels, run(): pl.pallas_call(body, grid_spec=pltpu.PrefetchScalarGridSpec(num_scalar_pr...  270 us
    ppermute x4, waiting for transfers between devices, line_step(): up = lax.ppermute(up, 'grp', [(i, i + 1) for i in range(t - 1, n_grp - 1)])  63.6 us
    ppermute x4, waiting for transfers between devices, line_step(): down = lax.ppermute(down, 'grp', [(i + 1, i) for i in range(n_grp - t)])  43.1 us
    all_to_all x1, blocking collectives, exchange(): return lax.all_to_all(rows, 'exp', split_axis=0, concat_axis=0, tiled=True)  40.8 us
    ppermute x9, waiting for transfers between devices, swap(): return lax.ppermute(a, 'exp', [(i, i ^ k) for i in range(n_exp)])  29.3 us
    all_to_all x5, starting transfers between devices, exchange(): return lax.all_to_all(rows, 'exp', split_axis=0, concat_axis=0, tiled=True)  24.2 us
    ppermute x4, starting transfers between devices, line_step(): up = lax.ppermute(up, 'grp', [(i, i + 1) for i in range(t - 1, n_grp - 1)])  23 us
    ppermute x6, starting transfers between devices, shift(): return lax.ppermute(a, 'grp', [(i, (i + k) % n_grp) for i in range(n_grp)])  20.1 us
  transfers between devices with their start and end apart: 30, of which 9 were waited for; matrix products, arithmetic and copies ran while one was open for 1% of the time, Pallas kernels for 47%

profile of v6, /device:TPU:0, one launch (start us, length us, event | category | flops | bytes accessed | tf_op | source)
XLA Modules:
  0.0 554.4 jit_solution(6643935539827949399)
XLA Ops:
  7.3 5.3 all-to-all-start
  13.2 1.6 collective-permute-start
  14.8 2.6 collective-permute-start.1
  17.4 1.3 collective-permute-start.2
  18.7 14.2 %shard_map.229.refs_5_ = bf16[1024,4096]{1,0:T(8,128)(2,1)} custom-call(bf16[1024,1024]{1,0:T(8,128)(2,1)} %refs_2_.1, bf16[1024,4096]{1,0:T(8,128)(2,1)} %bitcast.35), custom_call_target="tpu_custom_call" | custom-call | flops 5687000064 | bytes 1000000 | tf_op jit(solution)/shard_map/pallas_call | solution.py:74
  33.6 5.7 %shard_map.230 = (bf16[1024,1024]{1,0:T(8,128)(2,1)}, bf16[1024,1024]{1,0:T(8,128)(2,1)}) custom-call(s32[2]{0:T(128)} %pad_add_fusion.refs_0_, bf16[1024,4096]{1,0:T(8,128)(2,1)} %bitcast.33, bf16[1024,4096]{1,0:T(8,128)(2,1)} %bitcast.36), custom_call_target="tpu_custom_call" | custom-call | flops 2584999936 | bytes 1000000 | tf_op jit(solution)/shard_map/pallas_call | solution.py:74
  40.8 2.3 shard_map.231
  43.2 2.2 collective-permute-start.4
  45.5 1.5 collective-permute-start.6
  46.9 17.9 %collective-permute-done.4.refs_5_.refs_13_.refs_21_ = bf16[4,80,1024]{2,1,0:T(8,128)(2,1)S(1)} collective-permute-done((bf16[4,80,1024]{2,1,0:T(8,128)(2,1)}, bf16[4,80,1024]{2,1,0:T(8,128)(2,1)S(1)}, u32[]{:S(2)}, u32[]{:S(2)}) %collective-permute-start.4) | collective-permute-done | bytes 655392 | tf_op jit(solution)/shard_map/ppermute | solution.py:873
  66.7 1.6 collective-permute-done.6.refs_7_.refs_15_.refs_23_
  69.3 6.4 %collective-permute-done.10.refs_17_.refs_25_ = bf16[4,48,1024]{2,1,0:T(8,128)(2,1)} collective-permute-done((bf16[4,48,1024]{2,1,0:T(8,128)(2,1)S(1)}, bf16[4,48,1024]{2,1,0:T(8,128)(2,1)}, u32[]{:S(2)}, u32[]{:S(2)}) %collective-permute-start.10) | collective-permute-done | bytes 393248 | tf_op jit(solution)/shard_map/ppermute | solution.py:873
  75.7 3.3 collective-permute-done.8.refs_9_
  79.0 3.2 copy.41.refs_3_
  85.1 15.4 %shard_map.232 = (bf16[1024,1024]{1,0:T(8,128)(2,1)}, bf16[1024,1024]{1,0:T(8,128)(2,1)}, bf16[1024,1024]{1,0:T(8,128)(2,1)}, bf16[1024,1024]{1,0:T(8,128)(2,1)}...) custom-call(s32[2]{0:T(128)} %pad_add_fusion.refs_0_, ...), custom_call_target="tpu_custom_call" | custom-call | flops 7238000128 | bytes 1000000 | tf_op jit(solution)/shard_map/pallas_call | solution.py:74
  100.5 7.1 %shard_map.233 = (bf16[1024,1024]{1,0:T(8,128)(2,1)}, bf16[4,8,32,1024]{3,2,1,0:T(8,128)(2,1)}, bf16[1024,1024]{1,0:T(8,128)(2,1)}) custom-call(s32[2]{0:T(128)} %pad_add_fusion.refs_0_, bf16[1024,1024]{1,0:T(8,128)(2,1)} %get-tuple-element.72.refs_1_, bf16[8,4,64,1024]{3,2,1,0:T(8,128)(2,1)} %bitcast.51, ...), custom_call_target="tpu_custom_call", output_to_operand_aliasing={{2}: (3, {})} | custom-call | flops 2584999936 | bytes 1000000 | tf_op jit(solution)/shard_map/pallas_call | solution.py:74
  107.7 10.9 %shard_map.234 = (bf16[1024,1024]{1,0:T(8,128)(2,1)}, f32[8,8,1024]{2,1,0:T(8,128)}) custom-call(s32[1]{0:T(128)S(6)} %copy.48.refs_0_, bf16[1024,1024]{1,0:T(8,128)(2,1)} %get-tuple-element.70.refs_1_, bf16[1024,1024]{1,0:T(8,128)(2,1)} %get-tuple-element.71.refs_2_, bf16[1024,1024]{1,0:T(8,128)(2,1)} %get-tuple-element.74.refs_3_), custom_call_target="tpu_custom_call" | custom-call | flops 11374000128 | bytes 1000000 | tf_op jit(solution)/shard_map/pallas_call | solution.py:74
  118.6 22.3 %shard_map.235 = (bf16[4,8,32,1024]{3,2,1,0:T(8,128)(2,1)}, bf16[1024,1024]{1,0:T(8,128)(2,1)}) custom-call(s32[2]{0:T(128)} %pad_add_fusion.refs_0_, bf16[1024,1024]{1,0:T(8,128)(2,1)} %get-tuple-element.75.refs_1_.refs_0_.refs_4_, bf16[1024,1024]{1,0:T(8,128)(2,1)} %get-tuple-element.76.refs_2_.refs_6_, s32[1,1024]{1,0:T(1,128)} %refs_9_.1, ...), custom_call_target="tpu_custom_call" | custom-call | flops 4136000000 | bytes 1000000 | tf_op jit(solution)/shard_map/pallas_call | solution.py:74
  140.9 40.8 %all_to_all.55 = bf16[8,128,1024]{2,1,0:T(8,128)(2,1)} all-to-all(bf16[8,128,1024]{2,1,0:T(8,128)(2,1)} %bitcast.45), channel_id=1, replica_groups=mesh['grp'=4,'exp'=8] {'exp'}, dimensions={0} | all-to-all | bytes 4194304 | tf_op jit(solution)/shard_map/all_to_all | solution.py:879
  181.7 11.9 %collective-permute-start.12 = (bf16[1024,1024]{1,0:T(8,128)(2,1)}, bf16[1024,1024]{1,0:T(8,128)(2,1)}, u32[]{:S(2)}, u32[]{:S(2)}) collective-permute-start(bf16[1024,1024]{1,0:T(8,128)(2,1)} %bitcast.13.refs_0_.refs_1_), channel_id=1, source_target_pairs={{0,8},{8,16},{16,24},{1,9},{9,17},{17,25},{2,10},{10,18},{18,26},{... | collective-permute-start | bytes 6291464 | tf_op jit(solution)/shard_map/ppermute | solution.py:899
  194.9 30.4 %shard_map.236 = (bf16[1024,4096]{1,0:T(8,128)(2,1)}, bf16[1024,1024]{1,0:T(8,128)(2,1)}, f32[8,1024]{1,0:T(8,128)}) custom-call(bf16[1024,1024]{1,0:T(8,128)(2,1)} %bitcast.13.refs_0_.refs_1_, bf16[1024,1024]{1,0:T(8,128)(2,1)} %refs_2_.1, f32[1,1024]{1,0:T(1,128)} %get-tuple-element.78.refs_2_.refs_3_.refs_5_, ...), custom_call_target="tpu_custom_call" | custom-call | flops 17578000384 | bytes 1000000 | tf_op jit(solution)/shard_map/pallas_call | solution.py:74
  225.3 3.6 all-to-all-start.2
  228.9 14.8 %shard_map.237.refs_7_ = bf16[1024,1024]{1,0:T(8,128)(2,1)} custom-call(bf16[1024,1024]{1,0:T(8,128)(2,1)} %bitcast.13.refs_0_.refs_1_, bf16[1024,4096]{1,0:T(8,128)(2,1)} %get-tuple-element.80.refs_1_, bf16[1024,4096]{1,0:T(8,128)(2,1)} %bitcast.37), custom_call_target="tpu_custom_call" | custom-call | flops 6204000256 | bytes 1000000 | tf_op jit(solution)/shard_map/pallas_call | solution.py:74
  243.7 39.2 %collective-permute-done.12.refs_8_ = bf16[1024,1024]{1,0:T(8,128)(2,1)} collective-permute-done((bf16[1024,1024]{1,0:T(8,128)(2,1)}, bf16[1024,1024]{1,0:T(8,128)(2,1)}, u32[]{:S(2)}, u32[]{:S(2)}) %collective-permute-start.12) | collective-permute-done | bytes 2097184 | tf_op jit(solution)/shard_map/ppermute | solution.py:899
  282.9 23.4 %collective-permute-done.13.refs_9_ = bf16[1024,1024]{1,0:T(8,128)(2,1)} collective-permute-done((bf16[1024,1024]{1,0:T(8,128)(2,1)}, bf16[1024,1024]{1,0:T(8,128)(2,1)}, u32[]{:S(2)}, u32[]{:S(2)}) %collective-permute-start.13) | collective-permute-done | bytes 2097184 | tf_op jit(solution)/shard_map/ppermute | solution.py:900
  306.3 17.4 %shard_map.238 = (f32[1024,1024]{1,0:T(8,128)}, f32[1024,1024]{1,0:T(8,128)}, bf16[1024,1024]{1,0:T(8,128)(2,1)}, bf16[1024,1024]{1,0:T(8,128)(2,1)}) custom-call(s32[2]{0:T(128)} %pad_add_fusion.refs_0_, bf16[1024,1024]{1,0:T(8,128)(2,1)} %bitcast.13.refs_0_.refs_1_, bf16[1024,1024]{1,0:T(8,128)(2,1)} %refs_2_.1, ...), custom_call_target="tpu_custom_call", output_to_operand_aliasing={{2}: (8, {}), {3}: (9, {})} | custom-call | flops 9306000384 | bytes 1000000 | tf_op jit(solution)/shard_map/pallas_call | solution.py:74
  323.8 2.0 collective-permute-start.14
  327.1 1.3 copy-done.2
  328.4 8.5 %shard_map.239 = (bf16[1024,1024]{1,0:T(8,128)(2,1)}, bf16[1024,1024]{1,0:T(8,128)(2,1)}) custom-call(s32[1024,1]{1,0:T(8,128)} %copy.34.refs_1_.refs_0_, bf16[1024,1024]{1,0:T(8,128)(2,1)} %bitcast.61, bf16[1024,1024]{1,0:T(8,128)(2,1)} %bitcast.43, f32[1024,1024]{1,0:T(8,128)} %get-tuple-element.84.refs_3_.refs_9_, ...), custom_call_target="tpu_custom_call" | custom-call | flops 3619000064 | bytes 1000000 | tf_op jit(solution)/shard_map/pallas_call | solution.py:74
  336.9 6.1 %shard_map.240.refs_7_ = bf16[8,4,32,1024]{3,2,1,0:T(8,128)(2,1)} custom-call(bf16[1024,1024]{1,0:T(8,128)(2,1)} %get-tuple-element.75.refs_1_.refs_0_.refs_4_, bf16[1024,1024]{1,0:T(8,128)(2,1)} %get-tuple-element.86.refs_1_.refs_7_), custom_call_target="tpu_custom_call" | custom-call | flops 2068000000 | bytes 1000000 | tf_op jit(solution)/shard_map/pallas_call | solution.py:74
  343.0 3.8 all-to-all-start.3
  346.9 16.2 %shard_map.241 = (bf16[1024,1024]{1,0:T(8,128)(2,1)}, bf16[1024,1024]{1,0:T(8,128)(2,1)}, bf16[1024,1024]{1,0:T(8,128)(2,1)}) custom-call(s32[1]{0:T(128)S(6)} %copy.48.refs_0_, bf16[1024,1024]{1,0:T(8,128)(2,1)} %get-tuple-element.70.refs_1_, bf16[1024,1024]{1,0:T(8,128)(2,1)} %get-tuple-element.71.refs_2_, bf16[1024,1024]{1,0:T(8,128)(2,1)} %get-tuple-element.74.refs_3_, ...), custom_call_target="tpu_custom_call" | custom-call | flops 9306000384 | bytes 1000000 | tf_op jit(solution)/shard_map/pallas_call | solution.py:74
  363.1 13.6 %collective-permute-done.15.refs_10_ = bf16[1024,1024]{1,0:T(8,128)(2,1)} collective-permute-done((bf16[1024,1024]{1,0:T(8,128)(2,1)}, bf16[1024,1024]{1,0:T(8,128)(2,1)}, u32[]{:S(2)}, u32[]{:S(2)}) %collective-permute-start.15) | collective-permute-done | bytes 2097184 | tf_op jit(solution)/shard_map/ppermute | solution.py:900
  376.7 15.5 %shard_map.242 = (bf16[8,4,32,3200]{3,2,1,0:T(8,128)(2,1)}, bf16[1024,1024]{1,0:T(8,128)(2,1)}, bf16[1024,1024]{1,0:T(8,128)(2,1)}) custom-call(bf16[1024,1024]{1,0:T(8,128)(2,1)} %get-tuple-element.87.refs_0_, bf16[1024,1024]{1,0:T(8,128)(2,1)} %get-tuple-element.90.refs_1_.refs_0_, ...), custom_call_target="tpu_custom_call", output_to_operand_aliasing={{1}: (9, {}), {2}: (10, {})} | custom-call | flops 6204000256 | bytes 1000000 | tf_op jit(solution)/shard_map/pallas_call | solution.py:74
  393.5 7.1 %all-to-all-start.4 = ((bf16[8,4,32,3200]{3,2,1,0:T(8,128)(2,1)}), bf16[8,4,32,3200]{3,2,1,0:T(8,128)(2,1)}, u32[]{:S(2)}, u32[]{:S(2)}) async-start(bf16[8,4,32,3200]{3,2,1,0:T(8,128)(2,1)} %get-tuple-element.100.refs_11_), calls=%async_computation.4 | async-start | bytes 13107200 | tf_op jit(solution)/shard_map/all_to_all | solution.py:879
  400.6 7.0 %collective-permute-start.16 = (bf16[1024,1024]{1,0:T(8,128)(2,1)}, bf16[1024,1024]{1,0:T(8,128)(2,1)S(1)}, u32[]{:S(2)}, u32[]{:S(2)}) collective-permute-start(bf16[1024,1024]{1,0:T(8,128)(2,1)} %refs_2_.1), channel_id=1, source_target_pairs={{0,8},{8,16},{16,24},{1,9},{9,17},{17,25},{2,10},{10,18},{18,26},{... | collective-permute-start | bytes 6291464 | tf_op jit(solution)/shard_map/ppermute | solution.py:899
  408.9 2.0 collective-permute-start.21
  412.2 16.8 %shard_map.243.refs_11_.refs_5_ = bf16[1024,1024]{1,0:T(8,128)(2,1)} custom-call(bf16[1024,1024]{1,0:T(8,128)(2,1)} %get-tuple-element.90.refs_1_.refs_0_, bf16[1024,1024]{1,0:T(8,128)(2,1)} %get-tuple-element.91.refs_2_.refs_1_, bf16[1024,1024]{1,0:T(8,128)(2,1)} %get-tuple-element.92.refs_3_.refs_2_, bf16[1024,1024]{1,0:T(8,128)(2,1)} %bitcast.56, ...), custom_call_target="tpu_custom_call" | custom-call | flops 8272000000 | bytes 1000000 | tf_op jit(solution)/shard_map/pallas_call | solution.py:74
  429.0 24.4 %collective-permute-done.16.refs_3_ = bf16[1024,1024]{1,0:T(8,128)(2,1)S(1)} collective-permute-done((bf16[1024,1024]{1,0:T(8,128)(2,1)}, bf16[1024,1024]{1,0:T(8,128)(2,1)S(1)}, u32[]{:S(2)}, u32[]{:S(2)}) %collective-permute-start.16) | collective-permute-done | bytes 2097184 | tf_op jit(solution)/shard_map/ppermute | solution.py:899
  453.3 6.2 %collective-permute-done.17.refs_4_ = bf16[1024,1024]{1,0:T(8,128)(2,1)} collective-permute-done((bf16[1024,1024]{1,0:T(8,128)(2,1)}, bf16[1024,1024]{1,0:T(8,128)(2,1)}, u32[]{:S(2)}, u32[]{:S(2)}) %collective-permute-start.17) | collective-permute-done | bytes 2097184 | tf_op jit(solution)/shard_map/ppermute | solution.py:900
  459.5 18.5 %shard_map.244 = (f32[1024,1024]{1,0:T(8,128)}, f32[1024,1024]{1,0:T(8,128)}) custom-call(s32[2]{0:T(128)} %pad_add_fusion.refs_0_, bf16[1024,1024]{1,0:T(8,128)(2,1)} %get-tuple-element.98.refs_1_, bf16[1024,1024]{1,0:T(8,128)(2,1)} %get-tuple-element.99.refs_2_, bf16[1024,1024]{1,0:T(8,128)(2,1)} %copy-done.21, ...), custom_call_target="tpu_custom_call" | custom-call | flops 9306000384 | bytes 1000000 | tf_op jit(solution)/shard_map/pallas_call | solution.py:74
  478.0 18.8 %shard_map.245 = (f32[1024,1024]{1,0:T(8,128)}, f32[1024,1024]{1,0:T(8,128)}) custom-call(s32[2]{0:T(128)} %pad_add_fusion.refs_0_, bf16[1024,1024]{1,0:T(8,128)(2,1)} %get-tuple-element.101.refs_1_, bf16[1024,1024]{1,0:T(8,128)(2,1)} %get-tuple-element.102.refs_2_, bf16[4,1024,1024]{2,1,0:T(8,128)(2,1)} %bitcast.29, bf16[4,1024,1024]{2,1,0:T(8,128)(2,1)} %bitcast.30, ...), custom_call_target="tpu_custom_call" | custom-call | flops 9306000384 | bytes 1000000 | tf_op jit(solution)/shard_map/pallas_call | solution.py:74
  496.8 6.5 %shard_map.246 = (f32[32,4224]{1,0:T(8,128)}, bf16[32,4224]{1,0:T(8,128)(2,1)}, bf16[32,4224]{1,0:T(8,128)(2,1)}, bf16[32,4224]{1,0:T(8,128)(2,1)}, bf16[1024,1024]{1,0:T(8,128)(2,1)}) custom-call(s32[2]{0:T(128)} %pad_add_fusion.refs_0_, bf16[8,4,32,1024]{3,2,1,0:T(8,128)(2,1)} %copy-done.1, ...), custom_call_target="tpu_custom_call", output_to_operand_aliasing={{4}: (5, {})} | custom-call | flops 2584999936 | bytes 1000000 | tf_op jit(solution)/shard_map/pallas_call | solution.py:74
  503.3 4.4 all-to-all-start.5
  507.7 11.9 %collective-permute-start.18 = (bf16[32,4224]{1,0:T(8,128)(2,1)S(1)}, bf16[32,4224]{1,0:T(8,128)(2,1)S(1)}, u32[]{:S(2)}, u32[]{:S(2)}) collective-permute-start(bf16[32,4224]{1,0:T(8,128)(2,1)S(1)} %copy-done.9), channel_id=1, source_target_pairs={{0,8},{8,16},{16,24},{24,0},{1,9},{9,17},{17,25},{25,1},{2,10},{10... | collective-permute-start | bytes 811016 | tf_op jit(solution)/shard_map/ppermute | solution.py:876
  519.6 2.6 collective-permute-start.20
  522.2 20.2 %shard_map.248 = (f32[1024,1024]{1,0:T(8,128)}, f32[1024,1024]{1,0:T(8,128)}) custom-call(s32[2]{0:T(128)} %pad_add_fusion.refs_0_, bf16[1024,1024]{1,0:T(8,128)(2,1)} %collective-permute-done.21.refs_1_, bf16[1024,1024]{1,0:T(8,128)(2,1)} %collective-permute-done.22.refs_2_, bf16[4,1024,1024]{2,1,0:T(8,128)(2,1)} %bitcast.31, ...), custom_call_target="tpu_custom_call" | custom-call | flops 9306000384 | bytes 1000000 | tf_op jit(solution)/shard_map/pallas_call | solution.py:74
  543.9 2.1 shard_map.247
  (105 shorter events, 17.0 us)
Async XLA Ops:
  7.2 5.4 copy-start.17
  7.2 5.4 copy-start.18
  7.2 5.4 copy-start.19
  7.2 5.4 copy-start.20
  7.2 5.8 %copy-start.12 = (bf16[32,1024]{1,0:T(8,128)(2,1)S(1)}, bf16[32,1024]{1,0:T(8,128)(2,1)}, u32[]{:S(2)}) copy-start(bf16[32,1024]{1,0:T(8,128)(2,1)} %param.18) | copy-start | bytes 196612
  7.2 5.8 %copy-start.13 = (bf16[32,1024]{1,0:T(8,128)(2,1)S(1)}, bf16[32,1024]{1,0:T(8,128)(2,1)}, u32[]{:S(2)}) copy-start(bf16[32,1024]{1,0:T(8,128)(2,1)} %param.19) | copy-start | bytes 196612
  7.2 5.9 %copy-start.14 = (bf16[32,1024]{1,0:T(8,128)(2,1)S(1)}, bf16[32,1024]{1,0:T(8,128)(2,1)}, u32[]{:S(2)}) copy-start(bf16[32,1024]{1,0:T(8,128)(2,1)} %param.20) | copy-start | bytes 196612
  7.3 5.9 %copy-start.15 = (bf16[32,1024]{1,0:T(8,128)(2,1)S(1)}, bf16[32,1024]{1,0:T(8,128)(2,1)}, u32[]{:S(2)}) copy-start(bf16[32,1024]{1,0:T(8,128)(2,1)} %param.21) | copy-start | bytes 196612
  7.3 32.0 %all-to-all-start = ((bf16[8,128,1024]{2,1,0:T(8,128)(2,1)}), bf16[8,128,1024]{2,1,0:T(8,128)(2,1)S(1)}, u32[]{:S(2)}, u32[]{:S(2)}) async-start(bf16[8,128,1024]{2,1,0:T(8,128)(2,1)} %bitcast.42), calls=%async_computation | async-start | bytes 4194304 | tf_op jit(solution)/shard_map/all_to_all | solution.py:879
  12.6 88.0 %all-gather.5.cloned.1.call-start = ((), (), s32[]{:S(2)}) async-start(), calls=%async_computation.6 | async-start | bytes 4718592 | tf_op jit(solution)/shard_map/all_gather | solution.py:924
  13.1 19.8 %copy-start.3 = (bf16[144,1024]{1,0:T(8,128)(2,1)}, bf16[144,1024]{1,0:T(8,128)(2,1)S(1)}, u32[]{:S(2)}) copy-start(bf16[144,1024]{1,0:T(8,128)(2,1)S(1)} %constant_dynamic-update-slice_fusion.refs_0_) | copy-start | bytes 884740
  13.2 26.1 %collective-permute-start = (bf16[144,1024]{1,0:T(8,128)(2,1)S(1)}, bf16[144,1024]{1,0:T(8,128)(2,1)S(1)}, u32[]{:S(2)}, u32[]{:S(2)}) collective-permute-start(bf16[144,1024]{1,0:T(8,128)(2,1)S(1)} %constant_dynamic-update-slice_fusion.refs_0_), channel_id=1, source_target_pairs={{0,8},{8,16},{16,24},{24,0},{1,9},{9,17},{17,25},{25,1},{2,10},{10... | collective-permute-start | bytes 884744 | tf_op jit(solution)/shard_map/ppermute | solution.py:876
  14.8 24.5 %collective-permute-start.1 = (bf16[144,1024]{1,0:T(8,128)(2,1)S(1)}, bf16[144,1024]{1,0:T(8,128)(2,1)S(1)}, u32[]{:S(2)}, u32[]{:S(2)}) collective-permute-start(bf16[144,1024]{1,0:T(8,128)(2,1)S(1)} %constant_dynamic-update-slice_fusion.refs_0_), channel_id=1, source_target_pairs={{0,16},{8,24},{16,0},{24,8},{1,17},{9,25},{17,1},{25,9},{2,18},{10... | collective-permute-start | bytes 884744 | tf_op jit(solution)/shard_map/ppermute | solution.py:876
  17.4 21.9 %collective-permute-start.2 = (bf16[144,1024]{1,0:T(8,128)(2,1)S(1)}, bf16[144,1024]{1,0:T(8,128)(2,1)S(1)}, u32[]{:S(2)}, u32[]{:S(2)}) collective-permute-start(bf16[144,1024]{1,0:T(8,128)(2,1)S(1)} %constant_dynamic-update-slice_fusion.refs_0_), channel_id=1, source_target_pairs={{0,24},{8,0},{16,8},{24,16},{1,25},{9,1},{17,9},{25,17},{2,26},{10... | collective-permute-start | bytes 884744 | tf_op jit(solution)/shard_map/ppermute | solution.py:876
  39.3 1.6 copy-start
  43.2 434.8 %all-gather.7.cloned.1.call-start = ((), (), s32[]{:S(2)}) async-start(), calls=%async_computation.7 | async-start | bytes 10485760 | tf_op jit(solution)/shard_map/all_gather | solution.py:947
  43.2 21.6 %collective-permute-start.4 = (bf16[4,80,1024]{2,1,0:T(8,128)(2,1)}, bf16[4,80,1024]{2,1,0:T(8,128)(2,1)S(1)}, u32[]{:S(2)}, u32[]{:S(2)}) collective-permute-start(bf16[4,80,1024]{2,1,0:T(8,128)(2,1)} %get-tuple-element.69.refs_3_.refs_11_.refs_19_), channel_id=1, source_target_pairs={{0,2},{1,3},{2,0},{3,1},{4,6},{5,7},{6,4},{7,5},{8,10},{9,11},{10,... | collective-permute-start | bytes 1966088 | tf_op jit(solution)/shard_map/ppermute | solution.py:873
  45.5 22.9 %collective-permute-start.6 = (bf16[4,80,1024]{2,1,0:T(8,128)(2,1)}, bf16[4,80,1024]{2,1,0:T(8,128)(2,1)S(1)}, u32[]{:S(2)}, u32[]{:S(2)}) collective-permute-start(bf16[4,80,1024]{2,1,0:T(8,128)(2,1)} %get-tuple-element.69.refs_3_.refs_11_.refs_19_), channel_id=1, source_target_pairs={{0,4},{1,5},{2,6},{3,7},{4,0},{5,1},{6,2},{7,3},{8,12},{9,13},{10,... | collective-permute-start | bytes 1966088 | tf_op jit(solution)/shard_map/ppermute | solution.py:873
  64.9 17.3 %copy-start.10 = (bf16[4,80,1024]{2,1,0:T(8,128)(2,1)}, bf16[4,80,1024]{2,1,0:T(8,128)(2,1)S(1)}, u32[]{:S(2)}) copy-start(bf16[4,80,1024]{2,1,0:T(8,128)(2,1)S(1)} %collective-permute-done.4.refs_5_.refs_13_.refs_21_) | copy-start | bytes 1966084
  64.9 10.8 %collective-permute-start.10 = (bf16[4,48,1024]{2,1,0:T(8,128)(2,1)S(1)}, bf16[4,48,1024]{2,1,0:T(8,128)(2,1)}, u32[]{:S(2)}, u32[]{:S(2)}) collective-permute-start(bf16[4,48,1024]{2,1,0:T(8,128)(2,1)S(1)} %slice.9), channel_id=1, source_target_pairs={{0,4},{1,5},{2,6},{3,7},{4,0},{5,1},{6,2},{7,3},{8,12},{9,13},{10,... | collective-permute-start | bytes 1179656 | tf_op jit(solution)/shard_map/ppermute | solution.py:873
  66.2 17.6 %collective-permute-start.3 = (bf16[4,80,1024]{2,1,0:T(8,128)(2,1)}, bf16[4,80,1024]{2,1,0:T(8,128)(2,1)S(1)}, u32[]{:S(2)}, u32[]{:S(2)}) collective-permute-start(bf16[4,80,1024]{2,1,0:T(8,128)(2,1)} %get-tuple-element.69.refs_3_.refs_11_.refs_19_), channel_id=1, source_target_pairs={{0,1},{1,0},{2,3},{3,2},{4,5},{5,4},{6,7},{7,6},{8,9},{9,8},{10,11... | collective-permute-start | bytes 1966088 | tf_op jit(solution)/shard_map/ppermute | solution.py:873
  66.2 17.6 %collective-permute-start.5 = (bf16[4,80,1024]{2,1,0:T(8,128)(2,1)S(1)}, bf16[4,80,1024]{2,1,0:T(8,128)(2,1)S(1)}, u32[]{:S(2)}, u32[]{:S(2)}) collective-permute-start(bf16[4,80,1024]{2,1,0:T(8,128)(2,1)S(1)} %collective-permute-done.4.refs_5_.refs_13_.refs_21_), channel_id=1, source_target_pairs={{0,1},{1,0},{2,3},{3,2},{4,5},{5,4},{6,7},{7,6},{8,9},{9,8},{10,11... | collective-permute-start | bytes 1966088 | tf_op jit(solution)/shard_map/ppermute | solution.py:873
  68.4 13.8 %copy-start.11 = (bf16[4,80,1024]{2,1,0:T(8,128)(2,1)}, bf16[4,80,1024]{2,1,0:T(8,128)(2,1)S(1)}, u32[]{:S(2)}) copy-start(bf16[4,80,1024]{2,1,0:T(8,128)(2,1)S(1)} %collective-permute-done.6.refs_7_.refs_15_.refs_23_) | copy-start | bytes 1966084
  68.4 15.5 %collective-permute-start.7 = (bf16[4,80,1024]{2,1,0:T(8,128)(2,1)S(1)}, bf16[4,80,1024]{2,1,0:T(8,128)(2,1)S(1)}, u32[]{:S(2)}, u32[]{:S(2)}) collective-permute-start(bf16[4,80,1024]{2,1,0:T(8,128)(2,1)S(1)} %collective-permute-done.6.refs_7_.refs_15_.refs_23_), channel_id=1, source_target_pairs={{0,1},{1,0},{2,3},{3,2},{4,5},{5,4},{6,7},{7,6},{8,9},{9,8},{10,11... | collective-permute-start | bytes 1966088 | tf_op jit(solution)/shard_map/ppermute | solution.py:873
  68.4 13.7 %copy-start.16 = (s32[1,1024]{1,0:T(1,128)S(1)}, s32[1,1024]{1,0:T(1,128)}, u32[]{:S(2)}) copy-start(s32[1,1024]{1,0:T(1,128)} %refs_9_.1) | copy-start | bytes 12292
  68.4 10.6 %collective-permute-start.8 = (bf16[4,32,1024]{2,1,0:T(8,128)(2,1)S(1)}, bf16[4,32,1024]{2,1,0:T(8,128)(2,1)}, u32[]{:S(2)}, u32[]{:S(2)}) collective-permute-start(bf16[4,32,1024]{2,1,0:T(8,128)(2,1)S(1)} %slice.8), channel_id=1, source_target_pairs={{0,2},{1,3},{2,0},{3,1},{4,6},{5,7},{6,4},{7,5},{8,10},{9,11},{10,... | collective-permute-start | bytes 786440 | tf_op jit(solution)/shard_map/ppermute | solution.py:873
  75.7 8.2 %collective-permute-start.11 = (bf16[4,48,1024]{2,1,0:T(8,128)(2,1)}, bf16[4,48,1024]{2,1,0:T(8,128)(2,1)}, u32[]{:S(2)}, u32[]{:S(2)}) collective-permute-start(bf16[4,48,1024]{2,1,0:T(8,128)(2,1)} %collective-permute-done.10.refs_17_.refs_25_), channel_id=1, source_target_pairs={{0,1},{1,0},{2,3},{3,2},{4,5},{5,4},{6,7},{7,6},{8,9},{9,8},{10,11... | collective-permute-start | bytes 1179656 | tf_op jit(solution)/shard_map/ppermute | solution.py:873
  79.0 4.9 collective-permute-start.9
  181.7 101.3 %collective-permute-start.12 = (bf16[1024,1024]{1,0:T(8,128)(2,1)}, bf16[1024,1024]{1,0:T(8,128)(2,1)}, u32[]{:S(2)}, u32[]{:S(2)}) collective-permute-start(bf16[1024,1024]{1,0:T(8,128)(2,1)} %bitcast.13.refs_0_.refs_1_), channel_id=1, source_target_pairs={{0,8},{8,16},{16,24},{1,9},{9,17},{17,25},{2,10},{10,18},{18,26},{... | collective-permute-start | bytes 6291464 | tf_op jit(solution)/shard_map/ppermute | solution.py:899
  193.6 112.7 %collective-permute-start.13 = (bf16[1024,1024]{1,0:T(8,128)(2,1)}, bf16[1024,1024]{1,0:T(8,128)(2,1)}, u32[]{:S(2)}, u32[]{:S(2)}) collective-permute-start(bf16[1024,1024]{1,0:T(8,128)(2,1)} %bitcast.13.refs_0_.refs_1_), channel_id=1, source_target_pairs={{8,0},{16,8},{24,16},{9,1},{17,9},{25,17},{10,2},{18,10},{26,18},{... | collective-permute-start | bytes 6291464 | tf_op jit(solution)/shard_map/ppermute | solution.py:900
  225.3 101.8 %all-to-all-start.2 = ((bf16[8,128,1024]{2,1,0:T(8,128)(2,1)}), bf16[8,128,1024]{2,1,0:T(8,128)(2,1)S(1)}, u32[]{:S(2)}, u32[]{:S(2)}) async-start(bf16[8,128,1024]{2,1,0:T(8,128)(2,1)} %bitcast.44), calls=%async_computation.2 | async-start | bytes 4194304 | tf_op jit(solution)/shard_map/all_to_all | solution.py:879
  323.8 39.3 %collective-permute-start.14 = (bf16[1024,1024]{1,0:T(8,128)(2,1)}, bf16[1024,1024]{1,0:T(8,128)(2,1)}, u32[]{:S(2)}, u32[]{:S(2)}) collective-permute-start(bf16[1024,1024]{1,0:T(8,128)(2,1)} %get-tuple-element.98.refs_1_), channel_id=1, source_target_pairs={{8,16},{16,24},{9,17},{17,25},{10,18},{18,26},{11,19},{19,27},{12,... | collective-permute-start | bytes 6291464 | tf_op jit(solution)/shard_map/ppermute | solution.py:899
  325.8 50.9 %collective-permute-start.15 = (bf16[1024,1024]{1,0:T(8,128)(2,1)}, bf16[1024,1024]{1,0:T(8,128)(2,1)}, u32[]{:S(2)}, u32[]{:S(2)}) collective-permute-start(bf16[1024,1024]{1,0:T(8,128)(2,1)} %get-tuple-element.99.refs_2_), channel_id=1, source_target_pairs={{8,0},{16,8},{9,1},{17,9},{10,2},{18,10},{11,3},{19,11},{12,4},{20... | collective-permute-start | bytes 6291464 | tf_op jit(solution)/shard_map/ppermute | solution.py:900
  327.1 1.4 copy-start.2
  343.0 49.1 %all-to-all-start.3 = ((bf16[8,4,32,1024]{3,2,1,0:T(8,128)(2,1)}), bf16[8,4,32,1024]{3,2,1,0:T(8,128)(2,1)S(1)}, u32[]{:S(2)}, u32[]{:S(2)}) async-start(bf16[8,4,32,1024]{3,2,1,0:T(8,128)(2,1)} %shard_map.240.refs_7_), calls=%async_computation.3 | async-start | bytes 4194304 | tf_op jit(solution)/shard_map/all_to_all | solution.py:879
  393.5 103.3 %all-to-all-start.4 = ((bf16[8,4,32,3200]{3,2,1,0:T(8,128)(2,1)}), bf16[8,4,32,3200]{3,2,1,0:T(8,128)(2,1)}, u32[]{:S(2)}, u32[]{:S(2)}) async-start(bf16[8,4,32,3200]{3,2,1,0:T(8,128)(2,1)} %get-tuple-element.100.refs_11_), calls=%async_computation.4 | async-start | bytes 13107200 | tf_op jit(solution)/shard_map/all_to_all | solution.py:879
  400.6 52.8 %collective-permute-start.16 = (bf16[1024,1024]{1,0:T(8,128)(2,1)}, bf16[1024,1024]{1,0:T(8,128)(2,1)S(1)}, u32[]{:S(2)}, u32[]{:S(2)}) collective-permute-start(bf16[1024,1024]{1,0:T(8,128)(2,1)} %refs_2_.1), channel_id=1, source_target_pairs={{0,8},{8,16},{16,24},{1,9},{9,17},{17,25},{2,10},{10,18},{18,26},{... | collective-permute-start | bytes 6291464 | tf_op jit(solution)/shard_map/ppermute | solution.py:899
  407.6 51.9 %collective-permute-start.17 = (bf16[1024,1024]{1,0:T(8,128)(2,1)}, bf16[1024,1024]{1,0:T(8,128)(2,1)}, u32[]{:S(2)}, u32[]{:S(2)}) collective-permute-start(bf16[1024,1024]{1,0:T(8,128)(2,1)} %refs_2_.1), channel_id=1, source_target_pairs={{8,0},{16,8},{24,16},{9,1},{17,9},{25,17},{10,2},{18,10},{26,18},{... | collective-permute-start | bytes 6291464 | tf_op jit(solution)/shard_map/ppermute | solution.py:900
  408.9 113.3 %collective-permute-start.21 = (bf16[1024,1024]{1,0:T(8,128)(2,1)}, bf16[1024,1024]{1,0:T(8,128)(2,1)}, u32[]{:S(2)}, u32[]{:S(2)}) collective-permute-start(bf16[1024,1024]{1,0:T(8,128)(2,1)} %get-tuple-element.101.refs_1_), channel_id=1, source_target_pairs={{16,24},{17,25},{18,26},{19,27},{20,28},{21,29},{22,30},{23,31}} | collective-permute-start | bytes 6291464 | tf_op jit(solution)/shard_map/ppermute | solution.py:899
  410.9 111.3 %collective-permute-start.22 = (bf16[1024,1024]{1,0:T(8,128)(2,1)}, bf16[1024,1024]{1,0:T(8,128)(2,1)}, u32[]{:S(2)}, u32[]{:S(2)}) collective-permute-start(bf16[1024,1024]{1,0:T(8,128)(2,1)} %get-tuple-element.102.refs_2_), channel_id=1, source_target_pairs={{8,0},{9,1},{10,2},{11,3},{12,4},{13,5},{14,6},{15,7}} | collective-permute-start | bytes 6291464 | tf_op jit(solution)/shard_map/ppermute | solution.py:900
  453.3 6.2 %copy-start.21 = (bf16[1024,1024]{1,0:T(8,128)(2,1)}, bf16[1024,1024]{1,0:T(8,128)(2,1)S(1)}, u32[]{:S(2)}) copy-start(bf16[1024,1024]{1,0:T(8,128)(2,1)S(1)} %collective-permute-done.16.refs_3_) | copy-start | bytes 6291460
  503.3 4.4 copy-start.9
  503.3 16.3 %copy-start.8 = (bf16[32,4224]{1,0:T(8,128)(2,1)S(1)}, bf16[32,4224]{1,0:T(8,128)(2,1)}, u32[]{:S(2)}) copy-start(bf16[32,4224]{1,0:T(8,128)(2,1)} %get-tuple-element.112.refs_13_) | copy-start | bytes 811012
  503.3 16.3 %copy-start.7 = (bf16[32,4224]{1,0:T(8,128)(2,1)S(1)}, bf16[32,4224]{1,0:T(8,128)(2,1)}, u32[]{:S(2)}) copy-start(bf16[32,4224]{1,0:T(8,128)(2,1)} %get-tuple-element.113.refs_14_) | copy-start | bytes 811012
  503.3 42.7 %all-to-all-start.5 = ((bf16[8,128,1024]{2,1,0:T(8,128)(2,1)}), bf16[8,128,1024]{2,1,0:T(8,128)(2,1)S(1)}, u32[]{:S(2)}, u32[]{:S(2)}) async-start(bf16[8,128,1024]{2,1,0:T(8,128)(2,1)} %bitcast.41), calls=%async_computation.5 | async-start | bytes 4194304 | tf_op jit(solution)/shard_map/all_to_all | solution.py:879
  507.7 34.7 %collective-permute-start.18 = (bf16[32,4224]{1,0:T(8,128)(2,1)S(1)}, bf16[32,4224]{1,0:T(8,128)(2,1)S(1)}, u32[]{:S(2)}, u32[]{:S(2)}) collective-permute-start(bf16[32,4224]{1,0:T(8,128)(2,1)S(1)} %copy-done.9), channel_id=1, source_target_pairs={{0,8},{8,16},{16,24},{24,0},{1,9},{9,17},{17,25},{25,1},{2,10},{10... | collective-permute-start | bytes 811016 | tf_op jit(solution)/shard_map/ppermute | solution.py:876
  519.6 22.8 %collective-permute-start.19 = (bf16[32,4224]{1,0:T(8,128)(2,1)S(1)}, bf16[32,4224]{1,0:T(8,128)(2,1)S(1)}, u32[]{:S(2)}, u32[]{:S(2)}) collective-permute-start(bf16[32,4224]{1,0:T(8,128)(2,1)S(1)} %copy-done.8), channel_id=1, source_target_pairs={{0,16},{8,24},{16,0},{24,8},{1,17},{9,25},{17,1},{25,9},{2,18},{10... | collective-permute-start | bytes 811016 | tf_op jit(solution)/shard_map/ppermute | solution.py:876
  519.6 22.8 %collective-permute-start.20 = (bf16[32,4224]{1,0:T(8,128)(2,1)S(1)}, bf16[32,4224]{1,0:T(8,128)(2,1)S(1)}, u32[]{:S(2)}, u32[]{:S(2)}) collective-permute-start(bf16[32,4224]{1,0:T(8,128)(2,1)S(1)} %copy-done.7), channel_id=1, source_target_pairs={{0,24},{8,0},{16,8},{24,16},{1,25},{9,1},{17,9},{25,17},{2,26},{10... | collective-permute-start | bytes 811016 | tf_op jit(solution)/shard_map/ppermute | solution.py:876
  (10 other events, 9.1 us)
Sparse Core Ops, SparseCore 0:
  43.3 46.6 all-gather.4
  107.8 196.6 all-gather.6
